TPU v7x, 32 devices: a whole 2x2x4 slice. The times are simulated.
32 devices in a mesh: narrow: 4 (over x, core), wide: 8 (over z, y).
Axes of the slice: x: 2, y: 2, z: 4, core: 2. Of those that a mesh axis runs over, the one named last changes fastest.
Arguments:
- token_ids: int32 [16384], P(('narrow', 'wide')), may hold values from 0 to 50303
- seq_lengths: int32 [32], P(('narrow', 'wide')), may hold values from 128 to 512, as said below
- loss_slots: int32 [1024], P(('narrow', 'wide')), may hold values from -1 to 511, as said below
- target_ids: int32 [1024], P(('narrow', 'wide')), may hold values from 0 to 50303
- step_count: int32 [], replicated, may hold values from 2 to 20
- w_qkv: float32 [2, 1024, 3072], P(None, ('narrow', 'wide')), may hold values from -0.1875 to 0.1875
- w_out: float32 [2, 1024, 1024], P(None, ('narrow', 'wide')), may hold values from -0.75 to 0.75
- w_fc: float32 [2, 1024, 4096], P(None, ('narrow', 'wide')), may hold values from -0.1875 to 0.1875
- w_proj: float32 [2, 4096, 1024], P(None, ('narrow', 'wide')), may hold values from -0.09375 to 0.09375
- vectors: float32 [26624], P(('narrow', 'wide'))
- pos_table: float32 [1024, 1024], P(('narrow', 'wide')), may hold values from -0.6 to 0.6
- embed_table: float32 [50304, 1024], P(('narrow', 'wide')), may hold values from -1 to 1
- mom_qkv: float32 [2, 1024, 3072], P(None, ('narrow', 'wide')), may hold values from -1.4305115e-06 to 1.4305115e-06
- mom_out: float32 [2, 1024, 1024], P(None, ('narrow', 'wide')), may hold values from -1.4305115e-06 to 1.4305115e-06
- mom_fc: float32 [2, 1024, 4096], P(None, ('narrow', 'wide')), may hold values from -1.4305115e-06 to 1.4305115e-06
- mom_proj: float32 [2, 4096, 1024], P(None, ('narrow', 'wide')), may hold values from -1.4305115e-06 to 1.4305115e-06
- mom_vectors: float32 [26624], P(('narrow', 'wide')), may hold values from -5.722046e-06 to 5.722046e-06
- mom_pos: float32 [1024, 1024], P(('narrow', 'wide')), may hold values from -1.4305115e-06 to 1.4305115e-06
- mom_embed: float32 [50304, 1024], P(('narrow', 'wide')), may hold values from -1.4305115e-06 to 1.4305115e-06
- sec_qkv: float32 [2, 1024, 3072], P(None, ('narrow', 'wide')), may hold values from 5.144541e-14 to 2.0578164e-13
- sec_out: float32 [2, 1024, 1024], P(None, ('narrow', 'wide')), may hold values from 5.144541e-14 to 2.0578164e-13
- sec_fc: float32 [2, 1024, 4096], P(None, ('narrow', 'wide')), may hold values from 5.144541e-14 to 2.0578164e-13
- sec_proj: float32 [2, 4096, 1024], P(None, ('narrow', 'wide')), may hold values from 5.144541e-14 to 2.0578164e-13
- sec_vectors: float32 [26624], P(('narrow', 'wide')), may hold values from 8.2312656e-13 to 3.2925062e-12
- sec_pos: float32 [1024, 1024], P(('narrow', 'wide')), may hold values from 5.144541e-14 to 2.0578164e-13
- sec_embed: float32 [50304, 1024], P(('narrow', 'wide')), may hold values from 5.144541e-14 to 2.0578164e-13
Outputs:
- loss: float32 [], replicated
- grad_norm: float32 [], replicated
- new_qkv: float32 [2, 1024, 3072], P(None, ('narrow', 'wide'))
- new_out: float32 [2, 1024, 1024], P(None, ('narrow', 'wide'))
- new_fc: float32 [2, 1024, 4096], P(None, ('narrow', 'wide'))
- new_proj: float32 [2, 4096, 1024], P(None, ('narrow', 'wide'))
- new_vectors: float32 [26624], P(('narrow', 'wide'))
- new_pos: float32 [1024, 1024], P(('narrow', 'wide'))
- new_embed: float32 [50304, 1024], P(('narrow', 'wide'))
- first_qkv: float32 [2, 1024, 3072], P(None, ('narrow', 'wide'))
- first_out: float32 [2, 1024, 1024], P(None, ('narrow', 'wide'))
- first_fc: float32 [2, 1024, 4096], P(None, ('narrow', 'wide'))
- first_proj: float32 [2, 4096, 1024], P(None, ('narrow', 'wide'))
- first_vectors: float32 [26624], P(('narrow', 'wide'))
- first_pos: float32 [1024, 1024], P(('narrow', 'wide'))
- first_embed: float32 [50304, 1024], P(('narrow', 'wide'))
- second_qkv: float32 [2, 1024, 3072], P(None, ('narrow', 'wide'))
- second_out: float32 [2, 1024, 1024], P(None, ('narrow', 'wide'))
- second_fc: float32 [2, 1024, 4096], P(None, ('narrow', 'wide'))
- second_proj: float32 [2, 4096, 1024], P(None, ('narrow', 'wide'))
- second_vectors: float32 [26624], P(('narrow', 'wide'))
- second_pos: float32 [1024, 1024], P(('narrow', 'wide'))
- second_embed: float32 [50304, 1024], P(('narrow', 'wide'))
Inputs may be any that keep to these rules, and one draw needn't show every extreme that they name: `seq_lengths`: the last sequence has 512 tokens. `loss_slots`: each sequence owns 32 consecutive slots; a used slot holds a position below that sequence's length, an unused one holds -1; the first slot of every sequence is used and holds its last position; the last sequence uses all of its slots.
All inputs are finite; a program needn't handle non-finite values.
Results may differ from a plain program's by a relative error of at most 0.005.
The roundings to bfloat16 on the way count: a program that leaves them out, or rounds other values in their place, can miss the bound.
Values may be sent and summed in bfloat16 or wider, within the bound.
A program may use at most 384 MiB of HBM per device.

v0:
```python
import jax
import jax.numpy as jnp
from jax import lax
from jax.sharding import PartitionSpec as P

D = 1024
HEADS = 16
HD = 64
FF = 4096
POS = 1024
LAYERS = 2
LEN = 512
LOSS_DEV = 32


CLIP_LIMIT = 0.002
RATE_MATRIX = 0.03
RATE_VECTOR = 0.3
DECAY_MATRIX = 0.1


def joined(part, axis, combine):
    gathered = jax.tree.map(lambda a: lax.all_gather(a, axis), part)

    def take(source):
        return jax.tree.map(lambda a: lax.dynamic_index_in_dim(a, source, 0, False), gathered)

    return lax.fori_loop(
        1, lax.axis_size(axis), lambda source, state: combine(state, take(source)), take(0)
    )


def layer_norm(values, gain, shift):
    center = values - jnp.mean(values, axis=-1, keepdims=True)
    spread = jnp.mean(center * center, axis=-1, keepdims=True)
    return center * lax.rsqrt(spread + 1e-05) * gain + shift


def gelu_tanh(values):
    return jax.nn.gelu(values, approximate=True)


def fetch_layer(w_qkv, w_out, w_fc, w_proj, layer_at):
    return (
        lax.all_gather(
            w_qkv[layer_at].astype(jnp.bfloat16), ("narrow", "wide"), axis=0, tiled=True
        ),
        lax.all_gather(
            w_out[layer_at].astype(jnp.bfloat16), ("narrow", "wide"), axis=0, tiled=True
        ),
        lax.all_gather(w_fc[layer_at].astype(jnp.bfloat16), ("narrow", "wide"), axis=0, tiled=True),
        lax.all_gather(
            w_proj[layer_at].astype(jnp.bfloat16), ("narrow", "wide"), axis=0, tiled=True
        ),
    )


def reduce_layer(grad_wqkv, grad_wout, grad_wfc, grad_wproj):
    return (
        lax.psum_scatter(grad_wqkv, ("narrow", "wide"), scatter_dimension=0, tiled=True),
        lax.psum_scatter(grad_wout, ("narrow", "wide"), scatter_dimension=0, tiled=True),
        lax.psum_scatter(grad_wfc, ("narrow", "wide"), scatter_dimension=0, tiled=True),
        lax.psum_scatter(grad_wproj, ("narrow", "wide"), scatter_dimension=0, tiled=True),
    )


def attention_mask(seq_length):
    positions = jnp.arange(LEN)
    return (positions[None, :] <= positions[:, None]) & (positions[None, :] < seq_length)


def attention_scores(query_rows, key_rows, allowed):
    scores = (
        jnp.einsum("qhd,khd->hqk", query_rows, key_rows, preferred_element_type=jnp.float32) * 0.125
    )
    return jnp.where(allowed[None], scores, -1e30)


def layer_forward(stream, weights, vector, allowed):
    w_qkv, w_out, w_fc, w_proj = weights
    normed_low = layer_norm(stream, vector[0:D], vector[D : 2 * D]).astype(jnp.bfloat16)
    qkv_bias = jnp.concatenate(
        [vector[4 * D : 5 * D], jnp.zeros((D,), jnp.float32), vector[5 * D : 6 * D]]
    )
    projected = (jnp.dot(normed_low, w_qkv, preferred_element_type=jnp.float32) + qkv_bias).astype(
        jnp.bfloat16
    )
    heads_view = projected.reshape(LEN, 3, HEADS, HD)
    scores = attention_scores(heads_view[:, 0], heads_view[:, 1], allowed)
    row_max = jnp.max(scores, axis=-1, keepdims=True)
    log_total = row_max + jnp.log(jnp.sum(jnp.exp(scores - row_max), axis=-1, keepdims=True))
    attn_probs = jnp.exp(scores - log_total).astype(jnp.bfloat16)
    mixed_low = jnp.einsum(
        "hqk,khd->qhd", attn_probs, heads_view[:, 2], preferred_element_type=jnp.float32
    )
    mixed_low = mixed_low.reshape(LEN, D).astype(jnp.bfloat16)
    stream_mid = (
        stream
        + jnp.dot(mixed_low, w_out, preferred_element_type=jnp.float32)
        + vector[6 * D : 7 * D]
    )
    normed_two = layer_norm(stream_mid, vector[2 * D : 3 * D], vector[3 * D : 4 * D]).astype(
        jnp.bfloat16
    )
    hidden_pre = (
        jnp.dot(normed_two, w_fc, preferred_element_type=jnp.float32) + vector[8 * D : 8 * D + FF]
    )
    hidden_low = gelu_tanh(hidden_pre).astype(jnp.bfloat16)
    stream_out = (
        stream_mid
        + jnp.dot(hidden_low, w_proj, preferred_element_type=jnp.float32)
        + vector[7 * D : 8 * D]
    )
    return (
        stream_out,
        (
            stream,
            normed_low,
            projected,
            log_total,
            mixed_low,
            stream_mid,
            normed_two,
            hidden_pre,
            hidden_low,
        ),
    )


def layer_backward(grad_out, saved_acts, weights, vector, allowed):
    (
        stream,
        normed_low,
        projected,
        log_total,
        mixed_low,
        stream_mid,
        normed_two,
        hidden_pre,
        hidden_low,
    ) = saved_acts
    w_qkv, w_out, w_fc, w_proj = weights
    branch_low = grad_out.astype(jnp.bfloat16)
    grad_wproj = jnp.dot(hidden_low.T, branch_low, preferred_element_type=jnp.float32)
    grad_hidden = jnp.dot(branch_low, w_proj.T, preferred_element_type=jnp.float32)
    pre_low = jax.vjp(gelu_tanh, hidden_pre)[1](grad_hidden)[0].astype(jnp.bfloat16)
    grad_wfc = jnp.dot(normed_two.T, pre_low, preferred_element_type=jnp.float32)
    grad_normed_two = jnp.dot(pre_low, w_fc.T, preferred_element_type=jnp.float32)
    grad_mid, grad_gain_two, grad_shift_two = jax.vjp(
        layer_norm, stream_mid, vector[2 * D : 3 * D], vector[3 * D : 4 * D]
    )[1](grad_normed_two)
    grad_mid = grad_mid + grad_out
    attn_low = grad_mid.astype(jnp.bfloat16)
    grad_wout = jnp.dot(mixed_low.T, attn_low, preferred_element_type=jnp.float32)
    grad_mixed = (
        jnp.dot(attn_low, w_out.T, preferred_element_type=jnp.float32)
        .astype(jnp.bfloat16)
        .reshape(LEN, HEADS, HD)
    )
    heads_view = projected.reshape(LEN, 3, HEADS, HD)
    query_rows = heads_view[:, 0]
    key_rows = heads_view[:, 1]
    value_rows = heads_view[:, 2]
    attn_probs = jnp.exp(attention_scores(query_rows, key_rows, allowed) - log_total)
    grad_probs = jnp.einsum(
        "qhd,khd->hqk", grad_mixed, value_rows, preferred_element_type=jnp.float32
    )
    grad_values = jnp.einsum(
        "hqk,qhd->khd",
        attn_probs.astype(jnp.bfloat16),
        grad_mixed,
        preferred_element_type=jnp.float32,
    )
    row_dot = jnp.sum(grad_probs * attn_probs, axis=-1, keepdims=True)
    scores_low = (attn_probs * (grad_probs - row_dot)).astype(jnp.bfloat16)
    grad_queries = (
        jnp.einsum("hqk,khd->qhd", scores_low, key_rows, preferred_element_type=jnp.float32) * 0.125
    )
    grad_keys = (
        jnp.einsum("hqk,qhd->khd", scores_low, query_rows, preferred_element_type=jnp.float32)
        * 0.125
    )
    qkv_low = (
        jnp.stack([grad_queries, grad_keys, grad_values], axis=1)
        .reshape(LEN, 3 * D)
        .astype(jnp.bfloat16)
    )
    grad_wqkv = jnp.dot(normed_low.T, qkv_low, preferred_element_type=jnp.float32)
    grad_normed = jnp.dot(qkv_low, w_qkv.T, preferred_element_type=jnp.float32)
    grad_input, grad_gain_one, grad_shift_one = jax.vjp(
        layer_norm, stream, vector[0:D], vector[D : 2 * D]
    )[1](grad_normed)
    bias_qkv = jnp.sum(qkv_low.astype(jnp.float32), axis=0)
    grad_vector = jnp.concatenate(
        [
            grad_gain_one,
            grad_shift_one,
            grad_gain_two,
            grad_shift_two,
            bias_qkv[0:D],
            bias_qkv[2 * D : 3 * D],
            jnp.sum(attn_low.astype(jnp.float32), axis=0),
            jnp.sum(branch_low.astype(jnp.float32), axis=0),
            jnp.sum(pre_low.astype(jnp.float32), axis=0),
        ]
    )
    return (grad_input + grad_mid, (grad_wqkv, grad_wout, grad_wfc, grad_wproj), grad_vector)


def combine_stats(earlier, later):
    max_one, total_one, target_one = earlier
    max_two, total_two, target_two = later
    joint_max = jnp.maximum(max_one, max_two)
    joint_total = total_one * jnp.exp(max_one - joint_max) + total_two * jnp.exp(
        max_two - joint_max
    )
    return (joint_max, joint_total, target_one + target_two)


def adamw(weight, moment_one, moment_two, gradient, step_rate, decay_rate, step_float):
    one_new = 0.5 * moment_one + 0.5 * gradient
    two_new = 0.5 * moment_two + 0.5 * gradient * gradient
    fix_scale = 1.0 - jnp.power(0.5, step_float)
    update = one_new / fix_scale / (jnp.sqrt(two_new / fix_scale) + 1e-08)
    return (weight - step_rate * (update + decay_rate * weight), one_new, two_new)


def on_device(
    token_ids,
    seq_lengths,
    loss_slots,
    target_ids,
    step_count,
    w_qkv,
    w_out,
    w_fc,
    w_proj,
    vectors,
    pos_table,
    embed_table,
    mom_qkv,
    mom_out,
    mom_fc,
    mom_proj,
    mom_vectors,
    mom_pos,
    mom_embed,
    sec_qkv,
    sec_out,
    sec_fc,
    sec_proj,
    sec_vectors,
    sec_pos,
    sec_embed,
):
    per_layer = 8 * D + FF
    token_total = lax.psum(jnp.sum(seq_lengths.astype(jnp.float32)), ("narrow", "wide"))
    pos_low, vector_low = (
        lax.all_gather(pos_table.astype(jnp.bfloat16), ("narrow", "wide"), axis=0, tiled=True),
        lax.all_gather(vectors.astype(jnp.bfloat16), ("narrow", "wide"), axis=0, tiled=True),
    )
    vector_all = vector_low.astype(jnp.float32)
    table_low = lax.all_gather(embed_table.astype(jnp.bfloat16), "wide", axis=0, tiled=True)
    vocab_block = table_low.shape[0]
    narrow_at = lax.axis_index("narrow")
    vocab_start = narrow_at * vocab_block
    group_tokens, group_slots, group_targets = (
        lax.all_gather(token_ids, "narrow", axis=0, tiled=True),
        lax.all_gather(loss_slots, "narrow", axis=0, tiled=True),
        lax.all_gather(target_ids, "narrow", axis=0, tiled=True),
    )
    local_tokens = group_tokens - vocab_start
    token_inside = (local_tokens >= 0) & (local_tokens < vocab_block)
    token_clipped = jnp.clip(local_tokens, 0, vocab_block - 1)
    stream = lax.psum_scatter(
        jnp.where(token_inside[:, None], table_low[token_clipped].astype(jnp.float32), 0.0).astype(
            jnp.bfloat16
        ),
        "narrow",
        scatter_dimension=0,
        tiled=True,
    ).astype(jnp.float32) + pos_low[:LEN].astype(jnp.float32)
    allowed = attention_mask(seq_lengths[0])
    kept_weights = []
    saved_list = []
    for layer_at in range(LAYERS):
        weights = fetch_layer(w_qkv, w_out, w_fc, w_proj, layer_at)
        kept_weights.append(weights)
        stream, saved_acts = layer_forward(
            stream, weights, vector_all[layer_at * per_layer : (layer_at + 1) * per_layer], allowed
        )
        saved_list.append(saved_acts)
    tail_start = LAYERS * per_layer
    final_norm, final_pull = jax.vjp(
        layer_norm,
        stream,
        vector_all[tail_start : tail_start + D],
        vector_all[tail_start + D : tail_start + 2 * D],
    )
    slot_rows = jnp.maximum(loss_slots, 0)
    group_rows = lax.all_gather(
        final_norm[slot_rows].astype(jnp.bfloat16), "narrow", axis=0, tiled=True
    )
    logits = jnp.dot(group_rows, table_low.T, preferred_element_type=jnp.float32)
    local_targets = group_targets - vocab_start
    target_onehot = jnp.arange(vocab_block)[None, :] == local_targets[:, None]
    row_max = jnp.max(logits, axis=-1)
    row_total = jnp.sum(jnp.exp(logits - row_max[:, None]), axis=-1)
    target_logit = jnp.sum(jnp.where(target_onehot, logits, 0.0), axis=-1)
    merged_max, merged_total, merged_target = joined(
        (row_max, row_total, target_logit), "narrow", combine_stats
    )
    log_total = merged_max + jnp.log(merged_total)
    group_used = (group_slots >= 0).astype(jnp.float32)
    own_loss = jnp.sum(
        lax.dynamic_slice_in_dim(
            (log_total - merged_target) * group_used, narrow_at * LOSS_DEV, LOSS_DEV
        )
    )
    grad_logits = (
        (jnp.exp(logits - log_total[:, None]) - target_onehot.astype(jnp.float32))
        * (group_used / token_total)[:, None]
    ).astype(jnp.bfloat16)
    grad_table = jnp.dot(grad_logits.T, group_rows, preferred_element_type=jnp.float32)
    grad_rows = lax.psum_scatter(
        jnp.dot(grad_logits, table_low, preferred_element_type=jnp.float32),
        "narrow",
        scatter_dimension=0,
        tiled=True,
    )
    grad_final = jnp.zeros((LEN, D), jnp.float32).at[slot_rows].add(grad_rows)
    grad_stream, grad_gain_final, grad_shift_final = final_pull(grad_final)
    layer_shards = []
    vector_grads = []
    for layer_at in reversed(range(LAYERS)):
        weights = fetch_layer(w_qkv, w_out, w_fc, w_proj, layer_at)
        grad_stream, full_grads, grad_vector = layer_backward(
            grad_stream,
            saved_list[layer_at],
            weights,
            vector_all[layer_at * per_layer : (layer_at + 1) * per_layer],
            allowed,
        )
        grad_a, grad_b, grad_c, grad_d = full_grads
        layer_shards.insert(0, reduce_layer(grad_a, grad_b, grad_c, grad_d))
        vector_grads.insert(0, grad_vector)
    grad_group = lax.all_gather(grad_stream, "narrow", axis=0, tiled=True)
    grad_table = grad_table.at[token_clipped].add(jnp.where(token_inside[:, None], grad_group, 0.0))
    table_shard = lax.psum_scatter(grad_table, "wide", scatter_dimension=0, tiled=True)
    grad_pos = jnp.zeros((POS, D), jnp.float32).at[:LEN].set(grad_stream)
    grad_small = jnp.concatenate(vector_grads + [grad_gain_final, grad_shift_final])
    pos_shard, small_shard = (
        lax.psum_scatter(grad_pos, ("narrow", "wide"), scatter_dimension=0, tiled=True),
        lax.psum_scatter(grad_small, ("narrow", "wide"), scatter_dimension=0, tiled=True),
    )
    qkv_shard = jnp.stack([member[0] for member in layer_shards])
    out_shard = jnp.stack([member[1] for member in layer_shards])
    fc_shard = jnp.stack([member[2] for member in layer_shards])
    proj_shard = jnp.stack([member[3] for member in layer_shards])
    shards = (qkv_shard, out_shard, fc_shard, proj_shard, small_shard, pos_shard, table_shard)
    squares = jnp.sum(jnp.stack([jnp.sum(member * member) for member in shards]))
    loss_total, square_total = lax.psum((own_loss, squares), ("narrow", "wide"))
    loss_value = loss_total / token_total
    grad_norm = jnp.sqrt(square_total)
    factor = CLIP_LIMIT / jnp.maximum(grad_norm, CLIP_LIMIT)
    step_float = step_count.astype(jnp.float32)
    params = (w_qkv, w_out, w_fc, w_proj, vectors, pos_table, embed_table)
    moments_one = (mom_qkv, mom_out, mom_fc, mom_proj, mom_vectors, mom_pos, mom_embed)
    moments_two = (sec_qkv, sec_out, sec_fc, sec_proj, sec_vectors, sec_pos, sec_embed)
    step_rates = (
        RATE_MATRIX,
        RATE_MATRIX,
        RATE_MATRIX,
        RATE_MATRIX,
        RATE_VECTOR,
        RATE_MATRIX,
        RATE_MATRIX,
    )
    decay_rates = (
        DECAY_MATRIX,
        DECAY_MATRIX,
        DECAY_MATRIX,
        DECAY_MATRIX,
        0.0,
        DECAY_MATRIX,
        DECAY_MATRIX,
    )
    results = [
        adamw(
            params[where_at],
            moments_one[where_at],
            moments_two[where_at],
            shards[where_at] * factor,
            step_rates[where_at],
            decay_rates[where_at],
            step_float,
        )
        for where_at in range(7)
    ]
    return (
        loss_value,
        grad_norm,
        results[0][0],
        results[1][0],
        results[2][0],
        results[3][0],
        results[4][0],
        results[5][0],
        results[6][0],
        results[0][1],
        results[1][1],
        results[2][1],
        results[3][1],
        results[4][1],
        results[5][1],
        results[6][1],
        results[0][2],
        results[1][2],
        results[2][2],
        results[3][2],
        results[4][2],
        results[5][2],
        results[6][2],
    )


def solution(mesh):
    return jax.shard_map(
        on_device,
        mesh=mesh,
        in_specs=(
            P(("narrow", "wide")),
            P(("narrow", "wide")),
            P(("narrow", "wide")),
            P(("narrow", "wide")),
            P(),
            P(None, ("narrow", "wide"), None),
            P(None, ("narrow", "wide"), None),
            P(None, ("narrow", "wide"), None),
            P(None, ("narrow", "wide"), None),
            P(("narrow", "wide")),
            P(("narrow", "wide"), None),
            P(("narrow", "wide"), None),
            P(None, ("narrow", "wide"), None),
            P(None, ("narrow", "wide"), None),
            P(None, ("narrow", "wide"), None),
            P(None, ("narrow", "wide"), None),
            P(("narrow", "wide")),
            P(("narrow", "wide"), None),
            P(("narrow", "wide"), None),
            P(None, ("narrow", "wide"), None),
            P(None, ("narrow", "wide"), None),
            P(None, ("narrow", "wide"), None),
            P(None, ("narrow", "wide"), None),
            P(("narrow", "wide")),
            P(("narrow", "wide"), None),
            P(("narrow", "wide"), None),
        ),
        out_specs=(
            P(),
            P(),
            P(None, ("narrow", "wide"), None),
            P(None, ("narrow", "wide"), None),
            P(None, ("narrow", "wide"), None),
            P(None, ("narrow", "wide"), None),
            P(("narrow", "wide")),
            P(("narrow", "wide"), None),
            P(("narrow", "wide"), None),
            P(None, ("narrow", "wide"), None),
            P(None, ("narrow", "wide"), None),
            P(None, ("narrow", "wide"), None),
            P(None, ("narrow", "wide"), None),
            P(("narrow", "wide")),
            P(("narrow", "wide"), None),
            P(("narrow", "wide"), None),
            P(None, ("narrow", "wide"), None),
            P(None, ("narrow", "wide"), None),
            P(None, ("narrow", "wide"), None),
            P(None, ("narrow", "wide"), None),
            P(("narrow", "wide")),
            P(("narrow", "wide"), None),
            P(("narrow", "wide"), None),
        ),
        check_vma=False,
    )
```

profile of v0, /device:TPU:0, one launch (start us, length us, event | category | flops | bytes accessed | tf_op | source)
XLA Modules:
  0.0 4730.7 jit_solution(3373957019885606555)
XLA Ops:
  7.3 5.0 convert_bitcast_fusion
  13.1 6.1 all-gather.11
  19.9 488.0 %all-gather.48.cloned.1.call-done = bf16[8,1572,1024]{2,1,0:T(8,128)(2,1)} async-done(((bf16[1,1572,1024]{2,1,0:T(8,128)(2,1)}), bf16[8,1572,1024]{2,1,0:T(8,128)(2,1)}) %all-gather.48.cloned.1.call-update) | async-done | bytes 25755664 | tf_op jit(solution)/shard_map/all_gather | solution.py:263
  507.9 26.9 reshape.409
  534.8 22.6 gather_fusion
  569.4 40.1 all-reduce.2
  613.9 6.2 all-reduce.7
  620.1 41.1 psum.22
  666.5 22.1 all-gather.32.cloned.1.call-done
  688.6 7.9 add_convert_fusion.1
  699.7 7.3 fusion.8
  707.0 9.2 exponential_reduce_fusion.1
  716.8 9.2 convolution_convert_fusion.1
  726.1 21.4 all-gather.34.cloned.1.call-done
  751.8 75.7 %all-gather.36.cloned.1.call-done = bf16[1,1024,4096]{2,1,0:T(8,128)(2,1)} async-done(((bf16[1,32,4096]{2,1,0:T(8,128)(2,1)}), bf16[1,1024,4096]{2,1,0:T(8,128)(2,1)}) %all-gather.36.cloned.1.call-update) | async-done | bytes 8388624 | tf_op jit(solution)/shard_map/all_gather | solution.py:51
  827.5 10.3 fusion.40
  837.8 69.7 %all-gather.38.cloned.1.call-done = bf16[1,4096,1024]{2,1,0:T(8,128)(2,1)} async-done(((bf16[1,128,1024]{2,1,0:T(8,128)(2,1)}), bf16[1,4096,1024]{2,1,0:T(8,128)(2,1)}) %all-gather.38.cloned.1.call-update) | async-done | bytes 8388624 | tf_op jit(solution)/shard_map/all_gather | solution.py:52
  907.5 10.6 fusion.153
  919.8 59.7 %all-gather.40.cloned.1.call-done = bf16[1,1024,3072]{2,1,0:T(8,128)(2,1)} async-done(((bf16[1,32,3072]{2,1,0:T(8,128)(2,1)}), bf16[1,1024,3072]{2,1,0:T(8,128)(2,1)}) %all-gather.40.cloned.1.call-update) | async-done | bytes 6291472 | tf_op jit(solution)/shard_map/all_gather | solution.py:45
  979.5 8.6 add_convert_fusion
  991.4 7.7 fusion.9
  999.1 9.2 exponential_reduce_fusion
  1008.3 9.1 convolution_convert_fusion
  1017.3 21.2 all-gather.42.cloned.1.call-done
  1042.8 75.7 %all-gather.44.cloned.1.call-done = bf16[1,1024,4096]{2,1,0:T(8,128)(2,1)} async-done(((bf16[1,32,4096]{2,1,0:T(8,128)(2,1)}), bf16[1,1024,4096]{2,1,0:T(8,128)(2,1)}) %all-gather.44.cloned.1.call-update) | async-done | bytes 8388624 | tf_op jit(solution)/shard_map/all_gather | solution.py:51
  1118.5 10.7 fusion.32
  1129.3 69.3 %all-gather.46.cloned.1.call-done = bf16[1,4096,1024]{2,1,0:T(8,128)(2,1)} async-done(((bf16[1,128,1024]{2,1,0:T(8,128)(2,1)}), bf16[1,4096,1024]{2,1,0:T(8,128)(2,1)}) %all-gather.46.cloned.1.call-update) | async-done | bytes 8388624 | tf_op jit(solution)/shard_map/all_gather | solution.py:52
  1198.6 11.9 fusion.155
  1212.0 5.8 all_gather.87
  1217.8 12.0 fusion.156
  1229.8 5.2 all-gather.13
  1236.7 5.0 all-gather.14
  1247.6 15.6 fusion.123
  1263.4 20.4 reduce-scatter.16.cloned.1.call-done
  1291.1 16.6 convert_reduce_fusion
  1307.7 7.6 multiply_reduce_fusion.5
  1321.4 8.1 convolution_bitcast_fusion.1
  1329.6 12.4 multiply_reduce_fusion.1
  1342.0 12.2 multiply_convert_fusion.1
  1366.2 16.4 convert_reduce_fusion.1
  1382.6 8.1 multiply_reduce_fusion.7
  1397.1 8.1 convolution_bitcast_fusion
  1405.3 12.2 multiply_reduce_fusion
  1417.5 12.2 multiply_convert_fusion
  1462.4 8.7 fusion.125
  1472.7 8.8 fusion.127
  1483.1 10.5 fusion.126
  1495.2 10.7 fusion.124
  1507.1 15.5 fusion.129
  1523.9 15.5 fusion.128
  1540.3 22.9 fusion.122
  1563.3 5.9 broadcast_select_fusion
  1569.2 51.7 %scatter_fusion = f32[12576,1024]{1,0:T(8,128)} fusion(f32[12576,1024]{1,0:T(8,128)} %fusion.122, s32[2048]{0:T(1024)S(1)} %copy-done.60, f32[2048,1024]{1,0:T(8,128)} %broadcast_select_fusion), kind=kCustom, calls=%fused_computation.3 | custom fusion | flops 2097152 | bytes 25174016 | tf_op jit(solution)/shard_map/scatter-add | solution.py:348
  1620.9 1289.9 %fusion = f32[1584,1024]{1,0:T(8,128)} fusion(f32[12576,1024]{1,0:T(8,128)} %scatter_fusion), kind=kCustom, calls=%all-reduce-scatter | all-reduce-scatter fusion | flops 12976129 | bytes 57999872
  2923.6 18.3 concatenate.14
  2941.9 5.2 multiply_reduce_fusion.2
  2947.0 102.0 %reduce-scatter.20.cloned.1.call-done = f32[32,3072]{1,0:T(8,128)} async-done(((f32[1024,3072]{1,0:T(8,128)}), f32[32,3072]{1,0:T(8,128)}) %reduce-scatter.20.cloned.1.call-update) | async-done | bytes 393232 | tf_op jit(solution)/shard_map/reduce_scatter | solution.py:60
  3049.0 161.5 %reduce-scatter.18.cloned.1.call-done = f32[32,3072]{1,0:T(8,128)} async-done(((f32[1024,3072]{1,0:T(8,128)}), f32[32,3072]{1,0:T(8,128)}) %reduce-scatter.18.cloned.1.call-update) | async-done | bytes 393232 | tf_op jit(solution)/shard_map/reduce_scatter | solution.py:60
  3213.9 356.1 %reduce-scatter.28.cloned.1.call-done = f32[32,4096]{1,0:T(8,128)} async-done(((f32[1024,4096]{1,0:T(8,128)}), f32[32,4096]{1,0:T(8,128)}) %reduce-scatter.28.cloned.1.call-update) | async-done | bytes 524304 | tf_op jit(solution)/shard_map/reduce_scatter | solution.py:62
  3570.0 359.6 %reduce-scatter.26.cloned.1.call-done = f32[32,4096]{1,0:T(8,128)} async-done(((f32[1024,4096]{1,0:T(8,128)}), f32[32,4096]{1,0:T(8,128)}) %reduce-scatter.26.cloned.1.call-update) | async-done | bytes 524304 | tf_op jit(solution)/shard_map/reduce_scatter | solution.py:62
  3932.3 356.9 %reduce-scatter.32.cloned.1.call-done = f32[128,1024]{1,0:T(8,128)} async-done(((f32[4096,1024]{1,0:T(8,128)}), f32[128,1024]{1,0:T(8,128)}) %reduce-scatter.32.cloned.1.call-update) | async-done | bytes 524304 | tf_op jit(solution)/shard_map/reduce_scatter | solution.py:63
  4289.3 359.7 %reduce-scatter.30.cloned.1.call-done = f32[128,1024]{1,0:T(8,128)} async-done(((f32[4096,1024]{1,0:T(8,128)}), f32[128,1024]{1,0:T(8,128)}) %reduce-scatter.30.cloned.1.call-update) | async-done | bytes 524304 | tf_op jit(solution)/shard_map/reduce_scatter | solution.py:63
  4653.8 39.1 all-reduce.8
  4705.6 13.6 multiply_subtract_fusion
  (503 shorter events, 149.4 us)
Async XLA Ops:
  7.2 500.7 %all-gather.48.cloned.1.call-start = ((), (), s32[]{:S(2)}) async-start(), calls=%async_computation.32 | async-start | bytes 29048832 | tf_op jit(solution)/shard_map/all_gather | solution.py:263
  12.3 649.7 %all-gather.28.cloned.1.call-start = ((), (), s32[]{:S(2)}) async-start(), calls=%async_computation.12 | async-start | bytes 2162688 | tf_op jit(solution)/shard_map/all_gather | solution.py:259
  13.1 648.9 %reduce-scatter.14.cloned.1.call-start = ((), (), s32[]{:S(2)}) async-start(), calls=%async_computation.11 | async-start | bytes 5242880 | tf_op jit(solution)/shard_map/reduce_scatter | solution.py:275
  19.3 538.2 %copy-start.67 = (pred[1,4,4,128]{3,1,2,0:T(4,128)(4,1)}, pred[1,4,4,128]{3,1,2,0:T(4,128)(4,1)S(1)}, u32[]{:S(2)}) copy-start(pred[1,4,4,128]{3,1,2,0:T(4,128)(4,1)S(1)} %copy.99) | copy-start | bytes 6148
  561.6 127.0 %all-gather.32.cloned.1.call-start = ((), (), s32[]{:S(2)}) async-start(), calls=%async_computation.24 | async-start | bytes 6488064 | tf_op jit(solution)/shard_map/all_gather | solution.py:45
  562.7 48.1 %copy-start.139 = (u32[32]{0:T(128)S(1)}, u32[32]{0:T(128)}, u32[]{:S(2)}) copy-start(u32[32]{0:T(128)} %constant.194) | copy-start | bytes 388
  563.5 48.7 %copy-start.137 = (s32[32]{0:T(128)S(1)}, s32[32]{0:T(128)}, u32[]{:S(2)}) copy-start(s32[32]{0:T(128)} %param.32) | copy-start | bytes 388
  563.5 50.2 %copy-start.138 = (s32[32]{0:T(128)S(1)}, s32[32]{0:T(128)}, u32[]{:S(2)}) copy-start(s32[32]{0:T(128)} %param.33) | copy-start | bytes 388
  563.5 183.9 %all-gather.34.cloned.1.call-start = ((), (), s32[]{:S(2)}) async-start(), calls=%async_computation.25 | async-start | bytes 2162688 | tf_op jit(solution)/shard_map/all_gather | solution.py:48
  564.3 263.2 %all-gather.36.cloned.1.call-start = ((), (), s32[]{:S(2)}) async-start(), calls=%async_computation.26 | async-start | bytes 8650752 | tf_op jit(solution)/shard_map/all_gather | solution.py:51
  565.3 342.2 %all-gather.38.cloned.1.call-start = ((), (), s32[]{:S(2)}) async-start(), calls=%async_computation.27 | async-start | bytes 8650752 | tf_op jit(solution)/shard_map/all_gather | solution.py:52
  566.3 413.3 %all-gather.40.cloned.1.call-start = ((), (), s32[]{:S(2)}) async-start(), calls=%async_computation.28 | async-start | bytes 6488064 | tf_op jit(solution)/shard_map/all_gather | solution.py:45
  567.0 471.5 %all-gather.42.cloned.1.call-start = ((), (), s32[]{:S(2)}) async-start(), calls=%async_computation.29 | async-start | bytes 2162688 | tf_op jit(solution)/shard_map/all_gather | solution.py:48
  567.7 550.8 %all-gather.44.cloned.1.call-start = ((), (), s32[]{:S(2)}) async-start(), calls=%async_computation.30 | async-start | bytes 8650752 | tf_op jit(solution)/shard_map/all_gather | solution.py:51
  568.3 630.3 %all-gather.46.cloned.1.call-start = ((), (), s32[]{:S(2)}) async-start(), calls=%async_computation.31 | async-start | bytes 8650752 | tf_op jit(solution)/shard_map/all_gather | solution.py:52
  569.1 714.7 %reduce-scatter.16.cloned.1.call-start = ((), (), s32[]{:S(2)}) async-start(), calls=%async_computation.13 | async-start | bytes 655360 | tf_op jit(solution)/shard_map/reduce_scatter | solution.py:325
  610.1 86.4 %copy-start.96 = (f32[1024]{0:T(1024)}, f32[1024]{0:T(1024)S(1)}, u32[]{:S(2)}) copy-start(f32[1024]{0:T(1024)S(1)} %get-tuple-element.321) | copy-start | bytes 12292
  610.1 86.4 %copy-start.115 = (f32[1024]{0:T(1024)}, f32[1024]{0:T(1024)S(1)}, u32[]{:S(2)}) copy-start(f32[1024]{0:T(1024)S(1)} %get-tuple-element.322) | copy-start | bytes 12292
  610.1 217.4 %copy-start.91 = (f32[1024]{0:T(1024)}, f32[1024]{0:T(1024)S(1)}, u32[]{:S(2)}) copy-start(f32[1024]{0:T(1024)S(1)} %get-tuple-element.317) | copy-start | bytes 12292
  610.1 369.4 %copy-start.98 = (f32[1024]{0:T(1024)}, f32[1024]{0:T(1024)S(1)}, u32[]{:S(2)}) copy-start(f32[1024]{0:T(1024)S(1)} %get-tuple-element.313) | copy-start | bytes 12292
  610.1 508.4 %copy-start.93 = (f32[1024]{0:T(1024)}, f32[1024]{0:T(1024)S(1)}, u32[]{:S(2)}) copy-start(f32[1024]{0:T(1024)S(1)} %get-tuple-element.309) | copy-start | bytes 12292
  610.8 296.7 %copy-start.84 = (f32[4096]{0:T(1024)}, f32[4096]{0:T(1024)S(1)}, u32[]{:S(2)}) copy-start(f32[4096]{0:T(1024)S(1)} %get-tuple-element.326) | copy-start | bytes 49156
  612.2 49.8 %copy-start.132 = (s32[32]{0:T(128)}, s32[32]{0:T(128)S(1)}, u32[]{:S(2)}) copy-start(s32[32]{0:T(128)S(1)} %broadcast_maximum_fusion) | copy-start | bytes 388
  620.1 627.5 %copy-start.61 = (s32[128]{0:T(128)}, s32[128]{0:T(128)S(1)}, u32[]{:S(2)}) copy-start(s32[128]{0:T(128)S(1)} %broadcast_subtract_fusion) | copy-start | bytes 1540
  664.1 32.4 copy-start.71
  716.8 30.6 copy-start.122
  747.5 80.0 %copy-start.111 = (f32[1024]{0:T(1024)S(1)}, f32[1024]{0:T(1024)}, u32[]{:S(2)}) copy-start(f32[1024]{0:T(1024)} %get-tuple-element.318) | copy-start | bytes 12292
  751.4 156.1 %copy-start.12 = (f32[512,1024]{1,0:T(8,128)}, f32[512,1024]{1,0:T(8,128)S(1)}, u32[]{:S(2)}) copy-start(f32[512,1024]{1,0:T(8,128)S(1)} %get-tuple-element.339) | copy-start | bytes 6291460
  751.4 86.4 %copy-start.69 = (f32[512]{0:T(512)}, f32[512]{0:T(512)S(1)}, u32[]{:S(2)}) copy-start(f32[512]{0:T(512)S(1)} %broadcast_multiply_fusion.3) | copy-start | bytes 6148
  751.8 86.0 %copy-start.79 = (f32[512]{0:T(512)}, f32[512]{0:T(512)S(1)}, u32[]{:S(2)}) copy-start(f32[512]{0:T(512)S(1)} %multiply_reduce_fusion.16) | copy-start | bytes 6148
  751.8 86.0 %copy-start.102 = (f32[512]{0:T(512)}, f32[512]{0:T(512)S(1)}, u32[]{:S(2)}) copy-start(f32[512]{0:T(512)S(1)} %fusion.104) | copy-start | bytes 6148
  827.5 80.0 %copy-start.121 = (f32[1024]{0:T(1024)S(1)}, f32[1024]{0:T(1024)}, u32[]{:S(2)}) copy-start(f32[1024]{0:T(1024)} %get-tuple-element.319) | copy-start | bytes 12292
  907.5 72.0 %copy-start.117 = (f32[1024]{0:T(1024)S(1)}, f32[1024]{0:T(1024)}, u32[]{:S(2)}) copy-start(f32[1024]{0:T(1024)} %get-tuple-element.314) | copy-start | bytes 12292
  918.1 70.0 %copy-start.75 = (f32[512]{0:T(512)}, f32[512]{0:T(512)S(1)}, u32[]{:S(2)}) copy-start(f32[512]{0:T(512)S(1)} %broadcast_multiply_fusion.2) | copy-start | bytes 6148
  919.8 68.4 %copy-start.81 = (f32[512]{0:T(512)}, f32[512]{0:T(512)S(1)}, u32[]{:S(2)}) copy-start(f32[512]{0:T(512)S(1)} %multiply_reduce_fusion.15) | copy-start | bytes 6148
  919.8 68.4 %copy-start.109 = (f32[512]{0:T(512)}, f32[512]{0:T(512)S(1)}, u32[]{:S(2)}) copy-start(f32[512]{0:T(512)S(1)} %fusion.105) | copy-start | bytes 6148
  1008.3 30.3 copy-start.120
  1038.5 80.0 %copy-start.113 = (f32[1024]{0:T(1024)S(1)}, f32[1024]{0:T(1024)}, u32[]{:S(2)}) copy-start(f32[1024]{0:T(1024)} %get-tuple-element.310) | copy-start | bytes 12292
  1042.4 86.8 %copy-start.15 = (f32[512,1024]{1,0:T(8,128)}, f32[512,1024]{1,0:T(8,128)S(1)}, u32[]{:S(2)}) copy-start(f32[512,1024]{1,0:T(8,128)S(1)} %get-tuple-element.345) | copy-start | bytes 6291460
  1042.4 272.8 %copy-start.73 = (f32[512]{0:T(512)}, f32[512]{0:T(512)S(1)}, u32[]{:S(2)}) copy-start(f32[512]{0:T(512)S(1)} %broadcast_multiply_fusion.1) | copy-start | bytes 6148
  1042.8 86.5 %copy-start.106 = (f32[512]{0:T(512)}, f32[512]{0:T(512)S(1)}, u32[]{:S(2)}) copy-start(f32[512]{0:T(512)S(1)} %fusion.106) | copy-start | bytes 6148
  1118.5 80.1 %copy-start.86 = (f32[4096]{0:T(1024)S(1)}, f32[4096]{0:T(1024)}, u32[]{:S(2)}) copy-start(f32[4096]{0:T(1024)} %get-tuple-element.325) | copy-start | bytes 49156
  1118.5 80.1 %copy-start.119 = (f32[1024]{0:T(1024)S(1)}, f32[1024]{0:T(1024)}, u32[]{:S(2)}) copy-start(f32[1024]{0:T(1024)} %get-tuple-element.311) | copy-start | bytes 12292
  1263.3 300.0 %all-gather.30.cloned.1.call-start = ((), (), s32[]{:S(2)}) async-start(), calls=%async_computation.23 | async-start | bytes 10485760 | tf_op jit(solution)/shard_map/all_gather | solution.py:347
  1443.9 1475.0 %all-reduce.11.cloned.1.call-start = ((), (), s32[]{:S(2)}) async-start(), calls=%async_computation.33 | async-start | bytes 212992
  1445.2 1475.1 %reduce-scatter.24.cloned.1.call-start = ((), (), s32[]{:S(2)}) async-start(), calls=%async_computation.17 | async-start | bytes 4325376 | tf_op jit(solution)/shard_map/reduce_scatter | solution.py:61
  1450.2 1470.1 %reduce-scatter.22.cloned.1.call-start = ((), (), s32[]{:S(2)}) async-start(), calls=%async_computation.16 | async-start | bytes 4325376 | tf_op jit(solution)/shard_map/reduce_scatter | solution.py:61
  1456.7 1465.3 %reduce-scatter.34.cloned.1.call-start = ((), (), s32[]{:S(2)}) async-start(), calls=%async_computation.22 | async-start | bytes 4325376 | tf_op jit(solution)/shard_map/reduce_scatter | solution.py:353
  1460.8 1588.2 %reduce-scatter.20.cloned.1.call-start = ((), (), s32[]{:S(2)}) async-start(), calls=%async_computation.15 | async-start | bytes 12976128 | tf_op jit(solution)/shard_map/reduce_scatter | solution.py:60
  1471.1 1739.4 %reduce-scatter.18.cloned.1.call-start = ((), (), s32[]{:S(2)}) async-start(), calls=%async_computation.14 | async-start | bytes 12976128 | tf_op jit(solution)/shard_map/reduce_scatter | solution.py:60
  1481.5 2088.4 %reduce-scatter.28.cloned.1.call-start = ((), (), s32[]{:S(2)}) async-start(), calls=%async_computation.19 | async-start | bytes 17301504 | tf_op jit(solution)/shard_map/reduce_scatter | solution.py:62
  1493.6 2436.0 %reduce-scatter.26.cloned.1.call-start = ((), (), s32[]{:S(2)}) async-start(), calls=%async_computation.18 | async-start | bytes 17301504 | tf_op jit(solution)/shard_map/reduce_scatter | solution.py:62
  1505.9 2783.3 %reduce-scatter.32.cloned.1.call-start = ((), (), s32[]{:S(2)}) async-start(), calls=%async_computation.21 | async-start | bytes 17301504 | tf_op jit(solution)/shard_map/reduce_scatter | solution.py:63
  1522.7 3126.3 %reduce-scatter.30.cloned.1.call-start = ((), (), s32[]{:S(2)}) async-start(), calls=%async_computation.20 | async-start | bytes 17301504 | tf_op jit(solution)/shard_map/reduce_scatter | solution.py:63
  1620.9 1295.4 %copy-start.131 = (u32[32]{0:T(128)S(1)}, u32[32]{0:T(128)}, u32[]{:S(2)}) copy-start(u32[32]{0:T(128)} %constant.213) | copy-start | bytes 388
  1620.9 1297.3 %copy-start.133 = (f32[128]{0:T(128)S(1)}, f32[128]{0:T(128)}, u32[]{:S(2)}) copy-start(f32[128]{0:T(128)} %get-tuple-element.296) | copy-start | bytes 1540
  2911.9 11.7 collective-permute-start
  2941.9 1753.1 %copy-start.31 = (f32[2,32,3072]{2,1,0:T(8,128)S(1)}, f32[2,32,3072]{2,1,0:T(8,128)}, u32[]{:S(2)}) copy-start(f32[2,32,3072]{2,1,0:T(8,128)} %param.35) | copy-start | bytes 2359300
  3210.6 1488.0 %copy-start.39 = (f32[2,32,1024]{2,1,0:T(8,128)S(1)}, f32[2,32,1024]{2,1,0:T(8,128)}, u32[]{:S(2)}) copy-start(f32[2,32,1024]{2,1,0:T(8,128)} %param.36) | copy-start | bytes 786436
  3210.6 1488.0 %copy-start.48 = (f32[32,1024]{1,0:T(8,128)S(1)}, f32[32,1024]{1,0:T(8,128)}, u32[]{:S(2)}) copy-start(f32[32,1024]{1,0:T(8,128)} %reduce-scatter.24.cloned.1.call-done) | copy-start | bytes 393220
  3210.6 1488.0 %copy-start.49 = (f32[32,1024]{1,0:T(8,128)S(1)}, f32[32,1024]{1,0:T(8,128)}, u32[]{:S(2)}) copy-start(f32[32,1024]{1,0:T(8,128)} %reduce-scatter.22.cloned.1.call-done) | copy-start | bytes 393220
  4649.0 50.7 %copy-start.25 = (f32[2,32,4096]{2,1,0:T(8,128)S(1)}, f32[2,32,4096]{2,1,0:T(8,128)}, u32[]{:S(2)}) copy-start(f32[2,32,4096]{2,1,0:T(8,128)} %param.37) | copy-start | bytes 3145732
  4649.0 50.7 %copy-start.34 = (f32[32,4096]{1,0:T(8,128)S(1)}, f32[32,4096]{1,0:T(8,128)}, u32[]{:S(2)}) copy-start(f32[32,4096]{1,0:T(8,128)} %reduce-scatter.28.cloned.1.call-done) | copy-start | bytes 1572868
  4649.0 50.7 %copy-start.35 = (f32[32,4096]{1,0:T(8,128)S(1)}, f32[32,4096]{1,0:T(8,128)}, u32[]{:S(2)}) copy-start(f32[32,4096]{1,0:T(8,128)} %reduce-scatter.26.cloned.1.call-done) | copy-start | bytes 1572868
  (110 other events, 774.6 us)
Sparse Core Ops, SparseCore 0:
  12.4 495.4 all-gather.47
  511.5 56.4 all-gather.27
  571.1 44.0 reduce-scatter.13
  619.0 69.5 all-gather.31
  692.4 55.0 all-gather.33
  751.3 76.1 all-gather.35
  831.5 75.9 all-gather.37
  911.4 68.0 all-gather.39
  983.5 54.9 all-gather.41
  1042.3 76.1 all-gather.43
  1122.5 76.0 all-gather.45
  1263.4 20.2 reduce-scatter.15
  1444.0 58.2 all-gather.29
  1508.3 120.5 all-reduce.10
  1631.0 386.1 reduce-scatter.23
  2019.4 376.8 reduce-scatter.21
  2398.4 467.1 reduce-scatter.33
  2871.5 177.5 reduce-scatter.19
  3056.1 154.4 reduce-scatter.17
  3212.7 357.2 reduce-scatter.27
  3572.3 357.2 reduce-scatter.25
  3931.9 357.3 reduce-scatter.31
  4291.6 357.3 reduce-scatter.29
where the time goes:
time: 4720 us; the launch traced here: 4730 us
  waiting for transfers between devices  2620 us (56%)
  blocking collectives  1440 us (31%)
  matrix products  342 us (7%)
  other arithmetic  176 us (4%)
  local copies, waits for them, and re-layouts  112 us (2%)
    unnamed x3, blocking collectives  1340 us
    reduce_scatter x2, waiting for transfers between devices, reduce_layer(): lax.psum_scatter(grad_wproj, ('narrow', 'wide'), scatter_dimension=0, til...  717 us
    reduce_scatter x2, waiting for transfers between devices, reduce_layer(): lax.psum_scatter(grad_wfc, ('narrow', 'wide'), scatter_dimension=0, tiled...  716 us
    all_gather x1, waiting for transfers between devices, on_device(): lax.all_gather(embed_table.astype(jnp.bfloat16), 'wide', axis=0, tiled=True)  488 us
    reduce_scatter x2, waiting for transfers between devices, reduce_layer(): lax.psum_scatter(grad_wqkv, ('narrow', 'wide'), scatter_dimension=0, tile...  264 us
    all_gather x2, waiting for transfers between devices, fetch_layer(): lax.all_gather(w_fc[layer_at].astype(jnp.bfloat16), ('narrow', 'wide'), a...  151 us
    all_gather x2, waiting for transfers between devices, fetch_layer(): lax.all_gather(w_proj[layer_at].astype(jnp.bfloat16), ('narrow', 'wide'),...  139 us
  transfers between devices with their start and end apart: 24, of which 16 were waited for; matrix products, arithmetic and copies ran while one was open for 35% of the time, Pallas kernels for 0%

commit v1 on v0

--- a/solution.py
+++ b/solution.py
@@ -19,14 +19,188 @@
 DECAY_MATRIX = 0.1
 
 
-def joined(part, axis, combine):
-    gathered = jax.tree.map(lambda a: lax.all_gather(a, axis), part)
-
-    def take(source):
-        return jax.tree.map(lambda a: lax.dynamic_index_in_dim(a, source, 0, False), gathered)
-
-    return lax.fori_loop(
-        1, lax.axis_size(axis), lambda source, state: combine(state, take(source)), take(0)
+class Net:
+    def __init__(self):
+        self.narrow_at = lax.axis_index("narrow")
+        self.wide_at = lax.axis_index("wide")
+        self.narrow_size = lax.axis_size("narrow")
+        self.size = lax.axis_size("wide")
+        size = self.size
+        self.core = self.narrow_at % 2
+        self.half = self.narrow_at // 2
+        self.halves = self.narrow_size // 2
+        self.place = jnp.where(
+            self.wide_at % 2 == 0, self.wide_at // 2, size - 1 - (self.wide_at - 1) // 2
+        )
+        self.device = self.narrow_at * size + self.wide_at
+        order = list(range(0, size, 2)) + list(range(size - 1, 0, -2))
+        pairs = [(n, w) for n in range(self.narrow_size) for w in range(size)]
+        self.core_pairs = [(n * size + w, (n ^ 1) * size + w) for n, w in pairs]
+        self.half_pairs = [(n * size + w, (n ^ 2) * size + w) for n, w in pairs]
+        self.right = [
+            (n * size + order[i], n * size + order[(i + 1) % size])
+            for n in range(self.narrow_size)
+            for i in range(size)
+        ]
+        self.left = [(later, earlier) for earlier, later in self.right]
+
+    def step(self, array, pairs):
+        return lax.ppermute(array, ("narrow", "wide"), pairs)
+
+    def swap_core(self, array):
+        return self.step(array, self.core_pairs)
+
+    def swap_half(self, array):
+        return self.step(array, self.half_pairs)
+
+    def flip(self, array, bit):
+        size = self.size
+        pairs = [
+            (n * size + w, n * size + (w ^ bit))
+            for n in range(self.narrow_size)
+            for w in range(size)
+        ]
+        return self.step(array, pairs)
+
+    def wide_of(self, offset):
+        size = self.size
+        at = lax.rem(self.place + offset, size)
+        return jnp.where(at < size // 2, 2 * at, 2 * (size - 1 - at) + 1)
+
+    def ring_gather(self, block):
+        size = self.size
+        far = size // 2
+        cut = block.shape[0] // 2
+        pieces = {0: block}
+        going_right, going_left = block, block
+        for at in range(1, far):
+            going_right = self.step(going_right, self.right)
+            pieces[size - at] = going_right
+            going_left = self.step(going_left, self.left)
+            pieces[at] = going_left
+        pieces[far] = jnp.concatenate(
+            [self.step(going_right[:cut], self.right), self.step(going_left[cut:], self.left)]
+        )
+        return [pieces[at] for at in range(size)]
+
+    def ring_scatter(self, take, low):
+        size = self.size
+        far = size // 2
+        block = take(far)
+        cut = block.shape[0] // 2
+        from_left = self.step(block[:cut].astype(low), self.right)
+        from_right = self.step(block[cut:].astype(low), self.left)
+        for at in range(far - 1, 0, -1):
+            to_right = take(at).astype(jnp.float32)
+            to_left = take(size - at).astype(jnp.float32)
+            if at == far - 1:
+                to_right = jnp.concatenate(
+                    [to_right[:cut] + from_left.astype(jnp.float32), to_right[cut:]]
+                )
+                to_left = jnp.concatenate(
+                    [to_left[:cut], to_left[cut:] + from_right.astype(jnp.float32)]
+                )
+            else:
+                to_right = to_right + from_left.astype(jnp.float32)
+                to_left = to_left + from_right.astype(jnp.float32)
+            from_left = self.step(to_right.astype(low), self.right)
+            from_right = self.step(to_left.astype(low), self.left)
+        return (
+            take(0).astype(jnp.float32)
+            + from_left.astype(jnp.float32)
+            + from_right.astype(jnp.float32)
+        )
+
+    def gather_rows(self, shard, ring_first):
+        size, halves = self.size, self.halves
+        rows, columns = shard.shape
+        whole = jnp.zeros((halves, 2, size, rows, columns), shard.dtype)
+        zero = jnp.int32(0)
+        if ring_first:
+            pieces = self.ring_gather(shard)
+            for at in range(size):
+                whole = lax.dynamic_update_slice(
+                    whole,
+                    pieces[at][None, None, None],
+                    (self.half, self.core, self.wide_of(at), zero, zero),
+                )
+            mine = lax.dynamic_slice(
+                whole, (self.half, self.core, zero, zero, zero), (1, 1, size, rows, columns)
+            )
+            whole = lax.dynamic_update_slice(
+                whole, self.swap_half(mine), (1 - self.half, self.core, zero, zero, zero)
+            )
+        else:
+            other = self.swap_half(shard)
+            pair = jnp.where(
+                self.half == 0, jnp.stack([shard, other]), jnp.stack([other, shard])
+            )
+            pieces = self.ring_gather(pair)
+            for at in range(size):
+                whole = lax.dynamic_update_slice(
+                    whole,
+                    pieces[at][:, None, None],
+                    (zero, self.core, self.wide_of(at), zero, zero),
+                )
+        mine = lax.dynamic_slice(
+            whole, (zero, self.core, zero, zero, zero), (halves, 1, size, rows, columns)
+        )
+        whole = lax.dynamic_update_slice(
+            whole, self.swap_core(mine), (zero, 1 - self.core, zero, zero, zero)
+        )
+        return whole.reshape(halves * 2 * size * rows, columns)
+
+    def reduce_rows(self, array, half_first, low):
+        size, halves = self.size, self.halves
+        rows = array.shape[0] // (halves * 2 * size)
+        columns = array.shape[1]
+        split = array.reshape(halves, 2, size, rows, columns)
+
+        def pick(value, at, axis):
+            return lax.dynamic_index_in_dim(value, at, axis, keepdims=False)
+
+        def plus(one, two):
+            return one.astype(jnp.float32) + two.astype(jnp.float32)
+
+        chip = plus(
+            pick(split, self.core, 1), self.swap_core(pick(split, 1 - self.core, 1).astype(low))
+        ).astype(low)
+        if half_first:
+            pair = plus(
+                pick(chip, self.half, 0), self.swap_half(pick(chip, 1 - self.half, 0))
+            ).astype(low)
+            return self.ring_scatter(lambda at: pick(pair, self.wide_of(at), 0), low)
+        both = self.ring_scatter(lambda at: pick(chip, self.wide_of(at), 1), low)
+        return plus(
+            pick(both, self.half, 0), self.swap_half(pick(both, 1 - self.half, 0).astype(low))
+        )
+
+    def total(self, value):
+        value = value + self.swap_core(value)
+        value = value + self.swap_half(value)
+        bit = 1
+        while bit < self.size:
+            value = value + self.flip(value, bit)
+            bit *= 2
+        return value
+
+
+def fetch_layer(net, w_qkv, w_out, w_fc, w_proj, layer_at):
+    return (
+        net.gather_rows(w_qkv[layer_at].astype(jnp.bfloat16), True),
+        net.gather_rows(w_out[layer_at].astype(jnp.bfloat16), False),
+        net.gather_rows(w_fc[layer_at].astype(jnp.bfloat16), True),
+        net.gather_rows(w_proj[layer_at].astype(jnp.bfloat16), False),
+    )
+
+
+def reduce_layer(net, grad_wqkv, grad_wout, grad_wfc, grad_wproj):
+    low = jnp.bfloat16
+    return (
+        net.reduce_rows(grad_wqkv, True, low),
+        net.reduce_rows(grad_wout, False, low),
+        net.reduce_rows(grad_wfc, True, low),
+        net.reduce_rows(grad_wproj, False, low),
     )
 
 
@@ -38,30 +212,6 @@
 
 def gelu_tanh(values):
     return jax.nn.gelu(values, approximate=True)
-
-
-def fetch_layer(w_qkv, w_out, w_fc, w_proj, layer_at):
-    return (
-        lax.all_gather(
-            w_qkv[layer_at].astype(jnp.bfloat16), ("narrow", "wide"), axis=0, tiled=True
-        ),
-        lax.all_gather(
-            w_out[layer_at].astype(jnp.bfloat16), ("narrow", "wide"), axis=0, tiled=True
-        ),
-        lax.all_gather(w_fc[layer_at].astype(jnp.bfloat16), ("narrow", "wide"), axis=0, tiled=True),
-        lax.all_gather(
-            w_proj[layer_at].astype(jnp.bfloat16), ("narrow", "wide"), axis=0, tiled=True
-        ),
-    )
-
-
-def reduce_layer(grad_wqkv, grad_wout, grad_wfc, grad_wproj):
-    return (
-        lax.psum_scatter(grad_wqkv, ("narrow", "wide"), scatter_dimension=0, tiled=True),
-        lax.psum_scatter(grad_wout, ("narrow", "wide"), scatter_dimension=0, tiled=True),
-        lax.psum_scatter(grad_wfc, ("narrow", "wide"), scatter_dimension=0, tiled=True),
-        lax.psum_scatter(grad_wproj, ("narrow", "wide"), scatter_dimension=0, tiled=True),
-    )
 
 
 def attention_mask(seq_length):
@@ -141,17 +291,17 @@
     ) = saved_acts
     w_qkv, w_out, w_fc, w_proj = weights
     branch_low = grad_out.astype(jnp.bfloat16)
-    grad_wproj = jnp.dot(hidden_low.T, branch_low, preferred_element_type=jnp.float32)
+    grad_wproj = jnp.dot(hidden_low.T, branch_low, preferred_element_type=jnp.bfloat16)
     grad_hidden = jnp.dot(branch_low, w_proj.T, preferred_element_type=jnp.float32)
     pre_low = jax.vjp(gelu_tanh, hidden_pre)[1](grad_hidden)[0].astype(jnp.bfloat16)
-    grad_wfc = jnp.dot(normed_two.T, pre_low, preferred_element_type=jnp.float32)
+    grad_wfc = jnp.dot(normed_two.T, pre_low, preferred_element_type=jnp.bfloat16)
     grad_normed_two = jnp.dot(pre_low, w_fc.T, preferred_element_type=jnp.float32)
     grad_mid, grad_gain_two, grad_shift_two = jax.vjp(
         layer_norm, stream_mid, vector[2 * D : 3 * D], vector[3 * D : 4 * D]
     )[1](grad_normed_two)
     grad_mid = grad_mid + grad_out
     attn_low = grad_mid.astype(jnp.bfloat16)
-    grad_wout = jnp.dot(mixed_low.T, attn_low, preferred_element_type=jnp.float32)
+    grad_wout = jnp.dot(mixed_low.T, attn_low, preferred_element_type=jnp.bfloat16)
     grad_mixed = (
         jnp.dot(attn_low, w_out.T, preferred_element_type=jnp.float32)
         .astype(jnp.bfloat16)
@@ -185,7 +335,7 @@
         .reshape(LEN, 3 * D)
         .astype(jnp.bfloat16)
     )
-    grad_wqkv = jnp.dot(normed_low.T, qkv_low, preferred_element_type=jnp.float32)
+    grad_wqkv = jnp.dot(normed_low.T, qkv_low, preferred_element_type=jnp.bfloat16)
     grad_normed = jnp.dot(qkv_low, w_qkv.T, preferred_element_type=jnp.float32)
     grad_input, grad_gain_one, grad_shift_one = jax.vjp(
         layer_norm, stream, vector[0:D], vector[D : 2 * D]
@@ -254,37 +404,79 @@
     sec_embed,
 ):
     per_layer = 8 * D + FF
-    token_total = lax.psum(jnp.sum(seq_lengths.astype(jnp.float32)), ("narrow", "wide"))
-    pos_low, vector_low = (
-        lax.all_gather(pos_table.astype(jnp.bfloat16), ("narrow", "wide"), axis=0, tiled=True),
-        lax.all_gather(vectors.astype(jnp.bfloat16), ("narrow", "wide"), axis=0, tiled=True),
-    )
-    vector_all = vector_low.astype(jnp.float32)
-    table_low = lax.all_gather(embed_table.astype(jnp.bfloat16), "wide", axis=0, tiled=True)
-    vocab_block = table_low.shape[0]
-    narrow_at = lax.axis_index("narrow")
-    vocab_start = narrow_at * vocab_block
-    group_tokens, group_slots, group_targets = (
-        lax.all_gather(token_ids, "narrow", axis=0, tiled=True),
-        lax.all_gather(loss_slots, "narrow", axis=0, tiled=True),
-        lax.all_gather(target_ids, "narrow", axis=0, tiled=True),
-    )
-    local_tokens = group_tokens - vocab_start
-    token_inside = (local_tokens >= 0) & (local_tokens < vocab_block)
-    token_clipped = jnp.clip(local_tokens, 0, vocab_block - 1)
-    stream = lax.psum_scatter(
-        jnp.where(token_inside[:, None], table_low[token_clipped].astype(jnp.float32), 0.0).astype(
-            jnp.bfloat16
-        ),
-        "narrow",
-        scatter_dimension=0,
-        tiled=True,
-    ).astype(jnp.float32) + pos_low[:LEN].astype(jnp.float32)
+    net = Net()
+    size, halves = net.size, net.halves
+    same_core = halves * size
+    devices = 2 * same_core
+    low = jnp.bfloat16
+    near = LEN * 9 // 16
+    rest = LEN - near
+    slots = loss_slots.shape[0]
+
+    numbers = jnp.concatenate([token_ids, loss_slots, target_ids, seq_lengths])
+    numbers = net.ring_gather(jnp.stack([numbers, net.swap_half(numbers)], axis=1))
+    numbers = jnp.stack(numbers).transpose(2, 0, 1)
+    group_tokens = numbers[:, :, :LEN]
+    group_slots = numbers[:, :, LEN : LEN + slots].reshape(same_core * slots)
+    group_targets = numbers[:, :, LEN + slots : LEN + 2 * slots].reshape(same_core * slots)
+    core_total = jnp.sum(numbers[:, :, LEN + 2 * slots :].astype(jnp.float32))
+    token_total = core_total + net.swap_core(core_total[None])[0]
+
+    own_rows = embed_table.shape[0]
+    table_own = embed_table.astype(low)
+    table_low = jnp.concatenate([table_own, net.swap_core(table_own)])
+    chip_rows = 2 * own_rows
+    own_start = net.device * own_rows
+    other_start = (net.device + (1 - 2 * net.core) * size) * own_rows
+
+    def locate(ids):
+        mine = ids - own_start
+        other = ids - other_start
+        return jnp.where(
+            (mine >= 0) & (mine < own_rows),
+            mine,
+            jnp.where((other >= 0) & (other < own_rows), other + own_rows, -1),
+        )
+
+    def one_hot(ids):
+        return (ids[:, None] == jnp.arange(chip_rows)[None, :]).astype(low)
+
+    local_tokens = locate(group_tokens)
+
+    def look_up(ids):
+        return jnp.dot(
+            one_hot(ids.reshape(-1)), table_low, preferred_element_type=jnp.float32
+        ).astype(low)
+
+    shared = pos_table.shape[0]
+    vector_rows = -(-vectors.shape[0] // D)
+    padded = jnp.pad(vectors, (0, vector_rows * D - vectors.shape[0])).reshape(vector_rows, D)
+    small_low = net.gather_rows(jnp.concatenate([pos_table, padded]).astype(low), False)
+    small_low = small_low.reshape(devices, shared + vector_rows, D)
+    pos_low = small_low[:, :shared].reshape(devices * shared, D)
+    vector_all = (
+        small_low[:, shared:]
+        .reshape(devices, vector_rows * D)[:, : vectors.shape[0]]
+        .reshape(-1)
+        .astype(jnp.float32)
+    )
+
+    near_other = look_up(local_tokens[1, :, :near])
+    near_swapped = net.swap_half(near_other)
+    rest_both = look_up(local_tokens[:, :, near:].transpose(1, 0, 2)).reshape(
+        size, halves, rest, D
+    )
+    near_own = (look_up(local_tokens[0, :, :near]) + near_swapped).reshape(size, near, D)
+    near_rows = net.ring_scatter(lambda at: near_own[at], low)
+    rest_sum = net.ring_scatter(lambda at: rest_both[at], low)
+    rest_rows = rest_sum[0] + net.swap_half(rest_sum[1].astype(low)).astype(jnp.float32)
+    stream = jnp.concatenate([near_rows, rest_rows]) + pos_low[:LEN].astype(jnp.float32)
+
     allowed = attention_mask(seq_lengths[0])
     kept_weights = []
     saved_list = []
     for layer_at in range(LAYERS):
-        weights = fetch_layer(w_qkv, w_out, w_fc, w_proj, layer_at)
+        weights = fetch_layer(net, w_qkv, w_out, w_fc, w_proj, layer_at)
         kept_weights.append(weights)
         stream, saved_acts = layer_forward(
             stream, weights, vector_all[layer_at * per_layer : (layer_at + 1) * per_layer], allowed
@@ -298,68 +490,104 @@
         vector_all[tail_start + D : tail_start + 2 * D],
     )
     slot_rows = jnp.maximum(loss_slots, 0)
-    group_rows = lax.all_gather(
-        final_norm[slot_rows].astype(jnp.bfloat16), "narrow", axis=0, tiled=True
-    )
+    own_picked = final_norm[slot_rows].astype(low)
+    group_rows = net.ring_gather(jnp.stack([own_picked, net.swap_half(own_picked)]))
+    group_rows = jnp.stack(group_rows, axis=1).reshape(same_core * slots, D)
     logits = jnp.dot(group_rows, table_low.T, preferred_element_type=jnp.float32)
-    local_targets = group_targets - vocab_start
-    target_onehot = jnp.arange(vocab_block)[None, :] == local_targets[:, None]
+    target_onehot = locate(group_targets)[:, None] == jnp.arange(chip_rows)[None, :]
     row_max = jnp.max(logits, axis=-1)
     row_total = jnp.sum(jnp.exp(logits - row_max[:, None]), axis=-1)
     target_logit = jnp.sum(jnp.where(target_onehot, logits, 0.0), axis=-1)
-    merged_max, merged_total, merged_target = joined(
-        (row_max, row_total, target_logit), "narrow", combine_stats
-    )
-    log_total = merged_max + jnp.log(merged_total)
+    half_of = jnp.arange(halves)[:, None]
+    wide_index = jnp.arange(size)[None, :]
+    place_of = jnp.where(wide_index % 2 == 0, wide_index // 2, size - 1 - (wide_index - 1) // 2)
+    to_device = ((half_of ^ net.half) * size + (place_of - net.place) % size).reshape(-1)
+    offsets = (net.place + wide_index) % size
+    wide_there = jnp.where(offsets < size // 2, 2 * offsets, 2 * (size - 1 - offsets) + 1)
+    from_device = ((half_of ^ net.half) * size + wide_there).reshape(-1)
+    stats = jnp.stack([row_max, row_total, target_logit], axis=-1)
+    stats = jnp.take(stats.reshape(same_core, slots * 3), to_device, axis=0)
+    stats = stats.reshape(same_core * slots, 3).T
+
+    def merged(stats, there):
+        return jnp.stack(combine_stats((stats[0], stats[1], stats[2]), (there[0], there[1], there[2])))
+
+    stats = merged(stats, net.swap_half(stats))
+    bit = 1
+    while bit < size:
+        stats = merged(stats, net.flip(stats, bit))
+        bit *= 2
+    stats = jnp.stack([stats[0] + jnp.log(stats[1]), stats[2]]).reshape(2, same_core, slots)
+    stats = jnp.take(stats, from_device, axis=1).reshape(2, same_core * slots)
+    log_total, merged_target = stats[0], stats[1]
     group_used = (group_slots >= 0).astype(jnp.float32)
-    own_loss = jnp.sum(
-        lax.dynamic_slice_in_dim(
-            (log_total - merged_target) * group_used, narrow_at * LOSS_DEV, LOSS_DEV
-        )
-    )
+    own_loss = jnp.sum(((log_total - merged_target) * group_used)[:slots])
     grad_logits = (
         (jnp.exp(logits - log_total[:, None]) - target_onehot.astype(jnp.float32))
         * (group_used / token_total)[:, None]
-    ).astype(jnp.bfloat16)
-    grad_table = jnp.dot(grad_logits.T, group_rows, preferred_element_type=jnp.float32)
-    grad_rows = lax.psum_scatter(
-        jnp.dot(grad_logits, table_low, preferred_element_type=jnp.float32),
-        "narrow",
-        scatter_dimension=0,
-        tiled=True,
-    )
+    ).astype(low)
+    grad_rows = jnp.dot(grad_logits, table_low, preferred_element_type=jnp.float32)
+    grad_rows = grad_rows.reshape(halves, size, slots, D)
+    cut = D // 2
+    pair = grad_rows[0, :, :, :cut] + net.swap_half(grad_rows[1, :, :, :cut])
+    grad_one = net.ring_scatter(lambda at: pair[at], jnp.float32)
+    both = net.ring_scatter(lambda at: grad_rows[:, at, :, cut:], jnp.float32)
+    grad_two = both[0] + net.swap_half(both[1])
+    grad_rows = jnp.concatenate([grad_one, grad_two], axis=1)
     grad_final = jnp.zeros((LEN, D), jnp.float32).at[slot_rows].add(grad_rows)
     grad_stream, grad_gain_final, grad_shift_final = final_pull(grad_final)
     layer_shards = []
     vector_grads = []
     for layer_at in reversed(range(LAYERS)):
-        weights = fetch_layer(w_qkv, w_out, w_fc, w_proj, layer_at)
         grad_stream, full_grads, grad_vector = layer_backward(
             grad_stream,
             saved_list[layer_at],
-            weights,
+            kept_weights[layer_at],
             vector_all[layer_at * per_layer : (layer_at + 1) * per_layer],
             allowed,
         )
         grad_a, grad_b, grad_c, grad_d = full_grads
-        layer_shards.insert(0, reduce_layer(grad_a, grad_b, grad_c, grad_d))
+        layer_shards.insert(0, reduce_layer(net, grad_a, grad_b, grad_c, grad_d))
         vector_grads.insert(0, grad_vector)
-    grad_group = lax.all_gather(grad_stream, "narrow", axis=0, tiled=True)
-    grad_table = grad_table.at[token_clipped].add(jnp.where(token_inside[:, None], grad_group, 0.0))
-    table_shard = lax.psum_scatter(grad_table, "wide", scatter_dimension=0, tiled=True)
-    grad_pos = jnp.zeros((POS, D), jnp.float32).at[:LEN].set(grad_stream)
+    grad_low = grad_stream.astype(low)
+    grad_near, grad_rest = grad_low[:near], grad_low[near:]
+    near_own = jnp.stack(net.ring_gather(grad_near))
+    near_other = net.swap_half(near_own)
+    rest_all = jnp.stack(net.ring_gather(jnp.stack([grad_rest, net.swap_half(grad_rest)])))
+
+    def spread(ids, rows):
+        return jnp.dot(one_hot(ids.reshape(-1)).T, rows, preferred_element_type=jnp.float32)
+
+    grad_table = jnp.dot(grad_logits.T, group_rows, preferred_element_type=jnp.float32)
+    grad_table = grad_table + spread(local_tokens[0, :, :near], near_own.reshape(-1, D))
+    grad_table = grad_table + spread(
+        local_tokens[:, :, near:].transpose(1, 0, 2), rest_all.reshape(-1, D)
+    )
+    grad_table = grad_table + spread(local_tokens[1, :, :near], near_other.reshape(-1, D))
+    table_shard = grad_table[:own_rows] + net.swap_core(grad_table[own_rows:])
+    grad_pos = jnp.concatenate(
+        [
+            jnp.sum(near_own.astype(jnp.float32), axis=0)
+            + jnp.sum(near_other.astype(jnp.float32), axis=0),
+            jnp.sum(rest_all.astype(jnp.float32), axis=(0, 1)),
+        ]
+    )
+    grad_pos = jnp.pad(grad_pos, ((0, POS - LEN), (0, 0)))
+    other_device = net.device + (1 - 2 * net.core) * size
+    pos_shard = lax.dynamic_slice_in_dim(grad_pos, net.device * shared, shared) + net.swap_core(
+        lax.dynamic_slice_in_dim(grad_pos, other_device * shared, shared)
+    )
     grad_small = jnp.concatenate(vector_grads + [grad_gain_final, grad_shift_final])
-    pos_shard, small_shard = (
-        lax.psum_scatter(grad_pos, ("narrow", "wide"), scatter_dimension=0, tiled=True),
-        lax.psum_scatter(grad_small, ("narrow", "wide"), scatter_dimension=0, tiled=True),
-    )
+    small_shard = net.reduce_rows(
+        grad_small.reshape(devices * 2, -1), False, jnp.float32
+    ).reshape(-1)
     qkv_shard = jnp.stack([member[0] for member in layer_shards])
     out_shard = jnp.stack([member[1] for member in layer_shards])
     fc_shard = jnp.stack([member[2] for member in layer_shards])
     proj_shard = jnp.stack([member[3] for member in layer_shards])
     shards = (qkv_shard, out_shard, fc_shard, proj_shard, small_shard, pos_shard, table_shard)
     squares = jnp.sum(jnp.stack([jnp.sum(member * member) for member in shards]))
-    loss_total, square_total = lax.psum((own_loss, squares), ("narrow", "wide"))
+    loss_total, square_total = net.total(jnp.stack([own_loss, squares]))
     loss_value = loss_total / token_total
     grad_norm = jnp.sqrt(square_total)
     factor = CLIP_LIMIT / jnp.maximum(grad_norm, CLIP_LIMIT)

time: 4720 us -> 1900 us (0.40)
  waiting for transfers between devices: 2620 us -> 617 us
  blocking collectives: 1440 us -> 0 us
  starting transfers between devices: 5.93 us -> 267 us
  local copies, waits for them, and re-layouts: 112 us -> 322 us
  matrix products: 342 us -> 435 us
  other arithmetic: 176 us -> 233 us
    reduce_scatter x11 -> x0, waiting for transfers between devices: 1720 us -> none  [the longest x2 717 us: reduce_layer(): lax.psum_scatter(grad_wproj, ('narrow', 'wide'), scatter_dimension=0, til...]
    unnamed x3 -> x0, blocking collectives: 1340 us -> none
    all_gather x11 -> x0, waiting for transfers between devices: 903 us -> none  [the longest x1 488 us: on_device(): lax.all_gather(embed_table.astype(jnp.bfloat16), 'wide', axis=0, tiled=True)]
    ppermute x0 -> x265, waiting for transfers between devices: none -> 617 us  [step(): return lax.ppermute(array, ('narrow', 'wide'), pairs)]
    ppermute x0 -> x265, starting transfers between devices: none -> 267 us  [step(): return lax.ppermute(array, ('narrow', 'wide'), pairs)]
    dot_general x8 -> x14, matrix products: 78.9 us -> 223 us  [the longest x3 91.3 us: spread(): jnp.dot(one_hot(ids.reshape(-1)).T, rows, preferred_element_type=jnp.floa...]
    dynamic_update_slice x0 -> x73, local copies, waits for them, and re-layouts: none -> 133 us  [the longest x32 72.7 us: gather_rows(): lax.dynamic_update_slice(whole, pieces[at][:, None, None], (zero, self.co...]
    psum x2 -> x0, blocking collectives: 80.2 us -> none  [the longest x1 41.1 us: on_device(): lax.psum(jnp.sum(seq_lengths.astype(jnp.float32)), ('narrow', 'wide'))]
  transfers between devices with their start and end apart: 24 -> 265, of which waited for: 16 -> 120; matrix products, arithmetic and copies ran while one was open for 35% -> 31% of each run, Pallas kernels for 0% -> 0%
where the time goes in v1:
time: 1900 us; the launch traced here: 1890 us
  waiting for transfers between devices  617 us (32%)
  matrix products  435 us (23%)
  local copies, waits for them, and re-layouts  322 us (17%)
  starting transfers between devices  267 us (14%)
  other arithmetic  233 us (12%)
    ppermute x265, waiting for transfers between devices, step(): return lax.ppermute(array, ('narrow', 'wide'), pairs)  617 us
    ppermute x265, starting transfers between devices, step(): return lax.ppermute(array, ('narrow', 'wide'), pairs)  267 us
    dot_general x3, matrix products, spread(): jnp.dot(one_hot(ids.reshape(-1)).T, rows, preferred_element_type=jnp.floa...  91.3 us
    dot_general x3, matrix products, look_up(): jnp.dot(one_hot(ids.reshape(-1)), table_low, preferred_element_type=jnp.f...  72.9 us
    dynamic_update_slice x32, local copies, waits for them, and re-layouts, gather_rows(): lax.dynamic_update_slice(whole, pieces[at][:, None, None], (zero, self.co...  72.7 us
    unnamed x517, local copies, waits for them, and re-layouts  49.2 us
  transfers between devices with their start and end apart: 265, of which 120 were waited for; matrix products, arithmetic and copies ran while one was open for 31% of the time, Pallas kernels for 0%

profile of v1, /device:TPU:0, one launch (start us, length us, event | category | flops | bytes accessed | tf_op | source)
XLA Modules:
  0.0 1890.4 jit_solution(9813402529941949448)
XLA Ops:
  279.7 6.3 collective-permute-done.70
  293.0 6.6 collective-permute-done.110
  307.7 8.3 collective-permute-done.113
  321.1 10.0 collective-permute-done.74
  334.2 8.1 collective-permute-done.114
  371.3 20.8 %fusion.39 = bf16[2304,1024]{1,0:T(8,128)(2,1)} fusion(s32[2304]{0:T(1024)S(1)} %eq.54, bf16[1572,1024]{1,0:T(8,128)(2,1)} %collective-permute-done.9, bf16[1572,1024]{1,0:T(8,128)(2,1)} %convert_element_type.1222), kind=kOutput, calls=%fused_computation.88 | convolution fusion | flops 14857734144 | bytes 11166720 | tf_op jit(solution)/shard_map/dot_general | solution.py:447
  392.7 31.0 %fusion.34 = bf16[3584,1024]{1,0:T(8,128)(2,1)} fusion(s32[3584]{0:T(1024)S(1)} %eq.58, bf16[1572,1024]{1,0:T(8,128)(2,1)} %collective-permute-done.9, bf16[1572,1024]{1,0:T(8,128)(2,1)} %convert_element_type.1222), kind=kOutput, calls=%fused_computation.69 | convolution fusion | flops 23104876544 | bytes 13793280 | tf_op jit(solution)/shard_map/dot_general | solution.py:447
  444.8 14.4 collective-permute-done.24
  471.0 10.2 collective-permute-done.20
  485.2 81.4 %collective-permute-done.10 = bf16[2304,1024]{1,0:T(8,128)(2,1)} collective-permute-done((bf16[2304,1024]{1,0:T(8,128)(2,1)}, bf16[2304,1024]{1,0:T(8,128)(2,1)}, u32[]{:S(2)}, u32[]{:S(2)}) %collective-permute-start.10) | collective-permute-done | bytes 4718624 | tf_op jit(solution)/shard_map/ppermute | solution.py:48
  567.9 21.0 %fusion.40 = bf16[2304,1024]{1,0:T(8,128)(2,1)} fusion(bf16[2304,1024]{1,0:T(8,128)(2,1)} %collective-permute-done.10, s32[2304]{0:T(1024)S(1)} %copy-done.180, bf16[1572,1024]{1,0:T(8,128)(2,1)} %collective-permute-done.9, bf16[1572,1024]{1,0:T(8,128)(2,1)} %convert_element_type.1222), kind=kOutput, calls=%fused_computation.89 | convolution fusion | flops 14860093440 | bytes 15885312 | tf_op jit(solution)/shard_map/dot_general | solution.py:447
  590.3 14.5 collective-permute-done.106
  623.7 10.2 collective-permute-done.22
  640.7 8.1 collective-permute-done.12
  655.2 7.5 collective-permute-done.16
  664.3 11.2 collective-permute-done.13
  716.1 7.7 add_convert_fusion.1
  727.1 7.3 fusion.12
  734.4 9.2 exponential_reduce_fusion.1
  743.6 8.7 convolution_convert_fusion.3
  770.5 8.0 add_convert_fusion
  781.7 7.3 fusion.13
  788.9 9.2 exponential_reduce_fusion
  798.2 8.2 convolution_convert_fusion.2
  808.3 8.1 fusion.255
  851.1 6.8 fusion.289
  881.8 8.6 fusion.251
  907.0 11.4 fusion.250
  952.0 16.3 convert_reduce_fusion.3
  968.3 13.3 fusion.259
  981.7 8.3 multiply_reduce_fusion.5
  990.0 7.3 fusion.254
  1003.5 8.1 fusion.56
  1011.6 12.0 multiply_reduce_fusion.1
  1023.7 12.4 multiply_convert_fusion.1
  1041.8 6.3 multiply_reduce_fusion.6
  1050.7 15.8 convert_reduce_fusion.4
  1066.5 13.2 fusion.258
  1079.8 7.0 multiply_reduce_fusion.7
  1086.9 9.7 fusion.252
  1102.9 9.1 fusion.57
  1112.0 12.0 multiply_reduce_fusion
  1124.1 12.2 multiply_convert_fusion
  1165.4 5.8 dynamic-slice_bitcast_fusion.1
  1195.8 6.6 constant_dynamic-slice_fusion.17
  1230.5 6.9 collective-permute-done.185
  1245.4 11.3 collective-permute-done.182
  1280.0 9.3 collective-permute-done.187
  1310.7 6.7 collective-permute-done.253
  1326.2 35.8 %fusion.4 = f32[3144,1024]{1,0:T(8,128)} fusion(bf16[2304,1024]{1,0:T(8,128)(2,1)} %bitcast.412, s32[2304]{0:T(1024)S(1)} %copy-done.181), kind=kOutput, calls=%fused_computation.11 | convolution fusion | flops 14842497024 | bytes 17605632 | tf_op jit(solution)/shard_map/dot_general | solution.py:559
  1377.4 12.2 collective-permute-done.252
  1394.2 6.7 collective-permute-done.257
  1408.2 32.6 %fusion = f32[3144,1024]{1,0:T(8,128)} fusion(bf16[3584,1024]{1,0:T(8,128)(2,1)} %bitcast.413, s32[3584]{0:T(1024)S(1)} %copy-done.164), kind=kOutput, calls=%fused_computation.5 | convolution fusion | flops 23088328704 | bytes 20232192 | tf_op jit(solution)/shard_map/dot_general | solution.py:559
  1482.5 58.1 %collective-permute-done.161 = bf16[8,32,3072]{2,1,0:T(8,128)(2,1)} collective-permute-done((bf16[8,32,3072]{2,1,0:T(8,128)(2,1)}, bf16[8,32,3072]{2,1,0:T(8,128)(2,1)}, u32[]{:S(2)}, u32[]{:S(2)}) %collective-permute-start.161) | collective-permute-done | bytes 1572896 | tf_op jit(solution)/shard_map/ppermute | solution.py:48
  1543.6 29.3 %collective-permute-done.151 = bf16[8,32,3072]{2,1,0:T(8,128)(2,1)} collective-permute-done((bf16[8,32,3072]{2,1,0:T(8,128)(2,1)}, bf16[8,32,3072]{2,1,0:T(8,128)(2,1)}, u32[]{:S(2)}, u32[]{:S(2)}) %collective-permute-start.151) | collective-permute-done | bytes 1572896 | tf_op jit(solution)/shard_map/ppermute | solution.py:48
  1585.9 8.9 collective-permute-done.212
  1638.5 5.8 collective-permute-done.213
  1674.1 9.2 collective-permute-done.201
  1687.1 28.5 %collective-permute-done.191 = bf16[8,32,4096]{2,1,0:T(8,128)(2,1)} collective-permute-done((bf16[8,32,4096]{2,1,0:T(8,128)(2,1)}, bf16[8,32,4096]{2,1,0:T(8,128)(2,1)}, u32[]{:S(2)}, u32[]{:S(2)}) %collective-permute-start.191) | collective-permute-done | bytes 2097184 | tf_op jit(solution)/shard_map/ppermute | solution.py:48
  1731.2 7.7 collective-permute-done.228
  1753.3 22.9 %add_add_fusion = f32[3144,1024]{1,0:T(8,128)S(1)} fusion(f32[3144,1024]{1,0:T(8,128)} %fusion, f32[3144,1024]{1,0:T(8,128)} %fusion.250, f32[3144,1024]{1,0:T(8,128)} %fusion.4, bf16[2304,1024]{1,0:T(8,128)(2,1)} %bitcast.414, s32[2304]{0:T(1024)S(1)} %copy-done.179), kind=kOutput, calls=%fused_computation.30 | convolution fusion | flops 14852155392 | bytes 56239104 | tf_op jit(solution)/shard_map/dot_general | solution.py:559
  1808.3 6.4 collective-permute-done.198
  1827.5 7.0 multiply_reduce_fusion.2
  1868.2 19.7 %multiply_subtract_fusion = (f32[1572,1024]{1,0:T(8,128)}, f32[1572,1024]{1,0:T(8,128)}, f32[1572,1024]{1,0:T(8,128)}) fusion(f32[1572,1024]{1,0:T(8,128)} %param.37, f32[]{:T(128)S(6)} %sub.283, f32[]{:T(128)S(6)} %div.267, f32[1572,1024]{1,0:T(8,128)} %collective-permute-done.259, f32[3144,1024]{1,0:T(8,128)} %copy-done, f32[1572,1024]{1,0:T(8,128)} %param.51, ...), kind=kLoop, calls=%fused_computation.72 | loop fusion | flops 25755648 | bytes 51511304 | tf_op jit(solution)/shard_map/sub | solution.py:375
  (1545 shorter events, 1003.2 us)
Async XLA Ops:
  2.1 31.0 %collective-permute-start = (s32[577]{0:T(1024)S(1)}, s32[577]{0:T(1024)S(1)}, u32[]{:S(2)}, u32[]{:S(2)}) collective-permute-start(s32[577]{0:T(1024)S(1)} %pad_add_fusion.1), channel_id=1, source_target_pairs={{0,16},{1,17},{2,18},{3,19},{4,20},{5,21},{6,22},{7,23},{8,24},{9,... | collective-permute-start | bytes 6932 | tf_op jit(solution)/shard_map/ppermute | solution.py:48
  6.7 55.9 %collective-permute-start.28 = (bf16[33,1024]{1,0:T(8,128)(2,1)S(1)}, bf16[33,1024]{1,0:T(8,128)(2,1)S(1)}, u32[]{:S(2)}, u32[]{:S(2)}) collective-permute-start(bf16[33,1024]{1,0:T(8,128)(2,1)S(1)} %pad_maximum_fusion.32), channel_id=1, source_target_pairs={{0,16},{1,17},{2,18},{3,19},{4,20},{5,21},{6,22},{7,23},{8,24},{9,... | collective-permute-start | bytes 202760 | tf_op jit(solution)/shard_map/ppermute | solution.py:48
  7.7 53.0 %collective-permute-start.48 = (bf16[32,1024]{1,0:T(8,128)(2,1)S(1)}, bf16[32,1024]{1,0:T(8,128)(2,1)S(1)}, u32[]{:S(2)}, u32[]{:S(2)}) collective-permute-start(bf16[32,1024]{1,0:T(8,128)(2,1)S(1)} %bitcast.1180), channel_id=1, source_target_pairs={{0,16},{1,17},{2,18},{3,19},{4,20},{5,21},{6,22},{7,23},{8,24},{9,... | collective-permute-start | bytes 196616 | tf_op jit(solution)/shard_map/ppermute | solution.py:48
  9.8 48.7 %collective-permute-start.88 = (bf16[32,1024]{1,0:T(8,128)(2,1)S(1)}, bf16[32,1024]{1,0:T(8,128)(2,1)S(1)}, u32[]{:S(2)}, u32[]{:S(2)}) collective-permute-start(bf16[32,1024]{1,0:T(8,128)(2,1)S(1)} %bitcast.1178), channel_id=1, source_target_pairs={{0,16},{1,17},{2,18},{3,19},{4,20},{5,21},{6,22},{7,23},{8,24},{9,... | collective-permute-start | bytes 196616 | tf_op jit(solution)/shard_map/ppermute | solution.py:48
  58.5 43.0 %collective-permute-start.68 = (bf16[128,1024]{1,0:T(8,128)(2,1)S(1)}, bf16[128,1024]{1,0:T(8,128)(2,1)S(1)}, u32[]{:S(2)}, u32[]{:S(2)}) collective-permute-start(bf16[128,1024]{1,0:T(8,128)(2,1)S(1)} %bitcast.1159), channel_id=1, source_target_pairs={{0,16},{1,17},{2,18},{3,19},{4,20},{5,21},{6,22},{7,23},{8,24},{9,... | collective-permute-start | bytes 786440 | tf_op jit(solution)/shard_map/ppermute | solution.py:48
  60.8 37.3 %collective-permute-start.108 = (bf16[128,1024]{1,0:T(8,128)(2,1)S(1)}, bf16[128,1024]{1,0:T(8,128)(2,1)}, u32[]{:S(2)}, u32[]{:S(2)}) collective-permute-start(bf16[128,1024]{1,0:T(8,128)(2,1)S(1)} %bitcast.1157), channel_id=1, source_target_pairs={{0,16},{1,17},{2,18},{3,19},{4,20},{5,21},{6,22},{7,23},{8,24},{9,... | collective-permute-start | bytes 786440 | tf_op jit(solution)/shard_map/ppermute | solution.py:48
  116.9 31.9 %collective-permute-start.41 = (bf16[32,3072]{1,0:T(8,128)(2,1)}, bf16[32,3072]{1,0:T(8,128)(2,1)}, u32[]{:S(2)}, u32[]{:S(2)}) collective-permute-start(bf16[32,3072]{1,0:T(8,128)(2,1)} %get-tuple-element.208), channel_id=1, source_target_pairs={{0,2},{2,4},{4,6},{6,7},{7,5},{5,3},{3,1},{1,0},{8,10},{10,12},{12... | collective-permute-start | bytes 589832 | tf_op jit(solution)/shard_map/ppermute | solution.py:48
  146.7 36.7 %collective-permute-start.81 = (bf16[32,3072]{1,0:T(8,128)(2,1)}, bf16[32,3072]{1,0:T(8,128)(2,1)}, u32[]{:S(2)}, u32[]{:S(2)}) collective-permute-start(bf16[32,3072]{1,0:T(8,128)(2,1)} %get-tuple-element.207), channel_id=1, source_target_pairs={{0,2},{2,4},{4,6},{6,7},{7,5},{5,3},{3,1},{1,0},{8,10},{10,12},{12... | collective-permute-start | bytes 589832 | tf_op jit(solution)/shard_map/ppermute | solution.py:48
  148.8 81.7 %collective-permute-start.101 = (bf16[32,4096]{1,0:T(8,128)(2,1)}, bf16[32,4096]{1,0:T(8,128)(2,1)}, u32[]{:S(2)}, u32[]{:S(2)}) collective-permute-start(bf16[32,4096]{1,0:T(8,128)(2,1)} %get-tuple-element.203), channel_id=1, source_target_pairs={{0,2},{2,4},{4,6},{6,7},{7,5},{5,3},{3,1},{1,0},{8,10},{10,12},{12... | collective-permute-start | bytes 786440 | tf_op jit(solution)/shard_map/ppermute | solution.py:48
  150.2 33.3 %collective-permute-start.42 = (bf16[32,3072]{1,0:T(8,128)(2,1)}, bf16[32,3072]{1,0:T(8,128)(2,1)}, u32[]{:S(2)}, u32[]{:S(2)}) collective-permute-start(bf16[32,3072]{1,0:T(8,128)(2,1)} %collective-permute-done.41), channel_id=1, source_target_pairs={{0,2},{2,4},{4,6},{6,7},{7,5},{5,3},{3,1},{1,0},{8,10},{10,12},{12... | collective-permute-start | bytes 589832 | tf_op jit(solution)/shard_map/ppermute | solution.py:48
  183.4 49.4 %collective-permute-start.61 = (bf16[32,4096]{1,0:T(8,128)(2,1)}, bf16[32,4096]{1,0:T(8,128)(2,1)}, u32[]{:S(2)}, u32[]{:S(2)}) collective-permute-start(bf16[32,4096]{1,0:T(8,128)(2,1)} %get-tuple-element.204), channel_id=1, source_target_pairs={{0,2},{2,4},{4,6},{6,7},{7,5},{5,3},{3,1},{1,0},{8,10},{10,12},{12... | collective-permute-start | bytes 786440 | tf_op jit(solution)/shard_map/ppermute | solution.py:48
  217.1 62.5 %collective-permute-start.72 = (bf16[2,128,1024]{2,1,0:T(8,128)(2,1)S(1)}, bf16[2,128,1024]{2,1,0:T(8,128)(2,1)S(1)}, u32[]{:S(2)}, u32[]{:S(2)}) collective-permute-start(bf16[2,128,1024]{2,1,0:T(8,128)(2,1)S(1)} %copy-done.98), channel_id=1, source_target_pairs={{0,2},{2,4},{4,6},{6,7},{7,5},{5,3},{3,1},{1,0},{8,10},{10,12},{12... | collective-permute-start | bytes 1572872 | tf_op jit(solution)/shard_map/ppermute | solution.py:48
  253.3 38.5 %collective-permute-start.112 = (bf16[2,128,1024]{2,1,0:T(8,128)(2,1)S(1)}, bf16[2,128,1024]{2,1,0:T(8,128)(2,1)S(1)}, u32[]{:S(2)}, u32[]{:S(2)}) collective-permute-start(bf16[2,128,1024]{2,1,0:T(8,128)(2,1)S(1)} %copy-done.97), channel_id=1, source_target_pairs={{0,2},{2,4},{4,6},{6,7},{7,5},{5,3},{3,1},{1,0},{8,10},{10,12},{12... | collective-permute-start | bytes 1572872 | tf_op jit(solution)/shard_map/ppermute | solution.py:48
  256.1 46.1 %collective-permute-start.57 = (bf16[2,1,8,32,1024]{4,3,2,1,0:T(8,128)(2,1)S(1)}, bf16[2,1,8,32,1024]{4,3,2,1,0:T(8,128)(2,1)S(1)}, u32[]{:S(2)}, u32[]{:S(2)}) collective-permute-start(bf16[2,1,8,32,1024]{4,3,2,1,0:T(8,128)(2,1)S(1)} %copy-done.81), channel_id=1, source_target_pairs={{0,8},{1,9},{2,10},{3,11},{4,12},{5,13},{6,14},{7,15},{8,0},{9,1},... | collective-permute-start | bytes 3145736 | tf_op jit(solution)/shard_map/ppermute | solution.py:48
  271.6 30.8 %collective-permute-start.97 = (bf16[2,1,8,32,1024]{4,3,2,1,0:T(8,128)(2,1)S(1)}, bf16[2,1,8,32,1024]{4,3,2,1,0:T(8,128)(2,1)S(1)}, u32[]{:S(2)}, u32[]{:S(2)}) collective-permute-start(bf16[2,1,8,32,1024]{4,3,2,1,0:T(8,128)(2,1)S(1)} %copy-done.80), channel_id=1, source_target_pairs={{0,8},{1,9},{2,10},{3,11},{4,12},{5,13},{6,14},{7,15},{8,0},{9,1},... | collective-permute-start | bytes 3145736 | tf_op jit(solution)/shard_map/ppermute | solution.py:48
  279.6 38.0 %collective-permute-start.37 = (bf16[2,1,8,33,1024]{4,2,1,0,3:T(8,128)(2,1)S(1)}, bf16[2,1,8,33,1024]{4,2,1,0,3:T(8,128)(2,1)S(1)}, u32[]{:S(2)}, u32[]{:S(2)}) collective-permute-start(bf16[2,1,8,33,1024]{4,2,1,0,3:T(8,128)(2,1)S(1)} %constant_dynamic-slice_fusion.32), channel_id=1, source_target_pairs={{0,8},{1,9},{2,10},{3,11},{4,12},{5,13},{6,14},{7,15},{8,0},{9,1},... | collective-permute-start | bytes 3244040 | tf_op jit(solution)/shard_map/ppermute | solution.py:48
  302.2 69.1 %collective-permute-start.9 = (bf16[1572,1024]{1,0:T(8,128)(2,1)}, bf16[1572,1024]{1,0:T(8,128)(2,1)}, u32[]{:S(2)}, u32[]{:S(2)}) collective-permute-start(bf16[1572,1024]{1,0:T(8,128)(2,1)} %convert_element_type.1222), channel_id=1, source_target_pairs={{0,8},{1,9},{2,10},{3,11},{4,12},{5,13},{6,14},{7,15},{8,0},{9,1},... | collective-permute-start | bytes 9658376 | tf_op jit(solution)/shard_map/ppermute | solution.py:48
  302.3 30.4 %collective-permute-start.71 = (bf16[2,128,1024]{2,1,0:T(8,128)(2,1)}, bf16[2,128,1024]{2,1,0:T(8,128)(2,1)}, u32[]{:S(2)}, u32[]{:S(2)}) collective-permute-start(bf16[2,128,1024]{2,1,0:T(8,128)(2,1)} %collective-permute-done.70), channel_id=1, source_target_pairs={{2,0},{4,2},{6,4},{7,6},{5,7},{3,5},{1,3},{0,1},{10,8},{12,10},{14... | collective-permute-start | bytes 1572872 | tf_op jit(solution)/shard_map/ppermute | solution.py:48
  306.7 37.3 %collective-permute-start.111 = (bf16[2,128,1024]{2,1,0:T(8,128)(2,1)}, bf16[2,128,1024]{2,1,0:T(8,128)(2,1)}, u32[]{:S(2)}, u32[]{:S(2)}) collective-permute-start(bf16[2,128,1024]{2,1,0:T(8,128)(2,1)} %collective-permute-done.110), channel_id=1, source_target_pairs={{2,0},{4,2},{6,4},{7,6},{5,7},{3,5},{1,3},{0,1},{10,8},{12,10},{14... | collective-permute-start | bytes 1572872 | tf_op jit(solution)/shard_map/ppermute | solution.py:48
  349.2 78.2 %collective-permute-start.46 = (bf16[1,1,8,32,3072]{4,3,2,1,0:T(8,128)(2,1)}, bf16[1,1,8,32,3072]{4,3,2,1,0:T(8,128)(2,1)}, u32[]{:S(2)}, u32[]{:S(2)}) collective-permute-start(bf16[1,1,8,32,3072]{4,3,2,1,0:T(8,128)(2,1)} %constant_dynamic-slice_fusion.31), channel_id=1, source_target_pairs={{0,16},{1,17},{2,18},{3,19},{4,20},{5,21},{6,22},{7,23},{8,24},{9,... | collective-permute-start | bytes 4718600 | tf_op jit(solution)/shard_map/ppermute | solution.py:48
  350.7 85.7 %collective-permute-start.86 = (bf16[1,1,8,32,3072]{4,3,2,1,0:T(8,128)(2,1)}, bf16[1,1,8,32,3072]{4,3,2,1,0:T(8,128)(2,1)}, u32[]{:S(2)}, u32[]{:S(2)}) collective-permute-start(bf16[1,1,8,32,3072]{4,3,2,1,0:T(8,128)(2,1)} %constant_dynamic-slice_fusion.25), channel_id=1, source_target_pairs={{0,16},{1,17},{2,18},{3,19},{4,20},{5,21},{6,22},{7,23},{8,24},{9,... | collective-permute-start | bytes 4718600 | tf_op jit(solution)/shard_map/ppermute | solution.py:48
  352.1 113.4 %collective-permute-start.66 = (bf16[1,1,8,32,4096]{4,3,2,1,0:T(8,128)(2,1)S(1)}, bf16[1,1,8,32,4096]{4,3,2,1,0:T(8,128)(2,1)}, u32[]{:S(2)}, u32[]{:S(2)}) collective-permute-start(bf16[1,1,8,32,4096]{4,3,2,1,0:T(8,128)(2,1)S(1)} %copy-done.73), channel_id=1, source_target_pairs={{0,16},{1,17},{2,18},{3,19},{4,20},{5,21},{6,22},{7,23},{8,24},{9,... | collective-permute-start | bytes 6291464 | tf_op jit(solution)/shard_map/ppermute | solution.py:48
  392.1 174.5 %collective-permute-start.10 = (bf16[2304,1024]{1,0:T(8,128)(2,1)}, bf16[2304,1024]{1,0:T(8,128)(2,1)}, u32[]{:S(2)}, u32[]{:S(2)}) collective-permute-start(bf16[2304,1024]{1,0:T(8,128)(2,1)} %fusion.39), channel_id=1, source_target_pairs={{0,16},{1,17},{2,18},{3,19},{4,20},{5,21},{6,22},{7,23},{8,24},{9,... | collective-permute-start | bytes 14155784 | tf_op jit(solution)/shard_map/ppermute | solution.py:48
  434.2 170.5 %collective-permute-start.106 = (bf16[1,1,8,32,4096]{4,3,2,1,0:T(8,128)(2,1)}, bf16[1,1,8,32,4096]{4,3,2,1,0:T(8,128)(2,1)}, u32[]{:S(2)}, u32[]{:S(2)}) collective-permute-start(bf16[1,1,8,32,4096]{4,3,2,1,0:T(8,128)(2,1)} %constant_dynamic-slice_fusion.22), channel_id=1, source_target_pairs={{0,16},{1,17},{2,18},{3,19},{4,20},{5,21},{6,22},{7,23},{8,24},{9,... | collective-permute-start | bytes 6291464 | tf_op jit(solution)/shard_map/ppermute | solution.py:48
  435.9 168.8 %collective-permute-start.47 = (bf16[2,1,8,32,3072]{4,3,2,1,0:T(8,128)(2,1)}, bf16[2,1,8,32,3072]{4,3,2,1,0:T(8,128)(2,1)}, u32[]{:S(2)}, u32[]{:S(2)}) collective-permute-start(bf16[2,1,8,32,3072]{4,3,2,1,0:T(8,128)(2,1)} %constant_dynamic-slice_fusion.30), channel_id=1, source_target_pairs={{0,8},{1,9},{2,10},{3,11},{4,12},{5,13},{6,14},{7,15},{8,0},{9,1},... | collective-permute-start | bytes 9437192 | tf_op jit(solution)/shard_map/ppermute | solution.py:48
  481.3 129.1 %collective-permute-start.87 = (bf16[2,1,8,32,3072]{4,3,2,1,0:T(8,128)(2,1)}, bf16[2,1,8,32,3072]{4,3,2,1,0:T(8,128)(2,1)}, u32[]{:S(2)}, u32[]{:S(2)}) collective-permute-start(bf16[2,1,8,32,3072]{4,3,2,1,0:T(8,128)(2,1)} %constant_dynamic-slice_fusion.24), channel_id=1, source_target_pairs={{0,8},{1,9},{2,10},{3,11},{4,12},{5,13},{6,14},{7,15},{8,0},{9,1},... | collective-permute-start | bytes 9437192 | tf_op jit(solution)/shard_map/ppermute | solution.py:48
  482.8 122.4 %collective-permute-start.21 = (bf16[2,224,1024]{2,1,0:T(8,128)(2,1)}, bf16[2,224,1024]{2,1,0:T(8,128)(2,1)}, u32[]{:S(2)}, u32[]{:S(2)}) collective-permute-start(bf16[2,224,1024]{2,1,0:T(8,128)(2,1)} %fusion.49), channel_id=1, source_target_pairs={{0,2},{2,4},{4,6},{6,7},{7,5},{5,3},{3,1},{1,0},{8,10},{10,12},{12... | collective-permute-start | bytes 2752520 | tf_op jit(solution)/shard_map/ppermute | solution.py:48
  566.6 43.9 %collective-permute-start.26 = (bf16[2,224,1024]{2,1,0:T(8,128)(2,1)}, bf16[2,224,1024]{2,1,0:T(8,128)(2,1)S(1)}, u32[]{:S(2)}, u32[]{:S(2)}) collective-permute-start(bf16[2,224,1024]{2,1,0:T(8,128)(2,1)} %fusion.48), channel_id=1, source_target_pairs={{2,0},{4,2},{6,4},{7,6},{5,7},{3,5},{1,3},{0,1},{10,8},{12,10},{14... | collective-permute-start | bytes 2752520 | tf_op jit(solution)/shard_map/ppermute | solution.py:48
  604.7 74.2 %collective-permute-start.77 = (bf16[2,1,8,128,1024]{4,3,2,1,0:T(8,128)(2,1)}, bf16[2,1,8,128,1024]{4,3,2,1,0:T(8,128)(2,1)}, u32[]{:S(2)}, u32[]{:S(2)}) collective-permute-start(bf16[2,1,8,128,1024]{4,3,2,1,0:T(8,128)(2,1)} %constant_dynamic-slice_fusion.26), channel_id=1, source_target_pairs={{0,8},{1,9},{2,10},{3,11},{4,12},{5,13},{6,14},{7,15},{8,0},{9,1},... | collective-permute-start | bytes 12582920 | tf_op jit(solution)/shard_map/ppermute | solution.py:48
  604.7 79.6 %collective-permute-start.117 = (bf16[2,1,8,128,1024]{4,3,2,1,0:T(8,128)(2,1)}, bf16[2,1,8,128,1024]{4,3,2,1,0:T(8,128)(2,1)}, u32[]{:S(2)}, u32[]{:S(2)}) collective-permute-start(bf16[2,1,8,128,1024]{4,3,2,1,0:T(8,128)(2,1)} %constant_dynamic-slice_fusion.20), channel_id=1, source_target_pairs={{0,8},{1,9},{2,10},{3,11},{4,12},{5,13},{6,14},{7,15},{8,0},{9,1},... | collective-permute-start | bytes 12582920 | tf_op jit(solution)/shard_map/ppermute | solution.py:48
  610.4 82.4 %collective-permute-start.67 = (bf16[2,1,8,32,4096]{4,3,2,1,0:T(8,128)(2,1)}, bf16[2,1,8,32,4096]{4,3,2,1,0:T(8,128)(2,1)}, u32[]{:S(2)}, u32[]{:S(2)}) collective-permute-start(bf16[2,1,8,32,4096]{4,3,2,1,0:T(8,128)(2,1)} %constant_dynamic-slice_fusion.27), channel_id=1, source_target_pairs={{0,8},{1,9},{2,10},{3,11},{4,12},{5,13},{6,14},{7,15},{8,0},{9,1},... | collective-permute-start | bytes 12582920 | tf_op jit(solution)/shard_map/ppermute | solution.py:48
  622.4 73.2 %collective-permute-start.107 = (bf16[2,1,8,32,4096]{4,3,2,1,0:T(8,128)(2,1)}, bf16[2,1,8,32,4096]{4,3,2,1,0:T(8,128)(2,1)}, u32[]{:S(2)}, u32[]{:S(2)}) collective-permute-start(bf16[2,1,8,32,4096]{4,3,2,1,0:T(8,128)(2,1)} %constant_dynamic-slice_fusion.21), channel_id=1, source_target_pairs={{0,8},{1,9},{2,10},{3,11},{4,12},{5,13},{6,14},{7,15},{8,0},{9,1},... | collective-permute-start | bytes 12582920 | tf_op jit(solution)/shard_map/ppermute | solution.py:48
  1149.0 71.4 %collective-permute-start.240 = (bf16[288,1024]{1,0:T(8,128)(2,1)}, bf16[288,1024]{1,0:T(8,128)(2,1)}, u32[]{:S(2)}, u32[]{:S(2)}) collective-permute-start(bf16[288,1024]{1,0:T(8,128)(2,1)} %slice.1451), channel_id=1, source_target_pairs={{2,0},{4,2},{6,4},{7,6},{5,7},{3,5},{1,3},{0,1},{10,8},{12,10},{14... | collective-permute-start | bytes 1769480 | tf_op jit(solution)/shard_map/ppermute | solution.py:48
  1149.7 89.4 %collective-permute-start.243 = (bf16[288,1024]{1,0:T(8,128)(2,1)}, bf16[288,1024]{1,0:T(8,128)(2,1)}, u32[]{:S(2)}, u32[]{:S(2)}) collective-permute-start(bf16[288,1024]{1,0:T(8,128)(2,1)} %slice.1451), channel_id=1, source_target_pairs={{0,2},{2,4},{4,6},{6,7},{7,5},{5,3},{3,1},{1,0},{8,10},{10,12},{12... | collective-permute-start | bytes 1769480 | tf_op jit(solution)/shard_map/ppermute | solution.py:48
  1154.6 69.5 %collective-permute-start.180 = (bf16[2,8,32,1024]{3,2,0,1:T(8,128)(2,1)}, bf16[2,8,32,1024]{3,2,0,1:T(8,128)(2,1)}, u32[]{:S(2)}, u32[]{:S(2)}) collective-permute-start(bf16[2,8,32,1024]{3,2,0,1:T(8,128)(2,1)} %bitcast.1075), channel_id=1, source_target_pairs={{0,8},{1,9},{2,10},{3,11},{4,12},{5,13},{6,14},{7,15},{8,0},{9,1},... | collective-permute-start | bytes 3145736 | tf_op jit(solution)/shard_map/ppermute | solution.py:48
  1218.9 226.9 %collective-permute-start.220 = (bf16[2,8,128,1024]{3,2,0,1:T(8,128)(2,1)}, bf16[2,8,128,1024]{3,2,0,1:T(8,128)(2,1)}, u32[]{:S(2)}, u32[]{:S(2)}) collective-permute-start(bf16[2,8,128,1024]{3,2,0,1:T(8,128)(2,1)} %bitcast.1073), channel_id=1, source_target_pairs={{0,8},{1,9},{2,10},{3,11},{4,12},{5,13},{6,14},{7,15},{8,0},{9,1},... | collective-permute-start | bytes 12582920 | tf_op jit(solution)/shard_map/ppermute | solution.py:48
  1239.1 39.6 %collective-permute-start.250 = (bf16[2,224,1024]{2,1,0:T(8,128)(2,1)S(1)}, bf16[2,224,1024]{2,1,0:T(8,128)(2,1)S(1)}, u32[]{:S(2)}, u32[]{:S(2)}) collective-permute-start(bf16[2,224,1024]{2,1,0:T(8,128)(2,1)S(1)} %pad_maximum_fusion.8), channel_id=1, source_target_pairs={{2,0},{4,2},{6,4},{7,6},{5,7},{3,5},{1,3},{0,1},{10,8},{12,10},{14... | collective-permute-start | bytes 2752520 | tf_op jit(solution)/shard_map/ppermute | solution.py:48
  1239.8 32.5 %collective-permute-start.244 = (bf16[288,1024]{1,0:T(8,128)(2,1)}, bf16[288,1024]{1,0:T(8,128)(2,1)S(1)}, u32[]{:S(2)}, u32[]{:S(2)}) collective-permute-start(bf16[288,1024]{1,0:T(8,128)(2,1)} %collective-permute-done.243), channel_id=1, source_target_pairs={{0,2},{2,4},{4,6},{6,7},{7,5},{5,3},{3,1},{1,0},{8,10},{10,12},{12... | collective-permute-start | bytes 1769480 | tf_op jit(solution)/shard_map/ppermute | solution.py:48
  1272.3 32.8 %collective-permute-start.242 = (bf16[288,1024]{1,0:T(8,128)(2,1)S(1)}, bf16[288,1024]{1,0:T(8,128)(2,1)S(1)}, u32[]{:S(2)}, u32[]{:S(2)}) collective-permute-start(bf16[288,1024]{1,0:T(8,128)(2,1)S(1)} %collective-permute-done.241), channel_id=1, source_target_pairs={{2,0},{4,2},{6,4},{7,6},{5,7},{3,5},{1,3},{0,1},{10,8},{12,10},{14... | collective-permute-start | bytes 1769480 | tf_op jit(solution)/shard_map/ppermute | solution.py:48
  1274.1 31.2 %collective-permute-start.245 = (bf16[288,1024]{1,0:T(8,128)(2,1)S(1)}, bf16[288,1024]{1,0:T(8,128)(2,1)S(1)}, u32[]{:S(2)}, u32[]{:S(2)}) collective-permute-start(bf16[288,1024]{1,0:T(8,128)(2,1)S(1)} %collective-permute-done.244), channel_id=1, source_target_pairs={{0,2},{2,4},{4,6},{6,7},{7,5},{5,3},{3,1},{1,0},{8,10},{10,12},{12... | collective-permute-start | bytes 1769480 | tf_op jit(solution)/shard_map/ppermute | solution.py:48
  1305.2 63.5 %collective-permute-start.160 = (bf16[2,8,32,3072]{3,2,1,0:T(8,128)(2,1)S(1)}, bf16[2,8,32,3072]{3,2,1,0:T(8,128)(2,1)}, u32[]{:S(2)}, u32[]{:S(2)}) collective-permute-start(bf16[2,8,32,3072]{3,2,1,0:T(8,128)(2,1)S(1)} %copy-done.68), channel_id=1, source_target_pairs={{0,8},{1,9},{2,10},{3,11},{4,12},{5,13},{6,14},{7,15},{8,0},{9,1},... | collective-permute-start | bytes 9437192 | tf_op jit(solution)/shard_map/ppermute | solution.py:48
  1317.3 56.8 %collective-permute-start.150 = (bf16[2,8,32,3072]{3,2,1,0:T(8,128)(2,1)}, bf16[2,8,32,3072]{3,2,1,0:T(8,128)(2,1)}, u32[]{:S(2)}, u32[]{:S(2)}) collective-permute-start(bf16[2,8,32,3072]{3,2,1,0:T(8,128)(2,1)} %dynamic-slice_bitcast_fusion.3), channel_id=1, source_target_pairs={{0,8},{1,9},{2,10},{3,11},{4,12},{5,13},{6,14},{7,15},{8,0},{9,1},... | collective-permute-start | bytes 9437192 | tf_op jit(solution)/shard_map/ppermute | solution.py:48
  1317.3 48.2 %collective-permute-start.251 = (bf16[2,224,1024]{2,1,0:T(8,128)(2,1)S(1)}, bf16[2,224,1024]{2,1,0:T(8,128)(2,1)S(1)}, u32[]{:S(2)}, u32[]{:S(2)}) collective-permute-start(bf16[2,224,1024]{2,1,0:T(8,128)(2,1)S(1)} %collective-permute-done.250), channel_id=1, source_target_pairs={{2,0},{4,2},{6,4},{7,6},{5,7},{3,5},{1,3},{0,1},{10,8},{12,10},{14... | collective-permute-start | bytes 2752520 | tf_op jit(solution)/shard_map/ppermute | solution.py:48
  1320.5 47.0 %collective-permute-start.254 = (bf16[2,224,1024]{2,1,0:T(8,128)(2,1)S(1)}, bf16[2,224,1024]{2,1,0:T(8,128)(2,1)}, u32[]{:S(2)}, u32[]{:S(2)}) collective-permute-start(bf16[2,224,1024]{2,1,0:T(8,128)(2,1)S(1)} %collective-permute-done.253), channel_id=1, source_target_pairs={{0,2},{2,4},{4,6},{6,7},{7,5},{5,3},{3,1},{1,0},{8,10},{10,12},{12... | collective-permute-start | bytes 2752520 | tf_op jit(solution)/shard_map/ppermute | solution.py:48
  1365.5 86.5 %collective-permute-start.200 = (bf16[2,8,32,4096]{3,2,1,0:T(8,128)(2,1)}, bf16[2,8,32,4096]{3,2,1,0:T(8,128)(2,1)}, u32[]{:S(2)}, u32[]{:S(2)}) collective-permute-start(bf16[2,8,32,4096]{3,2,1,0:T(8,128)(2,1)} %dynamic-slice_bitcast_fusion), channel_id=1, source_target_pairs={{0,8},{1,9},{2,10},{3,11},{4,12},{5,13},{6,14},{7,15},{8,0},{9,1},... | collective-permute-start | bytes 12582920 | tf_op jit(solution)/shard_map/ppermute | solution.py:48
  1374.1 91.5 %collective-permute-start.210 = (bf16[2,8,128,1024]{3,2,0,1:T(8,128)(2,1)}, bf16[2,8,128,1024]{3,2,0,1:T(8,128)(2,1)}, u32[]{:S(2)}, u32[]{:S(2)}) collective-permute-start(bf16[2,8,128,1024]{3,2,0,1:T(8,128)(2,1)} %bitcast.1147), channel_id=1, source_target_pairs={{0,8},{1,9},{2,10},{3,11},{4,12},{5,13},{6,14},{7,15},{8,0},{9,1},... | collective-permute-start | bytes 12582920 | tf_op jit(solution)/shard_map/ppermute | solution.py:48
  1400.9 58.8 %collective-permute-start.190 = (bf16[2,8,32,4096]{3,2,1,0:T(8,128)(2,1)}, bf16[2,8,32,4096]{3,2,1,0:T(8,128)(2,1)}, u32[]{:S(2)}, u32[]{:S(2)}) collective-permute-start(bf16[2,8,32,4096]{3,2,1,0:T(8,128)(2,1)} %dynamic-slice_bitcast_fusion.1), channel_id=1, source_target_pairs={{0,8},{1,9},{2,10},{3,11},{4,12},{5,13},{6,14},{7,15},{8,0},{9,1},... | collective-permute-start | bytes 12582920 | tf_op jit(solution)/shard_map/ppermute | solution.py:48
  1401.9 351.4 %collective-permute-start.248 = (bf16[8,288,1024]{2,1,0:T(8,128)(2,1)}, bf16[8,288,1024]{2,1,0:T(8,128)(2,1)}, u32[]{:S(2)}, u32[]{:S(2)}) collective-permute-start(bf16[8,288,1024]{2,1,0:T(8,128)(2,1)} %bitcast_dynamic-update-slice_fusion.7), channel_id=1, source_target_pairs={{0,16},{1,17},{2,18},{3,19},{4,20},{5,21},{6,22},{7,23},{8,24},{9,... | collective-permute-start | bytes 14155784 | tf_op jit(solution)/shard_map/ppermute | solution.py:48
  1445.8 94.9 %collective-permute-start.161 = (bf16[8,32,3072]{2,1,0:T(8,128)(2,1)}, bf16[8,32,3072]{2,1,0:T(8,128)(2,1)}, u32[]{:S(2)}, u32[]{:S(2)}) collective-permute-start(bf16[8,32,3072]{2,1,0:T(8,128)(2,1)} %dynamic-slice_bitcast_fusion.6), channel_id=1, source_target_pairs={{0,16},{1,17},{2,18},{3,19},{4,20},{5,21},{6,22},{7,23},{8,24},{9,... | collective-permute-start | bytes 4718600 | tf_op jit(solution)/shard_map/ppermute | solution.py:48
  1452.1 120.8 %collective-permute-start.151 = (bf16[8,32,3072]{2,1,0:T(8,128)(2,1)}, bf16[8,32,3072]{2,1,0:T(8,128)(2,1)}, u32[]{:S(2)}, u32[]{:S(2)}) collective-permute-start(bf16[8,32,3072]{2,1,0:T(8,128)(2,1)} %dynamic-slice_bitcast_fusion.7), channel_id=1, source_target_pairs={{0,16},{1,17},{2,18},{3,19},{4,20},{5,21},{6,22},{7,23},{8,24},{9,... | collective-permute-start | bytes 4718600 | tf_op jit(solution)/shard_map/ppermute | solution.py:48
  1479.7 154.7 %collective-permute-start.226 = (bf16[2,128,1024]{2,1,0:T(8,128)(2,1)S(1)}, bf16[2,128,1024]{2,1,0:T(8,128)(2,1)S(1)}, u32[]{:S(2)}, u32[]{:S(2)}) collective-permute-start(bf16[2,128,1024]{2,1,0:T(8,128)(2,1)S(1)} %pad_maximum_fusion.15), channel_id=1, source_target_pairs={{2,0},{4,2},{6,4},{7,6},{5,7},{3,5},{1,3},{0,1},{10,8},{12,10},{14... | collective-permute-start | bytes 1572872 | tf_op jit(solution)/shard_map/ppermute | solution.py:48
  1481.0 103.3 %collective-permute-start.222 = (bf16[2,128,1024]{2,1,0:T(8,128)(2,1)S(1)}, bf16[2,128,1024]{2,1,0:T(8,128)(2,1)S(1)}, u32[]{:S(2)}, u32[]{:S(2)}) collective-permute-start(bf16[2,128,1024]{2,1,0:T(8,128)(2,1)S(1)} %pad_maximum_fusion.14), channel_id=1, source_target_pairs={{0,2},{2,4},{4,6},{6,7},{7,5},{5,3},{3,1},{1,0},{8,10},{10,12},{12... | collective-permute-start | bytes 1572872 | tf_op jit(solution)/shard_map/ppermute | solution.py:48
  1542.7 33.8 %collective-permute-start.162 = (bf16[16,3072]{1,0:T(8,128)(2,1)S(1)}, bf16[16,3072]{1,0:T(8,128)(2,1)S(1)}, u32[]{:S(2)}, u32[]{:S(2)}) collective-permute-start(bf16[16,3072]{1,0:T(8,128)(2,1)S(1)} %get-tuple-element.179), channel_id=1, source_target_pairs={{0,2},{2,4},{4,6},{6,7},{7,5},{5,3},{3,1},{1,0},{8,10},{10,12},{12... | collective-permute-start | bytes 294920 | tf_op jit(solution)/shard_map/ppermute | solution.py:48
  1581.2 56.7 %collective-permute-start.216 = (bf16[2,128,1024]{2,1,0:T(8,128)(2,1)S(1)}, bf16[2,128,1024]{2,1,0:T(8,128)(2,1)S(1)}, u32[]{:S(2)}, u32[]{:S(2)}) collective-permute-start(bf16[2,128,1024]{2,1,0:T(8,128)(2,1)S(1)} %pad_maximum_fusion.13), channel_id=1, source_target_pairs={{2,0},{4,2},{6,4},{7,6},{5,7},{3,5},{1,3},{0,1},{10,8},{12,10},{14... | collective-permute-start | bytes 1572872 | tf_op jit(solution)/shard_map/ppermute | solution.py:48
  1634.3 49.0 %collective-permute-start.201 = (bf16[8,32,4096]{2,1,0:T(8,128)(2,1)}, bf16[8,32,4096]{2,1,0:T(8,128)(2,1)}, u32[]{:S(2)}, u32[]{:S(2)}) collective-permute-start(bf16[8,32,4096]{2,1,0:T(8,128)(2,1)} %dynamic-slice_bitcast_fusion.4), channel_id=1, source_target_pairs={{0,16},{1,17},{2,18},{3,19},{4,20},{5,21},{6,22},{7,23},{8,24},{9,... | collective-permute-start | bytes 6291464 | tf_op jit(solution)/shard_map/ppermute | solution.py:48
  1635.3 80.3 %collective-permute-start.191 = (bf16[8,32,4096]{2,1,0:T(8,128)(2,1)}, bf16[8,32,4096]{2,1,0:T(8,128)(2,1)}, u32[]{:S(2)}, u32[]{:S(2)}) collective-permute-start(bf16[8,32,4096]{2,1,0:T(8,128)(2,1)} %dynamic-slice_bitcast_fusion.5), channel_id=1, source_target_pairs={{0,16},{1,17},{2,18},{3,19},{4,20},{5,21},{6,22},{7,23},{8,24},{9,... | collective-permute-start | bytes 6291464 | tf_op jit(solution)/shard_map/ppermute | solution.py:48
  1667.0 63.3 %collective-permute-start.224 = (bf16[2,128,1024]{2,1,0:T(8,128)(2,1)}, bf16[2,128,1024]{2,1,0:T(8,128)(2,1)S(1)}, u32[]{:S(2)}, u32[]{:S(2)}) collective-permute-start(bf16[2,128,1024]{2,1,0:T(8,128)(2,1)} %get-tuple-element.132), channel_id=1, source_target_pairs={{0,2},{2,4},{4,6},{6,7},{7,5},{5,3},{3,1},{1,0},{8,10},{10,12},{12... | collective-permute-start | bytes 1572872 | tf_op jit(solution)/shard_map/ppermute | solution.py:48
  1672.5 69.4 %collective-permute-start.214 = (bf16[2,128,1024]{2,1,0:T(8,128)(2,1)}, bf16[2,128,1024]{2,1,0:T(8,128)(2,1)S(1)}, u32[]{:S(2)}, u32[]{:S(2)}) collective-permute-start(bf16[2,128,1024]{2,1,0:T(8,128)(2,1)} %get-tuple-element.124), channel_id=1, source_target_pairs={{0,2},{2,4},{4,6},{6,7},{7,5},{5,3},{3,1},{1,0},{8,10},{10,12},{12... | collective-permute-start | bytes 1572872 | tf_op jit(solution)/shard_map/ppermute | solution.py:48
  1686.4 32.7 %collective-permute-start.202 = (bf16[16,4096]{1,0:T(8,128)(2,1)S(1)}, bf16[16,4096]{1,0:T(8,128)(2,1)S(1)}, u32[]{:S(2)}, u32[]{:S(2)}) collective-permute-start(bf16[16,4096]{1,0:T(8,128)(2,1)S(1)} %get-tuple-element.153), channel_id=1, source_target_pairs={{0,2},{2,4},{4,6},{6,7},{7,5},{5,3},{3,1},{1,0},{8,10},{10,12},{12... | collective-permute-start | bytes 393224 | tf_op jit(solution)/shard_map/ppermute | solution.py:48
  1730.3 66.1 %collective-permute-start.207 = (bf16[32,4096]{1,0:T(8,128)(2,1)}, bf16[32,4096]{1,0:T(8,128)(2,1)}, u32[]{:S(2)}, u32[]{:S(2)}) collective-permute-start(bf16[32,4096]{1,0:T(8,128)(2,1)} %pad_maximum_fusion.20), channel_id=1, source_target_pairs={{2,0},{4,2},{6,4},{7,6},{5,7},{3,5},{1,3},{0,1},{10,8},{12,10},{14... | collective-permute-start | bytes 786440 | tf_op jit(solution)/shard_map/ppermute | solution.py:48
  1741.9 57.7 %collective-permute-start.197 = (bf16[32,4096]{1,0:T(8,128)(2,1)}, bf16[32,4096]{1,0:T(8,128)(2,1)}, u32[]{:S(2)}, u32[]{:S(2)}) collective-permute-start(bf16[32,4096]{1,0:T(8,128)(2,1)} %pad_maximum_fusion.18), channel_id=1, source_target_pairs={{2,0},{4,2},{6,4},{7,6},{5,7},{3,5},{1,3},{0,1},{10,8},{12,10},{14... | collective-permute-start | bytes 786440 | tf_op jit(solution)/shard_map/ppermute | solution.py:48
  1749.2 37.9 %collective-permute-start.229 = (bf16[128,1024]{1,0:T(8,128)(2,1)}, bf16[128,1024]{1,0:T(8,128)(2,1)}, u32[]{:S(2)}, u32[]{:S(2)}) collective-permute-start(bf16[128,1024]{1,0:T(8,128)(2,1)} %fusion.128), channel_id=1, source_target_pairs={{0,16},{1,17},{2,18},{3,19},{4,20},{5,21},{6,22},{7,23},{8,24},{9,... | collective-permute-start | bytes 786440 | tf_op jit(solution)/shard_map/ppermute | solution.py:48
  1751.6 38.5 %collective-permute-start.219 = (bf16[128,1024]{1,0:T(8,128)(2,1)}, bf16[128,1024]{1,0:T(8,128)(2,1)S(1)}, u32[]{:S(2)}, u32[]{:S(2)}) collective-permute-start(bf16[128,1024]{1,0:T(8,128)(2,1)} %fusion.127), channel_id=1, source_target_pairs={{0,16},{1,17},{2,18},{3,19},{4,20},{5,21},{6,22},{7,23},{8,24},{9,... | collective-permute-start | bytes 786440 | tf_op jit(solution)/shard_map/ppermute | solution.py:48
  1782.8 44.7 %collective-permute-start.259 = (f32[1572,1024]{1,0:T(8,128)}, f32[1572,1024]{1,0:T(8,128)}, u32[]{:S(2)}, u32[]{:S(2)}) collective-permute-start(f32[1572,1024]{1,0:T(8,128)} %slice.1458), channel_id=1, source_target_pairs={{0,8},{1,9},{2,10},{3,11},{4,12},{5,13},{6,14},{7,15},{8,0},{9,1},... | collective-permute-start | bytes 19316744 | tf_op jit(solution)/shard_map/ppermute | solution.py:48
  (442 other events, 6322.6 us)

commit v2 on v1

--- a/solution.py
+++ b/solution.py
@@ -1,6 +1,10 @@
+import functools
+
 import jax
 import jax.numpy as jnp
 from jax import lax
+from jax.experimental import pallas as pl
+from jax.experimental.pallas import tpu as pltpu
 from jax.sharding import PartitionSpec as P
 
 D = 1024
@@ -111,45 +115,6 @@
             + from_right.astype(jnp.float32)
         )
 
-    def gather_rows(self, shard, ring_first):
-        size, halves = self.size, self.halves
-        rows, columns = shard.shape
-        whole = jnp.zeros((halves, 2, size, rows, columns), shard.dtype)
-        zero = jnp.int32(0)
-        if ring_first:
-            pieces = self.ring_gather(shard)
-            for at in range(size):
-                whole = lax.dynamic_update_slice(
-                    whole,
-                    pieces[at][None, None, None],
-                    (self.half, self.core, self.wide_of(at), zero, zero),
-                )
-            mine = lax.dynamic_slice(
-                whole, (self.half, self.core, zero, zero, zero), (1, 1, size, rows, columns)
-            )
-            whole = lax.dynamic_update_slice(
-                whole, self.swap_half(mine), (1 - self.half, self.core, zero, zero, zero)
-            )
-        else:
-            other = self.swap_half(shard)
-            pair = jnp.where(
-                self.half == 0, jnp.stack([shard, other]), jnp.stack([other, shard])
-            )
-            pieces = self.ring_gather(pair)
-            for at in range(size):
-                whole = lax.dynamic_update_slice(
-                    whole,
-                    pieces[at][:, None, None],
-                    (zero, self.core, self.wide_of(at), zero, zero),
-                )
-        mine = lax.dynamic_slice(
-            whole, (zero, self.core, zero, zero, zero), (halves, 1, size, rows, columns)
-        )
-        whole = lax.dynamic_update_slice(
-            whole, self.swap_core(mine), (zero, 1 - self.core, zero, zero, zero)
-        )
-        return whole.reshape(halves * 2 * size * rows, columns)
-
     def reduce_rows(self, array, half_first, low):
         size, halves = self.size, self.halves
         rows = array.shape[0] // (halves * 2 * size)
@@ -185,23 +150,432 @@
         return value
 
 
-def fetch_layer(net, w_qkv, w_out, w_fc, w_proj, layer_at):
-    return (
-        net.gather_rows(w_qkv[layer_at].astype(jnp.bfloat16), True),
-        net.gather_rows(w_out[layer_at].astype(jnp.bfloat16), False),
-        net.gather_rows(w_fc[layer_at].astype(jnp.bfloat16), True),
-        net.gather_rows(w_proj[layer_at].astype(jnp.bfloat16), False),
-    )
-
-
-def reduce_layer(net, grad_wqkv, grad_wout, grad_wfc, grad_wproj):
-    low = jnp.bfloat16
-    return (
-        net.reduce_rows(grad_wqkv, True, low),
-        net.reduce_rows(grad_wout, False, low),
-        net.reduce_rows(grad_wfc, True, low),
-        net.reduce_rows(grad_wproj, False, low),
-    )
+MESH = pl.DeviceIdType.MESH
+
+
+class Spot:
+    def __init__(self, size):
+        self.size = size
+        narrow, wide = lax.axis_index("narrow"), lax.axis_index("wide")
+        odd = lax.rem(wide, 2)
+        self.core, self.half = lax.rem(narrow, 2), lax.div(narrow, 2)
+        self.wide = wide
+        self.place = (1 - odd) * lax.div(wide, 2) + odd * (size - 1 - lax.div(wide, 2))
+        self.to_core = (narrow + 1 - 2 * self.core, wide)
+        self.to_half = (narrow + 2 - 4 * self.half, wide)
+        self.right = (narrow, self.wide_of(1))
+        self.left = (narrow, self.wide_of(size - 1))
+
+    def wide_of(self, offset):
+        at = lax.rem(self.place + offset, self.size)
+        late = lax.div(at, self.size // 2)
+        return (1 - late) * 2 * at + late * (2 * (self.size - 1 - at) + 1)
+
+    def index(self, turned, other_core, offset):
+        half = self.half + turned * (1 - 2 * self.half)
+        core = self.core + other_core * (1 - 2 * self.core)
+        return (2 * half + core) * self.size + self.wide_of(offset)
+
+    def meet(self, with_core):
+        barrier = pltpu.get_barrier_semaphore()
+        peers = [self.to_half, self.right, self.left] + ([self.to_core] if with_core else [])
+        for peer in peers:
+            pl.semaphore_signal(barrier, inc=1, device_id=peer, device_id_type=MESH)
+        pl.semaphore_wait(barrier, len(peers))
+
+
+def cut_of(rows):
+    return rows // 2 if rows % 32 == 0 else rows
+
+
+def gather_body(size, ring_first, across, *refs):
+    count = len(ring_first)
+    shards, wholes = refs[:count], refs[count : 2 * count]
+    ring_sem, half_sem, core_sem, send_sem, local_sem = refs[2 * count :]
+    spot = Spot(size)
+    far = size // 2
+
+    def index(turned, offset, toward=None):
+        if across:
+            return spot.index(turned, 0, offset % size)
+        if toward == "half":
+            turned = 1 - turned
+        offset = offset + {"right": -1, "left": 1}.get(toward, 0)
+        return turned * size + offset % size
+
+    def send(at, source, turned, offset, toward, sem, rows=None):
+        target = wholes[at].at[index(turned, offset, toward)]
+        if rows is not None:
+            source, target = source.at[rows], target.at[rows]
+        device = {
+            "half": spot.to_half,
+            "right": spot.right,
+            "left": spot.left,
+            "core": spot.to_core,
+        }[toward]
+        pltpu.make_async_remote_copy(
+            src_ref=source,
+            dst_ref=target,
+            send_sem=send_sem.at[at],
+            recv_sem=sem,
+            device_id=device,
+            device_id_type=MESH,
+        ).start()
+
+    def landed(region, sem):
+        pltpu.make_async_copy(region, region, sem).wait()
+
+    def piece(at, turned, offset):
+        return wholes[at].at[index(turned, offset)]
+
+    def on_core(at, source, turned, offset):
+        if across:
+            send(at, source, turned, offset, "core", core_sem.at[at])
+
+    def on_ring(at, turned, source, offset, way, step, rows=None):
+        toward = ("right", "left")[way]
+        send(at, source, turned, offset, toward, ring_sem.at[at, turned, way, step], rows)
+
+    spot.meet(across)
+    locals_ = []
+    for at in range(count):
+        copy = pltpu.make_async_copy(shards[at], piece(at, 0, 0), local_sem.at[at])
+        copy.start()
+        locals_.append(copy)
+    for at in range(count):
+        if not ring_first[at]:
+            send(at, shards[at], 0, 0, "half", half_sem.at[at, 0])
+    for at in range(count):
+        if ring_first[at]:
+            on_ring(at, 0, shards[at], 0, 0, 1)
+            on_ring(at, 0, shards[at], 0, 1, 1)
+            send(at, shards[at], 0, 0, "half", half_sem.at[at, 0])
+    for at in range(count):
+        on_core(at, shards[at], 0, 0)
+    for at in range(count):
+        if not ring_first[at]:
+            landed(piece(at, 1, 0), half_sem.at[at, 0])
+            for way in (0, 1):
+                on_ring(at, 0, shards[at], 0, way, 1)
+                on_ring(at, 1, piece(at, 1, 0), 0, way, 1)
+            on_core(at, piece(at, 1, 0), 1, 0)
+
+    def turned_arrivals(at, step):
+        offsets = (0,) if step == 0 else (far,) if step == far else (-step, step)
+        for offset in offsets:
+            landed(piece(at, 1, offset), half_sem.at[at, offset % size])
+            on_core(at, piece(at, 1, offset), 1, offset)
+
+    for step in range(1, far + 1):
+        for at in range(count):
+            rows = shards[at].shape[0]
+            cut = cut_of(rows)
+            if ring_first[at]:
+                if step < far:
+                    for way in (0, 1):
+                        offset = (-step, step)[way]
+                        here = piece(at, 0, offset)
+                        landed(here, ring_sem.at[at, 0, way, step])
+                        if step < far - 1:
+                            on_ring(at, 0, here, offset, way, step + 1)
+                        elif way == 0:
+                            on_ring(at, 0, here, offset, way, step + 1, pl.ds(0, cut))
+                        elif cut < rows:
+                            on_ring(at, 0, here, offset, way, step + 1, pl.ds(cut, rows - cut))
+                        send(at, here, 0, offset, "half", half_sem.at[at, offset % size])
+                        on_core(at, here, 0, offset)
+                else:
+                    here = piece(at, 0, far)
+                    landed(here.at[pl.ds(0, cut)], ring_sem.at[at, 0, 0, step])
+                    if cut < rows:
+                        landed(here.at[pl.ds(cut, rows - cut)], ring_sem.at[at, 0, 1, step])
+                    send(at, here, 0, far, "half", half_sem.at[at, far])
+                    on_core(at, here, 0, far)
+                turned_arrivals(at, step - 1)
+            else:
+                for way in (0, 1):
+                    for turned in (0, 1):
+                        if step == far and turned != way:
+                            continue
+                        offset = (-step, step)[way]
+                        here = piece(at, turned, offset)
+                        landed(here, ring_sem.at[at, turned, way, step])
+                        if step < far - 1 or (step == far - 1 and turned == way):
+                            on_ring(at, turned, here, offset, way, step + 1)
+                        on_core(at, here, turned, offset)
+    for at in range(count):
+        if ring_first[at]:
+            turned_arrivals(at, far)
+    for at in range(count):
+        locals_[at].wait()
+        if across:
+            landed(wholes[at].at[pl.ds(0, 2 * size)], core_sem.at[at])
+        sent = 4 * size - 1 if across else 2 * size - 1
+        landed(wholes[at].at[pl.ds(0, sent)], send_sem.at[at])
+
+
+def gather_call(size, shards, ring_first, across, number):
+    count = len(shards)
+    total = (4 if across else 2) * size
+    half_waits = size
+    outs = [jax.ShapeDtypeStruct((total,) + a.shape, a.dtype) for a in shards]
+    return pl.pallas_call(
+        functools.partial(gather_body, size, ring_first, across),
+        out_shape=outs,
+        in_specs=[pl.BlockSpec(memory_space=pl.ANY)] * count,
+        out_specs=[pl.BlockSpec(memory_space=pl.ANY)] * count,
+        scratch_shapes=[
+            pltpu.SemaphoreType.DMA((count, 2, 2, size // 2 + 1)),
+            pltpu.SemaphoreType.DMA((count, half_waits)),
+            pltpu.SemaphoreType.DMA((count,)),
+            pltpu.SemaphoreType.DMA((count,)),
+            pltpu.SemaphoreType.DMA((count,)),
+        ],
+        compiler_params=pltpu.CompilerParams(collective_id=number, has_side_effects=True),
+    )(*shards)
+
+
+def scatter_body(size, half_first, across, *refs):
+    count = len(half_first)
+    arrays, outs = refs[:count], refs[count : 2 * count]
+    own, core_in, half_in, ring_in = (
+        refs[(2 + part) * count : (3 + part) * count] for part in range(4)
+    )
+    local_sem, core_sem, half_sem, ring_sem, send_sem = refs[6 * count :]
+    spot = Spot(size)
+    far = size // 2
+    slots = [far] + [o for at in range(far - 1, 0, -1) for o in (at, -at)] + [0]
+    sent = []
+
+    def landed(region, sem):
+        pltpu.make_async_copy(region, region, sem).wait()
+
+    def send(source, target, device, number, at, sem):
+        copy = pltpu.make_async_remote_copy(
+            src_ref=source,
+            dst_ref=target,
+            send_sem=send_sem.at[at, number],
+            recv_sem=sem,
+            device_id=device,
+            device_id_type=MESH,
+        )
+        copy.start()
+        sent.append(copy)
+
+    def source_of(at, turned, other_core, offset):
+        if across:
+            return arrays[at].at[spot.index(turned, other_core, offset % size)]
+        return arrays[at].at[turned * size + offset % size]
+
+    def add(target, parts):
+        rows, columns = target.shape
+        width = 512 if columns % 512 == 0 else 256 if columns % 256 == 0 else 128
+
+        def one(step, nothing):
+            window = pl.ds(pl.multiple_of(step * width, width), width)
+            total = parts[0][0][:, window].astype(jnp.float32)
+            for part, first, last in parts[1:]:
+                if first == 0 and last == rows:
+                    total = total + part[:, window].astype(jnp.float32)
+            target[:, window] = total.astype(target.dtype)
+            for part, first, last in parts[1:]:
+                if first != 0 or last != rows:
+                    span = pl.ds(first, last - first)
+                    target[span, window] = (
+                        total[first:last] + part[span, window].astype(jnp.float32)
+                    ).astype(target.dtype)
+            return nothing
+
+        lax.fori_loop(0, columns // width, one, 0)
+
+    def ring_slot(way, step):
+        return way * far + step - 1
+
+    def base(at, turned, offset):
+        k = offset % size
+        rows = own[at].shape[1]
+        here = own[at].at[turned * size + k]
+        landed(here, local_sem.at[at, turned * size + k])
+        parts = [(here, 0, rows)]
+        if across:
+            there = core_in[at].at[turned * size + k]
+            landed(there, core_sem.at[at, turned * size + k])
+            parts.append((there, 0, rows))
+        return here, parts
+
+    def ring_parts(at, turned, offset):
+        parts = []
+        rows = own[at].shape[1]
+        cut = cut_of(rows)
+        ways = (0, 1) if offset == 0 else (0,) if offset > 0 else (1,)
+        for way in ways:
+            step = far - abs(offset)
+            slot = ring_slot(way, step)
+            if half_first[at]:
+                if step == 1:
+                    first, last = (0, cut) if way == 0 else (cut, rows)
+                else:
+                    first, last = 0, rows
+                if first == last:
+                    continue
+                region = ring_in[at].at[slot]
+                span = region if (first, last) == (0, rows) else region.at[pl.ds(first, last - first)]
+                landed(span, ring_sem.at[at, slot])
+                parts.append((region, first, last))
+            else:
+                if step == 1 and turned != way:
+                    continue
+                region = ring_in[at].at[turned * 2 * far + slot]
+                landed(region, ring_sem.at[at, turned * 2 * far + slot])
+                parts.append((region, 0, rows))
+        return parts
+
+    def ring_send(at, turned, offset):
+        here = own[at].at[turned * size + offset % size]
+        rows = own[at].shape[1]
+        cut = cut_of(rows)
+        step = far - abs(offset) + 1
+        if offset == far:
+            if half_first[at]:
+                spans = [(0, pl.ds(0, cut))] + ([(1, pl.ds(cut, rows - cut))] if cut < rows else [])
+                for way, span in spans:
+                    slot = ring_slot(way, 1)
+                    send(
+                        here.at[span],
+                        ring_in[at].at[slot].at[span],
+                        (spot.right, spot.left)[way],
+                        slot,
+                        at,
+                        ring_sem.at[at, slot],
+                    )
+                return
+            ways = (turned,)
+        else:
+            ways = (0,) if offset > 0 else (1,)
+        for way in ways:
+            slot = ring_slot(way, step) + (0 if half_first[at] else turned * 2 * far)
+            send(
+                here,
+                ring_in[at].at[slot],
+                (spot.right, spot.left)[way],
+                slot,
+                at,
+                ring_sem.at[at, slot],
+            )
+
+    spot.meet(across)
+    core_base = 4 * far + size
+    for offset in slots:
+        k = offset % size
+        for turned in (1, 0):
+            for at in range(count):
+                if across:
+                    send(
+                        source_of(at, turned, 1, offset),
+                        core_in[at].at[turned * size + k],
+                        spot.to_core,
+                        core_base + turned * size + k,
+                        at,
+                        core_sem.at[at, turned * size + k],
+                    )
+                pltpu.make_async_copy(
+                    source_of(at, turned, 0, offset),
+                    own[at].at[turned * size + k],
+                    local_sem.at[at, turned * size + k],
+                ).start()
+
+    def turned_half(offset):
+        for at in range(count):
+            if half_first[at]:
+                here, parts = base(at, 1, offset)
+                k = offset % size
+                if across:
+                    add(here, parts)
+                send(here, half_in[at].at[k], spot.to_half, 4 * far + k, at, half_sem.at[at, k])
+
+    def straight(offset):
+        for at in range(count):
+            if half_first[at]:
+                here, parts = base(at, 0, offset)
+                k = offset % size
+                landed(half_in[at].at[k], half_sem.at[at, k])
+                parts.append((half_in[at].at[k], 0, own[at].shape[1]))
+                parts += ring_parts(at, 0, offset) if offset != far else []
+                if offset == 0:
+                    add(outs[at], parts)
+                else:
+                    add(here, parts)
+                    ring_send(at, 0, offset)
+
+    def both(offset):
+        for at in range(count):
+            if not half_first[at]:
+                for turned in (1, 0):
+                    here, parts = base(at, turned, offset)
+                    parts += ring_parts(at, turned, offset) if offset != far else []
+                    if offset == 0 and turned == 0:
+                        landed(half_in[at].at[0], half_sem.at[at, 0])
+                        parts.append((half_in[at].at[0], 0, own[at].shape[1]))
+                        add(outs[at], parts)
+                        continue
+                    if len(parts) > 1:
+                        add(here, parts)
+                    if offset == 0:
+                        send(here, half_in[at].at[0], spot.to_half, 4 * far, at, half_sem.at[at, 0])
+                    else:
+                        ring_send(at, turned, offset)
+
+    groups = [[far]] + [[at, -at] for at in range(far - 1, 0, -1)] + [[0]]
+    for number, group in enumerate(groups):
+        for offset in group:
+            turned_half(offset)
+        for offset in group:
+            both(offset)
+        if number > 0:
+            for offset in groups[number - 1]:
+                straight(offset)
+    for offset in groups[-1]:
+        straight(offset)
+    for copy in sent:
+        copy.wait_send()
+
+
+def scatter_call(size, arrays, half_first, across, out_type, number):
+    count = len(arrays)
+    far = size // 2
+    pieces = [a.shape[1:] for a in arrays]
+    own = [pltpu.VMEM((2 * size,) + p, a.dtype) for p, a in zip(pieces, arrays)]
+    core_in = [
+        pltpu.VMEM((2 * size if across else 1,) + p, a.dtype) for p, a in zip(pieces, arrays)
+    ]
+    half_in = [
+        pltpu.VMEM((size if first else 1,) + p, a.dtype)
+        for p, a, first in zip(pieces, arrays, half_first)
+    ]
+    ring_in = [
+        pltpu.VMEM((2 * far if first else 4 * far,) + p, a.dtype)
+        for p, a, first in zip(pieces, arrays, half_first)
+    ]
+    return pl.pallas_call(
+        functools.partial(scatter_body, size, half_first, across),
+        out_shape=[jax.ShapeDtypeStruct(p, out_type) for p in pieces],
+        in_specs=[pl.BlockSpec(memory_space=pl.ANY)] * count,
+        out_specs=[pl.BlockSpec(memory_space=pltpu.VMEM)] * count,
+        scratch_shapes=own
+        + core_in
+        + half_in
+        + ring_in
+        + [
+            pltpu.SemaphoreType.DMA((count, 2 * size)),
+            pltpu.SemaphoreType.DMA((count, 2 * size)),
+            pltpu.SemaphoreType.DMA((count, size)),
+            pltpu.SemaphoreType.DMA((count, 4 * far)),
+            pltpu.SemaphoreType.DMA((count, 4 * far + 3 * size)),
+        ],
+        compiler_params=pltpu.CompilerParams(
+            collective_id=number, has_side_effects=True, vmem_limit_bytes=60 * 1024 * 1024
+        ),
+    )(*arrays)
 
 
 def layer_norm(values, gain, shift):
@@ -451,32 +825,57 @@
     shared = pos_table.shape[0]
     vector_rows = -(-vectors.shape[0] // D)
     padded = jnp.pad(vectors, (0, vector_rows * D - vectors.shape[0])).reshape(vector_rows, D)
-    small_low = net.gather_rows(jnp.concatenate([pos_table, padded]).astype(low), False)
-    small_low = small_low.reshape(devices, shared + vector_rows, D)
+    spare = -(shared + vector_rows) % 16
+    small_own = jnp.concatenate([pos_table, padded, jnp.zeros((spare, D), jnp.float32)])
+    shards_low = []
+    for layer_at in range(LAYERS):
+        shards_low += [part[layer_at].astype(low) for part in (w_qkv, w_fc, w_proj, w_out)]
+    gathered = gather_call(
+        size,
+        shards_low + [small_own.astype(low)],
+        (True, True, False, False) * LAYERS + (False,),
+        True,
+        1,
+    )
+    small_low = gathered[-1]
     pos_low = small_low[:, :shared].reshape(devices * shared, D)
     vector_all = (
-        small_low[:, shared:]
+        small_low[:, shared : shared + vector_rows]
         .reshape(devices, vector_rows * D)[:, : vectors.shape[0]]
         .reshape(-1)
         .astype(jnp.float32)
     )
 
-    near_other = look_up(local_tokens[1, :, :near])
-    near_swapped = net.swap_half(near_other)
-    rest_both = look_up(local_tokens[:, :, near:].transpose(1, 0, 2)).reshape(
-        size, halves, rest, D
-    )
-    near_own = (look_up(local_tokens[0, :, :near]) + near_swapped).reshape(size, near, D)
-    near_rows = net.ring_scatter(lambda at: near_own[at], low)
-    rest_sum = net.ring_scatter(lambda at: rest_both[at], low)
-    rest_rows = rest_sum[0] + net.swap_half(rest_sum[1].astype(low)).astype(jnp.float32)
-    stream = jnp.concatenate([near_rows, rest_rows]) + pos_low[:LEN].astype(jnp.float32)
+    near_all = look_up(local_tokens[:, :, :near]).reshape(same_core, near, D)
+    rest_all = look_up(local_tokens[:, :, near:]).reshape(same_core, rest, D)
+    bands = max(1, same_core // 16)
+    band = D // bands
+    stream = jnp.concatenate(
+        [
+            jnp.concatenate(
+                scatter_call(
+                    size,
+                    [part[:, :, at * band : (at + 1) * band] for part in (near_all, rest_all)],
+                    (True, False),
+                    False,
+                    low,
+                    2,
+                )
+            )
+            for at in range(bands)
+        ],
+        axis=1,
+    )
+    stream = stream.astype(jnp.float32) + pos_low[:LEN].astype(jnp.float32)
 
     allowed = attention_mask(seq_lengths[0])
     kept_weights = []
     saved_list = []
     for layer_at in range(LAYERS):
-        weights = fetch_layer(net, w_qkv, w_out, w_fc, w_proj, layer_at)
+        w_a, w_c, w_d, w_b = (
+            part.reshape(-1, part.shape[2]) for part in gathered[layer_at * 4 : layer_at * 4 + 4]
+        )
+        weights = (w_a, w_b, w_c, w_d)
         kept_weights.append(weights)
         stream, saved_acts = layer_forward(
             stream, weights, vector_all[layer_at * per_layer : (layer_at + 1) * per_layer], allowed
@@ -547,29 +946,31 @@
             allowed,
         )
         grad_a, grad_b, grad_c, grad_d = full_grads
-        layer_shards.insert(0, reduce_layer(net, grad_a, grad_b, grad_c, grad_d))
+        shard_a, shard_c, shard_d, shard_b = scatter_call(
+            size,
+            [part.reshape(devices, -1, part.shape[1]) for part in (grad_a, grad_c, grad_d, grad_b)],
+            (True, True, False, False),
+            True,
+            jnp.float32,
+            3,
+        )
+        layer_shards.insert(0, (shard_a, shard_b, shard_c, shard_d))
         vector_grads.insert(0, grad_vector)
     grad_low = grad_stream.astype(low)
     grad_near, grad_rest = grad_low[:near], grad_low[near:]
-    near_own = jnp.stack(net.ring_gather(grad_near))
-    near_other = net.swap_half(near_own)
-    rest_all = jnp.stack(net.ring_gather(jnp.stack([grad_rest, net.swap_half(grad_rest)])))
+    near_all, rest_all = gather_call(size, [grad_near, grad_rest], (True, False), False, 4)
 
     def spread(ids, rows):
         return jnp.dot(one_hot(ids.reshape(-1)).T, rows, preferred_element_type=jnp.float32)
 
     grad_table = jnp.dot(grad_logits.T, group_rows, preferred_element_type=jnp.float32)
-    grad_table = grad_table + spread(local_tokens[0, :, :near], near_own.reshape(-1, D))
-    grad_table = grad_table + spread(
-        local_tokens[:, :, near:].transpose(1, 0, 2), rest_all.reshape(-1, D)
-    )
-    grad_table = grad_table + spread(local_tokens[1, :, :near], near_other.reshape(-1, D))
+    grad_table = grad_table + spread(local_tokens[:, :, :near], near_all.reshape(-1, D))
+    grad_table = grad_table + spread(local_tokens[:, :, near:], rest_all.reshape(-1, D))
     table_shard = grad_table[:own_rows] + net.swap_core(grad_table[own_rows:])
     grad_pos = jnp.concatenate(
         [
-            jnp.sum(near_own.astype(jnp.float32), axis=0)
-            + jnp.sum(near_other.astype(jnp.float32), axis=0),
-            jnp.sum(rest_all.astype(jnp.float32), axis=(0, 1)),
+            jnp.sum(near_all.astype(jnp.float32), axis=0),
+            jnp.sum(rest_all.astype(jnp.float32), axis=0),
         ]
     )
     grad_pos = jnp.pad(grad_pos, ((0, POS - LEN), (0, 0)))

time: 1900 us -> 1420 us (0.75)
  Pallas kernels: 0 us -> 648 us
  waiting for transfers between devices: 617 us -> 59.8 us
  local copies, waits for them, and re-layouts: 322 us -> 51.3 us
  starting transfers between devices: 267 us -> 59.1 us
  other arithmetic: 233 us -> 163 us
  matrix products: 435 us -> 415 us
    pallas_call x0 -> x5, Pallas kernels: none -> 648 us  [the longest x3 342 us: scatter_call(): pl.pallas_call(functools.partial(scatter_body, size, half_first, across),...]
    ppermute x265 -> x59, waiting for transfers between devices: 617 us -> 59.8 us  [step(): return lax.ppermute(array, ('narrow', 'wide'), pairs)]
    ppermute x265 -> x59, starting transfers between devices: 267 us -> 59.1 us  [step(): return lax.ppermute(array, ('narrow', 'wide'), pairs)]
    dynamic_update_slice x73 -> x0, local copies, waits for them, and re-layouts: 133 us -> none  [the longest x32 72.7 us: gather_rows(): lax.dynamic_update_slice(whole, pieces[at][:, None, None], (zero, self.co...]
    dynamic_slice x19 -> x0, local copies, waits for them, and re-layouts: 55.1 us -> none  [the longest x9 24.8 us: gather_rows(): lax.dynamic_slice(whole, (zero, self.core, zero, zero, zero), (halves, 1,...]
    convert_element_type x44 -> x3, other arithmetic: 57.1 us -> 4.26 us  [the longest x2 4.25 us: on_device(): stream = stream.astype(jnp.float32) + pos_low[:LEN].astype(jnp.float32)]
    unnamed x517 -> x417, local copies, waits for them, and re-layouts: 49.2 us -> 15.3 us
    dot_general x3 -> x2, matrix products: 91.3 us -> 69.1 us  [spread(): jnp.dot(one_hot(ids.reshape(-1)).T, rows, preferred_element_type=jnp.floa...]
  transfers between devices with their start and end apart: 265 -> 59, of which waited for: 120 -> 30; matrix products, arithmetic and copies ran while one was open for 31% -> 6% of each run, Pallas kernels for 0% -> 29%
where the time goes in v2:
time: 1420 us; the launch traced here: 1410 us
  Pallas kernels  648 us (46%)
  matrix products  415 us (29%)
  other arithmetic  163 us (11%)
  waiting for transfers between devices  59.8 us (4%)
  starting transfers between devices  59.1 us (4%)
  local copies, waits for them, and re-layouts  51.3 us (4%)
  between operations  15.1 us (1%)
    pallas_call x3, Pallas kernels, scatter_call(): pl.pallas_call(functools.partial(scatter_body, size, half_first, across),...  342 us
    pallas_call x2, Pallas kernels, gather_call(): pl.pallas_call(functools.partial(gather_body, size, ring_first, across),...  305 us
    dot_general x2, matrix products, look_up(): jnp.dot(one_hot(ids.reshape(-1)), table_low, preferred_element_type=jnp.f...  70 us
    dot_general x2, matrix products, spread(): jnp.dot(one_hot(ids.reshape(-1)).T, rows, preferred_element_type=jnp.floa...  69.1 us
    ppermute x59, waiting for transfers between devices, step(): return lax.ppermute(array, ('narrow', 'wide'), pairs)  59.8 us
    ppermute x59, starting transfers between devices, step(): return lax.ppermute(array, ('narrow', 'wide'), pairs)  59.1 us
    dot_general x2, matrix products, layer_backward(): jnp.dot(branch_low, w_proj.T, preferred_element_type=jnp.float32)  33.3 us
    sub x7, other arithmetic, adamw(): weight - step_rate * (update + decay_rate * weight)  30.4 us
  transfers between devices with their start and end apart: 59, of which 30 were waited for; matrix products, arithmetic and copies ran while one was open for 6% of the time, Pallas kernels for 29%

profile of v2, /device:TPU:0, one launch (start us, length us, event | category | flops | bytes accessed | tf_op | source)
XLA Modules:
  0.0 1409.9 jit_solution(8945279419059201660)
XLA Ops:
  2.1 3.0 collective-permute-start
  5.1 5.0 convert_element_type.251
  14.9 191.5 %shard_map.426 = (bf16[32,32,3072]{2,1,0:T(8,128)(2,1)}, bf16[32,32,4096]{2,1,0:T(8,128)(2,1)}, bf16[32,128,1024]{2,1,0:T(8,128)(2,1)}, bf16[32,32,1024]{2,1,0:T...) custom-call(bf16[32,3072]{1,0:T(8,128)(2,1)} %get-tuple-element.165., ...), custom_call_target="tpu_custom_call" | custom-call | tf_op jit(solution)/shard_map/pallas_call | solution.py:322
  209.6 2.8 slice_convert_fusion
  229.9 38.5 %fusion.10 = bf16[4608,1024]{1,0:T(8,128)(2,1)} fusion(s32[4608]{0:T(1024)S(1)} %eq.40, bf16[1572,1024]{1,0:T(8,128)(2,1)} %collective-permute-done.9, bf16[1572,1024]{1,0:T(8,128)(2,1)} %convert_element_type.251), kind=kOutput, calls=%fused_computation.33 | convolution fusion | flops 29702590464 | bytes 15894528 | tf_op jit(solution)/shard_map/dot_general | solution.py:821
  268.5 31.5 %fusion.27 = bf16[3584,1024]{1,0:T(8,128)(2,1)} fusion(s32[3584]{0:T(1024)S(1)} %eq.81, bf16[1572,1024]{1,0:T(8,128)(2,1)} %collective-permute-done.9, bf16[1572,1024]{1,0:T(8,128)(2,1)} %convert_element_type.251), kind=kOutput, calls=%fused_computation.56 | convolution fusion | flops 23104876544 | bytes 13793280 | tf_op jit(solution)/shard_map/dot_general | solution.py:821
  300.0 123.9 %shard_map.425 = (bf16[288,1024]{1,0:T(8,128)(2,1)}, bf16[224,1024]{1,0:T(8,128)(2,1)}) custom-call(bf16[16,288,1024]{2,1,0:T(8,128)(2,1)} %bitcast.402, bf16[16,224,1024]{2,1,0:T(8,128)(2,1)} %bitcast.408), custom_call_target="tpu_custom_call" | custom-call | tf_op jit(solution)/shard_map/pallas_call | solution.py:559
  428.0 7.7 add_convert_fusion.1
  435.7 3.2 copy.205
  438.9 7.3 fusion.8
  446.3 9.2 exponential_reduce_fusion.1
  455.5 9.1 convolution_convert_fusion.3
  464.7 3.5 fusion.37
  472.1 7.3 fusion.131
  479.5 8.6 fusion.158
  489.5 5.2 add_convert_fusion
  494.7 3.2 copy.207
  497.9 7.5 fusion.9
  505.4 9.2 exponential_reduce_fusion
  514.6 8.8 convolution_convert_fusion.2
  525.3 7.8 fusion.133
  533.2 5.6 fusion.160
  542.1 3.1 collective-permute-done.10
  547.4 4.1 collective-permute-done.11
  553.5 3.6 collective-permute-done.12
  559.1 3.6 collective-permute-done.16
  568.8 6.8 fusion.161
  575.7 2.7 copy-done.4
  582.5 2.7 collective-permute-done.19
  586.1 3.0 collective-permute-done.20
  598.6 8.5 fusion.128
  623.0 10.6 iota_compare_fusion.16
  665.4 3.1 multiply_reduce_fusion.4
  670.1 16.5 %convert_reduce_fusion.2 = (f32[4096]{0:T(1024)}, bf16[512,4096]{1,0:T(8,128)(2,1)}) fusion(f32[512,4096]{1,0:T(8,128)} %copy-done.170, f32[4096]{0:T(1024)S(1)} %copy-done.120, bf16[512,1024]{1,0:T(8,128)(2,1)S(1)} %get-tuple-element.114, bf16[4096,1024]{1,0:T(8,128)(2,1)} %bitcast.479), kind=kOutput, calls=%fused_computation.52 | convolution fusion | flops 4343197696 | bytes 22052864 | tf_op jit(solution)/shard_map/dot_general | solution.py:669
  686.6 8.1 multiply_reduce_fusion.5
  702.3 12.8 multiply_reduce_fusion.1
  715.1 12.2 multiply_convert_fusion.1
  731.5 8.1 fusion.33
  741.2 4.6 multiply_reduce_fusion.6
  748.7 16.8 %convert_reduce_fusion.3 = (f32[4096]{0:T(1024)}, bf16[512,4096]{1,0:T(8,128)(2,1)}) fusion(f32[512,4096]{1,0:T(8,128)} %fusion.131, f32[4096]{0:T(1024)S(1)} %copy-done.123, bf16[512,1024]{1,0:T(8,128)(2,1)S(1)} %get-tuple-element.122, bf16[4096,1024]{1,0:T(8,128)(2,1)} %bitcast.471), kind=kOutput, calls=%fused_computation.53 | convolution fusion | flops 4343197696 | bytes 22052864 | tf_op jit(solution)/shard_map/dot_general | solution.py:669
  765.6 7.8 multiply_reduce_fusion.7
  781.1 12.3 multiply_reduce_fusion
  793.4 12.2 multiply_convert_fusion
  809.7 8.6 fusion.34
  819.9 4.1 multiply_reduce_fusion.3
  827.6 13.3 fusion.135
  840.9 7.4 fusion.130
  848.3 113.6 %shard_map.429 = (bf16[16,288,1024]{2,1,0:T(8,128)(2,1)}, bf16[16,224,1024]{2,1,0:T(8,128)(2,1)}) custom-call(bf16[288,1024]{1,0:T(8,128)(2,1)} %slice.671.refs_0_, bf16[224,1024]{1,0:T(8,128)(2,1)} %slice.672.refs_1_), custom_call_target="tpu_custom_call" | custom-call | tf_op jit(solution)/shard_map/pallas_call | solution.py:322
  962.0 6.0 convert_reduce_fusion.1
  968.0 32.8 %fusion.2 = f32[3144,1024]{1,0:T(8,128)} fusion(bf16[3584,1024]{1,0:T(8,128)(2,1)} %bitcast.407, s32[3584]{0:T(1024)S(1)} %copy-done.116), kind=kOutput, calls=%fused_computation.8 | convolution fusion | flops 23088328704 | bytes 20232192 | tf_op jit(solution)/shard_map/dot_general | solution.py:964
  1000.9 3.4 convert_reduce_fusion
  1004.2 36.3 %fusion = f32[3144,1024]{1,0:T(8,128)} fusion(bf16[4608,1024]{1,0:T(8,128)(2,1)S(1)} %bitcast.401, pred[4608,3144]{1,0:T(32,128)(4,1)} %iota_compare_fusion.16), kind=kOutput, calls=%fused_computation.5 | convolution fusion | flops 29670506496 | bytes 36802560 | tf_op jit(solution)/shard_map/dot_general | solution.py:964
  1040.6 15.2 %add_add_fusion = f32[3144,1024]{1,0:T(8,128)} fusion(f32[3144,1024]{1,0:T(8,128)} %fusion.2, f32[3144,1024]{1,0:T(8,128)} %fusion, bf16[512,1024]{1,0:T(8,128)(2,1)} %bitcast.410, f32[512,3144]{0,1:T(8,128)S(1)} %bitcast.396, f32[512]{0:T(512)S(1)} %copy-done.141, f32[512]{0:T(512)S(1)} %copy-done.87, s32[512]{0:T(512)S(1)} %copy-done.81), kind=kOutput, calls=%fused_computation.26 | convolution fusion | flops 3312820224 | bytes 46127104 | tf_op jit(solution)/shard_map/dot_general | solution.py:966
  1055.8 7.2 slice.674
  1068.5 7.4 fusion.162.refs_0_
  1076.0 5.4 fusion.163.refs_0_
  1081.4 7.3 fusion.132
  1088.7 8.7 fusion.136
  1105.0 109.2 %shard_map.427 = (f32[32,3072]{1,0:T(8,128)}, f32[32,4096]{1,0:T(8,128)}, f32[128,1024]{1,0:T(8,128)}, f32[32,1024]{1,0:T(8,128)}) custom-call(bf16[32,32,3072]{2,1,0:T(8,128)(2,1)} %fusion.162.refs_0_, bf16[32,32,4096]{2,1,0:T(8,128)(2,1)} %bitcast.404, bf16[32,128,1024]{2,1,0:T(8,128)(2,1)} %bitcast.403, bf16[32,32,1024]{2,1,0:T(8,128)(2,1)} %fusion.40.refs_3_), custom_call_target="tpu_custom_call" | custom-call | tf_op jit(solution)/shard_map/pallas_call | solution.py:559
  1214.2 109.2 %shard_map.428 = (f32[32,3072]{1,0:T(8,128)}, f32[32,4096]{1,0:T(8,128)}, f32[128,1024]{1,0:T(8,128)}, f32[32,1024]{1,0:T(8,128)}) custom-call(bf16[32,32,3072]{2,1,0:T(8,128)(2,1)} %fusion.163.refs_0_, bf16[32,32,4096]{2,1,0:T(8,128)(2,1)} %bitcast.405, bf16[32,128,1024]{2,1,0:T(8,128)(2,1)} %bitcast.406, bf16[32,32,1024]{2,1,0:T(8,128)(2,1)} %fusion.38.refs_3_), custom_call_target="tpu_custom_call" | custom-call | tf_op jit(solution)/shard_map/pallas_call | solution.py:559
  1348.3 7.0 multiply_reduce_fusion.2
  1371.6 3.0 collective-permute-done.58
  1376.7 4.1 multiply_subtract_fusion.1
  1387.7 19.7 %multiply_subtract_fusion = (f32[1572,1024]{1,0:T(8,128)}, f32[1572,1024]{1,0:T(8,128)}, f32[1572,1024]{1,0:T(8,128)}) fusion(f32[1572,1024]{1,0:T(8,128)} %param.37, f32[]{:T(128)S(6)} %sub.412, f32[]{:T(128)S(6)} %div.267, f32[1572,1024]{1,0:T(8,128)} %collective-permute-done.53, f32[3144,1024]{1,0:T(8,128)} %add_add_fusion, f32[1572,1024]{1,0:T(8,128)} %param.51, ...), kind=kLoop, calls=%fused_computation.59 | loop fusion | flops 25755648 | bytes 51511304 | tf_op jit(solution)/shard_map/sub | solution.py:749
  (762 shorter events, 203.2 us)
Async XLA Ops:
  2.1 210.9 %collective-permute-start = (s32[577]{0:T(1024)S(1)}, s32[577]{0:T(1024)S(1)}, u32[]{:S(2)}, u32[]{:S(2)}) collective-permute-start(s32[577]{0:T(1024)S(1)} %pad_add_fusion.1), channel_id=1, source_target_pairs={{0,16},{1,17},{2,18},{3,19},{4,20},{5,21},{6,22},{7,23},{8,24},{9,... | collective-permute-start | bytes 6932 | tf_op jit(solution)/shard_map/ppermute | solution.py:52
  10.1 219.8 %collective-permute-start.9 = (bf16[1572,1024]{1,0:T(8,128)(2,1)}, bf16[1572,1024]{1,0:T(8,128)(2,1)}, u32[]{:S(2)}, u32[]{:S(2)}) collective-permute-start(bf16[1572,1024]{1,0:T(8,128)(2,1)} %convert_element_type.251), channel_id=1, source_target_pairs={{0,8},{1,9},{2,10},{3,11},{4,12},{5,13},{6,14},{7,15},{8,0},{9,1},... | collective-permute-start | bytes 9658376 | tf_op jit(solution)/shard_map/ppermute | solution.py:52
  12.5 202.6 %copy-start.161 = (s32[32]{0:T(128)S(1)}, s32[32]{0:T(128)}, u32[]{:S(2)}) copy-start(s32[32]{0:T(128)} %param.28) | copy-start | bytes 388
  209.5 255.2 %copy-start.75 = (f32[1024]{0:T(1024)}, f32[1024]{0:T(1024)S(1)}, u32[]{:S(2)}) copy-start(f32[1024]{0:T(1024)S(1)} %get-tuple-element.185) | copy-start | bytes 12292
  209.5 260.5 %copy-start.127 = (f32[1024]{0:T(1024)}, f32[1024]{0:T(1024)S(1)}, u32[]{:S(2)}) copy-start(f32[1024]{0:T(1024)S(1)} %get-tuple-element.180) | copy-start | bytes 12292
  209.5 260.5 %copy-start.146 = (f32[1024]{0:T(1024)}, f32[1024]{0:T(1024)S(1)}, u32[]{:S(2)}) copy-start(f32[1024]{0:T(1024)S(1)} %get-tuple-element.179) | copy-start | bytes 12292
  213.1 3.7 collective-permute-start.4
  214.6 3.6 collective-permute-start.1
  216.7 3.6 collective-permute-start.5
  218.3 3.6 collective-permute-start.2
  220.4 3.6 collective-permute-start.6
  221.9 3.6 collective-permute-start.3
  224.0 3.8 collective-permute-start.7
  225.6 3.9 collective-permute-start.8
  540.9 4.3 collective-permute-start.10
  545.3 6.2 collective-permute-start.11
  545.9 6.2 collective-permute-start.14
  551.4 5.7 collective-permute-start.12
  552.1 5.7 collective-permute-start.15
  557.1 7.0 collective-permute-start.13
  557.8 5.0 collective-permute-start.16
  562.7 4.3 collective-permute-start.17
  564.1 4.5 collective-permute-start.18
  581.6 3.7 collective-permute-start.19
  585.3 3.7 collective-permute-start.20
  589.1 3.7 collective-permute-start.21
  592.8 4.6 collective-permute-start.22
  594.8 1.2 collective-permute-start.23
  608.5 4.3 collective-permute-start.33
  609.7 4.3 collective-permute-start.37
  614.9 5.4 collective-permute-start.34
  617.9 21.0 %collective-permute-start.24 = (f32[8,32,512]{2,1,0:T(8,128)}, f32[8,32,512]{2,1,0:T(8,128)}, u32[]{:S(2)}, u32[]{:S(2)}) collective-permute-start(f32[8,32,512]{2,1,0:T(8,128)} %slice_bitcast_fusion.18), channel_id=1, source_target_pairs={{0,16},{1,17},{2,18},{3,19},{4,20},{5,21},{6,22},{7,23},{8,24},{9,... | collective-permute-start | bytes 1572872 | tf_op jit(solution)/shard_map/ppermute | solution.py:52
  619.4 16.2 %collective-permute-start.38 = (f32[2,32,512]{2,1,0:T(8,128)}, f32[2,32,512]{2,1,0:T(8,128)}, u32[]{:S(2)}, u32[]{:S(2)}) collective-permute-start(f32[2,32,512]{2,1,0:T(8,128)} %pad_maximum_fusion.9), channel_id=1, source_target_pairs={{2,0},{4,2},{6,4},{7,6},{5,7},{3,5},{1,3},{0,1},{10,8},{12,10},{14... | collective-permute-start | bytes 393224 | tf_op jit(solution)/shard_map/ppermute | solution.py:52
  621.9 13.8 collective-permute-start.35
  636.8 5.5 collective-permute-start.39
  637.7 13.1 collective-permute-start.36
  640.2 4.0 collective-permute-start.25
  641.1 3.9 collective-permute-start.29
  643.2 7.6 collective-permute-start.40
  645.1 4.3 collective-permute-start.26
  646.5 5.3 collective-permute-start.30
  649.4 4.7 collective-permute-start.27
  654.1 4.3 collective-permute-start.31
  655.1 4.3 collective-permute-start.41
  656.1 4.3 collective-permute-start.28
  658.4 4.3 collective-permute-start.32
  1063.2 285.1 %collective-permute-start.53 = (f32[1572,1024]{1,0:T(8,128)}, f32[1572,1024]{1,0:T(8,128)}, u32[]{:S(2)}, u32[]{:S(2)}) collective-permute-start(f32[1572,1024]{1,0:T(8,128)} %slice.674), channel_id=1, source_target_pairs={{0,8},{1,9},{2,10},{3,11},{4,12},{5,13},{6,14},{7,15},{8,0},{9,1},... | collective-permute-start | bytes 19316744 | tf_op jit(solution)/shard_map/ppermute | solution.py:52
  1066.6 278.8 %collective-permute-start.52 = (f32[32,1024]{1,0:T(8,128)}, f32[32,1024]{1,0:T(8,128)}, u32[]{:S(2)}, u32[]{:S(2)}) collective-permute-start(f32[32,1024]{1,0:T(8,128)} %constant_dynamic-slice_fusion.3), channel_id=1, source_target_pairs={{0,8},{1,9},{2,10},{3,11},{4,12},{5,13},{6,14},{7,15},{8,0},{9,1},... | collective-permute-start | bytes 393224 | tf_op jit(solution)/shard_map/ppermute | solution.py:52
  1067.9 32.2 %collective-permute-start.42 = (f32[2,8,2,416]{3,2,1,0:T(2,128)S(1)}, f32[2,8,2,416]{3,2,1,0:T(2,128)S(1)}, u32[]{:S(2)}, u32[]{:S(2)}) collective-permute-start(f32[2,8,2,416]{3,2,1,0:T(2,128)S(1)} %dynamic-slice_bitcast_fusion), channel_id=1, source_target_pairs={{0,8},{1,9},{2,10},{3,11},{4,12},{5,13},{6,14},{7,15},{8,0},{9,1},... | collective-permute-start | bytes 159752 | tf_op jit(solution)/shard_map/ppermute | solution.py:52
  1100.1 223.4 %collective-permute-start.43 = (f32[1,2,416]{2,1,0:T(2,128)S(1)}, f32[1,2,416]{2,1,0:T(2,128)S(1)}, u32[]{:S(2)}, u32[]{:S(2)}) collective-permute-start(f32[1,2,416]{2,1,0:T(2,128)S(1)} %get-tuple-element.192), channel_id=1, source_target_pairs={{0,2},{2,4},{4,6},{6,7},{7,5},{5,3},{3,1},{1,0},{8,10},{10,12},{12... | collective-permute-start | bytes 9992 | tf_op jit(solution)/shard_map/ppermute | solution.py:52
  1101.1 222.4 %collective-permute-start.47 = (f32[1,2,416]{2,1,0:T(2,128)S(1)}, f32[1,2,416]{2,1,0:T(2,128)S(1)}, u32[]{:S(2)}, u32[]{:S(2)}) collective-permute-start(f32[1,2,416]{2,1,0:T(2,128)S(1)} %get-tuple-element.194), channel_id=1, source_target_pairs={{2,0},{4,2},{6,4},{7,6},{5,7},{3,5},{1,3},{0,1},{10,8},{12,10},{14... | collective-permute-start | bytes 9992 | tf_op jit(solution)/shard_map/ppermute | solution.py:52
  1214.2 125.7 %copy-start.58 = (f32[32,1024]{1,0:T(8,128)S(1)}, f32[32,1024]{1,0:T(8,128)}, u32[]{:S(2)}) copy-start(f32[32,1024]{1,0:T(8,128)} %get-tuple-element.57) | copy-start | bytes 393220
  1323.6 3.7 collective-permute-start.44
  1324.5 5.6 collective-permute-start.48
  1327.3 3.7 collective-permute-start.45
  1330.9 4.0 collective-permute-start.49
  1333.9 4.1 collective-permute-start.46
  1334.9 3.9 collective-permute-start.50
  1338.9 5.2 collective-permute-start.51
  1356.8 1.1 collective-permute-start.54
  1358.7 3.5 collective-permute-start.55
  1363.0 3.5 collective-permute-start.56
  1366.6 3.5 collective-permute-start.57
  1370.1 4.4 collective-permute-start.58
  (191 other events, 2190.6 us)

commit v3 on v2

--- a/solution.py
+++ b/solution.py
@@ -57,35 +57,10 @@
     def swap_half(self, array):
         return self.step(array, self.half_pairs)
 
-    def flip(self, array, bit):
-        size = self.size
-        pairs = [
-            (n * size + w, n * size + (w ^ bit))
-            for n in range(self.narrow_size)
-            for w in range(size)
-        ]
-        return self.step(array, pairs)
-
     def wide_of(self, offset):
         size = self.size
         at = lax.rem(self.place + offset, size)
         return jnp.where(at < size // 2, 2 * at, 2 * (size - 1 - at) + 1)
-
-    def ring_gather(self, block):
-        size = self.size
-        far = size // 2
-        cut = block.shape[0] // 2
-        pieces = {0: block}
-        going_right, going_left = block, block
-        for at in range(1, far):
-            going_right = self.step(going_right, self.right)
-            pieces[size - at] = going_right
-            going_left = self.step(going_left, self.left)
-            pieces[at] = going_left
-        pieces[far] = jnp.concatenate(
-            [self.step(going_right[:cut], self.right), self.step(going_left[cut:], self.left)]
-        )
-        return [pieces[at] for at in range(size)]
 
     def ring_scatter(self, take, low):
         size = self.size
@@ -140,15 +115,6 @@
             pick(both, self.half, 0), self.swap_half(pick(both, 1 - self.half, 0).astype(low))
         )
 
-    def total(self, value):
-        value = value + self.swap_core(value)
-        value = value + self.swap_half(value)
-        bit = 1
-        while bit < self.size:
-            value = value + self.flip(value, bit)
-            bit *= 2
-        return value
-
 
 MESH = pl.DeviceIdType.MESH
 
@@ -188,11 +154,9 @@
     return rows // 2 if rows % 32 == 0 else rows
 
 
-def gather_body(size, ring_first, across, *refs):
+def gather_steps(size, ring_first, across, shards, wholes, sems, spot, tick, ready):
     count = len(ring_first)
-    shards, wholes = refs[:count], refs[count : 2 * count]
-    ring_sem, half_sem, core_sem, send_sem, local_sem = refs[2 * count :]
-    spot = Spot(size)
+    ring_sem, half_sem, core_sem, send_sem, local_sem = sems
     far = size // 2
 
     def index(turned, offset, toward=None):
@@ -236,7 +200,6 @@
         toward = ("right", "left")[way]
         send(at, source, turned, offset, toward, ring_sem.at[at, turned, way, step], rows)
 
-    spot.meet(across)
     locals_ = []
     for at in range(count):
         copy = pltpu.make_async_copy(shards[at], piece(at, 0, 0), local_sem.at[at])
@@ -259,12 +222,27 @@
                 on_ring(at, 0, shards[at], 0, way, 1)
                 on_ring(at, 1, piece(at, 1, 0), 0, way, 1)
             on_core(at, piece(at, 1, 0), 1, 0)
+    for at in range(count):
+        locals_[at].wait()
+        ready(at, 0, 0)
+        if not ring_first[at]:
+            ready(at, 1, 0)
+        tick()
 
     def turned_arrivals(at, step):
         offsets = (0,) if step == 0 else (far,) if step == far else (-step, step)
         for offset in offsets:
             landed(piece(at, 1, offset), half_sem.at[at, offset % size])
             on_core(at, piece(at, 1, offset), 1, offset)
+            came.append((at, 1, offset))
+
+    came = []
+
+    def flush():
+        for one in came:
+            ready(*one)
+        came.clear()
+        tick()
 
     for step in range(1, far + 1):
         for at in range(count):
@@ -284,6 +262,7 @@
                             on_ring(at, 0, here, offset, way, step + 1, pl.ds(cut, rows - cut))
                         send(at, here, 0, offset, "half", half_sem.at[at, offset % size])
                         on_core(at, here, 0, offset)
+                        came.append((at, 0, offset))
                 else:
                     here = piece(at, 0, far)
                     landed(here.at[pl.ds(0, cut)], ring_sem.at[at, 0, 0, step])
@@ -291,6 +270,7 @@
                         landed(here.at[pl.ds(cut, rows - cut)], ring_sem.at[at, 0, 1, step])
                     send(at, here, 0, far, "half", half_sem.at[at, far])
                     on_core(at, here, 0, far)
+                    came.append((at, 0, far))
                 turned_arrivals(at, step - 1)
             else:
                 for way in (0, 1):
@@ -303,39 +283,318 @@
                         if step < far - 1 or (step == far - 1 and turned == way):
                             on_ring(at, turned, here, offset, way, step + 1)
                         on_core(at, here, turned, offset)
+                        came.append((at, turned, offset))
+            flush()
     for at in range(count):
         if ring_first[at]:
             turned_arrivals(at, far)
+            flush()
     for at in range(count):
-        locals_[at].wait()
         if across:
             landed(wholes[at].at[pl.ds(0, 2 * size)], core_sem.at[at])
         sent = 4 * size - 1 if across else 2 * size - 1
         landed(wholes[at].at[pl.ds(0, sent)], send_sem.at[at])
 
 
+def gather_sems(count, size):
+    return [
+        pltpu.SemaphoreType.DMA((count, 2, 2, size // 2 + 1)),
+        pltpu.SemaphoreType.DMA((count, size)),
+        pltpu.SemaphoreType.DMA((count,)),
+        pltpu.SemaphoreType.DMA((count,)),
+        pltpu.SemaphoreType.DMA((count,)),
+    ]
+
+
+def look_up_body(size, ring_first, *refs):
+    count = len(ring_first)
+    shards, (table_own, ids) = refs[:count], refs[count : count + 2]
+    refs = refs[count + 2 :]
+    wholes, (table_out, found) = refs[:count], refs[count : count + 2]
+    table, hot, stage, table_sem, stage_sem, *sems = refs[count + 2 :]
+    spot = Spot(size)
+    spot.meet(True)
+    height = table_own.shape[0]
+    mine = pltpu.make_async_copy(table_own, table.at[pl.ds(0, height)], table_sem.at[0])
+    mine.start()
+    swap = pltpu.make_async_remote_copy(
+        src_ref=table_own,
+        dst_ref=table.at[pl.ds(height, height)],
+        send_sem=table_sem.at[1],
+        recv_sem=table_sem.at[2],
+        device_id=spot.to_core,
+        device_id_type=MESH,
+    )
+    swap.start()
+    out = pltpu.make_async_copy(table, table_out, table_sem.at[3])
+    pieces, rows = found.shape[:2]
+    width = 256
+    state = {"ticks": 0, "done": 0}
+
+    def copy_out(number):
+        slot = lax.rem(number, 2)
+        return pltpu.make_async_copy(stage.at[slot], found.at[number], stage_sem.at[slot])
+
+    def work(first, last):
+        def one(number, nothing):
+            columns = lax.broadcasted_iota(jnp.int32, (rows, 2 * height), 1)
+            hot[...] = jnp.where(columns == ids[number], 1.0, 0.0).astype(jnp.bfloat16)
+
+            @pl.when(number >= 2)
+            def _():
+                copy_out(number - 2).wait()
+
+            def part(at, nothing):
+                window = pl.ds(pl.multiple_of(at * width, width), width)
+                stage[lax.rem(number, 2), :, window] = jnp.dot(
+                    hot[...], table[:, window], preferred_element_type=jnp.float32
+                ).astype(jnp.bfloat16)
+                return nothing
+
+            lax.fori_loop(0, D // width, part, 0)
+            copy_out(number).start()
+            return nothing
+
+        lax.fori_loop(first, last, one, 0)
+
+    def tick(share=1):
+        if state["done"] == pieces:
+            return
+        if state["done"] == 0:
+            mine.wait()
+            swap.wait_recv()
+            out.start()
+        last = min(pieces, state["done"] + share)
+        work(state["done"], last)
+        state["done"] = last
+
+    gather_steps(
+        size, ring_first, True, shards, wholes, sems, spot, tick, lambda at, turned, offset: None
+    )
+    tick(pieces)
+    copy_out(pieces - 2).wait()
+    copy_out(pieces - 1).wait()
+    out.wait()
+    swap.wait_send()
+
+
+def look_up_call(size, shards, ring_first, table_own, ids, number):
+    count = len(shards)
+    height = table_own.shape[0]
+    found = ids.shape[:2] + (D,)
+    outs = [jax.ShapeDtypeStruct((4 * size,) + a.shape, a.dtype) for a in shards]
+    outs.append(jax.ShapeDtypeStruct((2 * height, D), table_own.dtype))
+    outs.append(jax.ShapeDtypeStruct(found, table_own.dtype))
+    return pl.pallas_call(
+        functools.partial(look_up_body, size, ring_first),
+        out_shape=outs,
+        in_specs=[pl.BlockSpec(memory_space=pl.ANY)] * (count + 1)
+        + [pl.BlockSpec(memory_space=pltpu.VMEM)],
+        out_specs=[pl.BlockSpec(memory_space=pl.ANY)] * (count + 2),
+        scratch_shapes=[
+            pltpu.VMEM((2 * height, D), table_own.dtype),
+            pltpu.VMEM((ids.shape[1], 2 * height), table_own.dtype),
+            pltpu.VMEM((2,) + found[1:], table_own.dtype),
+            pltpu.SemaphoreType.DMA((4,)),
+            pltpu.SemaphoreType.DMA((2,)),
+        ]
+        + gather_sems(count, size),
+        compiler_params=pltpu.CompilerParams(
+            collective_id=number, has_side_effects=True, vmem_limit_bytes=48 * 1024 * 1024
+        ),
+    )(*shards, table_own, ids)
+
+
+def spread_body(size, *refs):
+    near, rest, ids_near, ids_rest, start = refs[:5]
+    table_out, place_out = refs[5:7]
+    near_all, rest_all, total, core_in, table_sem, *sems = refs[7:]
+    ids = (ids_near, ids_rest)
+    wholes = (near_all, rest_all)
+    spot = Spot(size)
+    spot.meet(True)
+    height = table_out.shape[0]
+    block = 2 * height // 8
+    first = pltpu.make_async_copy(start, total, table_sem.at[0])
+    first.start()
+    place_out[...] = jnp.zeros_like(place_out)
+    waiting = []
+
+    def spread(pieces, blocks):
+        def one(number, nothing):
+            window = pl.ds(pl.multiple_of(number * block, 16), block)
+            row = number * block + lax.broadcasted_iota(jnp.int32, (block, near.shape[0]), 0)
+            value = total[window, :]
+            for at, piece in pieces:
+                hot = jnp.where(row == ids[at][piece], 1.0, 0.0).astype(jnp.bfloat16)
+                value = value + jnp.dot(
+                    hot, wholes[at][piece], preferred_element_type=jnp.float32
+                )
+            total[window, :] = value
+            return nothing
+
+        lax.fori_loop(blocks[0], blocks[1], one, 0)
+
+    def place(pieces):
+        for at, piece in pieces:
+            rows = pl.ds(at * near.shape[0], near.shape[0])
+            place_out[rows, :] += wholes[at][piece].astype(jnp.float32)
+
+    def ready(at, turned, offset):
+        waiting.append((at, turned * size + offset % size))
+
+    def tick():
+        if tick.first:
+            first.wait()
+            tick.first = False
+        if len(waiting) >= 4:
+            spread(waiting, (0, 8))
+            place(waiting)
+            waiting.clear()
+
+    tick.first = True
+    gather_steps(size, (True, False), False, (near, rest), wholes, sems, spot, tick, ready)
+    if waiting:
+        spread(waiting, (4, 8))
+    swap = pltpu.make_async_remote_copy(
+        src_ref=total.at[pl.ds(height, height)],
+        dst_ref=core_in,
+        send_sem=table_sem.at[1],
+        recv_sem=table_sem.at[2],
+        device_id=spot.to_core,
+        device_id_type=MESH,
+    )
+    swap.start()
+    if waiting:
+        spread(waiting, (0, 4))
+        place(waiting)
+    swap.wait_recv()
+    step = height // 4
+
+    def add(number, nothing):
+        window = pl.ds(pl.multiple_of(number * step, 16), step)
+        total[window, :] += core_in[window, :]
+        return nothing
+
+    lax.fori_loop(0, 4, add, 0)
+    out = pltpu.make_async_copy(total.at[pl.ds(0, height)], table_out, table_sem.at[0])
+    out.start()
+    swap.wait_send()
+    out.wait()
+
+
+def spread_call(size, near, rest, ids, start, number):
+    height = start.shape[0] // 2
+    pieces = (2 * size,) + near.shape
+    return pl.pallas_call(
+        functools.partial(spread_body, size),
+        out_shape=[
+            jax.ShapeDtypeStruct((height, D), jnp.float32),
+            jax.ShapeDtypeStruct((LEN, D), jnp.float32),
+        ],
+        in_specs=[pl.BlockSpec(memory_space=pl.ANY)] * 2
+        + [pl.BlockSpec(memory_space=pltpu.VMEM)] * 2
+        + [pl.BlockSpec(memory_space=pl.ANY)],
+        out_specs=[
+            pl.BlockSpec(memory_space=pl.ANY),
+            pl.BlockSpec(memory_space=pltpu.VMEM),
+        ],
+        scratch_shapes=[
+            pltpu.VMEM(pieces, near.dtype),
+            pltpu.VMEM(pieces, near.dtype),
+            pltpu.VMEM((2 * height, D), jnp.float32),
+            pltpu.VMEM((height, D), jnp.float32),
+            pltpu.SemaphoreType.DMA((3,)),
+        ]
+        + gather_sems(2, size),
+        compiler_params=pltpu.CompilerParams(
+            collective_id=number, has_side_effects=True, vmem_limit_bytes=60 * 1024 * 1024
+        ),
+    )(near, rest, *ids, start)
+
+
+def plain_gather_body(size, ring_first, across, *refs):
+    count = len(ring_first)
+    spot = Spot(size)
+    spot.meet(across)
+    gather_steps(
+        size,
+        ring_first,
+        across,
+        refs[:count],
+        refs[count : 2 * count],
+        refs[2 * count :],
+        spot,
+        lambda: None,
+        lambda at, turned, offset: None,
+    )
+
+
 def gather_call(size, shards, ring_first, across, number):
     count = len(shards)
     total = (4 if across else 2) * size
-    half_waits = size
-    outs = [jax.ShapeDtypeStruct((total,) + a.shape, a.dtype) for a in shards]
     return pl.pallas_call(
-        functools.partial(gather_body, size, ring_first, across),
-        out_shape=outs,
+        functools.partial(plain_gather_body, size, ring_first, across),
+        out_shape=[jax.ShapeDtypeStruct((total,) + a.shape, a.dtype) for a in shards],
         in_specs=[pl.BlockSpec(memory_space=pl.ANY)] * count,
         out_specs=[pl.BlockSpec(memory_space=pl.ANY)] * count,
-        scratch_shapes=[
-            pltpu.SemaphoreType.DMA((count, 2, 2, size // 2 + 1)),
-            pltpu.SemaphoreType.DMA((count, half_waits)),
-            pltpu.SemaphoreType.DMA((count,)),
-            pltpu.SemaphoreType.DMA((count,)),
-            pltpu.SemaphoreType.DMA((count,)),
-        ],
+        scratch_shapes=gather_sems(count, size),
         compiler_params=pltpu.CompilerParams(collective_id=number, has_side_effects=True),
     )(*shards)
 
 
-def scatter_body(size, half_first, across, *refs):
+def cast_body(size, everyone, own_ref, out_ref, come_sem, send_sem, local_sem):
+    spot = Spot(size)
+    group = (4 if everyone else 2) * size
+    narrow = lax.axis_index("narrow")
+    mine = (narrow if everyone else spot.half) * size + spot.wide
+
+    def device(step):
+        at = lax.rem(mine + step, group)
+        block = lax.div(at, size)
+        return (block if everyone else 2 * block + spot.core, lax.rem(at, size))
+
+    barrier = pltpu.get_barrier_semaphore()
+
+    def greet(step, nothing):
+        pl.semaphore_signal(barrier, inc=1, device_id=device(step), device_id_type=MESH)
+        return nothing
+
+    def tell(step, nothing):
+        pltpu.make_async_remote_copy(
+            src_ref=own_ref,
+            dst_ref=out_ref.at[mine],
+            send_sem=send_sem,
+            recv_sem=come_sem,
+            device_id=device(step),
+            device_id_type=MESH,
+        ).start()
+        return nothing
+
+    lax.fori_loop(1, group, greet, 0)
+    keep = pltpu.make_async_copy(own_ref, out_ref.at[mine], local_sem)
+    keep.start()
+    pl.semaphore_wait(barrier, group - 1)
+    lax.fori_loop(1, group, tell, 0)
+    others = out_ref.at[pl.ds(0, group - 1)]
+    pltpu.make_async_copy(others, others, come_sem).wait()
+    pltpu.make_async_copy(others, others, send_sem).wait()
+    keep.wait()
+
+
+def cast_call(size, block, everyone, number):
+    group = (4 if everyone else 2) * size
+    return pl.pallas_call(
+        functools.partial(cast_body, size, everyone),
+        out_shape=jax.ShapeDtypeStruct((group,) + block.shape, block.dtype),
+        in_specs=[pl.BlockSpec(memory_space=pltpu.VMEM)],
+        out_specs=pl.BlockSpec(memory_space=pltpu.VMEM),
+        scratch_shapes=[pltpu.SemaphoreType.DMA] * 3,
+        compiler_params=pltpu.CompilerParams(collective_id=number, has_side_effects=True),
+    )(block)
+
+
+def scatter_body(size, half_first, across, bases, *refs):
     count = len(half_first)
     arrays, outs = refs[:count], refs[count : 2 * count]
     own, core_in, half_in, ring_in = (
@@ -365,7 +624,8 @@
     def source_of(at, turned, other_core, offset):
         if across:
             return arrays[at].at[spot.index(turned, other_core, offset % size)]
-        return arrays[at].at[turned * size + offset % size]
+        base, stride = bases[at]
+        return arrays[at].at[base + stride * (turned * size + offset % size)]
 
     def add(target, parts):
         rows, columns = target.shape
@@ -540,7 +800,7 @@
         copy.wait_send()
 
 
-def scatter_call(size, arrays, half_first, across, out_type, number):
+def scatter_call(size, arrays, half_first, across, out_type, number, bases=None):
     count = len(arrays)
     far = size // 2
     pieces = [a.shape[1:] for a in arrays]
@@ -557,7 +817,7 @@
         for p, a, first in zip(pieces, arrays, half_first)
     ]
     return pl.pallas_call(
-        functools.partial(scatter_body, size, half_first, across),
+        functools.partial(scatter_body, size, half_first, across, bases or ((0, 1),) * count),
         out_shape=[jax.ShapeDtypeStruct(p, out_type) for p in pieces],
         in_specs=[pl.BlockSpec(memory_space=pl.ANY)] * count,
         out_specs=[pl.BlockSpec(memory_space=pltpu.VMEM)] * count,
@@ -588,19 +848,137 @@
     return jax.nn.gelu(values, approximate=True)
 
 
-def attention_mask(seq_length):
-    positions = jnp.arange(LEN)
-    return (positions[None, :] <= positions[:, None]) & (positions[None, :] < seq_length)
-
-
-def attention_scores(query_rows, key_rows, allowed):
-    scores = (
-        jnp.einsum("qhd,khd->hqk", query_rows, key_rows, preferred_element_type=jnp.float32) * 0.125
-    )
-    return jnp.where(allowed[None], scores, -1e30)
-
-
-def layer_forward(stream, weights, vector, allowed):
+def fill_mask(mask_ref, length):
+    row = lax.broadcasted_iota(jnp.int32, mask_ref.shape, 0)
+    column = lax.broadcasted_iota(jnp.int32, mask_ref.shape, 1)
+    mask_ref[...] = jnp.where((column <= row) & (column < length), 0.0, -1e30)
+
+
+def masked_scores(query, key, mask):
+    scores = lax.dot_general(
+        query * 0.125, key, (((1,), (1,)), ((), ())), preferred_element_type=jnp.float32
+    )
+    return scores + mask
+
+
+def softmax_rows(scores):
+    top = jnp.max(scores, axis=-1, keepdims=True)
+    raised = jnp.exp(scores - top)
+    return raised * (1.0 / jnp.sum(raised, axis=-1, keepdims=True))
+
+
+def attend_body(length_ref, query_ref, key_ref, value_ref, mixed_ref, mask_ref):
+    @pl.when(pl.program_id(0) == 0)
+    def _():
+        fill_mask(mask_ref, length_ref[0])
+
+    rows = query_ref.shape[0]
+    block = rows // 2
+    for head in range(2):
+        lanes = slice(head * HD, (head + 1) * HD)
+        for at in range(2):
+            here, seen = slice(at * block, (at + 1) * block), slice(0, (at + 1) * block)
+            scores = masked_scores(
+                query_ref[here, lanes], key_ref[seen, lanes], mask_ref[here, seen]
+            )
+            probs = softmax_rows(scores).astype(jnp.bfloat16)
+            mixed_ref[here, lanes] = jnp.dot(
+                probs, value_ref[seen, lanes], preferred_element_type=jnp.float32
+            ).astype(jnp.bfloat16)
+
+
+def attend(projected, seq_lengths):
+    rows = projected.shape[0]
+    pairs = HEADS // 2
+    return pl.pallas_call(
+        attend_body,
+        grid=(pairs,),
+        out_shape=jax.ShapeDtypeStruct((rows, D), jnp.bfloat16),
+        in_specs=[
+            pl.BlockSpec(memory_space=pltpu.SMEM),
+            pl.BlockSpec((rows, 2 * HD), lambda p: (0, p)),
+            pl.BlockSpec((rows, 2 * HD), lambda p: (0, pairs + p)),
+            pl.BlockSpec((rows, 2 * HD), lambda p: (0, 2 * pairs + p)),
+        ],
+        out_specs=pl.BlockSpec((rows, 2 * HD), lambda p: (0, p)),
+        scratch_shapes=[pltpu.VMEM((rows, rows), jnp.float32)],
+        compiler_params=pltpu.CompilerParams(vmem_limit_bytes=32 * 1024 * 1024),
+        cost_estimate=pl.CostEstimate(
+            flops=4 * HEADS * rows * rows * HD, bytes_accessed=8 * rows * D, transcendentals=0
+        ),
+    )(seq_lengths, projected, projected, projected)
+
+
+def attend_back_body(length_ref, query_ref, key_ref, value_ref, grad_ref, out_ref, mask_ref):
+    @pl.when(pl.program_id(0) == 0)
+    def _():
+        fill_mask(mask_ref, length_ref[0])
+
+    rows = query_ref.shape[0]
+    block = rows // 2
+    pair = pl.program_id(0)
+    low = jnp.bfloat16
+    columns = (((0,), (0,)), ((), ()))
+    across = (((1,), (1,)), ((), ()))
+    grads = []
+    for head in range(2):
+        lanes = slice(head * HD, (head + 1) * HD)
+        grad_query, grad_key, grad_value = [], [], []
+        for at in range(2):
+            here, seen = slice(at * block, (at + 1) * block), slice(0, (at + 1) * block)
+            query, key = query_ref[here, lanes], key_ref[seen, lanes]
+            grad = grad_ref[here, lanes]
+            probs = softmax_rows(masked_scores(query, key, mask_ref[here, seen]))
+            grad_probs = lax.dot_general(
+                grad, value_ref[seen, lanes], across, preferred_element_type=jnp.float32
+            )
+            grad_value.append(
+                lax.dot_general(
+                    probs.astype(low), grad, columns, preferred_element_type=jnp.float32
+                )
+            )
+            row_dot = jnp.sum(grad_probs * probs, axis=-1, keepdims=True)
+            scores_low = (probs * (grad_probs - row_dot)).astype(low)
+            grad_query.append(jnp.dot(scores_low, key, preferred_element_type=jnp.float32) * 0.125)
+            grad_key.append(
+                lax.dot_general(scores_low, query, columns, preferred_element_type=jnp.float32)
+                * 0.125
+            )
+        joined = []
+        for parts in (grad_key, grad_value):
+            joined.append(jnp.concatenate([parts[0] + parts[1][:block], parts[1][block:]]))
+        grads.append((jnp.concatenate(grad_query), joined[0], joined[1]))
+    for part in range(3):
+        window = pl.ds(pl.multiple_of(part * D + pair * 2 * HD, 2 * HD), 2 * HD)
+        out_ref[:, window] = jnp.concatenate(
+            [grads[0][part].astype(low), grads[1][part].astype(low)], axis=1
+        )
+
+
+def attend_back(projected, grad_mixed, seq_lengths):
+    rows = projected.shape[0]
+    pairs = HEADS // 2
+    return pl.pallas_call(
+        attend_back_body,
+        grid=(pairs,),
+        out_shape=jax.ShapeDtypeStruct((rows, 3 * D), jnp.bfloat16),
+        in_specs=[
+            pl.BlockSpec(memory_space=pltpu.SMEM),
+            pl.BlockSpec((rows, 2 * HD), lambda p: (0, p)),
+            pl.BlockSpec((rows, 2 * HD), lambda p: (0, pairs + p)),
+            pl.BlockSpec((rows, 2 * HD), lambda p: (0, 2 * pairs + p)),
+            pl.BlockSpec((rows, 2 * HD), lambda p: (0, p)),
+        ],
+        out_specs=pl.BlockSpec((rows, 3 * D), lambda p: (0, 0)),
+        scratch_shapes=[pltpu.VMEM((rows, rows), jnp.float32)],
+        compiler_params=pltpu.CompilerParams(vmem_limit_bytes=48 * 1024 * 1024),
+        cost_estimate=pl.CostEstimate(
+            flops=10 * HEADS * rows * rows * HD, bytes_accessed=16 * rows * D, transcendentals=0
+        ),
+    )(seq_lengths, projected, projected, projected, grad_mixed)
+
+
+def layer_forward(stream, weights, vector, seq_lengths):
     w_qkv, w_out, w_fc, w_proj = weights
     normed_low = layer_norm(stream, vector[0:D], vector[D : 2 * D]).astype(jnp.bfloat16)
     qkv_bias = jnp.concatenate(
@@ -609,15 +987,7 @@
     projected = (jnp.dot(normed_low, w_qkv, preferred_element_type=jnp.float32) + qkv_bias).astype(
         jnp.bfloat16
     )
-    heads_view = projected.reshape(LEN, 3, HEADS, HD)
-    scores = attention_scores(heads_view[:, 0], heads_view[:, 1], allowed)
-    row_max = jnp.max(scores, axis=-1, keepdims=True)
-    log_total = row_max + jnp.log(jnp.sum(jnp.exp(scores - row_max), axis=-1, keepdims=True))
-    attn_probs = jnp.exp(scores - log_total).astype(jnp.bfloat16)
-    mixed_low = jnp.einsum(
-        "hqk,khd->qhd", attn_probs, heads_view[:, 2], preferred_element_type=jnp.float32
-    )
-    mixed_low = mixed_low.reshape(LEN, D).astype(jnp.bfloat16)
+    mixed_low = attend(projected, seq_lengths)
     stream_mid = (
         stream
         + jnp.dot(mixed_low, w_out, preferred_element_type=jnp.float32)
@@ -641,7 +1011,6 @@
             stream,
             normed_low,
             projected,
-            log_total,
             mixed_low,
             stream_mid,
             normed_two,
@@ -651,12 +1020,11 @@
     )
 
 
-def layer_backward(grad_out, saved_acts, weights, vector, allowed):
+def layer_backward(grad_out, saved_acts, weights, vector, seq_lengths):
     (
         stream,
         normed_low,
         projected,
-        log_total,
         mixed_low,
         stream_mid,
         normed_two,
@@ -676,39 +1044,10 @@
     grad_mid = grad_mid + grad_out
     attn_low = grad_mid.astype(jnp.bfloat16)
     grad_wout = jnp.dot(mixed_low.T, attn_low, preferred_element_type=jnp.bfloat16)
-    grad_mixed = (
-        jnp.dot(attn_low, w_out.T, preferred_element_type=jnp.float32)
-        .astype(jnp.bfloat16)
-        .reshape(LEN, HEADS, HD)
-    )
-    heads_view = projected.reshape(LEN, 3, HEADS, HD)
-    query_rows = heads_view[:, 0]
-    key_rows = heads_view[:, 1]
-    value_rows = heads_view[:, 2]
-    attn_probs = jnp.exp(attention_scores(query_rows, key_rows, allowed) - log_total)
-    grad_probs = jnp.einsum(
-        "qhd,khd->hqk", grad_mixed, value_rows, preferred_element_type=jnp.float32
-    )
-    grad_values = jnp.einsum(
-        "hqk,qhd->khd",
-        attn_probs.astype(jnp.bfloat16),
-        grad_mixed,
-        preferred_element_type=jnp.float32,
-    )
-    row_dot = jnp.sum(grad_probs * attn_probs, axis=-1, keepdims=True)
-    scores_low = (attn_probs * (grad_probs - row_dot)).astype(jnp.bfloat16)
-    grad_queries = (
-        jnp.einsum("hqk,khd->qhd", scores_low, key_rows, preferred_element_type=jnp.float32) * 0.125
-    )
-    grad_keys = (
-        jnp.einsum("hqk,qhd->khd", scores_low, query_rows, preferred_element_type=jnp.float32)
-        * 0.125
-    )
-    qkv_low = (
-        jnp.stack([grad_queries, grad_keys, grad_values], axis=1)
-        .reshape(LEN, 3 * D)
-        .astype(jnp.bfloat16)
-    )
+    grad_mixed = jnp.dot(attn_low, w_out.T, preferred_element_type=jnp.float32).astype(
+        jnp.bfloat16
+    )
+    qkv_low = attend_back(projected, grad_mixed, seq_lengths)
     grad_wqkv = jnp.dot(normed_low.T, qkv_low, preferred_element_type=jnp.bfloat16)
     grad_normed = jnp.dot(qkv_low, w_qkv.T, preferred_element_type=jnp.float32)
     grad_input, grad_gain_one, grad_shift_one = jax.vjp(
@@ -729,16 +1068,6 @@
         ]
     )
     return (grad_input + grad_mid, (grad_wqkv, grad_wout, grad_wfc, grad_wproj), grad_vector)
-
-
-def combine_stats(earlier, later):
-    max_one, total_one, target_one = earlier
-    max_two, total_two, target_two = later
-    joint_max = jnp.maximum(max_one, max_two)
-    joint_total = total_one * jnp.exp(max_one - joint_max) + total_two * jnp.exp(
-        max_two - joint_max
-    )
-    return (joint_max, joint_total, target_one + target_two)
 
 
 def adamw(weight, moment_one, moment_two, gradient, step_rate, decay_rate, step_float):
@@ -783,23 +1112,33 @@
     same_core = halves * size
     devices = 2 * same_core
     low = jnp.bfloat16
-    near = LEN * 9 // 16
+    near = LEN // 2
+    fused = size <= 8
     rest = LEN - near
     slots = loss_slots.shape[0]
 
+    half_of = jnp.arange(halves)[:, None]
+    wide_index = jnp.arange(size)[None, :]
+    place_of = jnp.where(wide_index % 2 == 0, wide_index // 2, size - 1 - (wide_index - 1) // 2)
+    to_device = ((half_of ^ net.half) * size + (place_of - net.place) % size).reshape(-1)
+    offsets = (net.place + wide_index) % size
+    wide_there = jnp.where(offsets < size // 2, 2 * offsets, 2 * (size - 1 - offsets) + 1)
+    from_device = ((half_of ^ net.half) * size + wide_there).reshape(-1)
+
     numbers = jnp.concatenate([token_ids, loss_slots, target_ids, seq_lengths])
-    numbers = net.ring_gather(jnp.stack([numbers, net.swap_half(numbers)], axis=1))
-    numbers = jnp.stack(numbers).transpose(2, 0, 1)
+    numbers = jnp.pad(numbers, (0, -numbers.shape[0] % 1024)).reshape(-1, 128)
+    numbers = cast_call(size, numbers, False, 5).reshape(same_core, -1)
+    numbers = jnp.take(numbers, from_device, axis=0).reshape(halves, size, -1)
     group_tokens = numbers[:, :, :LEN]
     group_slots = numbers[:, :, LEN : LEN + slots].reshape(same_core * slots)
     group_targets = numbers[:, :, LEN + slots : LEN + 2 * slots].reshape(same_core * slots)
-    core_total = jnp.sum(numbers[:, :, LEN + 2 * slots :].astype(jnp.float32))
+    core_total = jnp.sum(numbers[:, :, LEN + 2 * slots].astype(jnp.float32))
     token_total = core_total + net.swap_core(core_total[None])[0]
 
     own_rows = embed_table.shape[0]
-    table_own = embed_table.astype(low)
-    table_low = jnp.concatenate([table_own, net.swap_core(table_own)])
-    chip_rows = 2 * own_rows
+    height = own_rows + -own_rows % 64
+    chip_rows = 2 * height
+    table_own = jnp.pad(embed_table.astype(low), ((0, height - own_rows), (0, 0)))
     own_start = net.device * own_rows
     other_start = (net.device + (1 - 2 * net.core) * size) * own_rows
 
@@ -809,18 +1148,14 @@
         return jnp.where(
             (mine >= 0) & (mine < own_rows),
             mine,
-            jnp.where((other >= 0) & (other < own_rows), other + own_rows, -1),
+            jnp.where((other >= 0) & (other < own_rows), other + height, -1),
         )
 
     def one_hot(ids):
         return (ids[:, None] == jnp.arange(chip_rows)[None, :]).astype(low)
 
-    local_tokens = locate(group_tokens)
-
-    def look_up(ids):
-        return jnp.dot(
-            one_hot(ids.reshape(-1)), table_low, preferred_element_type=jnp.float32
-        ).astype(low)
+    local_tokens = locate(group_tokens).reshape(same_core, LEN)
+    ids_near, ids_rest = local_tokens[:, :near], local_tokens[:, near:]
 
     shared = pos_table.shape[0]
     vector_rows = -(-vectors.shape[0] // D)
@@ -830,13 +1165,32 @@
     shards_low = []
     for layer_at in range(LAYERS):
         shards_low += [part[layer_at].astype(low) for part in (w_qkv, w_fc, w_proj, w_out)]
-    gathered = gather_call(
-        size,
-        shards_low + [small_own.astype(low)],
-        (True, True, False, False) * LAYERS + (False,),
-        True,
-        1,
-    )
+    shards_low.append(small_own.astype(low))
+    ring_first = (True, True, False, False) * LAYERS + (False,)
+    if fused:
+        *gathered, table_low, found = look_up_call(
+            size, shards_low, ring_first, table_own, jnp.concatenate([ids_near, ids_rest])[..., None], 1
+        )
+        stream = scatter_call(
+            size, [found, found], (True, False), False, low, 2, ((0, 1), (same_core, 1))
+        )
+        stream = jnp.concatenate(stream)
+    else:
+        gathered = gather_call(size, shards_low, ring_first, True, 1)
+        table_low = jnp.concatenate([table_own, net.swap_core(table_own)])
+        found = [
+            jnp.dot(
+                one_hot(ids.reshape(-1)), table_low, preferred_element_type=jnp.float32
+            ).astype(low).reshape(same_core, -1, D)
+            for ids in (ids_near, ids_rest)
+        ]
+        bands = max(1, same_core // 16)
+        band = D // bands
+        parts = []
+        for at in range(bands):
+            window = [part[:, :, at * band : (at + 1) * band] for part in found]
+            parts.append(jnp.concatenate(scatter_call(size, window, (True, False), False, low, 2)))
+        stream = jnp.concatenate(parts, axis=1)
     small_low = gathered[-1]
     pos_low = small_low[:, :shared].reshape(devices * shared, D)
     vector_all = (
@@ -846,29 +1200,8 @@
         .astype(jnp.float32)
     )
 
-    near_all = look_up(local_tokens[:, :, :near]).reshape(same_core, near, D)
-    rest_all = look_up(local_tokens[:, :, near:]).reshape(same_core, rest, D)
-    bands = max(1, same_core // 16)
-    band = D // bands
-    stream = jnp.concatenate(
-        [
-            jnp.concatenate(
-                scatter_call(
-                    size,
-                    [part[:, :, at * band : (at + 1) * band] for part in (near_all, rest_all)],
-                    (True, False),
-                    False,
-                    low,
-                    2,
-                )
-            )
-            for at in range(bands)
-        ],
-        axis=1,
-    )
     stream = stream.astype(jnp.float32) + pos_low[:LEN].astype(jnp.float32)
 
-    allowed = attention_mask(seq_lengths[0])
     kept_weights = []
     saved_list = []
     for layer_at in range(LAYERS):
@@ -878,7 +1211,7 @@
         weights = (w_a, w_b, w_c, w_d)
         kept_weights.append(weights)
         stream, saved_acts = layer_forward(
-            stream, weights, vector_all[layer_at * per_layer : (layer_at + 1) * per_layer], allowed
+            stream, weights, vector_all[layer_at * per_layer : (layer_at + 1) * per_layer], seq_lengths
         )
         saved_list.append(saved_acts)
     tail_start = LAYERS * per_layer
@@ -890,33 +1223,29 @@
     )
     slot_rows = jnp.maximum(loss_slots, 0)
     own_picked = final_norm[slot_rows].astype(low)
-    group_rows = net.ring_gather(jnp.stack([own_picked, net.swap_half(own_picked)]))
-    group_rows = jnp.stack(group_rows, axis=1).reshape(same_core * slots, D)
-    logits = jnp.dot(group_rows, table_low.T, preferred_element_type=jnp.float32)
+    some = slots // 2
+    group_rows = jnp.concatenate(
+        gather_call(size, [own_picked[:some], own_picked[some:]], (True, False), False, 6), axis=1
+    ).reshape(same_core * slots, D)
+    real = jnp.arange(chip_rows) % height < own_rows
+    logits = jnp.where(
+        real, jnp.dot(group_rows, table_low.T, preferred_element_type=jnp.float32), -1e30
+    )
     target_onehot = locate(group_targets)[:, None] == jnp.arange(chip_rows)[None, :]
     row_max = jnp.max(logits, axis=-1)
     row_total = jnp.sum(jnp.exp(logits - row_max[:, None]), axis=-1)
     target_logit = jnp.sum(jnp.where(target_onehot, logits, 0.0), axis=-1)
-    half_of = jnp.arange(halves)[:, None]
-    wide_index = jnp.arange(size)[None, :]
-    place_of = jnp.where(wide_index % 2 == 0, wide_index // 2, size - 1 - (wide_index - 1) // 2)
-    to_device = ((half_of ^ net.half) * size + (place_of - net.place) % size).reshape(-1)
-    offsets = (net.place + wide_index) % size
-    wide_there = jnp.where(offsets < size // 2, 2 * offsets, 2 * (size - 1 - offsets) + 1)
-    from_device = ((half_of ^ net.half) * size + wide_there).reshape(-1)
     stats = jnp.stack([row_max, row_total, target_logit], axis=-1)
     stats = jnp.take(stats.reshape(same_core, slots * 3), to_device, axis=0)
-    stats = stats.reshape(same_core * slots, 3).T
-
-    def merged(stats, there):
-        return jnp.stack(combine_stats((stats[0], stats[1], stats[2]), (there[0], there[1], there[2])))
-
-    stats = merged(stats, net.swap_half(stats))
-    bit = 1
-    while bit < size:
-        stats = merged(stats, net.flip(stats, bit))
-        bit *= 2
-    stats = jnp.stack([stats[0] + jnp.log(stats[1]), stats[2]]).reshape(2, same_core, slots)
+    stats = stats.reshape(same_core * slots, 3).T.reshape(-1)
+    entries = stats.shape[0]
+    stats = jnp.pad(stats, (0, -entries % 1024)).reshape(-1, 128)
+    stats = cast_call(size, stats, False, 7).reshape(same_core, -1)[:, :entries]
+    stats = stats.reshape(same_core, 3, same_core * slots)
+    joint_max = jnp.max(stats[:, 0], axis=0)
+    joint_total = jnp.sum(stats[:, 1] * jnp.exp(stats[:, 0] - joint_max), axis=0)
+    stats = jnp.stack([joint_max + jnp.log(joint_total), jnp.sum(stats[:, 2], axis=0)])
+    stats = stats.reshape(2, same_core, slots)
     stats = jnp.take(stats, from_device, axis=1).reshape(2, same_core * slots)
     log_total, merged_target = stats[0], stats[1]
     group_used = (group_slots >= 0).astype(jnp.float32)
@@ -926,13 +1255,18 @@
         * (group_used / token_total)[:, None]
     ).astype(low)
     grad_rows = jnp.dot(grad_logits, table_low, preferred_element_type=jnp.float32)
-    grad_rows = grad_rows.reshape(halves, size, slots, D)
-    cut = D // 2
-    pair = grad_rows[0, :, :, :cut] + net.swap_half(grad_rows[1, :, :, :cut])
-    grad_one = net.ring_scatter(lambda at: pair[at], jnp.float32)
-    both = net.ring_scatter(lambda at: grad_rows[:, at, :, cut:], jnp.float32)
-    grad_two = both[0] + net.swap_half(both[1])
-    grad_rows = jnp.concatenate([grad_one, grad_two], axis=1)
+    grad_rows = grad_rows.reshape(2 * same_core, some, D)
+    grad_rows = jnp.concatenate(
+        scatter_call(
+            size,
+            [grad_rows, grad_rows],
+            (True, False),
+            False,
+            jnp.float32,
+            8,
+            ((0, 2), (1, 2)),
+        )
+    )
     grad_final = jnp.zeros((LEN, D), jnp.float32).at[slot_rows].add(grad_rows)
     grad_stream, grad_gain_final, grad_shift_final = final_pull(grad_final)
     layer_shards = []
@@ -943,7 +1277,7 @@
             saved_list[layer_at],
             kept_weights[layer_at],
             vector_all[layer_at * per_layer : (layer_at + 1) * per_layer],
-            allowed,
+            seq_lengths,
         )
         grad_a, grad_b, grad_c, grad_d = full_grads
         shard_a, shard_c, shard_d, shard_b = scatter_call(
@@ -958,21 +1292,21 @@
         vector_grads.insert(0, grad_vector)
     grad_low = grad_stream.astype(low)
     grad_near, grad_rest = grad_low[:near], grad_low[near:]
-    near_all, rest_all = gather_call(size, [grad_near, grad_rest], (True, False), False, 4)
-
-    def spread(ids, rows):
-        return jnp.dot(one_hot(ids.reshape(-1)).T, rows, preferred_element_type=jnp.float32)
-
     grad_table = jnp.dot(grad_logits.T, group_rows, preferred_element_type=jnp.float32)
-    grad_table = grad_table + spread(local_tokens[:, :, :near], near_all.reshape(-1, D))
-    grad_table = grad_table + spread(local_tokens[:, :, near:], rest_all.reshape(-1, D))
-    table_shard = grad_table[:own_rows] + net.swap_core(grad_table[own_rows:])
-    grad_pos = jnp.concatenate(
-        [
-            jnp.sum(near_all.astype(jnp.float32), axis=0),
-            jnp.sum(rest_all.astype(jnp.float32), axis=0),
-        ]
-    )
+    if fused:
+        ids = [part[:, None] for part in (ids_near, ids_rest)]
+        grad_table, grad_pos = spread_call(size, grad_near, grad_rest, ids, grad_table, 4)
+    else:
+        wholes = gather_call(size, [grad_near, grad_rest], (True, False), False, 4)
+        for ids, whole in zip((ids_near, ids_rest), wholes):
+            grad_table = grad_table + jnp.dot(
+                one_hot(ids.reshape(-1)).T, whole.reshape(-1, D), preferred_element_type=jnp.float32
+            )
+        grad_table = grad_table[:height] + net.swap_core(grad_table[height:])
+        grad_pos = jnp.concatenate(
+            [jnp.sum(whole.astype(jnp.float32), axis=0) for whole in wholes]
+        )
+    table_shard = grad_table[:own_rows]
     grad_pos = jnp.pad(grad_pos, ((0, POS - LEN), (0, 0)))
     other_device = net.device + (1 - 2 * net.core) * size
     pos_shard = lax.dynamic_slice_in_dim(grad_pos, net.device * shared, shared) + net.swap_core(
@@ -988,7 +1322,9 @@
     proj_shard = jnp.stack([member[3] for member in layer_shards])
     shards = (qkv_shard, out_shard, fc_shard, proj_shard, small_shard, pos_shard, table_shard)
     squares = jnp.sum(jnp.stack([jnp.sum(member * member) for member in shards]))
-    loss_total, square_total = net.total(jnp.stack([own_loss, squares]))
+    sums = jnp.pad(jnp.stack([own_loss, squares]), (0, 1022)).reshape(8, 128)
+    sums = jnp.sum(cast_call(size, sums, True, 9), axis=0)
+    loss_total, square_total = sums[0, 0], sums[0, 1]
     loss_value = loss_total / token_total
     grad_norm = jnp.sqrt(square_total)
     factor = CLIP_LIMIT / jnp.maximum(grad_norm, CLIP_LIMIT)

time: 1420 us -> 1200 us (0.85)
  matrix products: 415 us -> 188 us
  Pallas kernels: 648 us -> 849 us
  other arithmetic: 163 us -> 82.4 us
  waiting for transfers between devices: 59.8 us -> 3.36 us
  starting transfers between devices: 59.1 us -> 10.8 us
    dot_general x16 -> x0, matrix products: 222 us -> none  [the longest x2 70 us: look_up(): jnp.dot(one_hot(ids.reshape(-1)), table_low, preferred_element_type=jnp.f...]
    pallas_call x5 -> x14, Pallas kernels: 648 us -> 849 us  [the longest x4 373 us: scatter_call(): pl.pallas_call(functools.partial(scatter_body, size, half_first, across,...]
    ppermute x59 -> x12, waiting for transfers between devices: 59.8 us -> 3.36 us  [step(): return lax.ppermute(array, ('narrow', 'wide'), pairs)]
    ppermute x59 -> x12, starting transfers between devices: 59.1 us -> 10.8 us  [step(): return lax.ppermute(array, ('narrow', 'wide'), pairs)]
    reduce_sum x5 -> x3, other arithmetic: 28.4 us -> 1.69 us  [the longest x1 0.98 us: on_device(): sums = jnp.sum(cast_call(size, sums, True, 9), axis=0)]
    convert_element_type x3 -> x2, other arithmetic: 29.4 us -> 4.76 us  [the longest x1 4.26 us: on_device(): grad_logits = ((jnp.exp(logits - log_total[:, None]) - target_onehot.asty...]
  transfers between devices with their start and end apart: 59 -> 12, of which waited for: 30 -> 3; matrix products, arithmetic and copies ran while one was open for 6% -> 9% of each run, Pallas kernels for 29% -> 63%
where the time goes in v3:
time: 1200 us; the launch traced here: 1190 us
  Pallas kernels  849 us (71%)
  matrix products  188 us (16%)
  other arithmetic  82.4 us (7%)
  local copies, waits for them, and re-layouts  38.1 us (3%)
  between operations  14.1 us (1%)
    pallas_call x4, Pallas kernels, scatter_call(): pl.pallas_call(functools.partial(scatter_body, size, half_first, across,...  373 us
    pallas_call x1, Pallas kernels, look_up_call(): pl.pallas_call(functools.partial(look_up_body, size, ring_first), out_sha...  193 us
    pallas_call x1, Pallas kernels, spread_call(): pl.pallas_call(functools.partial(spread_body, size), out_shape=[jax.Shape...  150 us
    pallas_call x2, Pallas kernels, attend_back(): pl.pallas_call(attend_back_body, grid=(pairs,), out_shape=jax.ShapeDtypeS...  50 us
    pallas_call x2, Pallas kernels, attend(): pl.pallas_call(attend_body, grid=(pairs,), out_shape=jax.ShapeDtypeStruct...  32.6 us
    dot_general x2, matrix products, layer_backward(): jnp.dot(branch_low, w_proj.T, preferred_element_type=jnp.float32)  31.5 us
    pallas_call x3, Pallas kernels, cast_call(): pl.pallas_call(functools.partial(cast_body, size, everyone), out_shape=ja...  30.1 us
    dot_general x2, matrix products, layer_backward(): jnp.dot(hidden_low.T, branch_low, preferred_element_type=jnp.bfloat16)  26.2 us
  transfers between devices with their start and end apart: 12, of which 3 were waited for; matrix products, arithmetic and copies ran while one was open for 9% of the time, Pallas kernels for 63%

profile of v3, /device:TPU:0, one launch (start us, length us, event | category | flops | bytes accessed | tf_op | source)
XLA Modules:
  0.0 1185.2 jit_solution(5147647299993654911)
XLA Ops:
  2.9 11.0 shard_map.425
  18.1 2.5 copy-done.13
  21.1 2.0 pad.27.refs_9_
  23.2 2.7 copy.65.refs_10_
  26.0 193.5 %shard_map.426 = (bf16[32,32,3072]{2,1,0:T(8,128)(2,1)}, bf16[32,32,4096]{2,1,0:T(8,128)(2,1)}, bf16[32,128,1024]{2,1,0:T(8,128)(2,1)}, bf16[32,32,1024]{2,1,0:T...) custom-call(bf16[32,3072]{1,0:T(8,128)(2,1)S(1)} %get-tuple-element., ...), custom_call_target="tpu_custom_call" | custom-call | tf_op jit(solution)/shard_map/pallas_call | solution.py:388
  219.6 1.4 copy-done.6
  223.5 128.6 %shard_map.427 = (bf16[256,1024]{1,0:T(8,128)(2,1)}, bf16[256,1024]{1,0:T(8,128)(2,1)}) custom-call(bf16[32,256,1024]{2,1,0:T(8,128)(2,1)} %get-tuple-element.50.refs_0_.refs_1_, bf16[32,256,1024]{2,1,0:T(8,128)(2,1)} %get-tuple-element.50.refs_0_.refs_1_), custom_call_target="tpu_custom_call" | custom-call | tf_op jit(solution)/shard_map/pallas_call | solution.py:819
  352.1 1.6 maximum_convert_fusion
  355.1 1.6 slice_convert_fusion
  358.0 1.8 add_convert_fusion.7
  359.8 6.4 add_convert_fusion.1.query_ref.key_ref.value_ref
  366.2 16.4 %shard_map.428 = bf16[512,1024]{1,0:T(8,128)(2,1)S(1)} custom-call(s32[1]{0:T(128)S(6)} %copy.112.length_ref, bf16[512,3072]{1,0:T(8,128)(2,1)S(1)} %add_convert_fusion.1.query_ref.key_ref.value_ref, bf16[512,3072]{1,0:T(8,128)(2,1)S(1)} %add_convert_fusion.1.query_ref.key_ref.value_ref, bf16[512,3072]{1,0:T(8,128)(2,1)S(1)} %add_convert_fusion.1.query_ref.key_ref.value_ref), custom_call_target="tpu_custom_call" | custom-call | flops 1073741824 | bytes 4194304 | tf_op jit(solution)/shard_map/pallas_call | solution.py:893
  382.7 1.5 fusion.19
  387.3 1.8 slice-done.3
  389.1 4.7 fusion.75
  393.9 5.6 fusion.103
  399.9 4.4 add_convert_fusion.query_ref.key_ref.value_ref
  404.4 16.2 %shard_map.429 = bf16[512,1024]{1,0:T(8,128)(2,1)S(1)} custom-call(s32[1]{0:T(128)S(6)} %copy.112.length_ref, bf16[512,3072]{1,0:T(8,128)(2,1)S(1)} %add_convert_fusion.query_ref.key_ref.value_ref, bf16[512,3072]{1,0:T(8,128)(2,1)S(1)} %add_convert_fusion.query_ref.key_ref.value_ref, bf16[512,3072]{1,0:T(8,128)(2,1)S(1)} %add_convert_fusion.query_ref.key_ref.value_ref), custom_call_target="tpu_custom_call" | custom-call | flops 1073741824 | bytes 4194304 | tf_op jit(solution)/shard_map/pallas_call | solution.py:893
  423.6 1.5 slice-done.7
  425.2 7.1 fusion.78
  432.3 8.5 fusion.105
  443.0 19.7 %shard_map.430 = (bf16[16,16,1024]{2,1,0:T(8,128)(2,1)}, bf16[16,16,1024]{2,1,0:T(8,128)(2,1)}) custom-call(bf16[16,1024]{1,0:T(8,128)(2,1)} %get-tuple-element.188.refs_0_, bf16[16,1024]{1,0:T(8,128)(2,1)} %get-tuple-element.187.refs_1_), custom_call_target="tpu_custom_call" | custom-call | tf_op jit(solution)/shard_map/pallas_call | solution.py:536
  464.1 6.9 fusion.106
  471.0 2.0 exponential_reduce_fusion
  477.6 8.9 shard_map.431
  493.4 4.3 multiply_convert_fusion.2
  497.7 9.1 fusion.107
  506.8 25.6 %shard_map.432 = (f32[16,1024]{1,0:T(8,128)}, f32[16,1024]{1,0:T(8,128)}) custom-call(f32[32,16,1024]{2,1,0:T(8,128)} %bitcast.200, f32[32,16,1024]{2,1,0:T(8,128)} %bitcast.201), custom_call_target="tpu_custom_call" | custom-call | tf_op jit(solution)/shard_map/pallas_call | solution.py:819
  532.5 2.6 scatter_custom_fusion
  535.1 3.1 multiply_reduce_fusion.2
  539.7 15.9 %convert_reduce_fusion = (f32[4096]{0:T(1024)S(1)}, bf16[512,4096]{1,0:T(8,128)(2,1)}) fusion(f32[512,4096]{1,0:T(8,128)} %fusion.78, f32[4096]{0:T(1024)S(1)} %get-tuple-element.175, bf16[512,1024]{1,0:T(8,128)(2,1)S(1)} %get-tuple-element.126, bf16[4096,1024]{1,0:T(8,128)(2,1)} %bitcast.247), kind=kOutput, calls=%fused_computation.25 | convolution fusion | flops 4343197696 | bytes 22052864 | tf_op jit(solution)/shard_map/dot_general | solution.py:1037
  555.6 7.1 multiply_reduce_fusion.3
  562.7 9.6 fusion.77
  572.3 13.0 %fusion.80 = bf16[4096,1024]{1,0:T(8,128)(2,1)} fusion(bf16[512,1024]{1,0:T(8,128)(2,1)S(1)} %get-tuple-element.126, f32[512,4096]{1,0:T(8,128)} %fusion.78, f32[4096]{0:T(1024)S(1)} %get-tuple-element.175), kind=kOutput, calls=%fused_computation.317 | convolution fusion | flops 4315938816 | bytes 17842176 | tf_op jit(solution)/shard_map/dot_general | solution.py:1036
  589.0 2.7 fusion.70
  591.7 24.8 %shard_map.433 = bf16[512,3072]{1,0:T(8,128)(2,1)S(1)} custom-call(s32[1]{0:T(128)S(6)} %copy.112.length_ref, bf16[512,3072]{1,0:T(8,128)(2,1)} %copy-done.1, bf16[512,3072]{1,0:T(8,128)(2,1)} %copy-done.1, bf16[512,3072]{1,0:T(8,128)(2,1)} %copy-done.1, bf16[512,1024]{1,0:T(8,128)(2,1)S(1)} %convolution_convert_fusion.1.grad_ref), custom_call_target="tpu_custom_call" | custom-call | flops 2684354560 | bytes 8388608 | tf_op jit(solution)/shard_map/pallas_call | solution.py:961
  616.5 5.8 fusion.76
  622.3 6.1 multiply_reduce_fusion.4
  629.8 15.7 %convert_reduce_fusion.1 = (f32[4096]{0:T(1024)S(1)}, bf16[512,4096]{1,0:T(8,128)(2,1)}) fusion(f32[512,4096]{1,0:T(8,128)} %copy-done.88, f32[4096]{0:T(1024)S(1)} %copy-done.76, bf16[512,1024]{1,0:T(8,128)(2,1)S(1)} %get-tuple-element.132, bf16[4096,1024]{1,0:T(8,128)(2,1)} %bitcast.237), kind=kOutput, calls=%fused_computation.26 | convolution fusion | flops 4343197696 | bytes 22052864 | tf_op jit(solution)/shard_map/dot_general | solution.py:1037
  645.5 8.7 multiply_reduce_fusion.5
  654.2 9.4 fusion.74
  663.6 13.1 %fusion.79 = bf16[4096,1024]{1,0:T(8,128)(2,1)} fusion(bf16[512,1024]{1,0:T(8,128)(2,1)S(1)} %get-tuple-element.132, f32[512,4096]{1,0:T(8,128)} %copy-done.88, f32[4096]{0:T(1024)S(1)} %copy-done.76), kind=kOutput, calls=%fused_computation.316 | convolution fusion | flops 4315938816 | bytes 17842176 | tf_op jit(solution)/shard_map/dot_general | solution.py:1036
  680.4 25.2 %shard_map.434 = bf16[512,3072]{1,0:T(8,128)(2,1)S(1)} custom-call(s32[1]{0:T(128)S(6)} %copy.112.length_ref, bf16[512,3072]{1,0:T(8,128)(2,1)} %copy-done, bf16[512,3072]{1,0:T(8,128)(2,1)} %copy-done, bf16[512,3072]{1,0:T(8,128)(2,1)} %copy-done, bf16[512,1024]{1,0:T(8,128)(2,1)S(1)} %convolution_convert_fusion.grad_ref), custom_call_target="tpu_custom_call" | custom-call | flops 2684354560 | bytes 8388608 | tf_op jit(solution)/shard_map/pallas_call | solution.py:961
  705.7 8.0 multiply_reduce_fusion.1
  715.6 6.6 fusion.108.refs_4_
  722.2 5.3 fusion.15.refs_0_
  728.0 2.9 fusion.89
  732.2 150.3 %shard_map.437 = (f32[1600,1024]{1,0:T(8,128)}, f32[512,1024]{1,0:T(8,128)}) custom-call(bf16[256,1024]{1,0:T(8,128)(2,1)} %get-tuple-element.146.refs_0_, bf16[256,1024]{1,0:T(8,128)(2,1)} %get-tuple-element.145.refs_1_, s32[16,1,256]{2,1,0:T(1,128)} %copy.70.refs_2_, s32[16,1,256]{2,1,0:T(1,128)} %broadcast_in_dim.182.refs_3_, f32[3200,1024]{1,0:T(8,128)} %fusion.108.refs_4_), custom_call_target="tpu_custom_call" | custom-call | tf_op jit(solution)/shard_map/pallas_call | solution.py:489
  882.6 1.6 pad_dynamic-slice_fusion
  884.1 1.8 collective-permute-start.11
  886.0 5.2 multiply_reduce_fusion
  891.2 2.6 fusion.67
  897.3 109.2 %shard_map.436 = (f32[32,3072]{1,0:T(8,128)}, f32[32,4096]{1,0:T(8,128)}, f32[128,1024]{1,0:T(8,128)}, f32[32,1024]{1,0:T(8,128)}) custom-call(bf16[32,32,3072]{2,1,0:T(8,128)(2,1)} %bitcast.202, bf16[32,32,4096]{2,1,0:T(8,128)(2,1)} %bitcast.196, bf16[32,128,1024]{2,1,0:T(8,128)(2,1)} %bitcast.197, bf16[32,32,1024]{2,1,0:T(8,128)(2,1)} %bitcast.204), custom_call_target="tpu_custom_call" | custom-call | tf_op jit(solution)/shard_map/pallas_call | solution.py:819
  1006.4 109.2 %shard_map.435 = (f32[32,3072]{1,0:T(8,128)}, f32[32,4096]{1,0:T(8,128)}, f32[128,1024]{1,0:T(8,128)}, f32[32,1024]{1,0:T(8,128)}) custom-call(bf16[32,32,3072]{2,1,0:T(8,128)(2,1)} %fusion.15.refs_0_, bf16[32,32,4096]{2,1,0:T(8,128)(2,1)} %bitcast.198, bf16[32,128,1024]{2,1,0:T(8,128)(2,1)} %bitcast.199, bf16[32,32,1024]{2,1,0:T(8,128)(2,1)} %bitcast.205), custom_call_target="tpu_custom_call" | custom-call | tf_op jit(solution)/shard_map/pallas_call | solution.py:819
  1117.9 1.6 collective-permute-done.3
  1120.4 1.9 multiply_reduce_fusion.17
  1124.1 1.9 multiply_reduce_fusion.16
  1128.7 1.9 multiply_reduce_fusion.18
  1137.7 2.2 multiply_reduce_fusion.20
  1142.5 10.2 shard_map.438
  1155.9 3.6 multiply_subtract_fusion.3
  1161.1 4.0 multiply_subtract_fusion.2
  1165.1 2.3 multiply_subtract_fusion.1
  1167.5 13.5 %multiply_subtract_fusion = (f32[1572,1024]{1,0:T(8,128)}, f32[1572,1024]{1,0:T(8,128)}, f32[1572,1024]{1,0:T(8,128)}) fusion(f32[1572,1024]{1,0:T(8,128)S(1)} %bitcast.193, f32[]{:T(128)S(6)} %sub.302, f32[]{:T(128)S(6)} %div.267, f32[1600,1024]{1,0:T(8,128)} %get-tuple-element.76, f32[1572,1024]{1,0:T(8,128)} %param.51, f32[1572,1024]{1,0:T(8,128)} %param.44), kind=kLoop, calls=%fused_computation.34 | loop fusion | flops 24145920 | bytes 45072392 | tf_op jit(solution)/shard_map/sub | solution.py:1078
  (407 shorter events, 65.3 us)
Async XLA Ops:
  0.7 17.1 %copy-start.27 = (f32[2,32,4096]{2,1,0:T(8,128)S(1)}, f32[2,32,4096]{2,1,0:T(8,128)}, u32[]{:S(2)}) copy-start(f32[2,32,4096]{2,1,0:T(8,128)} %param.33) | copy-start | bytes 3145732
  16.4 475.1 %collective-permute-start = (f32[1]{0:T(128)}, f32[1]{0:T(128)}, u32[]{:S(2)}, u32[]{:S(2)}) collective-permute-start(f32[1]{0:T(128)} %bitcast.36), channel_id=1, source_target_pairs={{0,8},{1,9},{2,10},{3,11},{4,12},{5,13},{6,14},{7,15},{8,0},{9,1},... | collective-permute-start | bytes 20 | tf_op jit(solution)/shard_map/ppermute | solution.py:52
  355.1 27.5 %copy-start.60 = (f32[512]{0:T(512)}, f32[512]{0:T(512)S(1)}, u32[]{:S(2)}) copy-start(f32[512]{0:T(512)S(1)} %div.248) | copy-start | bytes 6148
  356.9 25.8 %copy-start.58 = (f32[1024]{0:T(1024)}, f32[1024]{0:T(1024)S(1)}, u32[]{:S(2)}) copy-start(f32[1024]{0:T(1024)S(1)} %get-tuple-element.174) | copy-start | bytes 12292
  356.9 29.9 %copy-start.77 = (f32[1024]{0:T(1024)}, f32[1024]{0:T(1024)S(1)}, u32[]{:S(2)}) copy-start(f32[1024]{0:T(1024)S(1)} %get-tuple-element.169) | copy-start | bytes 12292
  356.9 29.9 %copy-start.85 = (f32[1024]{0:T(1024)}, f32[1024]{0:T(1024)S(1)}, u32[]{:S(2)}) copy-start(f32[1024]{0:T(1024)S(1)} %get-tuple-element.168) | copy-start | bytes 12292
  356.9 36.9 %copy-start.75 = (f32[4096]{0:T(1024)}, f32[4096]{0:T(1024)S(1)}, u32[]{:S(2)}) copy-start(f32[4096]{0:T(1024)S(1)} %get-tuple-element.176) | copy-start | bytes 49156
  357.9 8.3 copy-start.64
  357.9 24.7 %copy-start.62 = (f32[512]{0:T(512)}, f32[512]{0:T(512)S(1)}, u32[]{:S(2)}) copy-start(f32[512]{0:T(512)S(1)} %rsqrt.62) | copy-start | bytes 6148
  366.2 16.4 %copy-start = (bf16[512,3072]{1,0:T(8,128)(2,1)}, bf16[512,3072]{1,0:T(8,128)(2,1)S(1)}, u32[]{:S(2)}) copy-start(bf16[512,3072]{1,0:T(8,128)(2,1)S(1)} %add_convert_fusion.1.query_ref.key_ref.value_ref) | copy-start | bytes 9437188
  386.4 7.5 copy-start.17
  386.4 7.4 copy-start.66
  386.4 7.5 slice-start.4
  386.8 7.0 copy-start.68
  386.8 7.0 copy-start.81
  399.5 21.1 %copy-start.19 = (f32[512,1024]{1,0:T(8,128)}, f32[512,1024]{1,0:T(8,128)S(1)}, u32[]{:S(2)}) copy-start(f32[512,1024]{1,0:T(8,128)S(1)} %get-tuple-element.205) | copy-start | bytes 6291460
  404.3 16.2 %copy-start.1 = (bf16[512,3072]{1,0:T(8,128)(2,1)}, bf16[512,3072]{1,0:T(8,128)(2,1)S(1)}, u32[]{:S(2)}) copy-start(bf16[512,3072]{1,0:T(8,128)(2,1)S(1)} %add_convert_fusion.query_ref.key_ref.value_ref) | copy-start | bytes 9437188
  404.4 16.2 %copy-start.10 = (bf16[32,32,1024]{2,1,0:T(8,128)(2,1)S(1)}, bf16[32,32,1024]{2,1,0:T(8,128)(2,1)}, u32[]{:S(2)}) copy-start(bf16[32,32,1024]{2,1,0:T(8,128)(2,1)} %copy-done.9) | copy-start | bytes 6291460
  420.6 11.7 slice-start.10
  422.0 10.3 copy-start.21
  425.2 7.1 slice-start.11
  473.7 15.1 %copy-start.31 = (bf16[1024,512]{0,1:T(8,128)(2,1)S(1)}, bf16[1024,512]{0,1:T(8,128)(2,1)}, u32[]{:S(2)}) copy-start(bf16[1024,512]{0,1:T(8,128)(2,1)} %get-tuple-element.139) | copy-start | bytes 3145732
  497.7 9.2 copy-start.32
  538.1 17.5 %slice-start.8 = ((s8[8388608]{0:T(1024)(128)(4,1)}), s8[4194304]{0:T(1024)(128)(4,1)S(1)}, s32[]{:S(2)}) async-start(s8[8388608]{0:T(1024)(128)(4,1)} %bitcast.244), calls=%async_computation.8 | async-start | bytes 8388608
  539.7 15.9 %copy-start.22 = (f32[512,1024]{1,0:T(8,128)S(1)}, f32[512,1024]{1,0:T(8,128)}, u32[]{:S(2)}) copy-start(f32[512,1024]{1,0:T(8,128)} %copy-done.21) | copy-start | bytes 6291460
  539.7 15.9 %slice-start.9 = ((s8[8388608]{0:T(1024)(128)(4,1)}), s8[4194304]{0:T(1024)(128)(4,1)S(1)}, s32[]{:S(2)}) async-start(s8[8388608]{0:T(1024)(128)(4,1)} %bitcast.244), calls=%async_computation.9 | async-start | bytes 8388608
  591.7 24.8 %copy-start.20 = (f32[512,1024]{1,0:T(8,128)S(1)}, f32[512,1024]{1,0:T(8,128)}, u32[]{:S(2)}) copy-start(f32[512,1024]{1,0:T(8,128)} %copy-done.19) | copy-start | bytes 6291460
  629.8 15.7 %copy-start.18 = (f32[512,1024]{1,0:T(8,128)S(1)}, f32[512,1024]{1,0:T(8,128)}, u32[]{:S(2)}) copy-start(f32[512,1024]{1,0:T(8,128)} %copy-done.17) | copy-start | bytes 6291460
  629.8 15.7 %copy-start.67 = (f32[512]{0:T(512)S(1)}, f32[512]{0:T(512)}, u32[]{:S(2)}) copy-start(f32[512]{0:T(512)} %copy-done.66) | copy-start | bytes 6148
  629.8 15.7 %copy-start.78 = (f32[1024]{0:T(1024)S(1)}, f32[1024]{0:T(1024)}, u32[]{:S(2)}) copy-start(f32[1024]{0:T(1024)} %copy-done.77) | copy-start | bytes 12292
  629.8 15.7 %copy-start.82 = (f32[512]{0:T(512)S(1)}, f32[512]{0:T(512)}, u32[]{:S(2)}) copy-start(f32[512]{0:T(512)} %copy-done.81) | copy-start | bytes 6148
  645.5 8.7 copy-start.86
  663.6 13.1 %copy-start.69 = (f32[512]{0:T(512)S(1)}, f32[512]{0:T(512)}, u32[]{:S(2)}) copy-start(f32[512]{0:T(512)} %copy-done.68) | copy-start | bytes 6148
  680.4 25.3 %copy-start.16 = (f32[512,1024]{1,0:T(8,128)S(1)}, f32[512,1024]{1,0:T(8,128)}, u32[]{:S(2)}) copy-start(f32[512,1024]{1,0:T(8,128)} %copy-done.15) | copy-start | bytes 6291460
  680.4 25.3 %copy-start.59 = (f32[1024]{0:T(1024)S(1)}, f32[1024]{0:T(1024)}, u32[]{:S(2)}) copy-start(f32[1024]{0:T(1024)} %copy-done.58) | copy-start | bytes 12292
  680.4 25.3 %copy-start.61 = (f32[512]{0:T(512)S(1)}, f32[512]{0:T(512)}, u32[]{:S(2)}) copy-start(f32[512]{0:T(512)} %copy-done.60) | copy-start | bytes 6148
  680.4 25.3 %copy-start.63 = (f32[512]{0:T(512)S(1)}, f32[512]{0:T(512)}, u32[]{:S(2)}) copy-start(f32[512]{0:T(512)} %copy-done.62) | copy-start | bytes 6148
  705.7 9.3 copy-start.33
  727.9 165.9 %collective-permute-start.1 = (f32[2,8,2,416]{3,2,1,0:T(2,128)S(1)}, f32[2,8,2,416]{3,2,1,0:T(2,128)S(1)}, u32[]{:S(2)}, u32[]{:S(2)}) collective-permute-start(f32[2,8,2,416]{3,2,1,0:T(2,128)S(1)} %dynamic-slice_bitcast_fusion), channel_id=1, source_target_pairs={{0,8},{1,9},{2,10},{3,11},{4,12},{5,13},{6,14},{7,15},{8,0},{9,1},... | collective-permute-start | bytes 159752 | tf_op jit(solution)/shard_map/ppermute | solution.py:52
  884.1 253.6 %collective-permute-start.11 = (f32[32,1024]{1,0:T(8,128)}, f32[32,1024]{1,0:T(8,128)}, u32[]{:S(2)}, u32[]{:S(2)}) collective-permute-start(f32[32,1024]{1,0:T(8,128)} %pad_dynamic-slice_fusion), channel_id=1, source_target_pairs={{0,8},{1,9},{2,10},{3,11},{4,12},{5,13},{6,14},{7,15},{8,0},{9,1},... | collective-permute-start | bytes 393224 | tf_op jit(solution)/shard_map/ppermute | solution.py:52
  893.8 229.3 %copy-start.55 = (f32[2,8,2,416]{3,2,1,0:T(2,128)}, f32[2,8,2,416]{3,2,1,0:T(2,128)S(1)}, u32[]{:S(2)}) copy-start(f32[2,8,2,416]{3,2,1,0:T(2,128)S(1)} %bitcast_add_fusion.1) | copy-start | bytes 159748
  893.9 221.8 %collective-permute-start.2 = (f32[1,2,416]{2,1,0:T(2,128)S(1)}, f32[1,2,416]{2,1,0:T(2,128)S(1)}, u32[]{:S(2)}, u32[]{:S(2)}) collective-permute-start(f32[1,2,416]{2,1,0:T(2,128)S(1)} %get-tuple-element.181), channel_id=1, source_target_pairs={{0,2},{2,4},{4,6},{6,7},{7,5},{5,3},{3,1},{1,0},{8,10},{10,12},{12... | collective-permute-start | bytes 9992 | tf_op jit(solution)/shard_map/ppermute | solution.py:52
  894.9 220.9 %collective-permute-start.6 = (f32[1,2,416]{2,1,0:T(2,128)S(1)}, f32[1,2,416]{2,1,0:T(2,128)S(1)}, u32[]{:S(2)}, u32[]{:S(2)}) collective-permute-start(f32[1,2,416]{2,1,0:T(2,128)S(1)} %get-tuple-element.183), channel_id=1, source_target_pairs={{2,0},{4,2},{6,4},{7,6},{5,7},{3,5},{1,3},{0,1},{10,8},{12,10},{14... | collective-permute-start | bytes 9992 | tf_op jit(solution)/shard_map/ppermute | solution.py:52
  1006.4 113.9 %copy-start.36 = (f32[32,4096]{1,0:T(8,128)S(1)}, f32[32,4096]{1,0:T(8,128)}, u32[]{:S(2)}) copy-start(f32[32,4096]{1,0:T(8,128)} %get-tuple-element.72) | copy-start | bytes 1572868
  1006.4 117.6 %copy-start.35 = (f32[128,1024]{1,0:T(8,128)S(1)}, f32[128,1024]{1,0:T(8,128)}, u32[]{:S(2)}) copy-start(f32[128,1024]{1,0:T(8,128)} %get-tuple-element.74) | copy-start | bytes 1572868
  1115.7 17.5 %copy-start.47 = (f32[32,1024]{1,0:T(8,128)S(1)}, f32[32,1024]{1,0:T(8,128)}, u32[]{:S(2)}) copy-start(f32[32,1024]{1,0:T(8,128)} %get-tuple-element.70) | copy-start | bytes 393220
  1115.7 17.5 %copy-start.48 = (f32[32,1024]{1,0:T(8,128)S(1)}, f32[32,1024]{1,0:T(8,128)}, u32[]{:S(2)}) copy-start(f32[32,1024]{1,0:T(8,128)} %get-tuple-element.69) | copy-start | bytes 393220
  1115.7 22.0 %copy-start.23 = (f32[512,1024]{1,0:T(8,128)S(1)}, f32[512,1024]{1,0:T(8,128)}, u32[]{:S(2)}) copy-start(f32[512,1024]{1,0:T(8,128)} %get-tuple-element.75) | copy-start | bytes 6291460
  1115.8 3.7 collective-permute-start.3
  1116.7 5.6 collective-permute-start.7
  1119.5 3.7 collective-permute-start.4
  1123.2 4.0 collective-permute-start.8
  1126.0 29.8 %copy-start.34 = (f32[2,32,3072]{2,1,0:T(8,128)S(1)}, f32[2,32,3072]{2,1,0:T(8,128)}, u32[]{:S(2)}) copy-start(f32[2,32,3072]{2,1,0:T(8,128)} %param.31) | copy-start | bytes 2359300
  1126.0 4.7 collective-permute-start.5
  1127.9 3.7 collective-permute-start.9
  1132.2 4.2 collective-permute-start.10
  1155.8 11.6 slice-start
  1167.4 13.6 %copy-start.74 = (f32[832]{0:T(1024)S(1)}, f32[832]{0:T(1024)}, u32[]{:S(2)}) copy-start(f32[832]{0:T(1024)} %param.35) | copy-start | bytes 9988
  1167.4 13.6 %copy-start.83 = (f32[832]{0:T(1024)S(1)}, f32[832]{0:T(1024)}, u32[]{:S(2)}) copy-start(f32[832]{0:T(1024)} %param.49) | copy-start | bytes 9988
  1167.4 13.6 %copy-start.84 = (f32[832]{0:T(1024)S(1)}, f32[832]{0:T(1024)}, u32[]{:S(2)}) copy-start(f32[832]{0:T(1024)} %param.42) | copy-start | bytes 9988
  1167.5 14.2 %copy-start.50 = (f32[32,1024]{1,0:T(8,128)S(1)}, f32[32,1024]{1,0:T(8,128)}, u32[]{:S(2)}) copy-start(f32[32,1024]{1,0:T(8,128)} %get-tuple-element.120) | copy-start | bytes 393220
  1167.5 14.2 %copy-start.52 = (f32[32,1024]{1,0:T(8,128)S(1)}, f32[32,1024]{1,0:T(8,128)}, u32[]{:S(2)}) copy-start(f32[32,1024]{1,0:T(8,128)} %param.36) | copy-start | bytes 393220
  1167.5 14.2 %copy-start.56 = (f32[32,1024]{1,0:T(8,128)S(1)}, f32[32,1024]{1,0:T(8,128)}, u32[]{:S(2)}) copy-start(f32[32,1024]{1,0:T(8,128)} %param.50) | copy-start | bytes 393220
  1167.5 14.2 %copy-start.57 = (f32[32,1024]{1,0:T(8,128)S(1)}, f32[32,1024]{1,0:T(8,128)}, u32[]{:S(2)}) copy-start(f32[32,1024]{1,0:T(8,128)} %param.43) | copy-start | bytes 393220
  (51 other events, 178.3 us)

commit v4 on v3

--- a/solution.py
+++ b/solution.py
@@ -61,59 +61,6 @@
         size = self.size
         at = lax.rem(self.place + offset, size)
         return jnp.where(at < size // 2, 2 * at, 2 * (size - 1 - at) + 1)
-
-    def ring_scatter(self, take, low):
-        size = self.size
-        far = size // 2
-        block = take(far)
-        cut = block.shape[0] // 2
-        from_left = self.step(block[:cut].astype(low), self.right)
-        from_right = self.step(block[cut:].astype(low), self.left)
-        for at in range(far - 1, 0, -1):
-            to_right = take(at).astype(jnp.float32)
-            to_left = take(size - at).astype(jnp.float32)
-            if at == far - 1:
-                to_right = jnp.concatenate(
-                    [to_right[:cut] + from_left.astype(jnp.float32), to_right[cut:]]
-                )
-                to_left = jnp.concatenate(
-                    [to_left[:cut], to_left[cut:] + from_right.astype(jnp.float32)]
-                )
-            else:
-                to_right = to_right + from_left.astype(jnp.float32)
-                to_left = to_left + from_right.astype(jnp.float32)
-            from_left = self.step(to_right.astype(low), self.right)
-            from_right = self.step(to_left.astype(low), self.left)
-        return (
-            take(0).astype(jnp.float32)
-            + from_left.astype(jnp.float32)
-            + from_right.astype(jnp.float32)
-        )
-
-    def reduce_rows(self, array, half_first, low):
-        size, halves = self.size, self.halves
-        rows = array.shape[0] // (halves * 2 * size)
-        columns = array.shape[1]
-        split = array.reshape(halves, 2, size, rows, columns)
-
-        def pick(value, at, axis):
-            return lax.dynamic_index_in_dim(value, at, axis, keepdims=False)
-
-        def plus(one, two):
-            return one.astype(jnp.float32) + two.astype(jnp.float32)
-
-        chip = plus(
-            pick(split, self.core, 1), self.swap_core(pick(split, 1 - self.core, 1).astype(low))
-        ).astype(low)
-        if half_first:
-            pair = plus(
-                pick(chip, self.half, 0), self.swap_half(pick(chip, 1 - self.half, 0))
-            ).astype(low)
-            return self.ring_scatter(lambda at: pick(pair, self.wide_of(at), 0), low)
-        both = self.ring_scatter(lambda at: pick(chip, self.wide_of(at), 1), low)
-        return plus(
-            pick(both, self.half, 0), self.swap_half(pick(both, 1 - self.half, 0).astype(low))
-        )
 
 
 MESH = pl.DeviceIdType.MESH
@@ -407,8 +354,8 @@
 
 def spread_body(size, *refs):
     near, rest, ids_near, ids_rest, start = refs[:5]
-    table_out, place_out = refs[5:7]
-    near_all, rest_all, total, core_in, table_sem, *sems = refs[7:]
+    table_out, place_out, squares_ref = refs[5:8]
+    near_all, rest_all, total, core_in, table_sem, *sems = refs[8:]
     ids = (ids_near, ids_rest)
     wholes = (near_all, rest_all)
     spot = Spot(size)
@@ -471,12 +418,14 @@
     swap.wait_recv()
     step = height // 4
 
-    def add(number, nothing):
+    def add(number, squares):
         window = pl.ds(pl.multiple_of(number * step, 16), step)
-        total[window, :] += core_in[window, :]
-        return nothing
-
-    lax.fori_loop(0, 4, add, 0)
+        value = total[window, :] + core_in[window, :]
+        total[window, :] = value
+        return squares + jnp.sum(value * value, axis=0, keepdims=True)
+
+    squares = lax.fori_loop(0, 4, add, jnp.zeros((1, D), jnp.float32))
+    squares_ref[...] = jnp.broadcast_to(squares, squares_ref.shape)
     out = pltpu.make_async_copy(total.at[pl.ds(0, height)], table_out, table_sem.at[0])
     out.start()
     swap.wait_send()
@@ -491,12 +440,14 @@
         out_shape=[
             jax.ShapeDtypeStruct((height, D), jnp.float32),
             jax.ShapeDtypeStruct((LEN, D), jnp.float32),
+            jax.ShapeDtypeStruct((8, D), jnp.float32),
         ],
         in_specs=[pl.BlockSpec(memory_space=pl.ANY)] * 2
         + [pl.BlockSpec(memory_space=pltpu.VMEM)] * 2
         + [pl.BlockSpec(memory_space=pl.ANY)],
         out_specs=[
             pl.BlockSpec(memory_space=pl.ANY),
+            pl.BlockSpec(memory_space=pltpu.VMEM),
             pl.BlockSpec(memory_space=pltpu.VMEM),
         ],
         scratch_shapes=[
@@ -594,13 +545,20 @@
     )(block)
 
 
-def scatter_body(size, half_first, across, bases, *refs):
+def scatter_body(size, half_first, across, bases, working, *refs):
     count = len(half_first)
-    arrays, outs = refs[:count], refs[count : 2 * count]
+    extra_in = FeedBack.INPUTS if working else 0
+    extra_out = FeedBack.OUTPUTS if working else 0
+    arrays, refs = refs[:count], refs[count:]
+    work_in, refs = refs[:extra_in], refs[extra_in:]
+    outs, squares_ref, refs = refs[:count], refs[count], refs[count + 1 :]
+    work_out, refs = refs[:extra_out], refs[extra_out:]
     own, core_in, half_in, ring_in = (
-        refs[(2 + part) * count : (3 + part) * count] for part in range(4)
-    )
-    local_sem, core_sem, half_sem, ring_sem, send_sem = refs[6 * count :]
+        refs[part * count : (1 + part) * count] for part in range(4)
+    )
+    local_sem, core_sem, half_sem, ring_sem, send_sem = refs[4 * count : 4 * count + 5]
+    work = FeedBack(work_in, work_out, refs[4 * count + 5 :]) if working else None
+    squares = []
     spot = Spot(size)
     far = size // 2
     slots = [far] + [o for at in range(far - 1, 0, -1) for o in (at, -at)] + [0]
@@ -633,6 +591,11 @@
 
         def one(step, nothing):
             window = pl.ds(pl.multiple_of(step * width, width), width)
+            if len(parts) == 2 and parts[1][1:] == (0, rows):
+                one, two = parts[0][0][:, window], parts[1][0][:, window]
+                if one.dtype == target.dtype:
+                    target[:, window] = one + two
+                    return nothing
             total = parts[0][0][:, window].astype(jnp.float32)
             for part, first, last in parts[1:]:
                 if first == 0 and last == rows:
@@ -647,6 +610,17 @@
             return nothing
 
         lax.fori_loop(0, columns // width, one, 0)
+
+    def square_sum(ref):
+        width = 128
+
+        def one(step, total):
+            part = ref[:, pl.ds(pl.multiple_of(step * width, width), width)].astype(jnp.float32)
+            return total + jnp.sum(part * part, axis=0, keepdims=True)
+
+        return lax.fori_loop(
+            0, ref.shape[1] // width, one, jnp.zeros((1, width), jnp.float32)
+        )
 
     def ring_slot(way, step):
         return way * far + step - 1
@@ -744,6 +718,9 @@
                     local_sem.at[at, turned * size + k],
                 ).start()
 
+    if working:
+        work.start()
+
     def turned_half(offset):
         for at in range(count):
             if half_first[at]:
@@ -763,6 +740,7 @@
                 parts += ring_parts(at, 0, offset) if offset != far else []
                 if offset == 0:
                     add(outs[at], parts)
+                    squares.append(square_sum(outs[at]))
                 else:
                     add(here, parts)
                     ring_send(at, 0, offset)
@@ -777,6 +755,7 @@
                         landed(half_in[at].at[0], half_sem.at[at, 0])
                         parts.append((half_in[at].at[0], 0, own[at].shape[1]))
                         add(outs[at], parts)
+                        squares.append(square_sum(outs[at]))
                         continue
                     if len(parts) > 1:
                         add(here, parts)
@@ -786,21 +765,35 @@
                         ring_send(at, turned, offset)
 
     groups = [[far]] + [[at, -at] for at in range(far - 1, 0, -1)] + [[0]]
+    def tick():
+        if working:
+            work.tick()
+
+    tick()
     for number, group in enumerate(groups):
         for offset in group:
             turned_half(offset)
+        tick()
         for offset in group:
             both(offset)
+        tick()
         if number > 0:
             for offset in groups[number - 1]:
                 straight(offset)
+            tick()
     for offset in groups[-1]:
         straight(offset)
+    total = squares[0]
+    for one in squares[1:]:
+        total = total + one
+    squares_ref[...] = jnp.broadcast_to(total, squares_ref.shape)
+    if working:
+        work.finish()
     for copy in sent:
         copy.wait_send()
 
 
-def scatter_call(size, arrays, half_first, across, out_type, number, bases=None):
+def scatter_call(size, arrays, half_first, across, out_type, number, bases=None, work=None):
     count = len(arrays)
     far = size // 2
     pieces = [a.shape[1:] for a in arrays]
@@ -816,12 +809,12 @@
         pltpu.VMEM((2 * far if first else 4 * far,) + p, a.dtype)
         for p, a, first in zip(pieces, arrays, half_first)
     ]
-    return pl.pallas_call(
-        functools.partial(scatter_body, size, half_first, across, bases or ((0, 1),) * count),
-        out_shape=[jax.ShapeDtypeStruct(p, out_type) for p in pieces],
-        in_specs=[pl.BlockSpec(memory_space=pl.ANY)] * count,
-        out_specs=[pl.BlockSpec(memory_space=pltpu.VMEM)] * count,
-        scratch_shapes=own
+    outs = [jax.ShapeDtypeStruct(p, out_type) for p in pieces]
+    outs.append(jax.ShapeDtypeStruct((8, 128), jnp.float32))
+    in_specs = [pl.BlockSpec(memory_space=pl.ANY)] * count
+    out_specs = [pl.BlockSpec(memory_space=pltpu.VMEM)] * (count + 1)
+    scratch = (
+        own
         + core_in
         + half_in
         + ring_in
@@ -831,11 +824,25 @@
             pltpu.SemaphoreType.DMA((count, size)),
             pltpu.SemaphoreType.DMA((count, 4 * far)),
             pltpu.SemaphoreType.DMA((count, 4 * far + 3 * size)),
-        ],
+        ]
+    )
+    if work is not None:
+        in_specs += FeedBack.in_specs()
+        outs += FeedBack.out_shape(work[0], work[4])
+        out_specs += FeedBack.out_specs()
+        scratch += FeedBack.scratch(work[0].shape[0])
+    return pl.pallas_call(
+        functools.partial(
+            scatter_body, size, half_first, across, bases or ((0, 1),) * count, work is not None
+        ),
+        out_shape=outs,
+        in_specs=in_specs,
+        out_specs=out_specs,
+        scratch_shapes=scratch,
         compiler_params=pltpu.CompilerParams(
             collective_id=number, has_side_effects=True, vmem_limit_bytes=60 * 1024 * 1024
         ),
-    )(*arrays)
+    )(*arrays, *(work or ()))
 
 
 def layer_norm(values, gain, shift):
@@ -848,23 +855,28 @@
     return jax.nn.gelu(values, approximate=True)
 
 
+INNER = (((1,), (1,)), ((), ()))
+OUTER = (((0,), (0,)), ((), ()))
+
+
+def dot_inner(one, two):
+    return lax.dot_general(one, two, INNER, preferred_element_type=jnp.float32)
+
+
+def dot_outer(one, two):
+    return lax.dot_general(one, two, OUTER, preferred_element_type=jnp.float32)
+
+
 def fill_mask(mask_ref, length):
-    row = lax.broadcasted_iota(jnp.int32, mask_ref.shape, 0)
-    column = lax.broadcasted_iota(jnp.int32, mask_ref.shape, 1)
-    mask_ref[...] = jnp.where((column <= row) & (column < length), 0.0, -1e30)
-
-
-def masked_scores(query, key, mask):
-    scores = lax.dot_general(
-        query * 0.125, key, (((1,), (1,)), ((), ())), preferred_element_type=jnp.float32
-    )
-    return scores + mask
-
-
-def softmax_rows(scores):
-    top = jnp.max(scores, axis=-1, keepdims=True)
-    raised = jnp.exp(scores - top)
-    return raised * (1.0 / jnp.sum(raised, axis=-1, keepdims=True))
+    key = lax.broadcasted_iota(jnp.int32, mask_ref.shape, 0)
+    query = lax.broadcasted_iota(jnp.int32, mask_ref.shape, 1)
+    mask_ref[...] = jnp.where((key <= query) & (key < length), 0.0, -1e30)
+
+
+def probs_by_key(query, key, mask):
+    scores = dot_inner(key, query * 0.125) + mask
+    raised = jnp.exp(scores - jnp.max(scores, axis=0, keepdims=True))
+    return raised * (1.0 / jnp.sum(raised, axis=0, keepdims=True))
 
 
 def attend_body(length_ref, query_ref, key_ref, value_ref, mixed_ref, mask_ref):
@@ -874,17 +886,14 @@
 
     rows = query_ref.shape[0]
     block = rows // 2
-    for head in range(2):
-        lanes = slice(head * HD, (head + 1) * HD)
-        for at in range(2):
-            here, seen = slice(at * block, (at + 1) * block), slice(0, (at + 1) * block)
-            scores = masked_scores(
-                query_ref[here, lanes], key_ref[seen, lanes], mask_ref[here, seen]
-            )
-            probs = softmax_rows(scores).astype(jnp.bfloat16)
-            mixed_ref[here, lanes] = jnp.dot(
-                probs, value_ref[seen, lanes], preferred_element_type=jnp.float32
-            ).astype(jnp.bfloat16)
+    for at in range(2):
+        here, seen = slice(at * block, (at + 1) * block), slice(0, (at + 1) * block)
+        mixed = []
+        for head in range(2):
+            lanes = slice(head * HD, (head + 1) * HD)
+            probs = probs_by_key(query_ref[here, lanes], key_ref[seen, lanes], mask_ref[seen, here])
+            mixed.append(dot_outer(value_ref[seen, lanes], probs.astype(jnp.bfloat16)))
+        mixed_ref[here, :] = jnp.concatenate(mixed).T.astype(jnp.bfloat16)
 
 
 def attend(projected, seq_lengths):
@@ -918,41 +927,30 @@
     block = rows // 2
     pair = pl.program_id(0)
     low = jnp.bfloat16
-    columns = (((0,), (0,)), ((), ()))
-    across = (((1,), (1,)), ((), ()))
-    grads = []
-    for head in range(2):
-        lanes = slice(head * HD, (head + 1) * HD)
-        grad_query, grad_key, grad_value = [], [], []
-        for at in range(2):
-            here, seen = slice(at * block, (at + 1) * block), slice(0, (at + 1) * block)
+    grad_query, grad_key, grad_value = [], [], []
+    for at in range(2):
+        here, seen = slice(at * block, (at + 1) * block), slice(0, (at + 1) * block)
+        heads = []
+        for head in range(2):
+            lanes = slice(head * HD, (head + 1) * HD)
             query, key = query_ref[here, lanes], key_ref[seen, lanes]
             grad = grad_ref[here, lanes]
-            probs = softmax_rows(masked_scores(query, key, mask_ref[here, seen]))
-            grad_probs = lax.dot_general(
-                grad, value_ref[seen, lanes], across, preferred_element_type=jnp.float32
-            )
-            grad_value.append(
-                lax.dot_general(
-                    probs.astype(low), grad, columns, preferred_element_type=jnp.float32
-                )
-            )
-            row_dot = jnp.sum(grad_probs * probs, axis=-1, keepdims=True)
-            scores_low = (probs * (grad_probs - row_dot)).astype(low)
-            grad_query.append(jnp.dot(scores_low, key, preferred_element_type=jnp.float32) * 0.125)
-            grad_key.append(
-                lax.dot_general(scores_low, query, columns, preferred_element_type=jnp.float32)
-                * 0.125
-            )
-        joined = []
-        for parts in (grad_key, grad_value):
-            joined.append(jnp.concatenate([parts[0] + parts[1][:block], parts[1][block:]]))
-        grads.append((jnp.concatenate(grad_query), joined[0], joined[1]))
-    for part in range(3):
+            probs = probs_by_key(query, key, mask_ref[seen, here])
+            grad_probs = dot_inner(value_ref[seen, lanes], grad)
+            value_part = jnp.dot(probs.astype(low), grad, preferred_element_type=jnp.float32)
+            key_dot = jnp.sum(grad_probs * probs, axis=0, keepdims=True)
+            scores_low = (probs * (grad_probs - key_dot)).astype(low)
+            key_part = jnp.dot(scores_low, query, preferred_element_type=jnp.float32) * 0.125
+            heads.append((dot_outer(key, scores_low) * 0.125, key_part, value_part))
+        grad_query.append(jnp.concatenate([part[0] for part in heads]).T)
+        grad_key.append(jnp.concatenate([part[1] for part in heads], axis=1))
+        grad_value.append(jnp.concatenate([part[2] for part in heads], axis=1))
+    for part, parts in enumerate((grad_query, grad_key, grad_value)):
         window = pl.ds(pl.multiple_of(part * D + pair * 2 * HD, 2 * HD), 2 * HD)
-        out_ref[:, window] = jnp.concatenate(
-            [grads[0][part].astype(low), grads[1][part].astype(low)], axis=1
-        )
+        first = parts[0] if part == 0 else parts[0] + parts[1][:block]
+        out_ref[:block, window] = first.astype(low)
+        second = parts[1] if part == 0 else parts[1][block:]
+        out_ref[block:, window] = second.astype(low)
 
 
 def attend_back(projected, grad_mixed, seq_lengths):
@@ -978,6 +976,147 @@
     )(seq_lengths, projected, projected, projected, grad_mixed)
 
 
+class FeedBack:
+    CHUNK = 256
+    INPUTS = 6
+    OUTPUTS = 4
+
+    def __init__(self, ins, outs, scratch):
+        self.branch, self.turned, pre, hidden, w_fc, w_proj = ins
+        self.grad_normed, self.bias, self.grad_fc, self.grad_proj = outs
+        pre_in, hidden_in, fc_in, proj_in, self.fc_out, self.proj_out, self.in_sem, self.out_sem = scratch
+        self.chunks = w_proj.shape[0] // self.CHUNK
+        self.sources = (pre, hidden, w_fc, w_proj)
+        self.slots = (pre_in, hidden_in, fc_in, proj_in)
+        self.done = 0
+
+    def span(self, number):
+        return pl.ds(pl.multiple_of(number * self.CHUNK, self.CHUNK), self.CHUNK)
+
+    def loads(self, number):
+        slot = lax.rem(number, 2)
+        for at, (source, place) in enumerate(zip(self.sources, self.slots)):
+            here = source.at[self.span(number)] if at == 3 else source.at[:, self.span(number)]
+            yield pltpu.make_async_copy(here, place.at[slot], self.in_sem.at[at, slot])
+
+    def stores(self, number):
+        slot = lax.rem(number, 2)
+        yield pltpu.make_async_copy(
+            self.fc_out.at[slot], self.grad_fc.at[:, self.span(number)], self.out_sem.at[0, slot]
+        )
+        yield pltpu.make_async_copy(
+            self.proj_out.at[slot], self.grad_proj.at[self.span(number)], self.out_sem.at[1, slot]
+        )
+
+    def start(self):
+        self.grad_normed[...] = jnp.zeros_like(self.grad_normed)
+        for copy in self.loads(0):
+            copy.start()
+
+    def run(self, first, last):
+        def one(number, nothing):
+            slot = lax.rem(number, 2)
+            for copy in self.loads(number):
+                copy.wait()
+
+            @pl.when(number + 1 < self.chunks)
+            def _():
+                for copy in self.loads(number + 1):
+                    copy.start()
+
+            @pl.when(number >= 2)
+            def _():
+                for copy in self.stores(number - 2):
+                    copy.wait()
+
+            low = jnp.bfloat16
+            pre_in, hidden_in, fc_in, proj_in = self.slots
+            grad_hidden = dot_inner(self.branch[...], proj_in[slot])
+            value = pre_in[slot]
+            square = value * value
+            bent = jnp.tanh(0.7978845608 * value * (1.0 + 0.044715 * square))
+            slope = 0.5 * (1.0 + bent) + 0.5 * value * (1.0 - bent * bent) * (
+                0.7978845608 * (1.0 + 3.0 * 0.044715 * square)
+            )
+            pre_low = (grad_hidden * slope).astype(low)
+            self.bias[:, self.span(number)] = jnp.sum(
+                pre_low.astype(jnp.float32), axis=0, keepdims=True
+            )
+            self.grad_normed[...] += dot_inner(pre_low, fc_in[slot])
+            self.fc_out[slot] = jnp.dot(
+                self.turned[...], pre_low, preferred_element_type=jnp.float32
+            ).astype(low)
+            self.proj_out[slot] = dot_outer(hidden_in[slot], self.branch[...]).astype(low)
+            for copy in self.stores(number):
+                copy.start()
+            return nothing
+
+        lax.fori_loop(first, last, one, 0)
+
+    def tick(self):
+        if self.done < self.chunks:
+            self.run(self.done, self.done + 1)
+            self.done += 1
+
+    def finish(self):
+        if self.done < self.chunks:
+            self.run(self.done, self.chunks)
+        for number in (self.chunks - 2, self.chunks - 1):
+            for copy in self.stores(jnp.int32(number)):
+                copy.wait()
+
+    @classmethod
+    def in_specs(cls):
+        return [pl.BlockSpec(memory_space=pltpu.VMEM)] * 2 + [pl.BlockSpec(memory_space=pl.ANY)] * 4
+
+    @classmethod
+    def out_specs(cls):
+        return [pl.BlockSpec(memory_space=pltpu.VMEM)] * 2 + [pl.BlockSpec(memory_space=pl.ANY)] * 2
+
+    @classmethod
+    def out_shape(cls, branch, w_fc):
+        hidden = w_fc.shape[1]
+        return [
+            jax.ShapeDtypeStruct(branch.shape, jnp.float32),
+            jax.ShapeDtypeStruct((1, hidden), jnp.float32),
+            jax.ShapeDtypeStruct((D, hidden), jnp.bfloat16),
+            jax.ShapeDtypeStruct((hidden, D), jnp.bfloat16),
+        ]
+
+    @classmethod
+    def scratch(cls, rows):
+        low, chunk = jnp.bfloat16, cls.CHUNK
+        return [
+            pltpu.VMEM((2, rows, chunk), jnp.float32),
+            pltpu.VMEM((2, rows, chunk), low),
+            pltpu.VMEM((2, D, chunk), low),
+            pltpu.VMEM((2, chunk, D), low),
+            pltpu.VMEM((2, D, chunk), low),
+            pltpu.VMEM((2, chunk, D), low),
+            pltpu.SemaphoreType.DMA((4, 2)),
+            pltpu.SemaphoreType.DMA((2, 2)),
+        ]
+
+
+def feed_back_body(*refs):
+    ins, outs = FeedBack.INPUTS, FeedBack.OUTPUTS
+    work = FeedBack(refs[:ins], refs[ins : ins + outs], refs[ins + outs :])
+    work.start()
+    work.finish()
+
+
+def feed_back(operands):
+    branch, w_fc = operands[0], operands[4]
+    return pl.pallas_call(
+        feed_back_body,
+        out_shape=FeedBack.out_shape(branch, w_fc),
+        in_specs=FeedBack.in_specs(),
+        out_specs=FeedBack.out_specs(),
+        scratch_shapes=FeedBack.scratch(branch.shape[0]),
+        compiler_params=pltpu.CompilerParams(vmem_limit_bytes=40 * 1024 * 1024),
+    )(*operands)
+
+
 def layer_forward(stream, weights, vector, seq_lengths):
     w_qkv, w_out, w_fc, w_proj = weights
     normed_low = layer_norm(stream, vector[0:D], vector[D : 2 * D]).astype(jnp.bfloat16)
@@ -1020,7 +1159,18 @@
     )
 
 
-def layer_backward(grad_out, saved_acts, weights, vector, seq_lengths):
+def feed_plain(operands):
+    branch_low, normed_turned, hidden_pre, hidden_low, w_fc, w_proj = operands
+    grad_wproj = jnp.dot(hidden_low.T, branch_low, preferred_element_type=jnp.bfloat16)
+    grad_hidden = jnp.dot(branch_low, w_proj.T, preferred_element_type=jnp.float32)
+    pre_low = jax.vjp(gelu_tanh, hidden_pre)[1](grad_hidden)[0].astype(jnp.bfloat16)
+    grad_wfc = jnp.dot(normed_turned, pre_low, preferred_element_type=jnp.bfloat16)
+    grad_normed_two = jnp.dot(pre_low, w_fc.T, preferred_element_type=jnp.float32)
+    bias = jnp.sum(pre_low.astype(jnp.float32), axis=0)
+    return grad_normed_two, bias, grad_wfc, grad_wproj
+
+
+def layer_backward(grad_out, saved_acts, weights, vector, seq_lengths, feed):
     (
         stream,
         normed_low,
@@ -1033,11 +1183,9 @@
     ) = saved_acts
     w_qkv, w_out, w_fc, w_proj = weights
     branch_low = grad_out.astype(jnp.bfloat16)
-    grad_wproj = jnp.dot(hidden_low.T, branch_low, preferred_element_type=jnp.bfloat16)
-    grad_hidden = jnp.dot(branch_low, w_proj.T, preferred_element_type=jnp.float32)
-    pre_low = jax.vjp(gelu_tanh, hidden_pre)[1](grad_hidden)[0].astype(jnp.bfloat16)
-    grad_wfc = jnp.dot(normed_two.T, pre_low, preferred_element_type=jnp.bfloat16)
-    grad_normed_two = jnp.dot(pre_low, w_fc.T, preferred_element_type=jnp.float32)
+    grad_normed_two, grad_bias, grad_wfc, grad_wproj = feed(
+        (branch_low, normed_two.T, hidden_pre, hidden_low, w_fc, w_proj)
+    )
     grad_mid, grad_gain_two, grad_shift_two = jax.vjp(
         layer_norm, stream_mid, vector[2 * D : 3 * D], vector[3 * D : 4 * D]
     )[1](grad_normed_two)
@@ -1064,7 +1212,7 @@
             bias_qkv[2 * D : 3 * D],
             jnp.sum(attn_low.astype(jnp.float32), axis=0),
             jnp.sum(branch_low.astype(jnp.float32), axis=0),
-            jnp.sum(pre_low.astype(jnp.float32), axis=0),
+            grad_bias.reshape(-1),
         ]
     )
     return (grad_input + grad_mid, (grad_wqkv, grad_wout, grad_wfc, grad_wproj), grad_vector)
@@ -1174,7 +1322,7 @@
         stream = scatter_call(
             size, [found, found], (True, False), False, low, 2, ((0, 1), (same_core, 1))
         )
-        stream = jnp.concatenate(stream)
+        stream = jnp.concatenate(stream[:2])
     else:
         gathered = gather_call(size, shards_low, ring_first, True, 1)
         table_low = jnp.concatenate([table_own, net.swap_core(table_own)])
@@ -1189,7 +1337,9 @@
         parts = []
         for at in range(bands):
             window = [part[:, :, at * band : (at + 1) * band] for part in found]
-            parts.append(jnp.concatenate(scatter_call(size, window, (True, False), False, low, 2)))
+            parts.append(
+                jnp.concatenate(scatter_call(size, window, (True, False), False, low, 2)[:2])
+            )
         stream = jnp.concatenate(parts, axis=1)
     small_low = gathered[-1]
     pos_low = small_low[:, :shared].reshape(devices * shared, D)
@@ -1265,37 +1415,61 @@
             jnp.float32,
             8,
             ((0, 2), (1, 2)),
-        )
+        )[:2]
     )
     grad_final = jnp.zeros((LEN, D), jnp.float32).at[slot_rows].add(grad_rows)
     grad_stream, grad_gain_final, grad_shift_final = final_pull(grad_final)
     layer_shards = []
     vector_grads = []
+    squares = jnp.float32(0)
+    pending = None
+
+    def reduce_layers(full_grads, number, more=(), work=None):
+        grad_a, grad_b, grad_c, grad_d = full_grads
+        arrays = [part.reshape(devices, -1, part.shape[1]) for part in (grad_a, grad_c, grad_d, grad_b)]
+        arrays += more
+        outs = scatter_call(
+            size,
+            arrays,
+            (True, True, False, False) + (False,) * len(more),
+            True,
+            jnp.float32,
+            number,
+            work=work,
+        )
+        shard_a, shard_c, shard_d, shard_b, *rest = outs
+        layer_shards.insert(0, (shard_a, shard_b, shard_c, shard_d))
+        return rest
+
     for layer_at in reversed(range(LAYERS)):
+        feed = feed_plain
+        if pending is not None:
+            held = []
+
+            def feed(operands):
+                sums, *results = reduce_layers(pending, 3, work=operands)
+                held.append(jnp.sum(sums[0]))
+                return results
+
         grad_stream, full_grads, grad_vector = layer_backward(
             grad_stream,
             saved_list[layer_at],
             kept_weights[layer_at],
             vector_all[layer_at * per_layer : (layer_at + 1) * per_layer],
             seq_lengths,
+            feed,
         )
-        grad_a, grad_b, grad_c, grad_d = full_grads
-        shard_a, shard_c, shard_d, shard_b = scatter_call(
-            size,
-            [part.reshape(devices, -1, part.shape[1]) for part in (grad_a, grad_c, grad_d, grad_b)],
-            (True, True, False, False),
-            True,
-            jnp.float32,
-            3,
-        )
-        layer_shards.insert(0, (shard_a, shard_b, shard_c, shard_d))
+        if pending is not None:
+            squares = squares + held[0]
+        pending = full_grads
         vector_grads.insert(0, grad_vector)
     grad_low = grad_stream.astype(low)
     grad_near, grad_rest = grad_low[:near], grad_low[near:]
     grad_table = jnp.dot(grad_logits.T, group_rows, preferred_element_type=jnp.float32)
     if fused:
         ids = [part[:, None] for part in (ids_near, ids_rest)]
-        grad_table, grad_pos = spread_call(size, grad_near, grad_rest, ids, grad_table, 4)
+        grad_table, grad_pos, sums = spread_call(size, grad_near, grad_rest, ids, grad_table, 4)
+        squares = squares + jnp.sum(sums[0])
     else:
         wholes = gather_call(size, [grad_near, grad_rest], (True, False), False, 4)
         for ids, whole in zip((ids_near, ids_rest), wholes):
@@ -1303,6 +1477,7 @@
                 one_hot(ids.reshape(-1)).T, whole.reshape(-1, D), preferred_element_type=jnp.float32
             )
         grad_table = grad_table[:height] + net.swap_core(grad_table[height:])
+        squares = squares + jnp.sum(grad_table * grad_table)
         grad_pos = jnp.concatenate(
             [jnp.sum(whole.astype(jnp.float32), axis=0) for whole in wholes]
         )
@@ -1313,15 +1488,16 @@
         lax.dynamic_slice_in_dim(grad_pos, other_device * shared, shared)
     )
     grad_small = jnp.concatenate(vector_grads + [grad_gain_final, grad_shift_final])
-    small_shard = net.reduce_rows(
-        grad_small.reshape(devices * 2, -1), False, jnp.float32
-    ).reshape(-1)
+    own_small = vectors.shape[0]
+    grad_small = jnp.pad(grad_small.reshape(devices, own_small), ((0, 0), (0, -own_small % 1024)))
+    small_shard, sums = reduce_layers(pending, 10, [grad_small.reshape(devices, -1, 128)])
+    small_shard = small_shard.reshape(-1)[:own_small]
+    squares = squares + jnp.sum(sums[0]) + jnp.sum(pos_shard * pos_shard)
     qkv_shard = jnp.stack([member[0] for member in layer_shards])
     out_shard = jnp.stack([member[1] for member in layer_shards])
     fc_shard = jnp.stack([member[2] for member in layer_shards])
     proj_shard = jnp.stack([member[3] for member in layer_shards])
     shards = (qkv_shard, out_shard, fc_shard, proj_shard, small_shard, pos_shard, table_shard)
-    squares = jnp.sum(jnp.stack([jnp.sum(member * member) for member in shards]))
     sums = jnp.pad(jnp.stack([own_loss, squares]), (0, 1022)).reshape(8, 128)
     sums = jnp.sum(cast_call(size, sums, True, 9), axis=0)
     loss_total, square_total = sums[0, 0], sums[0, 1]

time: 1200 us -> 1150 us (0.958)
  matrix products: 188 us -> 148 us
    dot_general x8 -> x4, matrix products: 92.5 us -> 45.7 us  [the longest x1 16.1 us: feed_plain(): jnp.dot(branch_low, w_proj.T, preferred_element_type=jnp.float32)]
    pallas_call x4, Pallas kernels: 373 us -> 387 us  [scatter_call(): pl.pallas_call(functools.partial(scatter_body, size, half_first, across,...]
  transfers between devices with their start and end apart: 12 -> 2, of which waited for: 3 -> 0; matrix products, arithmetic and copies ran while one was open for 9% -> 8% of each run, Pallas kernels for 63% -> 43%
where the time goes in v4:
time: 1150 us; the launch traced here: 1140 us
  Pallas kernels  855 us (74%)
  matrix products  148 us (13%)
  other arithmetic  77 us (7%)
  local copies, waits for them, and re-layouts  42.9 us (4%)
  between operations  12 us (1%)
    pallas_call x4, Pallas kernels, scatter_call(): pl.pallas_call(functools.partial(scatter_body, size, half_first, across,...  387 us
    pallas_call x1, Pallas kernels, look_up_call(): pl.pallas_call(functools.partial(look_up_body, size, ring_first), out_sha...  193 us
    pallas_call x1, Pallas kernels, spread_call(): pl.pallas_call(functools.partial(spread_body, size), out_shape=[jax.Shape...  150 us
    pallas_call x2, Pallas kernels, attend_back(): pl.pallas_call(attend_back_body, grid=(pairs,), out_shape=jax.ShapeDtypeS...  42 us
    pallas_call x2, Pallas kernels, attend(): pl.pallas_call(attend_body, grid=(pairs,), out_shape=jax.ShapeDtypeStruct...  32.2 us
    pallas_call x3, Pallas kernels, cast_call(): pl.pallas_call(functools.partial(cast_body, size, everyone), out_shape=ja...  30.8 us
    sub x7, other arithmetic, adamw(): weight - step_rate * (update + decay_rate * weight)  26.7 us
  transfers between devices with their start and end apart: 2, of which 0 were waited for; matrix products, arithmetic and copies ran while one was open for 8% of the time, Pallas kernels for 43%

profile of v4, /device:TPU:0, one launch (start us, length us, event | category | flops | bytes accessed | tf_op | source)
XLA Modules:
  0.0 1136.7 jit_solution(12606780077144070964)
XLA Ops:
  2.9 10.9 shard_map.425
  18.1 2.5 copy-done.17
  21.1 2.0 pad.31.refs_9_
  23.2 2.7 copy.54.refs_10_
  26.0 193.5 %shard_map.426 = (bf16[32,32,3072]{2,1,0:T(8,128)(2,1)}, bf16[32,32,4096]{2,1,0:T(8,128)(2,1)}, bf16[32,128,1024]{2,1,0:T(8,128)(2,1)}, bf16[32,32,1024]{2,1,0:T...) custom-call(bf16[32,3072]{1,0:T(8,128)(2,1)S(1)} %get-tuple-element., ...), custom_call_target="tpu_custom_call" | custom-call | tf_op jit(solution)/shard_map/pallas_call | solution.py:335
  223.3 129.0 %shard_map.427 = (bf16[256,1024]{1,0:T(8,128)(2,1)}, bf16[256,1024]{1,0:T(8,128)(2,1)}, f32[8,128]{1,0:T(8,128)}) custom-call(bf16[32,256,1024]{2,1,0:T(8,128)(2,1)} %get-tuple-element.58.refs_0_.refs_1_, bf16[32,256,1024]{2,1,0:T(8,128)(2,1)} %get-tuple-element.58.refs_0_.refs_1_), custom_call_target="tpu_custom_call" | custom-call | tf_op jit(solution)/shard_map/pallas_call | solution.py:834
  352.3 1.4 maximum_convert_fusion
  353.8 1.5 fusion.25
  355.4 1.7 multiply_reduce_fusion.14
  357.1 1.6 slice_convert_fusion
  359.9 1.8 add_convert_fusion.7
  361.7 6.4 add_convert_fusion.1.query_ref.key_ref.value_ref
  368.1 16.1 %shard_map.428 = bf16[512,1024]{1,0:T(8,128)(2,1)S(1)} custom-call(s32[1]{0:T(128)S(6)} %copy.103.length_ref, bf16[512,3072]{1,0:T(8,128)(2,1)S(1)} %add_convert_fusion.1.query_ref.key_ref.value_ref, bf16[512,3072]{1,0:T(8,128)(2,1)S(1)} %add_convert_fusion.1.query_ref.key_ref.value_ref, bf16[512,3072]{1,0:T(8,128)(2,1)S(1)} %add_convert_fusion.1.query_ref.key_ref.value_ref), custom_call_target="tpu_custom_call" | custom-call | flops 1073741824 | bytes 4194304 | tf_op jit(solution)/shard_map/pallas_call | solution.py:902
  384.3 1.5 fusion.20
  386.6 1.4 fusion.88
  389.0 1.6 slice-done.1
  390.6 9.4 fusion.14
  400.0 4.6 fusion.89
  405.1 7.0 add_convert_fusion.query_ref.key_ref.value_ref
  412.1 16.1 %shard_map.429 = bf16[512,1024]{1,0:T(8,128)(2,1)S(1)} custom-call(s32[1]{0:T(128)S(6)} %copy.103.length_ref, bf16[512,3072]{1,0:T(8,128)(2,1)S(1)} %add_convert_fusion.query_ref.key_ref.value_ref, bf16[512,3072]{1,0:T(8,128)(2,1)S(1)} %add_convert_fusion.query_ref.key_ref.value_ref, bf16[512,3072]{1,0:T(8,128)(2,1)S(1)} %add_convert_fusion.query_ref.key_ref.value_ref), custom_call_target="tpu_custom_call" | custom-call | flops 1073741824 | bytes 4194304 | tf_op jit(solution)/shard_map/pallas_call | solution.py:902
  428.3 1.3 fusion.90
  430.0 1.3 slice-done.4
  431.3 1.5 slice-done.5
  432.8 7.1 fusion.65
  439.9 8.1 fusion.91
  448.4 1.4 multiply_add_fusion.1
  449.8 2.0 gather_fusion.1
  452.7 19.7 %shard_map.430 = (bf16[16,16,1024]{2,1,0:T(8,128)(2,1)}, bf16[16,16,1024]{2,1,0:T(8,128)(2,1)}) custom-call(bf16[16,1024]{1,0:T(8,128)(2,1)} %get-tuple-element.194.refs_0_, bf16[16,1024]{1,0:T(8,128)(2,1)} %get-tuple-element.193.refs_1_), custom_call_target="tpu_custom_call" | custom-call | tf_op jit(solution)/shard_map/pallas_call | solution.py:487
  473.7 6.9 fusion.92
  480.6 2.0 exponential_reduce_fusion
  487.2 8.9 shard_map.431
  500.3 2.3 copy.60
  505.3 4.6 multiply_convert_fusion.1
  509.9 9.1 fusion.93
  519.1 26.0 %shard_map.432 = (f32[16,1024]{1,0:T(8,128)}, f32[16,1024]{1,0:T(8,128)}, f32[8,128]{1,0:T(8,128)}) custom-call(f32[32,16,1024]{2,1,0:T(8,128)} %bitcast.166, f32[32,16,1024]{2,1,0:T(8,128)} %bitcast.167), custom_call_target="tpu_custom_call" | custom-call | tf_op jit(solution)/shard_map/pallas_call | solution.py:834
  545.0 2.6 scatter_custom_fusion
  547.6 2.5 multiply_reduce_fusion
  551.2 16.1 %convert_reduce_fusion = (f32[4096]{0:T(1024)S(1)}, bf16[512,4096]{1,0:T(8,128)(2,1)}) fusion(f32[512,4096]{1,0:T(8,128)} %fusion.65, f32[4096]{0:T(1024)S(1)} %get-tuple-element.189, bf16[512,1024]{1,0:T(8,128)(2,1)S(1)} %get-tuple-element.140, bf16[4096,1024]{1,0:T(8,128)(2,1)} %bitcast.200), kind=kOutput, calls=%fused_computation.25 | convolution fusion | flops 4343197696 | bytes 22052864 | tf_op jit(solution)/shard_map/dot_general | solution.py:1165
  567.2 7.0 multiply_reduce_fusion.1
  574.3 9.4 fusion.64
  583.7 13.2 %fusion.67 = bf16[4096,1024]{1,0:T(8,128)(2,1)} fusion(bf16[512,1024]{1,0:T(8,128)(2,1)S(1)} %get-tuple-element.140, f32[512,4096]{1,0:T(8,128)} %fusion.65, f32[4096]{0:T(1024)S(1)} %get-tuple-element.189), kind=kOutput, calls=%fused_computation.284 | convolution fusion | flops 4315938816 | bytes 17842176 | tf_op jit(solution)/shard_map/dot_general | solution.py:1164
  598.0 1.8 copy-done.13
  601.1 2.7 fusion.59
  603.8 21.0 %shard_map.433 = bf16[512,3072]{1,0:T(8,128)(2,1)S(1)} custom-call(s32[1]{0:T(128)S(6)} %copy.103.length_ref, bf16[512,3072]{1,0:T(8,128)(2,1)} %copy-done.1, bf16[512,3072]{1,0:T(8,128)(2,1)} %copy-done.1, bf16[512,3072]{1,0:T(8,128)(2,1)} %copy-done.1, bf16[512,1024]{1,0:T(8,128)(2,1)S(1)} %convolution_convert_fusion.1.grad_ref), custom_call_target="tpu_custom_call" | custom-call | flops 2684354560 | bytes 8388608 | tf_op jit(solution)/shard_map/pallas_call | solution.py:959
  624.8 6.0 fusion.63
  630.9 6.2 multiply_reduce_fusion.2
  637.2 6.7 fusion.94.refs_4_
  644.7 1.5 convert_reduce_fusion.5
  646.3 120.7 %shard_map.434 = (f32[32,3072]{1,0:T(8,128)}, f32[32,4096]{1,0:T(8,128)}, f32[128,1024]{1,0:T(8,128)}, f32[32,1024]{1,0:T(8,128)}, f32[8,128]{1,0:T(8,128)}, /*i...) custom-call(bf16[32,32,3072]{2,1,0:T(8,128)(2,1)} %bitcast.168, ...), custom_call_target="tpu_custom_call" | custom-call | tf_op jit(solution)/shard_map/pallas_call | solution.py:834
  767.0 3.1 multiply_reduce_fusion.3
  775.6 2.6 fusion.56
  778.3 21.0 %shard_map.435 = bf16[512,3072]{1,0:T(8,128)(2,1)S(1)} custom-call(s32[1]{0:T(128)S(6)} %copy.103.length_ref, bf16[512,3072]{1,0:T(8,128)(2,1)} %copy-done, bf16[512,3072]{1,0:T(8,128)(2,1)} %copy-done, bf16[512,3072]{1,0:T(8,128)(2,1)} %copy-done, bf16[512,1024]{1,0:T(8,128)(2,1)S(1)} %convolution_convert_fusion.grad_ref), custom_call_target="tpu_custom_call" | custom-call | flops 2684354560 | bytes 8388608 | tf_op jit(solution)/shard_map/pallas_call | solution.py:959
  799.3 7.4 multiply_reduce_fusion.4
  811.3 149.5 %shard_map.436 = (f32[1600,1024]{1,0:T(8,128)}, f32[512,1024]{1,0:T(8,128)}, f32[8,1024]{1,0:T(8,128)}) custom-call(bf16[256,1024]{1,0:T(8,128)(2,1)} %get-tuple-element.160.refs_0_, bf16[256,1024]{1,0:T(8,128)(2,1)} %get-tuple-element.159.refs_1_, s32[16,1,256]{2,1,0:T(1,128)} %copy.59.refs_2_, s32[16,1,256]{2,1,0:T(1,128)} %broadcast_in_dim.182.refs_3_, ...), custom_call_target="tpu_custom_call" | custom-call | tf_op jit(solution)/shard_map/pallas_call | solution.py:438
  960.8 1.4 slice_reduce_fusion.3
  962.2 6.5 fusion.16.refs_0_
  970.6 2.3 collective-permute-start.1
  972.9 111.2 %shard_map.437 = (f32[32,3072]{1,0:T(8,128)}, f32[32,4096]{1,0:T(8,128)}, f32[128,1024]{1,0:T(8,128)}, f32[32,1024]{1,0:T(8,128)}, f32[8,128]{1,0:T(8,128)}, /*index=5*/f32[8,128]{1,0:T(8,128)}) custom-call(bf16[32,32,3072]{2,1,0:T(8,128)(2,1)} %fusion.16.refs_0_, bf16[32,32,4096]{2,1,0:T(8,128)(2,1)} %bitcast.162, bf16[32,128,1024]{2,1,0:T(8,128)(2,1)} %bitcast.163, ...), custom_call_target="tpu_custom_call" | custom-call | tf_op jit(solution)/shard_map/pallas_call | solution.py:834
  1084.2 1.3 slice_reduce_fusion.4
  1091.4 11.0 shard_map.438
  1106.8 17.8 %multiply_subtract_fusion = (f32[1572,1024]{1,0:T(8,128)}, f32[1572,1024]{1,0:T(8,128)}, f32[1572,1024]{1,0:T(8,128)}) fusion(f32[1572,1024]{1,0:T(8,128)} %param.37, f32[]{:T(128)S(6)} %sub.258, f32[]{:T(128)S(6)} %div.267, f32[1600,1024]{1,0:T(8,128)} %get-tuple-element.92, f32[1572,1024]{1,0:T(8,128)} %param.51, f32[1572,1024]{1,0:T(8,128)} %param.44), kind=kLoop, calls=%fused_computation.32 | loop fusion | flops 24145920 | bytes 45072392 | tf_op jit(solution)/shard_map/sub | solution.py:1226
  1124.8 1.9 multiply_subtract_fusion.3
  1128.4 2.3 multiply_subtract_fusion.2
  1131.7 2.3 multiply_subtract_fusion.1
  (364 shorter events, 50.7 us)
Async XLA Ops:
  0.7 17.1 %copy-start.34 = (f32[2,32,4096]{2,1,0:T(8,128)S(1)}, f32[2,32,4096]{2,1,0:T(8,128)}, u32[]{:S(2)}) copy-start(f32[2,32,4096]{2,1,0:T(8,128)} %param.33) | copy-start | bytes 3145732
  16.4 486.9 %collective-permute-start = (f32[1]{0:T(128)}, f32[1]{0:T(128)}, u32[]{:S(2)}, u32[]{:S(2)}) collective-permute-start(f32[1]{0:T(128)} %bitcast.34), channel_id=1, source_target_pairs={{0,8},{1,9},{2,10},{3,11},{4,12},{5,13},{6,14},{7,15},{8,0},{9,1},... | collective-permute-start | bytes 20 | tf_op jit(solution)/shard_map/ppermute | solution.py:52
  355.4 28.9 %copy-start.73 = (f32[512]{0:T(512)}, f32[512]{0:T(512)S(1)}, u32[]{:S(2)}) copy-start(f32[512]{0:T(512)S(1)} %div.262) | copy-start | bytes 6148
  358.8 25.4 %copy-start.65 = (f32[1024]{0:T(1024)}, f32[1024]{0:T(1024)S(1)}, u32[]{:S(2)}) copy-start(f32[1024]{0:T(1024)S(1)} %get-tuple-element.188) | copy-start | bytes 12292
  358.8 30.0 %copy-start.67 = (f32[1024]{0:T(1024)}, f32[1024]{0:T(1024)S(1)}, u32[]{:S(2)}) copy-start(f32[1024]{0:T(1024)S(1)} %get-tuple-element.183) | copy-start | bytes 12292
  359.9 8.3 copy-start.77
  359.9 24.4 %copy-start.75 = (f32[512]{0:T(512)}, f32[512]{0:T(512)S(1)}, u32[]{:S(2)}) copy-start(f32[512]{0:T(512)S(1)} %rsqrt.62) | copy-start | bytes 6148
  368.1 16.1 %copy-start = (bf16[512,3072]{1,0:T(8,128)(2,1)}, bf16[512,3072]{1,0:T(8,128)(2,1)S(1)}, u32[]{:S(2)}) copy-start(bf16[512,3072]{1,0:T(8,128)(2,1)S(1)} %add_convert_fusion.1.query_ref.key_ref.value_ref) | copy-start | bytes 9437188
  384.3 4.7 slice-start
  386.6 4.0 slice-start.1
  388.0 12.0 %copy-start.14 = (f32[512,1024]{1,0:T(8,128)}, f32[512,1024]{1,0:T(8,128)S(1)}, u32[]{:S(2)}) copy-start(f32[512,1024]{1,0:T(8,128)S(1)} %get-tuple-element.209) | copy-start | bytes 6291460
  388.4 11.6 %copy-start.79 = (f32[512]{0:T(512)}, f32[512]{0:T(512)S(1)}, u32[]{:S(2)}) copy-start(f32[512]{0:T(512)S(1)} %multiply_reduce_fusion.13) | copy-start | bytes 6148
  388.4 11.6 %copy-start.71 = (f32[512]{0:T(512)}, f32[512]{0:T(512)S(1)}, u32[]{:S(2)}) copy-start(f32[512]{0:T(512)S(1)} %fusion.46) | copy-start | bytes 6148
  388.4 11.6 %slice-start.2 = ((s8[8388608]{0:T(1024)(128)(4,1)}), s8[4194304]{0:T(1024)(128)(4,1)S(1)}, s32[]{:S(2)}) async-start(s8[8388608]{0:T(1024)(128)(4,1)} %bitcast.159), calls=%async_computation.2 | async-start | bytes 8388608
  390.6 9.4 slice-start.3
  400.0 4.7 copy-start.33
  404.7 23.5 %copy-start.25 = (f32[512,1024]{1,0:T(8,128)}, f32[512,1024]{1,0:T(8,128)S(1)}, u32[]{:S(2)}) copy-start(f32[512,1024]{1,0:T(8,128)S(1)} %get-tuple-element.213) | copy-start | bytes 6291460
  405.0 7.0 copy-start.81
  412.1 16.1 %copy-start.1 = (bf16[512,3072]{1,0:T(8,128)(2,1)}, bf16[512,3072]{1,0:T(8,128)(2,1)S(1)}, u32[]{:S(2)}) copy-start(bf16[512,3072]{1,0:T(8,128)(2,1)S(1)} %add_convert_fusion.query_ref.key_ref.value_ref) | copy-start | bytes 9437188
  412.1 16.1 %copy-start.12 = (bf16[32,32,1024]{2,1,0:T(8,128)(2,1)S(1)}, bf16[32,32,1024]{2,1,0:T(8,128)(2,1)}, u32[]{:S(2)}) copy-start(bf16[32,32,1024]{2,1,0:T(8,128)(2,1)} %copy-done.11) | copy-start | bytes 6291460
  428.2 3.1 slice-start.4
  428.2 4.6 slice-start.5
  428.2 11.7 %slice-start.8 = ((s8[8388608]{0:T(1024)(128)(4,1)}), s8[4194304]{0:T(1024)(128)(4,1)S(1)}, s32[]{:S(2)}) async-start(s8[8388608]{0:T(1024)(128)(4,1)} %bitcast.201), calls=%async_computation.8 | async-start | bytes 8388608
  429.6 10.3 copy-start.27
  432.8 7.1 slice-start.9
  473.7 6.9 copy-start.43
  509.9 9.2 copy-start.38
  550.1 17.1 %slice-start.6 = ((s8[8388608]{0:T(1024)(128)(4,1)}), s8[4194304]{0:T(1024)(128)(4,1)S(1)}, s32[]{:S(2)}) async-start(s8[8388608]{0:T(1024)(128)(4,1)} %bitcast.197), calls=%async_computation.6 | async-start | bytes 8388608
  551.1 16.1 %copy-start.28 = (f32[512,1024]{1,0:T(8,128)S(1)}, f32[512,1024]{1,0:T(8,128)}, u32[]{:S(2)}) copy-start(f32[512,1024]{1,0:T(8,128)} %copy-done.27) | copy-start | bytes 6291460
  551.1 16.1 %slice-start.7 = ((s8[8388608]{0:T(1024)(128)(4,1)}), s8[4194304]{0:T(1024)(128)(4,1)S(1)}, s32[]{:S(2)}) async-start(s8[8388608]{0:T(1024)(128)(4,1)} %bitcast.197), calls=%async_computation.7 | async-start | bytes 8388608
  598.0 46.6 %copy-start.18 = (f32[512,1024]{1,0:T(8,128)}, f32[512,1024]{1,0:T(8,128)S(1)}, u32[]{:S(2)}) copy-start(f32[512,1024]{1,0:T(8,128)S(1)} %get-tuple-element.142) | copy-start | bytes 6291460
  603.8 21.0 %copy-start.26 = (f32[512,1024]{1,0:T(8,128)S(1)}, f32[512,1024]{1,0:T(8,128)}, u32[]{:S(2)}) copy-start(f32[512,1024]{1,0:T(8,128)} %copy-done.25) | copy-start | bytes 6291460
  630.9 6.3 copy-start.39
  630.9 6.3 copy-start.44
  637.1 6.8 copy-start.82
  646.3 120.7 %copy-start.68 = (f32[1024]{0:T(1024)S(1)}, f32[1024]{0:T(1024)}, u32[]{:S(2)}) copy-start(f32[1024]{0:T(1024)} %copy-done.67) | copy-start | bytes 12292
  646.3 120.7 %copy-start.70 = (f32[512]{0:T(512)S(1)}, f32[512]{0:T(512)}, u32[]{:S(2)}) copy-start(f32[512]{0:T(512)} %copy-done.69) | copy-start | bytes 6148
  646.3 120.7 %copy-start.72 = (f32[512]{0:T(512)S(1)}, f32[512]{0:T(512)}, u32[]{:S(2)}) copy-start(f32[512]{0:T(512)} %copy-done.71) | copy-start | bytes 6148
  767.0 3.2 copy-start.80
  767.0 3.2 copy-start.15
  767.0 3.5 copy-start.30
  778.2 21.0 %copy-start.24 = (f32[512,1024]{1,0:T(8,128)S(1)}, f32[512,1024]{1,0:T(8,128)}, u32[]{:S(2)}) copy-start(f32[512,1024]{1,0:T(8,128)} %copy-done.23) | copy-start | bytes 6291460
  778.2 21.0 %copy-start.66 = (f32[1024]{0:T(1024)S(1)}, f32[1024]{0:T(1024)}, u32[]{:S(2)}) copy-start(f32[1024]{0:T(1024)} %copy-done.65) | copy-start | bytes 12292
  778.3 21.1 %copy-start.74 = (f32[512]{0:T(512)S(1)}, f32[512]{0:T(512)}, u32[]{:S(2)}) copy-start(f32[512]{0:T(512)} %copy-done.73) | copy-start | bytes 6148
  778.3 21.1 %copy-start.76 = (f32[512]{0:T(512)S(1)}, f32[512]{0:T(512)}, u32[]{:S(2)}) copy-start(f32[512]{0:T(512)} %copy-done.75) | copy-start | bytes 6148
  799.3 7.4 copy-start.2
  811.3 150.9 %copy-start.3 = (bf16[512,3072]{1,0:T(8,128)(2,1)S(1)}, bf16[512,3072]{1,0:T(8,128)(2,1)}, u32[]{:S(2)}) copy-start(bf16[512,3072]{1,0:T(8,128)(2,1)} %copy-done.2) | copy-start | bytes 9437188
  962.2 6.6 copy-start.83
  970.6 118.1 %collective-permute-start.1 = (f32[32,1024]{1,0:T(8,128)S(1)}, f32[32,1024]{1,0:T(8,128)S(1)}, u32[]{:S(2)}, u32[]{:S(2)}) collective-permute-start(f32[32,1024]{1,0:T(8,128)S(1)} %pad_dynamic-slice_fusion), channel_id=1, source_target_pairs={{0,8},{1,9},{2,10},{3,11},{4,12},{5,13},{6,14},{7,15},{8,0},{9,1},... | collective-permute-start | bytes 393224 | tf_op jit(solution)/shard_map/ppermute | solution.py:52
  972.9 115.8 %copy-start.29 = (f32[512,1024]{1,0:T(8,128)S(1)}, f32[512,1024]{1,0:T(8,128)}, u32[]{:S(2)}) copy-start(f32[512,1024]{1,0:T(8,128)} %get-tuple-element.82) | copy-start | bytes 6291460
  1084.1 21.2 %copy-start.85 = (f32[832]{0:T(1024)S(1)}, f32[832]{0:T(1024)}, u32[]{:S(2)}) copy-start(f32[832]{0:T(1024)} %param.35) | copy-start | bytes 9988
  1084.1 21.2 %copy-start.86 = (f32[832]{0:T(1024)S(1)}, f32[832]{0:T(1024)}, u32[]{:S(2)}) copy-start(f32[832]{0:T(1024)} %param.49) | copy-start | bytes 9988
  1084.1 21.2 %copy-start.87 = (f32[832]{0:T(1024)S(1)}, f32[832]{0:T(1024)}, u32[]{:S(2)}) copy-start(f32[832]{0:T(1024)} %param.42) | copy-start | bytes 9988
  1084.1 21.2 %copy-start.88 = (f32[8,128]{1,0:T(8,128)S(1)}, f32[8,128]{1,0:T(8,128)}, u32[]{:S(2)}) copy-start(f32[8,128]{1,0:T(8,128)} %get-tuple-element.91) | copy-start | bytes 12292
  1084.2 21.8 %copy-start.52 = (f32[32,1024]{1,0:T(8,128)S(1)}, f32[32,1024]{1,0:T(8,128)}, u32[]{:S(2)}) copy-start(f32[32,1024]{1,0:T(8,128)} %param.36) | copy-start | bytes 393220
  1084.2 21.8 %copy-start.63 = (f32[32,1024]{1,0:T(8,128)S(1)}, f32[32,1024]{1,0:T(8,128)}, u32[]{:S(2)}) copy-start(f32[32,1024]{1,0:T(8,128)} %param.50) | copy-start | bytes 393220
  1084.2 21.8 %copy-start.64 = (f32[32,1024]{1,0:T(8,128)S(1)}, f32[32,1024]{1,0:T(8,128)}, u32[]{:S(2)}) copy-start(f32[32,1024]{1,0:T(8,128)} %param.43) | copy-start | bytes 393220
  1106.8 17.8 %copy-start.40 = (f32[2,32,3072]{2,1,0:T(8,128)S(1)}, f32[2,32,3072]{2,1,0:T(8,128)}, u32[]{:S(2)}) copy-start(f32[2,32,3072]{2,1,0:T(8,128)} %param.31) | copy-start | bytes 2359300
  1106.8 17.9 %copy-start.49 = (f32[2,32,3072]{2,1,0:T(8,128)S(1)}, f32[2,32,3072]{2,1,0:T(8,128)}, u32[]{:S(2)}) copy-start(f32[2,32,3072]{2,1,0:T(8,128)} %param.45) | copy-start | bytes 2359300
  1106.8 17.9 %copy-start.50 = (f32[2,32,3072]{2,1,0:T(8,128)S(1)}, f32[2,32,3072]{2,1,0:T(8,128)}, u32[]{:S(2)}) copy-start(f32[2,32,3072]{2,1,0:T(8,128)} %param.38) | copy-start | bytes 2359300
  1106.8 17.9 %copy-start.57 = (f32[32,3072]{1,0:T(8,128)S(1)}, f32[32,3072]{1,0:T(8,128)}, u32[]{:S(2)}) copy-start(f32[32,3072]{1,0:T(8,128)} %get-tuple-element.84) | copy-start | bytes 1179652
  1106.8 17.9 %copy-start.58 = (f32[32,3072]{1,0:T(8,128)S(1)}, f32[32,3072]{1,0:T(8,128)}, u32[]{:S(2)}) copy-start(f32[32,3072]{1,0:T(8,128)} %get-tuple-element.83) | copy-start | bytes 1179652
  1128.4 3.1 copy-start.53
  1128.4 3.3 copy-start.55
  (38 other events, 76.4 us)

commit v5 on v4

--- a/solution.py
+++ b/solution.py
@@ -139,9 +139,21 @@
     def piece(at, turned, offset):
         return wholes[at].at[index(turned, offset)]
 
+    expected, due = [], []
+
     def on_core(at, source, turned, offset):
         if across:
-            send(at, source, turned, offset, "core", core_sem.at[at])
+            number = turned * size + offset % size
+            send(at, source, turned, offset, "core", core_sem.at[at, number])
+            expected.append((at, turned, offset))
+
+    def core_arrivals():
+        for at, turned, offset in due:
+            region = wholes[at].at[spot.index(turned, 1, offset % size)]
+            landed(region, core_sem.at[at, turned * size + offset % size])
+            ready(at, turned, offset, 1)
+        due[:] = expected
+        expected.clear()
 
     def on_ring(at, turned, source, offset, way, step, rows=None):
         toward = ("right", "left")[way]
@@ -171,9 +183,9 @@
             on_core(at, piece(at, 1, 0), 1, 0)
     for at in range(count):
         locals_[at].wait()
-        ready(at, 0, 0)
+        ready(at, 0, 0, 0)
         if not ring_first[at]:
-            ready(at, 1, 0)
+            ready(at, 1, 0, 0)
         tick()
 
     def turned_arrivals(at, step):
@@ -187,8 +199,9 @@
 
     def flush():
         for one in came:
-            ready(*one)
+            ready(*one, 0)
         came.clear()
+        core_arrivals()
         tick()
 
     for step in range(1, far + 1):
@@ -236,9 +249,9 @@
         if ring_first[at]:
             turned_arrivals(at, far)
             flush()
+    core_arrivals()
+    core_arrivals()
     for at in range(count):
-        if across:
-            landed(wholes[at].at[pl.ds(0, 2 * size)], core_sem.at[at])
         sent = 4 * size - 1 if across else 2 * size - 1
         landed(wholes[at].at[pl.ds(0, sent)], send_sem.at[at])
 
@@ -247,7 +260,7 @@
     return [
         pltpu.SemaphoreType.DMA((count, 2, 2, size // 2 + 1)),
         pltpu.SemaphoreType.DMA((count, size)),
-        pltpu.SemaphoreType.DMA((count,)),
+        pltpu.SemaphoreType.DMA((count, 2 * size)),
         pltpu.SemaphoreType.DMA((count,)),
         pltpu.SemaphoreType.DMA((count,)),
     ]
@@ -316,7 +329,7 @@
         state["done"] = last
 
     gather_steps(
-        size, ring_first, True, shards, wholes, sems, spot, tick, lambda at, turned, offset: None
+        size, ring_first, True, shards, wholes, sems, spot, tick, lambda at, turned, offset, other: None
     )
     tick(pieces)
     copy_out(pieces - 2).wait()
@@ -352,7 +365,7 @@
     )(*shards, table_own, ids)
 
 
-def spread_body(size, *refs):
+def spread_body(size, shared, *refs):
     near, rest, ids_near, ids_rest, start = refs[:5]
     table_out, place_out, squares_ref = refs[5:8]
     near_all, rest_all, total, core_in, table_sem, *sems = refs[8:]
@@ -360,17 +373,35 @@
     wholes = (near_all, rest_all)
     spot = Spot(size)
     spot.meet(True)
-    height = table_out.shape[0]
-    block = 2 * height // 8
-    first = pltpu.make_async_copy(start, total, table_sem.at[0])
+    height, length = table_out.shape[0], near.shape[0]
+    block = height // 4
+    first = pltpu.make_async_copy(start.at[pl.ds(0, height)], total, table_sem.at[0])
     first.start()
+    swap = pltpu.make_async_remote_copy(
+        src_ref=start.at[pl.ds(height, height)],
+        dst_ref=core_in,
+        send_sem=table_sem.at[1],
+        recv_sem=table_sem.at[2],
+        device_id=spot.to_core,
+        device_id_type=MESH,
+    )
+    swap.start()
     place_out[...] = jnp.zeros_like(place_out)
+    device = (2 * spot.half + spot.core) * size + spot.wide
+    own_place = pl.ds(pl.multiple_of(lax.rem(device * shared, length), 16), shared)
     waiting = []
-
-    def spread(pieces, blocks):
+    state = {"started": False}
+
+    def spread():
+        pieces = list(waiting)
+        waiting.clear()
+        if not state["started"]:
+            first.wait()
+            state["started"] = True
+
         def one(number, nothing):
             window = pl.ds(pl.multiple_of(number * block, 16), block)
-            row = number * block + lax.broadcasted_iota(jnp.int32, (block, near.shape[0]), 0)
+            row = number * block + lax.broadcasted_iota(jnp.int32, (block, length), 0)
             value = total[window, :]
             for at, piece in pieces:
                 hot = jnp.where(row == ids[at][piece], 1.0, 0.0).astype(jnp.bfloat16)
@@ -380,41 +411,20 @@
             total[window, :] = value
             return nothing
 
-        lax.fori_loop(blocks[0], blocks[1], one, 0)
-
-    def place(pieces):
+        lax.fori_loop(0, 4, one, 0)
         for at, piece in pieces:
-            rows = pl.ds(at * near.shape[0], near.shape[0])
-            place_out[rows, :] += wholes[at][piece].astype(jnp.float32)
-
-    def ready(at, turned, offset):
-        waiting.append((at, turned * size + offset % size))
+            place_out[at] += wholes[at][piece, own_place, :].astype(jnp.float32)
+
+    def ready(at, turned, offset, other):
+        waiting.append((at, spot.index(turned, other, offset % size)))
 
     def tick():
-        if tick.first:
-            first.wait()
-            tick.first = False
-        if len(waiting) >= 4:
-            spread(waiting, (0, 8))
-            place(waiting)
-            waiting.clear()
-
-    tick.first = True
-    gather_steps(size, (True, False), False, (near, rest), wholes, sems, spot, tick, ready)
+        if len(waiting) >= 6:
+            spread()
+
+    gather_steps(size, (True, False), True, (near, rest), wholes, sems, spot, tick, ready)
     if waiting:
-        spread(waiting, (4, 8))
-    swap = pltpu.make_async_remote_copy(
-        src_ref=total.at[pl.ds(height, height)],
-        dst_ref=core_in,
-        send_sem=table_sem.at[1],
-        recv_sem=table_sem.at[2],
-        device_id=spot.to_core,
-        device_id_type=MESH,
-    )
-    swap.start()
-    if waiting:
-        spread(waiting, (0, 4))
-        place(waiting)
+        spread()
     swap.wait_recv()
     step = height // 4
 
@@ -426,20 +436,20 @@
 
     squares = lax.fori_loop(0, 4, add, jnp.zeros((1, D), jnp.float32))
     squares_ref[...] = jnp.broadcast_to(squares, squares_ref.shape)
-    out = pltpu.make_async_copy(total.at[pl.ds(0, height)], table_out, table_sem.at[0])
+    out = pltpu.make_async_copy(total, table_out, table_sem.at[0])
     out.start()
     swap.wait_send()
     out.wait()
 
 
-def spread_call(size, near, rest, ids, start, number):
+def spread_call(size, near, rest, ids, start, shared, number):
     height = start.shape[0] // 2
-    pieces = (2 * size,) + near.shape
+    pieces = (4 * size,) + near.shape
     return pl.pallas_call(
-        functools.partial(spread_body, size),
+        functools.partial(spread_body, size, shared),
         out_shape=[
             jax.ShapeDtypeStruct((height, D), jnp.float32),
-            jax.ShapeDtypeStruct((LEN, D), jnp.float32),
+            jax.ShapeDtypeStruct((2, shared, D), jnp.float32),
             jax.ShapeDtypeStruct((8, D), jnp.float32),
         ],
         in_specs=[pl.BlockSpec(memory_space=pl.ANY)] * 2
@@ -453,7 +463,7 @@
         scratch_shapes=[
             pltpu.VMEM(pieces, near.dtype),
             pltpu.VMEM(pieces, near.dtype),
-            pltpu.VMEM((2 * height, D), jnp.float32),
+            pltpu.VMEM((height, D), jnp.float32),
             pltpu.VMEM((height, D), jnp.float32),
             pltpu.SemaphoreType.DMA((3,)),
         ]
@@ -477,7 +487,7 @@
         refs[2 * count :],
         spot,
         lambda: None,
-        lambda at, turned, offset: None,
+        lambda at, turned, offset, other: None,
     )
 
 
@@ -1275,13 +1285,14 @@
 
     numbers = jnp.concatenate([token_ids, loss_slots, target_ids, seq_lengths])
     numbers = jnp.pad(numbers, (0, -numbers.shape[0] % 1024)).reshape(-1, 128)
-    numbers = cast_call(size, numbers, False, 5).reshape(same_core, -1)
-    numbers = jnp.take(numbers, from_device, axis=0).reshape(halves, size, -1)
+    numbers = cast_call(size, numbers, True, 5).reshape(devices, -1)
+    all_tokens = numbers[:, :LEN]
+    token_total = jnp.sum(numbers[:, LEN + 2 * slots].astype(jnp.float32))
+    on_core = from_device + (from_device // size + net.core) * size
+    numbers = jnp.take(numbers, on_core, axis=0).reshape(halves, size, -1)
     group_tokens = numbers[:, :, :LEN]
     group_slots = numbers[:, :, LEN : LEN + slots].reshape(same_core * slots)
     group_targets = numbers[:, :, LEN + slots : LEN + 2 * slots].reshape(same_core * slots)
-    core_total = jnp.sum(numbers[:, :, LEN + 2 * slots].astype(jnp.float32))
-    token_total = core_total + net.swap_core(core_total[None])[0]
 
     own_rows = embed_table.shape[0]
     height = own_rows + -own_rows % 64
@@ -1467,9 +1478,17 @@
     grad_near, grad_rest = grad_low[:near], grad_low[near:]
     grad_table = jnp.dot(grad_logits.T, group_rows, preferred_element_type=jnp.float32)
     if fused:
-        ids = [part[:, None] for part in (ids_near, ids_rest)]
-        grad_table, grad_pos, sums = spread_call(size, grad_near, grad_rest, ids, grad_table, 4)
+        ids = all_tokens - own_start
+        ids = jnp.where((ids >= 0) & (ids < own_rows), ids, -1)[:, None]
+        ids = [ids[:, :, :near], ids[:, :, near:]]
+        grad_table, places, sums = spread_call(
+            size, grad_near, grad_rest, ids, grad_table, shared, 4
+        )
         squares = squares + jnp.sum(sums[0])
+        first_place = net.device * shared
+        pos_shard = jnp.where(
+            first_place < near, places[0], jnp.where(first_place < LEN, places[1], 0.0)
+        )
     else:
         wholes = gather_call(size, [grad_near, grad_rest], (True, False), False, 4)
         for ids, whole in zip((ids_near, ids_rest), wholes):
@@ -1481,12 +1500,12 @@
         grad_pos = jnp.concatenate(
             [jnp.sum(whole.astype(jnp.float32), axis=0) for whole in wholes]
         )
+        grad_pos = jnp.pad(grad_pos, ((0, POS - LEN), (0, 0)))
+        other_device = net.device + (1 - 2 * net.core) * size
+        pos_shard = lax.dynamic_slice_in_dim(grad_pos, net.device * shared, shared) + net.swap_core(
+            lax.dynamic_slice_in_dim(grad_pos, other_device * shared, shared)
+        )
     table_shard = grad_table[:own_rows]
-    grad_pos = jnp.pad(grad_pos, ((0, POS - LEN), (0, 0)))
-    other_device = net.device + (1 - 2 * net.core) * size
-    pos_shard = lax.dynamic_slice_in_dim(grad_pos, net.device * shared, shared) + net.swap_core(
-        lax.dynamic_slice_in_dim(grad_pos, other_device * shared, shared)
-    )
     grad_small = jnp.concatenate(vector_grads + [grad_gain_final, grad_shift_final])
     own_small = vectors.shape[0]
     grad_small = jnp.pad(grad_small.reshape(devices, own_small), ((0, 0), (0, -own_small % 1024)))

time: 1150 us -> 1130 us (0.983)
  transfers between devices with their start and end apart: 2 -> 0, of which waited for: 0 -> 0; matrix products, arithmetic and copies ran while one was open for 8% -> 0% of each run, Pallas kernels for 43% -> 0%
where the time goes in v5:
time: 1130 us; the launch traced here: 1110 us
  Pallas kernels  847 us (75%)
  matrix products  142 us (13%)
  other arithmetic  77.5 us (7%)
  local copies, waits for them, and re-layouts  37 us (3%)
  between operations  11.8 us (1%)
    pallas_call x4, Pallas kernels, scatter_call(): pl.pallas_call(functools.partial(scatter_body, size, half_first, across,...  388 us
    pallas_call x1, Pallas kernels, look_up_call(): pl.pallas_call(functools.partial(look_up_body, size, ring_first), out_sha...  196 us
    pallas_call x1, Pallas kernels, spread_call(): pl.pallas_call(functools.partial(spread_body, size, shared), out_shape=[j...  139 us
    pallas_call x2, Pallas kernels, attend_back(): pl.pallas_call(attend_back_body, grid=(pairs,), out_shape=jax.ShapeDtypeS...  42 us
    pallas_call x2, Pallas kernels, attend(): pl.pallas_call(attend_body, grid=(pairs,), out_shape=jax.ShapeDtypeStruct...  32.2 us
    pallas_call x3, Pallas kernels, cast_call(): pl.pallas_call(functools.partial(cast_body, size, everyone), out_shape=ja...  30.8 us
    sub x7, other arithmetic, adamw(): weight - step_rate * (update + decay_rate * weight)  23.4 us

profile of v5, /device:TPU:0, one launch (start us, length us, event | category | flops | bytes accessed | tf_op | source)
XLA Modules:
  0.0 1114.8 jit_solution(1569282134676225532)
XLA Ops:
  2.8 1.4 convert.32
  6.4 2.0 pad.27.refs_9_
  9.1 12.6 %shard_map.425 = s32[32,8,128]{2,1,0:T(8,128)} custom-call(s32[8,128]{1,0:T(8,128)} %pad_bitcast_fusion.2.own_ref), custom_call_target="tpu_custom_call" | custom-call | tf_op jit(solution)/shard_map/pallas_call | solution.py:548
  23.7 2.7 copy.52.refs_10_
  26.4 195.9 %shard_map.426 = (bf16[32,32,3072]{2,1,0:T(8,128)(2,1)}, bf16[32,32,4096]{2,1,0:T(8,128)(2,1)}, bf16[32,128,1024]{2,1,0:T(8,128)(2,1)}, bf16[32,32,1024]{2,1,0:T...) custom-call(bf16[32,3072]{1,0:T(8,128)(2,1)S(1)} %get-tuple-element., ...), custom_call_target="tpu_custom_call" | custom-call | tf_op jit(solution)/shard_map/pallas_call | solution.py:348
  222.3 1.3 copy-done.8
  223.7 1.3 copy-done.11
  226.3 128.6 %shard_map.427 = (bf16[256,1024]{1,0:T(8,128)(2,1)}, bf16[256,1024]{1,0:T(8,128)(2,1)}, f32[8,128]{1,0:T(8,128)}) custom-call(bf16[32,256,1024]{2,1,0:T(8,128)(2,1)} %get-tuple-element.58.refs_0_.refs_1_, bf16[32,256,1024]{2,1,0:T(8,128)(2,1)} %get-tuple-element.58.refs_0_.refs_1_), custom_call_target="tpu_custom_call" | custom-call | tf_op jit(solution)/shard_map/pallas_call | solution.py:844
  354.9 1.4 maximum_convert_fusion
  356.4 1.5 fusion.25
  358.0 1.7 multiply_reduce_fusion.14
  359.8 1.6 slice_convert_fusion
  361.4 1.5 fusion.20
  363.0 2.5 add_convert_fusion.7
  365.5 3.7 add_convert_fusion.1.query_ref.key_ref.value_ref
  369.2 16.1 %shard_map.428 = bf16[512,1024]{1,0:T(8,128)(2,1)S(1)} custom-call(s32[1]{0:T(128)S(6)} %copy.100.length_ref, bf16[512,3072]{1,0:T(8,128)(2,1)S(1)} %add_convert_fusion.1.query_ref.key_ref.value_ref, bf16[512,3072]{1,0:T(8,128)(2,1)S(1)} %add_convert_fusion.1.query_ref.key_ref.value_ref, bf16[512,3072]{1,0:T(8,128)(2,1)S(1)} %add_convert_fusion.1.query_ref.key_ref.value_ref), custom_call_target="tpu_custom_call" | custom-call | flops 1073741824 | bytes 4194304 | tf_op jit(solution)/shard_map/pallas_call | solution.py:912
  385.4 1.4 fusion.89
  388.4 1.5 slice-done.3
  389.9 9.3 fusion.14
  399.3 4.6 fusion.90
  404.3 4.0 add_convert_fusion.query_ref.key_ref.value_ref
  408.4 16.1 %shard_map.429 = bf16[512,1024]{1,0:T(8,128)(2,1)S(1)} custom-call(s32[1]{0:T(128)S(6)} %copy.100.length_ref, bf16[512,3072]{1,0:T(8,128)(2,1)S(1)} %add_convert_fusion.query_ref.key_ref.value_ref, bf16[512,3072]{1,0:T(8,128)(2,1)S(1)} %add_convert_fusion.query_ref.key_ref.value_ref, bf16[512,3072]{1,0:T(8,128)(2,1)S(1)} %add_convert_fusion.query_ref.key_ref.value_ref), custom_call_target="tpu_custom_call" | custom-call | flops 1073741824 | bytes 4194304 | tf_op jit(solution)/shard_map/pallas_call | solution.py:912
  424.6 1.4 fusion.91
  426.3 1.4 slice-done.7
  427.7 7.4 fusion.65
  435.1 8.2 fusion.92
  445.9 19.7 %shard_map.430 = (bf16[16,16,1024]{2,1,0:T(8,128)(2,1)}, bf16[16,16,1024]{2,1,0:T(8,128)(2,1)}) custom-call(bf16[16,1024]{1,0:T(8,128)(2,1)} %get-tuple-element.196.refs_0_, bf16[16,1024]{1,0:T(8,128)(2,1)} %get-tuple-element.195.refs_1_), custom_call_target="tpu_custom_call" | custom-call | tf_op jit(solution)/shard_map/pallas_call | solution.py:497
  465.6 1.3 pad_maximum_fusion
  466.9 9.1 fusion.93
  476.3 3.8 exponential_reduce_fusion
  482.6 9.1 shard_map.431
  496.0 4.4 multiply_convert_fusion.1
  500.5 9.2 fusion.94
  509.7 25.9 %shard_map.432 = (f32[16,1024]{1,0:T(8,128)}, f32[16,1024]{1,0:T(8,128)}, f32[8,128]{1,0:T(8,128)}) custom-call(f32[32,16,1024]{2,1,0:T(8,128)} %bitcast.171, f32[32,16,1024]{2,1,0:T(8,128)} %bitcast.172), custom_call_target="tpu_custom_call" | custom-call | tf_op jit(solution)/shard_map/pallas_call | solution.py:844
  535.6 2.6 scatter_custom_fusion
  538.2 3.1 multiply_reduce_fusion
  542.7 13.2 %convert_reduce_fusion = (f32[4096]{0:T(1024)S(1)}, bf16[512,4096]{1,0:T(8,128)(2,1)S(1)}) fusion(f32[512,4096]{1,0:T(8,128)} %fusion.65, f32[4096]{0:T(1024)S(1)} %get-tuple-element.189, bf16[512,1024]{1,0:T(8,128)(2,1)S(1)} %get-tuple-element.140, bf16[4096,1024]{1,0:T(8,128)(2,1)} %bitcast.205), kind=kOutput, calls=%fused_computation.25 | convolution fusion | flops 4343197696 | bytes 22052864 | tf_op jit(solution)/shard_map/dot_general | solution.py:1175
  555.9 7.4 multiply_reduce_fusion.1
  565.8 21.0 %shard_map.433 = bf16[512,3072]{1,0:T(8,128)(2,1)S(1)} custom-call(s32[1]{0:T(128)S(6)} %copy.100.length_ref, bf16[512,3072]{1,0:T(8,128)(2,1)} %copy-done.1, bf16[512,3072]{1,0:T(8,128)(2,1)} %copy-done.1, bf16[512,3072]{1,0:T(8,128)(2,1)} %copy-done.1, bf16[512,1024]{1,0:T(8,128)(2,1)S(1)} %convolution_convert_fusion.1.grad_ref), custom_call_target="tpu_custom_call" | custom-call | flops 2684354560 | bytes 8388608 | tf_op jit(solution)/shard_map/pallas_call | solution.py:969
  586.8 6.0 fusion.63
  592.8 7.1 fusion.64
  599.9 13.1 %fusion.67 = bf16[4096,1024]{1,0:T(8,128)(2,1)} fusion(bf16[512,1024]{1,0:T(8,128)(2,1)S(1)} %get-tuple-element.140, f32[512,4096]{1,0:T(8,128)} %fusion.65, f32[4096]{0:T(1024)S(1)} %get-tuple-element.189), kind=kOutput, calls=%fused_computation.297 | convolution fusion | flops 4315938816 | bytes 17842176 | tf_op jit(solution)/shard_map/dot_general | solution.py:1174
  613.0 2.7 fusion.59
  615.7 6.2 multiply_reduce_fusion.2
  625.4 1.4 fusion.66
  626.8 2.3 copy.56.refs_5_
  629.0 120.6 %shard_map.434 = (f32[32,3072]{1,0:T(8,128)}, f32[32,4096]{1,0:T(8,128)}, f32[128,1024]{1,0:T(8,128)}, f32[32,1024]{1,0:T(8,128)}, f32[8,128]{1,0:T(8,128)}, /*i...) custom-call(bf16[32,32,3072]{2,1,0:T(8,128)(2,1)} %bitcast.173, ...), custom_call_target="tpu_custom_call" | custom-call | tf_op jit(solution)/shard_map/pallas_call | solution.py:844
  750.9 3.1 multiply_reduce_fusion.3
  757.1 1.5 copy-done.10
  759.9 21.0 %shard_map.435 = bf16[512,3072]{1,0:T(8,128)(2,1)S(1)} custom-call(s32[1]{0:T(128)S(6)} %copy.100.length_ref, bf16[512,3072]{1,0:T(8,128)(2,1)} %copy-done, bf16[512,3072]{1,0:T(8,128)(2,1)} %copy-done, bf16[512,3072]{1,0:T(8,128)(2,1)} %copy-done, bf16[512,1024]{1,0:T(8,128)(2,1)S(1)} %convolution_convert_fusion.grad_ref), custom_call_target="tpu_custom_call" | custom-call | flops 2684354560 | bytes 8388608 | tf_op jit(solution)/shard_map/pallas_call | solution.py:969
  781.0 7.2 multiply_reduce_fusion.4
  791.6 6.8 fusion.95.refs_4_
  798.4 138.9 %shard_map.436 = (f32[1600,1024]{1,0:T(8,128)}, f32[2,32,1024]{2,1,0:T(8,128)}, f32[8,1024]{1,0:T(8,128)}) custom-call(bf16[256,1024]{1,0:T(8,128)(2,1)} %get-tuple-element.160.refs_0_, bf16[256,1024]{1,0:T(8,128)(2,1)} %get-tuple-element.159.refs_1_, s32[32,1,256]{2,1,0:T(1,128)} %get-tuple-element.192.refs_2_, s32[32,1,256]{2,1,0:T(1,128)} %get-tuple-element.191.refs_3_, ...), custom_call_target="tpu_custom_call" | custom-call | tf_op jit(solution)/shard_map/pallas_call | solution.py:448
  937.3 1.4 slice_reduce_fusion.3
  940.0 2.3 copy.57
  942.3 8.5 fusion.16.refs_0_
  950.8 2.6 fusion.56
  955.7 112.5 %shard_map.437 = (f32[32,3072]{1,0:T(8,128)}, f32[32,4096]{1,0:T(8,128)}, f32[128,1024]{1,0:T(8,128)}, f32[32,1024]{1,0:T(8,128)}, f32[8,128]{1,0:T(8,128)}, /*index=5*/f32[8,128]{1,0:T(8,128)}) custom-call(bf16[32,32,3072]{2,1,0:T(8,128)(2,1)} %fusion.16.refs_0_, bf16[32,32,4096]{2,1,0:T(8,128)(2,1)} %bitcast.167, bf16[32,128,1024]{2,1,0:T(8,128)(2,1)} %bitcast.168, ...), custom_call_target="tpu_custom_call" | custom-call | tf_op jit(solution)/shard_map/pallas_call | solution.py:844
  1072.7 1.3 fusion.44.own_ref
  1074.0 9.2 shard_map.438
  1087.6 3.0 multiply_subtract_fusion.3
  1092.1 2.3 multiply_subtract_fusion.2
  1095.2 2.3 multiply_subtract_fusion.1
  1098.9 13.5 %multiply_subtract_fusion = (f32[1572,1024]{1,0:T(8,128)}, f32[1572,1024]{1,0:T(8,128)}, f32[1572,1024]{1,0:T(8,128)}) fusion(f32[1572,1024]{1,0:T(8,128)S(1)} %bitcast.156, f32[]{:T(128)S(6)} %sub.273, f32[]{:T(128)S(6)} %div.295, f32[1600,1024]{1,0:T(8,128)} %get-tuple-element.92, f32[1572,1024]{1,0:T(8,128)} %param.51, f32[1572,1024]{1,0:T(8,128)} %param.44), kind=kLoop, calls=%fused_computation.32 | loop fusion | flops 24145920 | bytes 45072392 | tf_op jit(solution)/shard_map/sub | solution.py:1236
  (376 shorter events, 45.5 us)
Async XLA Ops:
  2.6 3.2 copy-start.18
  226.3 136.7 %copy-start.66 = (f32[1024]{0:T(1024)}, f32[1024]{0:T(1024)S(1)}, u32[]{:S(2)}) copy-start(f32[1024]{0:T(1024)S(1)} %get-tuple-element.188) | copy-start | bytes 12292
  226.3 160.9 %copy-start.68 = (f32[1024]{0:T(1024)}, f32[1024]{0:T(1024)S(1)}, u32[]{:S(2)}) copy-start(f32[1024]{0:T(1024)S(1)} %get-tuple-element.183) | copy-start | bytes 12292
  226.3 160.9 %copy-start.82 = (f32[1024]{0:T(1024)}, f32[1024]{0:T(1024)S(1)}, u32[]{:S(2)}) copy-start(f32[1024]{0:T(1024)S(1)} %get-tuple-element.182) | copy-start | bytes 12292
  358.0 3.4 copy-start.74
  359.8 3.2 copy-start.78
  359.8 3.2 copy-start.76
  359.8 5.7 slice-start.10
  361.4 4.1 slice-start.11
  363.0 22.4 %copy-start.26 = (f32[512,1024]{1,0:T(8,128)}, f32[512,1024]{1,0:T(8,128)S(1)}, u32[]{:S(2)}) copy-start(f32[512,1024]{1,0:T(8,128)S(1)} %get-tuple-element.148) | copy-start | bytes 6291460
  369.2 16.1 %copy-start = (bf16[512,3072]{1,0:T(8,128)(2,1)}, bf16[512,3072]{1,0:T(8,128)(2,1)S(1)}, u32[]{:S(2)}) copy-start(bf16[512,3072]{1,0:T(8,128)(2,1)S(1)} %add_convert_fusion.1.query_ref.key_ref.value_ref) | copy-start | bytes 9437188
  369.2 16.1 %copy-start.9 = (bf16[32,32,1024]{2,1,0:T(8,128)(2,1)S(1)}, bf16[32,32,1024]{2,1,0:T(8,128)(2,1)}, u32[]{:S(2)}) copy-start(bf16[32,32,1024]{2,1,0:T(8,128)(2,1)} %copy-done.8) | copy-start | bytes 6291460
  385.4 4.6 slice-start.3
  386.8 12.5 %copy-start.13 = (f32[512,1024]{1,0:T(8,128)}, f32[512,1024]{1,0:T(8,128)S(1)}, u32[]{:S(2)}) copy-start(f32[512,1024]{1,0:T(8,128)S(1)} %get-tuple-element.212) | copy-start | bytes 6291460
  386.8 12.4 %copy-start.70 = (f32[512]{0:T(512)}, f32[512]{0:T(512)S(1)}, u32[]{:S(2)}) copy-start(f32[512]{0:T(512)S(1)} %broadcast_multiply_fusion.4) | copy-start | bytes 6148
  386.8 12.4 %slice-start.4 = ((s8[8388608]{0:T(1024)(128)(4,1)}), s8[4194304]{0:T(1024)(128)(4,1)S(1)}, s32[]{:S(2)}) async-start(s8[8388608]{0:T(1024)(128)(4,1)} %bitcast.164), calls=%async_computation.4 | async-start | bytes 8388608
  387.2 12.0 %copy-start.80 = (f32[512]{0:T(512)}, f32[512]{0:T(512)S(1)}, u32[]{:S(2)}) copy-start(f32[512]{0:T(512)S(1)} %multiply_reduce_fusion.13) | copy-start | bytes 6148
  389.9 9.3 copy-start.72
  389.9 9.3 slice-start.5
  399.2 4.7 copy-start.35
  399.2 5.1 slice-start.12
  399.3 5.0 slice-start.13
  403.9 20.6 %copy-start.28 = (f32[512,1024]{1,0:T(8,128)}, f32[512,1024]{1,0:T(8,128)S(1)}, u32[]{:S(2)}) copy-start(f32[512,1024]{1,0:T(8,128)S(1)} %get-tuple-element.216) | copy-start | bytes 6291460
  408.4 16.1 %copy-start.1 = (bf16[512,3072]{1,0:T(8,128)(2,1)}, bf16[512,3072]{1,0:T(8,128)(2,1)S(1)}, u32[]{:S(2)}) copy-start(bf16[512,3072]{1,0:T(8,128)(2,1)S(1)} %add_convert_fusion.query_ref.key_ref.value_ref) | copy-start | bytes 9437188
  408.4 16.1 %copy-start.12 = (bf16[32,32,1024]{2,1,0:T(8,128)(2,1)S(1)}, bf16[32,32,1024]{2,1,0:T(8,128)(2,1)}, u32[]{:S(2)}) copy-start(bf16[32,32,1024]{2,1,0:T(8,128)(2,1)} %copy-done.11) | copy-start | bytes 6291460
  408.4 17.9 %slice-start.6 = ((s8[8388608]{0:T(1024)(128)(4,1)}), s8[4194304]{0:T(1024)(128)(4,1)S(1)}, s32[]{:S(2)}) async-start(s8[8388608]{0:T(1024)(128)(4,1)} %bitcast.202), calls=%async_computation.6 | async-start | bytes 8388608
  424.5 3.2 slice-start.7
  424.5 10.5 slice-start.8
  425.9 9.1 copy-start.30
  427.7 7.4 slice-start.9
  466.9 9.1 copy-start.44
  500.5 9.2 copy-start.39
  538.2 3.1 copy-start.17
  538.2 3.5 copy-start.23
  542.7 13.2 %copy-start.31 = (f32[512,1024]{1,0:T(8,128)S(1)}, f32[512,1024]{1,0:T(8,128)}, u32[]{:S(2)}) copy-start(f32[512,1024]{1,0:T(8,128)} %copy-done.30) | copy-start | bytes 6291460
  564.5 58.2 %copy-start.19 = (f32[512,1024]{1,0:T(8,128)}, f32[512,1024]{1,0:T(8,128)S(1)}, u32[]{:S(2)}) copy-start(f32[512,1024]{1,0:T(8,128)S(1)} %get-tuple-element.142) | copy-start | bytes 6291460
  565.8 21.0 %copy-start.29 = (f32[512,1024]{1,0:T(8,128)S(1)}, f32[512,1024]{1,0:T(8,128)}, u32[]{:S(2)}) copy-start(f32[512,1024]{1,0:T(8,128)} %copy-done.28) | copy-start | bytes 6291460
  599.9 13.1 %copy-start.7 = (bf16[512,1024]{1,0:T(8,128)(2,1)S(1)}, bf16[512,1024]{1,0:T(8,128)(2,1)}, u32[]{:S(2)}) copy-start(bf16[512,1024]{1,0:T(8,128)(2,1)} %copy-done.6) | copy-start | bytes 3145732
  750.9 3.1 copy-start.81
  750.9 3.2 copy-start.15
  750.9 3.5 copy-start.32
  757.1 31.9 %copy-start.24 = (f32[512,1024]{1,0:T(8,128)}, f32[512,1024]{1,0:T(8,128)S(1)}, u32[]{:S(2)}) copy-start(f32[512,1024]{1,0:T(8,128)S(1)} %get-tuple-element.146) | copy-start | bytes 6291460
  759.9 21.1 %copy-start.27 = (f32[512,1024]{1,0:T(8,128)S(1)}, f32[512,1024]{1,0:T(8,128)}, u32[]{:S(2)}) copy-start(f32[512,1024]{1,0:T(8,128)} %copy-done.26) | copy-start | bytes 6291460
  759.9 21.1 %copy-start.67 = (f32[1024]{0:T(1024)S(1)}, f32[1024]{0:T(1024)}, u32[]{:S(2)}) copy-start(f32[1024]{0:T(1024)} %copy-done.66) | copy-start | bytes 12292
  759.9 21.1 %copy-start.75 = (f32[512]{0:T(512)S(1)}, f32[512]{0:T(512)}, u32[]{:S(2)}) copy-start(f32[512]{0:T(512)} %copy-done.74) | copy-start | bytes 6148
  759.9 21.1 %copy-start.77 = (f32[512]{0:T(512)S(1)}, f32[512]{0:T(512)}, u32[]{:S(2)}) copy-start(f32[512]{0:T(512)} %copy-done.76) | copy-start | bytes 6148
  781.0 7.2 copy-start.2
  781.0 7.2 copy-start.79
  942.3 8.5 copy-start.5
  942.3 8.5 copy-start.25
  955.7 114.4 %copy-start.61 = (f32[2,32,1024]{2,1,0:T(8,128)S(1)}, f32[2,32,1024]{2,1,0:T(8,128)}, u32[]{:S(2)}) copy-start(f32[2,32,1024]{2,1,0:T(8,128)} %get-tuple-element.82) | copy-start | bytes 786436
  955.7 131.8 %copy-start.41 = (f32[2,32,3072]{2,1,0:T(8,128)S(1)}, f32[2,32,3072]{2,1,0:T(8,128)}, u32[]{:S(2)}) copy-start(f32[2,32,3072]{2,1,0:T(8,128)} %param.31) | copy-start | bytes 2359300
  955.7 131.8 %copy-start.50 = (f32[2,32,3072]{2,1,0:T(8,128)S(1)}, f32[2,32,3072]{2,1,0:T(8,128)}, u32[]{:S(2)}) copy-start(f32[2,32,3072]{2,1,0:T(8,128)} %param.45) | copy-start | bytes 2359300
  955.7 131.8 %copy-start.51 = (f32[2,32,3072]{2,1,0:T(8,128)S(1)}, f32[2,32,3072]{2,1,0:T(8,128)}, u32[]{:S(2)}) copy-start(f32[2,32,3072]{2,1,0:T(8,128)} %param.38) | copy-start | bytes 2359300
  955.7 131.8 %copy-start.58 = (f32[32,3072]{1,0:T(8,128)S(1)}, f32[32,3072]{1,0:T(8,128)}, u32[]{:S(2)}) copy-start(f32[32,3072]{1,0:T(8,128)} %get-tuple-element.84) | copy-start | bytes 1179652
  1087.5 3.1 copy-start.43
  1087.6 4.1 copy-start.46
  1087.6 4.1 copy-start.47
  1087.6 4.1 copy-start.55
  1087.6 4.1 copy-start.57
  1087.6 6.8 copy-start.56
  1090.6 3.8 copy-start.54
  1092.1 6.8 slice-start
  1095.2 3.8 slice-start.1
  (42 other events, 96.1 us)

commit v6 on v5

--- a/solution.py
+++ b/solution.py
@@ -419,7 +419,7 @@
         waiting.append((at, spot.index(turned, other, offset % size)))
 
     def tick():
-        if len(waiting) >= 6:
+        if len(waiting) >= 4:
             spread()
 
     gather_steps(size, (True, False), True, (near, rest), wholes, sems, spot, tick, ready)
@@ -867,6 +867,7 @@
 
 INNER = (((1,), (1,)), ((), ()))
 OUTER = (((0,), (0,)), ((), ()))
+GROUP = 8
 
 
 def dot_inner(one, two):
@@ -894,32 +895,30 @@
     def _():
         fill_mask(mask_ref, length_ref[0])
 
-    rows = query_ref.shape[0]
-    block = rows // 2
-    for at in range(2):
-        here, seen = slice(at * block, (at + 1) * block), slice(0, (at + 1) * block)
-        mixed = []
-        for head in range(2):
-            lanes = slice(head * HD, (head + 1) * HD)
-            probs = probs_by_key(query_ref[here, lanes], key_ref[seen, lanes], mask_ref[seen, here])
-            mixed.append(dot_outer(value_ref[seen, lanes], probs.astype(jnp.bfloat16)))
-        mixed_ref[here, :] = jnp.concatenate(mixed).T.astype(jnp.bfloat16)
+    mixed = []
+    for head in range(GROUP):
+        lanes = slice(head * HD, (head + 1) * HD)
+        probs = probs_by_key(query_ref[:, lanes], key_ref[:, lanes], mask_ref[...])
+        mixed.append(dot_outer(value_ref[:, lanes], probs.astype(jnp.bfloat16)))
+    mixed_ref[...] = jnp.concatenate(mixed).T.astype(jnp.bfloat16)
+
+
+def attend_specs(rows, steps):
+    return [pl.BlockSpec(memory_space=pltpu.SMEM)] + [
+        pl.BlockSpec((rows, GROUP * HD), lambda p, part=part: (0, part * steps + p))
+        for part in range(3)
+    ]
 
 
 def attend(projected, seq_lengths):
     rows = projected.shape[0]
-    pairs = HEADS // 2
+    steps = HEADS // GROUP
     return pl.pallas_call(
         attend_body,
-        grid=(pairs,),
+        grid=(steps,),
         out_shape=jax.ShapeDtypeStruct((rows, D), jnp.bfloat16),
-        in_specs=[
-            pl.BlockSpec(memory_space=pltpu.SMEM),
-            pl.BlockSpec((rows, 2 * HD), lambda p: (0, p)),
-            pl.BlockSpec((rows, 2 * HD), lambda p: (0, pairs + p)),
-            pl.BlockSpec((rows, 2 * HD), lambda p: (0, 2 * pairs + p)),
-        ],
-        out_specs=pl.BlockSpec((rows, 2 * HD), lambda p: (0, p)),
+        in_specs=attend_specs(rows, steps),
+        out_specs=pl.BlockSpec((rows, GROUP * HD), lambda p: (0, p)),
         scratch_shapes=[pltpu.VMEM((rows, rows), jnp.float32)],
         compiler_params=pltpu.CompilerParams(vmem_limit_bytes=32 * 1024 * 1024),
         cost_estimate=pl.CostEstimate(
@@ -933,50 +932,38 @@
     def _():
         fill_mask(mask_ref, length_ref[0])
 
-    rows = query_ref.shape[0]
-    block = rows // 2
-    pair = pl.program_id(0)
+    step = pl.program_id(0)
     low = jnp.bfloat16
     grad_query, grad_key, grad_value = [], [], []
-    for at in range(2):
-        here, seen = slice(at * block, (at + 1) * block), slice(0, (at + 1) * block)
-        heads = []
-        for head in range(2):
-            lanes = slice(head * HD, (head + 1) * HD)
-            query, key = query_ref[here, lanes], key_ref[seen, lanes]
-            grad = grad_ref[here, lanes]
-            probs = probs_by_key(query, key, mask_ref[seen, here])
-            grad_probs = dot_inner(value_ref[seen, lanes], grad)
-            value_part = jnp.dot(probs.astype(low), grad, preferred_element_type=jnp.float32)
-            key_dot = jnp.sum(grad_probs * probs, axis=0, keepdims=True)
-            scores_low = (probs * (grad_probs - key_dot)).astype(low)
-            key_part = jnp.dot(scores_low, query, preferred_element_type=jnp.float32) * 0.125
-            heads.append((dot_outer(key, scores_low) * 0.125, key_part, value_part))
-        grad_query.append(jnp.concatenate([part[0] for part in heads]).T)
-        grad_key.append(jnp.concatenate([part[1] for part in heads], axis=1))
-        grad_value.append(jnp.concatenate([part[2] for part in heads], axis=1))
-    for part, parts in enumerate((grad_query, grad_key, grad_value)):
-        window = pl.ds(pl.multiple_of(part * D + pair * 2 * HD, 2 * HD), 2 * HD)
-        first = parts[0] if part == 0 else parts[0] + parts[1][:block]
-        out_ref[:block, window] = first.astype(low)
-        second = parts[1] if part == 0 else parts[1][block:]
-        out_ref[block:, window] = second.astype(low)
+    for head in range(GROUP):
+        lanes = slice(head * HD, (head + 1) * HD)
+        query, key, grad = query_ref[:, lanes], key_ref[:, lanes], grad_ref[:, lanes]
+        probs = probs_by_key(query, key, mask_ref[...])
+        grad_probs = dot_inner(value_ref[:, lanes], grad)
+        grad_value.append(jnp.dot(probs.astype(low), grad, preferred_element_type=jnp.float32))
+        key_dot = jnp.sum(grad_probs * probs, axis=0, keepdims=True)
+        scores_low = (probs * (grad_probs - key_dot)).astype(low)
+        grad_key.append(jnp.dot(scores_low, query, preferred_element_type=jnp.float32) * 0.125)
+        grad_query.append(dot_outer(key, scores_low) * 0.125)
+    results = (
+        jnp.concatenate(grad_query).T,
+        jnp.concatenate(grad_key, axis=1),
+        jnp.concatenate(grad_value, axis=1),
+    )
+    for part, value in enumerate(results):
+        window = pl.ds(pl.multiple_of(part * D + step * GROUP * HD, GROUP * HD), GROUP * HD)
+        out_ref[:, window] = value.astype(low)
 
 
 def attend_back(projected, grad_mixed, seq_lengths):
     rows = projected.shape[0]
-    pairs = HEADS // 2
+    steps = HEADS // GROUP
     return pl.pallas_call(
         attend_back_body,
-        grid=(pairs,),
+        grid=(steps,),
         out_shape=jax.ShapeDtypeStruct((rows, 3 * D), jnp.bfloat16),
-        in_specs=[
-            pl.BlockSpec(memory_space=pltpu.SMEM),
-            pl.BlockSpec((rows, 2 * HD), lambda p: (0, p)),
-            pl.BlockSpec((rows, 2 * HD), lambda p: (0, pairs + p)),
-            pl.BlockSpec((rows, 2 * HD), lambda p: (0, 2 * pairs + p)),
-            pl.BlockSpec((rows, 2 * HD), lambda p: (0, p)),
-        ],
+        in_specs=attend_specs(rows, steps)
+        + [pl.BlockSpec((rows, GROUP * HD), lambda p: (0, p))],
         out_specs=pl.BlockSpec((rows, 3 * D), lambda p: (0, 0)),
         scratch_shapes=[pltpu.VMEM((rows, rows), jnp.float32)],
         compiler_params=pltpu.CompilerParams(vmem_limit_bytes=48 * 1024 * 1024),
@@ -1432,7 +1419,7 @@
     grad_stream, grad_gain_final, grad_shift_final = final_pull(grad_final)
     layer_shards = []
     vector_grads = []
-    squares = jnp.float32(0)
+    squares = jnp.zeros((128,), jnp.float32)
     pending = None
 
     def reduce_layers(full_grads, number, more=(), work=None):
@@ -1459,7 +1446,7 @@
 
             def feed(operands):
                 sums, *results = reduce_layers(pending, 3, work=operands)
-                held.append(jnp.sum(sums[0]))
+                held.append(sums[0])
                 return results
 
         grad_stream, full_grads, grad_vector = layer_backward(
@@ -1484,7 +1471,7 @@
         grad_table, places, sums = spread_call(
             size, grad_near, grad_rest, ids, grad_table, shared, 4
         )
-        squares = squares + jnp.sum(sums[0])
+        squares = squares + jnp.sum(sums[0].reshape(-1, 128), axis=0)
         first_place = net.device * shared
         pos_shard = jnp.where(
             first_place < near, places[0], jnp.where(first_place < LEN, places[1], 0.0)
@@ -1496,7 +1483,7 @@
                 one_hot(ids.reshape(-1)).T, whole.reshape(-1, D), preferred_element_type=jnp.float32
             )
         grad_table = grad_table[:height] + net.swap_core(grad_table[height:])
-        squares = squares + jnp.sum(grad_table * grad_table)
+        squares = squares + jnp.sum(grad_table * grad_table, axis=0).reshape(-1, 128).sum(axis=0)
         grad_pos = jnp.concatenate(
             [jnp.sum(whole.astype(jnp.float32), axis=0) for whole in wholes]
         )
@@ -1511,15 +1498,16 @@
     grad_small = jnp.pad(grad_small.reshape(devices, own_small), ((0, 0), (0, -own_small % 1024)))
     small_shard, sums = reduce_layers(pending, 10, [grad_small.reshape(devices, -1, 128)])
     small_shard = small_shard.reshape(-1)[:own_small]
-    squares = squares + jnp.sum(sums[0]) + jnp.sum(pos_shard * pos_shard)
+    pos_squares = jnp.sum(pos_shard * pos_shard, axis=0).reshape(-1, 128)
+    squares = squares + sums[0] + jnp.sum(pos_squares, axis=0)
     qkv_shard = jnp.stack([member[0] for member in layer_shards])
     out_shard = jnp.stack([member[1] for member in layer_shards])
     fc_shard = jnp.stack([member[2] for member in layer_shards])
     proj_shard = jnp.stack([member[3] for member in layer_shards])
     shards = (qkv_shard, out_shard, fc_shard, proj_shard, small_shard, pos_shard, table_shard)
-    sums = jnp.pad(jnp.stack([own_loss, squares]), (0, 1022)).reshape(8, 128)
-    sums = jnp.sum(cast_call(size, sums, True, 9), axis=0)
-    loss_total, square_total = sums[0, 0], sums[0, 1]
+    sums = jnp.stack([squares, jnp.pad(own_loss[None], (0, 127))])
+    sums = cast_call(size, jnp.pad(sums, ((0, 6), (0, 0))), True, 9)
+    square_total, loss_total = jnp.sum(sums[:, 0]), jnp.sum(sums[:, 1])
     loss_value = loss_total / token_total
     grad_norm = jnp.sqrt(square_total)
     factor = CLIP_LIMIT / jnp.maximum(grad_norm, CLIP_LIMIT)

time: 1130 us -> 1110 us (0.982)
  Pallas kernels: 847 us -> 829 us
    pallas_call x4, Pallas kernels: 74.2 us -> 56.4 us  [the longest x2 36.2 us: attend_back(): pl.pallas_call(attend_back_body, grid=(steps,), out_shape=jax.ShapeDtypeS...]
where the time goes in v6:
time: 1110 us; the launch traced here: 1100 us
  Pallas kernels  829 us (75%)
  matrix products  143 us (13%)
  other arithmetic  72 us (6%)
  local copies, waits for them, and re-layouts  41.4 us (4%)
    pallas_call x4, Pallas kernels, scatter_call(): pl.pallas_call(functools.partial(scatter_body, size, half_first, across,...  387 us
    pallas_call x1, Pallas kernels, look_up_call(): pl.pallas_call(functools.partial(look_up_body, size, ring_first), out_sha...  196 us
    pallas_call x1, Pallas kernels, spread_call(): pl.pallas_call(functools.partial(spread_body, size, shared), out_shape=[j...  139 us
    pallas_call x2, Pallas kernels, attend_back(): pl.pallas_call(attend_back_body, grid=(steps,), out_shape=jax.ShapeDtypeS...  36.2 us
    pallas_call x3, Pallas kernels, cast_call(): pl.pallas_call(functools.partial(cast_body, size, everyone), out_shape=ja...  31.6 us
    sub x7, other arithmetic, adamw(): weight - step_rate * (update + decay_rate * weight)  23.5 us

profile of v6, /device:TPU:0, one launch (start us, length us, event | category | flops | bytes accessed | tf_op | source)
XLA Modules:
  0.0 1095.6 jit_solution(15251780236639328801)
XLA Ops:
  2.8 12.6 %shard_map.425 = s32[32,8,128]{2,1,0:T(8,128)} custom-call(s32[8,128]{1,0:T(8,128)} %pad_bitcast_fusion.2.own_ref), custom_call_target="tpu_custom_call" | custom-call | tf_op jit(solution)/shard_map/pallas_call | solution.py:548
  20.7 2.3 copy-done.18
  23.6 2.0 pad.30.refs_9_
  25.6 2.7 copy.58.refs_10_
  28.3 195.9 %shard_map.426 = (bf16[32,32,3072]{2,1,0:T(8,128)(2,1)}, bf16[32,32,4096]{2,1,0:T(8,128)(2,1)}, bf16[32,128,1024]{2,1,0:T(8,128)(2,1)}, bf16[32,32,1024]{2,1,0:T...) custom-call(bf16[32,3072]{1,0:T(8,128)(2,1)S(1)} %get-tuple-element., ...), custom_call_target="tpu_custom_call" | custom-call | tf_op jit(solution)/shard_map/pallas_call | solution.py:348
  224.2 1.3 copy-done.8
  225.6 1.3 copy-done.11
  228.2 128.6 %shard_map.427 = (bf16[256,1024]{1,0:T(8,128)(2,1)}, bf16[256,1024]{1,0:T(8,128)(2,1)}, f32[8,128]{1,0:T(8,128)}) custom-call(bf16[32,256,1024]{2,1,0:T(8,128)(2,1)} %get-tuple-element.58.refs_0_.refs_1_, bf16[32,256,1024]{2,1,0:T(8,128)(2,1)} %get-tuple-element.58.refs_0_.refs_1_), custom_call_target="tpu_custom_call" | custom-call | tf_op jit(solution)/shard_map/pallas_call | solution.py:844
  356.8 1.4 maximum_convert_fusion
  358.3 1.5 fusion.25
  359.9 1.7 multiply_reduce_fusion.14
  361.7 1.6 slice_convert_fusion
  363.3 1.5 fusion.20
  364.9 2.5 add_convert_fusion.7
  367.5 3.7 add_convert_fusion.1.query_ref.key_ref.value_ref
  371.1 10.2 shard_map.428
  381.4 1.4 fusion.88
  384.4 1.5 slice-done.3
  385.9 9.5 fusion.14
  395.6 4.6 fusion.89
  400.6 4.0 add_convert_fusion.query_ref.key_ref.value_ref
  404.6 10.0 shard_map.429
  414.7 1.4 fusion.90
  417.7 1.5 slice-done.7
  419.2 7.2 fusion.65
  426.5 8.1 fusion.91
  437.3 19.7 %shard_map.430 = (bf16[16,16,1024]{2,1,0:T(8,128)(2,1)}, bf16[16,16,1024]{2,1,0:T(8,128)(2,1)}) custom-call(bf16[16,1024]{1,0:T(8,128)(2,1)} %get-tuple-element.198.refs_0_, bf16[16,1024]{1,0:T(8,128)(2,1)} %get-tuple-element.197.refs_1_), custom_call_target="tpu_custom_call" | custom-call | tf_op jit(solution)/shard_map/pallas_call | solution.py:497
  457.0 1.3 pad_maximum_fusion
  458.3 9.1 fusion.92
  467.6 3.8 exponential_reduce_fusion
  473.9 9.1 shard_map.431
  487.1 4.7 multiply_convert_fusion.1
  491.8 9.1 fusion.93
  501.0 25.9 %shard_map.432 = (f32[16,1024]{1,0:T(8,128)}, f32[16,1024]{1,0:T(8,128)}, f32[8,128]{1,0:T(8,128)}) custom-call(f32[32,16,1024]{2,1,0:T(8,128)} %bitcast.179, f32[32,16,1024]{2,1,0:T(8,128)} %bitcast.180), custom_call_target="tpu_custom_call" | custom-call | tf_op jit(solution)/shard_map/pallas_call | solution.py:844
  526.9 2.6 scatter_custom_fusion
  529.5 3.1 multiply_reduce_fusion
  534.0 15.7 %convert_reduce_fusion = (f32[4096]{0:T(1024)S(1)}, bf16[512,4096]{1,0:T(8,128)(2,1)}) fusion(f32[512,4096]{1,0:T(8,128)} %fusion.65, f32[4096]{0:T(1024)S(1)} %get-tuple-element.191, bf16[512,1024]{1,0:T(8,128)(2,1)S(1)} %get-tuple-element.140, bf16[4096,1024]{1,0:T(8,128)(2,1)} %bitcast.216), kind=kOutput, calls=%fused_computation.25 | convolution fusion | flops 4343197696 | bytes 22052864 | tf_op jit(solution)/shard_map/dot_general | solution.py:1162
  549.7 7.0 multiply_reduce_fusion.1
  559.1 18.0 %shard_map.433 = bf16[512,3072]{1,0:T(8,128)(2,1)S(1)} custom-call(s32[1]{0:T(128)S(6)} %copy.106.length_ref, bf16[512,3072]{1,0:T(8,128)(2,1)} %copy-done.1, bf16[512,3072]{1,0:T(8,128)(2,1)} %copy-done.1, bf16[512,3072]{1,0:T(8,128)(2,1)} %copy-done.1, bf16[512,1024]{1,0:T(8,128)(2,1)S(1)} %convolution_convert_fusion.1.grad_ref), custom_call_target="tpu_custom_call" | custom-call | flops 2684354560 | bytes 8388608 | tf_op jit(solution)/shard_map/pallas_call | solution.py:961
  577.1 6.1 multiply_reduce_fusion.2
  583.9 5.8 fusion.63
  589.7 7.2 fusion.64
  596.9 13.1 %fusion.67 = bf16[4096,1024]{1,0:T(8,128)(2,1)} fusion(bf16[512,1024]{1,0:T(8,128)(2,1)S(1)} %get-tuple-element.140, f32[512,4096]{1,0:T(8,128)} %fusion.65, f32[4096]{0:T(1024)S(1)} %get-tuple-element.191), kind=kOutput, calls=%fused_computation.300 | convolution fusion | flops 4315938816 | bytes 17842176 | tf_op jit(solution)/shard_map/dot_general | solution.py:1161
  610.0 2.6 fusion.59
  614.6 1.4 fusion.66
  616.0 2.7 copy.62.refs_5_
  618.7 120.5 %shard_map.434 = (f32[32,3072]{1,0:T(8,128)}, f32[32,4096]{1,0:T(8,128)}, f32[128,1024]{1,0:T(8,128)}, f32[32,1024]{1,0:T(8,128)}, f32[8,128]{1,0:T(8,128)}, /*i...) custom-call(bf16[32,32,3072]{2,1,0:T(8,128)(2,1)} %bitcast.181, ...), custom_call_target="tpu_custom_call" | custom-call | tf_op jit(solution)/shard_map/pallas_call | solution.py:844
  739.2 3.1 multiply_reduce_fusion.3
  745.3 1.5 copy-done.10
  746.9 1.3 convolution_convert_fusion.grad_ref
  748.2 18.3 %shard_map.435 = bf16[512,3072]{1,0:T(8,128)(2,1)S(1)} custom-call(s32[1]{0:T(128)S(6)} %copy.106.length_ref, bf16[512,3072]{1,0:T(8,128)(2,1)} %copy-done, bf16[512,3072]{1,0:T(8,128)(2,1)} %copy-done, bf16[512,3072]{1,0:T(8,128)(2,1)} %copy-done, bf16[512,1024]{1,0:T(8,128)(2,1)S(1)} %convolution_convert_fusion.grad_ref), custom_call_target="tpu_custom_call" | custom-call | flops 2684354560 | bytes 8388608 | tf_op jit(solution)/shard_map/pallas_call | solution.py:961
  766.6 7.2 multiply_reduce_fusion.4
  777.2 6.8 fusion.94.refs_4_
  784.0 138.6 %shard_map.436 = (f32[1600,1024]{1,0:T(8,128)}, f32[2,32,1024]{2,1,0:T(8,128)}, f32[8,1024]{1,0:T(8,128)}) custom-call(bf16[256,1024]{1,0:T(8,128)(2,1)} %get-tuple-element.162.refs_0_, bf16[256,1024]{1,0:T(8,128)(2,1)} %get-tuple-element.161.refs_1_, s32[32,1,256]{2,1,0:T(1,128)} %get-tuple-element.194.refs_2_, s32[32,1,256]{2,1,0:T(1,128)} %get-tuple-element.193.refs_3_, ...), custom_call_target="tpu_custom_call" | custom-call | tf_op jit(solution)/shard_map/pallas_call | solution.py:448
  924.4 2.3 copy.63
  926.7 8.5 fusion.16.refs_0_
  935.2 2.6 fusion.56
  940.1 112.1 %shard_map.437 = (f32[32,3072]{1,0:T(8,128)}, f32[32,4096]{1,0:T(8,128)}, f32[128,1024]{1,0:T(8,128)}, f32[32,1024]{1,0:T(8,128)}, f32[8,128]{1,0:T(8,128)}, /*index=5*/f32[8,128]{1,0:T(8,128)}) custom-call(bf16[32,32,3072]{2,1,0:T(8,128)(2,1)} %fusion.16.refs_0_, bf16[32,32,4096]{2,1,0:T(8,128)(2,1)} %bitcast.175, bf16[32,128,1024]{2,1,0:T(8,128)(2,1)} %bitcast.176, ...), custom_call_target="tpu_custom_call" | custom-call | tf_op jit(solution)/shard_map/pallas_call | solution.py:844
  1053.5 9.9 shard_map.438
  1063.5 1.6 slice_reduce_fusion.1
  1068.0 3.1 multiply_subtract_fusion.3
  1072.6 2.3 multiply_subtract_fusion.2
  1075.7 2.3 multiply_subtract_fusion.1
  1079.4 13.5 %multiply_subtract_fusion = (f32[1572,1024]{1,0:T(8,128)}, f32[1572,1024]{1,0:T(8,128)}, f32[1572,1024]{1,0:T(8,128)}) fusion(f32[1572,1024]{1,0:T(8,128)S(1)} %bitcast.164, f32[]{:T(128)S(6)} %sub.276, f32[]{:T(128)S(6)} %div.295, f32[1600,1024]{1,0:T(8,128)} %get-tuple-element.92, f32[1572,1024]{1,0:T(8,128)} %param.51, f32[1572,1024]{1,0:T(8,128)} %param.44), kind=kLoop, calls=%fused_computation.32 | loop fusion | flops 24145920 | bytes 45072392 | tf_op jit(solution)/shard_map/sub | solution.py:1223
  (386 shorter events, 42.5 us)
Async XLA Ops:
  0.7 19.5 %copy-start.36 = (f32[2,32,4096]{2,1,0:T(8,128)S(1)}, f32[2,32,4096]{2,1,0:T(8,128)}, u32[]{:S(2)}) copy-start(f32[2,32,4096]{2,1,0:T(8,128)} %param.33) | copy-start | bytes 3145732
  228.2 136.7 %copy-start.67 = (f32[1024]{0:T(1024)}, f32[1024]{0:T(1024)S(1)}, u32[]{:S(2)}) copy-start(f32[1024]{0:T(1024)S(1)} %get-tuple-element.190) | copy-start | bytes 12292
  228.2 155.0 %copy-start.69 = (f32[1024]{0:T(1024)}, f32[1024]{0:T(1024)S(1)}, u32[]{:S(2)}) copy-start(f32[1024]{0:T(1024)S(1)} %get-tuple-element.185) | copy-start | bytes 12292
  228.2 155.0 %copy-start.83 = (f32[1024]{0:T(1024)}, f32[1024]{0:T(1024)S(1)}, u32[]{:S(2)}) copy-start(f32[1024]{0:T(1024)S(1)} %get-tuple-element.184) | copy-start | bytes 12292
  359.9 3.4 copy-start.75
  361.6 3.2 copy-start.79
  361.7 3.2 copy-start.77
  361.7 5.8 slice-start.12
  363.3 4.1 slice-start.13
  364.9 16.5 %copy-start.26 = (f32[512,1024]{1,0:T(8,128)}, f32[512,1024]{1,0:T(8,128)S(1)}, u32[]{:S(2)}) copy-start(f32[512,1024]{1,0:T(8,128)S(1)} %get-tuple-element.148) | copy-start | bytes 6291460
  371.1 10.2 copy-start
  371.1 10.2 copy-start.9
  381.4 4.6 slice-start.3
  382.8 12.7 %copy-start.13 = (f32[512,1024]{1,0:T(8,128)}, f32[512,1024]{1,0:T(8,128)S(1)}, u32[]{:S(2)}) copy-start(f32[512,1024]{1,0:T(8,128)S(1)} %get-tuple-element.212) | copy-start | bytes 6291460
  382.8 12.7 %copy-start.71 = (f32[512]{0:T(512)}, f32[512]{0:T(512)S(1)}, u32[]{:S(2)}) copy-start(f32[512]{0:T(512)S(1)} %broadcast_multiply_fusion.4) | copy-start | bytes 6148
  382.8 12.7 %slice-start.4 = ((s8[8388608]{0:T(1024)(128)(4,1)}), s8[4194304]{0:T(1024)(128)(4,1)S(1)}, s32[]{:S(2)}) async-start(s8[8388608]{0:T(1024)(128)(4,1)} %bitcast.172), calls=%async_computation.4 | async-start | bytes 8388608
  383.2 12.3 %copy-start.81 = (f32[512]{0:T(512)}, f32[512]{0:T(512)S(1)}, u32[]{:S(2)}) copy-start(f32[512]{0:T(512)S(1)} %multiply_reduce_fusion.13) | copy-start | bytes 6148
  385.9 9.5 copy-start.73
  385.9 9.6 slice-start.5
  395.5 4.7 copy-start.35
  395.5 5.1 slice-start.14
  395.5 5.0 slice-start.15
  400.2 14.5 %copy-start.28 = (f32[512,1024]{1,0:T(8,128)}, f32[512,1024]{1,0:T(8,128)S(1)}, u32[]{:S(2)}) copy-start(f32[512,1024]{1,0:T(8,128)S(1)} %get-tuple-element.216) | copy-start | bytes 6291460
  404.6 10.0 copy-start.1
  404.6 10.0 copy-start.12
  414.7 4.6 slice-start.7
  414.7 11.8 %slice-start.10 = ((s8[8388608]{0:T(1024)(128)(4,1)}), s8[4194304]{0:T(1024)(128)(4,1)S(1)}, s32[]{:S(2)}) async-start(s8[8388608]{0:T(1024)(128)(4,1)} %bitcast.217), calls=%async_computation.10 | async-start | bytes 8388608
  416.1 10.4 copy-start.30
  419.2 7.2 slice-start.11
  458.3 9.1 copy-start.47
  491.8 9.2 copy-start.42
  529.5 3.5 copy-start.23
  533.0 16.7 %slice-start.8 = ((s8[8388608]{0:T(1024)(128)(4,1)}), s8[4194304]{0:T(1024)(128)(4,1)S(1)}, s32[]{:S(2)}) async-start(s8[8388608]{0:T(1024)(128)(4,1)} %bitcast.213), calls=%async_computation.8 | async-start | bytes 8388608
  534.0 15.7 %copy-start.31 = (f32[512,1024]{1,0:T(8,128)S(1)}, f32[512,1024]{1,0:T(8,128)}, u32[]{:S(2)}) copy-start(f32[512,1024]{1,0:T(8,128)} %copy-done.30) | copy-start | bytes 6291460
  534.0 15.7 %slice-start.9 = ((s8[8388608]{0:T(1024)(128)(4,1)}), s8[4194304]{0:T(1024)(128)(4,1)S(1)}, s32[]{:S(2)}) async-start(s8[8388608]{0:T(1024)(128)(4,1)} %bitcast.213), calls=%async_computation.9 | async-start | bytes 8388608
  557.8 54.8 %copy-start.19 = (f32[512,1024]{1,0:T(8,128)}, f32[512,1024]{1,0:T(8,128)S(1)}, u32[]{:S(2)}) copy-start(f32[512,1024]{1,0:T(8,128)S(1)} %get-tuple-element.142) | copy-start | bytes 6291460
  559.1 18.0 %copy-start.29 = (f32[512,1024]{1,0:T(8,128)S(1)}, f32[512,1024]{1,0:T(8,128)}, u32[]{:S(2)}) copy-start(f32[512,1024]{1,0:T(8,128)} %copy-done.28) | copy-start | bytes 6291460
  583.9 28.8 %copy-start.21 = (f32[512,1024]{1,0:T(8,128)}, f32[512,1024]{1,0:T(8,128)S(1)}, u32[]{:S(2)}) copy-start(f32[512,1024]{1,0:T(8,128)S(1)} %get-tuple-element.156) | copy-start | bytes 6291460
  583.9 5.8 copy-start.93
  596.9 13.1 %copy-start.7 = (bf16[512,1024]{1,0:T(8,128)(2,1)S(1)}, bf16[512,1024]{1,0:T(8,128)(2,1)}, u32[]{:S(2)}) copy-start(bf16[512,1024]{1,0:T(8,128)(2,1)} %copy-done.6) | copy-start | bytes 3145732
  739.2 3.5 copy-start.32
  745.3 29.1 %copy-start.24 = (f32[512,1024]{1,0:T(8,128)}, f32[512,1024]{1,0:T(8,128)S(1)}, u32[]{:S(2)}) copy-start(f32[512,1024]{1,0:T(8,128)S(1)} %get-tuple-element.146) | copy-start | bytes 6291460
  748.2 18.3 %copy-start.27 = (f32[512,1024]{1,0:T(8,128)S(1)}, f32[512,1024]{1,0:T(8,128)}, u32[]{:S(2)}) copy-start(f32[512,1024]{1,0:T(8,128)} %copy-done.26) | copy-start | bytes 6291460
  748.2 18.3 %copy-start.68 = (f32[1024]{0:T(1024)S(1)}, f32[1024]{0:T(1024)}, u32[]{:S(2)}) copy-start(f32[1024]{0:T(1024)} %copy-done.67) | copy-start | bytes 12292
  748.2 18.3 %copy-start.76 = (f32[512]{0:T(512)S(1)}, f32[512]{0:T(512)}, u32[]{:S(2)}) copy-start(f32[512]{0:T(512)} %copy-done.75) | copy-start | bytes 6148
  748.2 18.3 %copy-start.78 = (f32[512]{0:T(512)S(1)}, f32[512]{0:T(512)}, u32[]{:S(2)}) copy-start(f32[512]{0:T(512)} %copy-done.77) | copy-start | bytes 6148
  766.5 7.2 copy-start.2
  766.5 7.2 copy-start.80
  926.7 8.5 copy-start.5
  926.7 8.5 copy-start.25
  940.1 112.8 %copy-start.91 = (f32[1,128]{1,0:T(1,128)S(1)}, f32[1,128]{1,0:T(1,128)}, u32[]{:S(2)}) copy-start(f32[1,128]{1,0:T(1,128)} %pad_bitcast_fusion.3) | copy-start | bytes 1540
  940.1 127.7 %copy-start.44 = (f32[2,32,3072]{2,1,0:T(8,128)S(1)}, f32[2,32,3072]{2,1,0:T(8,128)}, u32[]{:S(2)}) copy-start(f32[2,32,3072]{2,1,0:T(8,128)} %param.31) | copy-start | bytes 2359300
  940.1 127.7 %copy-start.53 = (f32[2,32,3072]{2,1,0:T(8,128)S(1)}, f32[2,32,3072]{2,1,0:T(8,128)}, u32[]{:S(2)}) copy-start(f32[2,32,3072]{2,1,0:T(8,128)} %param.45) | copy-start | bytes 2359300
  940.1 127.7 %copy-start.54 = (f32[2,32,3072]{2,1,0:T(8,128)S(1)}, f32[2,32,3072]{2,1,0:T(8,128)}, u32[]{:S(2)}) copy-start(f32[2,32,3072]{2,1,0:T(8,128)} %param.38) | copy-start | bytes 2359300
  1067.9 3.2 copy-start.46
  1067.9 3.2 copy-start.61
  1067.9 4.2 copy-start.49
  1067.9 4.2 copy-start.50
  1067.9 4.2 copy-start.58
  1068.0 4.2 copy-start.60
  1068.0 6.9 copy-start.59
  1071.1 3.8 copy-start.57
  1072.6 6.8 slice-start
  1075.7 3.8 slice-start.1
  (46 other events, 101.0 us)

commit v7 on v6

--- a/solution.py
+++ b/solution.py
@@ -419,7 +419,7 @@
         waiting.append((at, spot.index(turned, other, offset % size)))
 
     def tick():
-        if len(waiting) >= 4:
+        if len(waiting) >= 3:
             spread()
 
     gather_steps(size, (True, False), True, (near, rest), wholes, sems, spot, tick, ready)

time: 1110 us -> 1110 us (level)
  no operation moved by 1% of the time
where the time goes in v7:
time: 1110 us; the launch traced here: 1100 us
  Pallas kernels  829 us (75%)
  matrix products  143 us (13%)
  other arithmetic  72 us (6%)
  local copies, waits for them, and re-layouts  41.4 us (4%)
    pallas_call x4, Pallas kernels, scatter_call(): pl.pallas_call(functools.partial(scatter_body, size, half_first, across,...  388 us
    pallas_call x1, Pallas kernels, look_up_call(): pl.pallas_call(functools.partial(look_up_body, size, ring_first), out_sha...  196 us
    pallas_call x1, Pallas kernels, spread_call(): pl.pallas_call(functools.partial(spread_body, size, shared), out_shape=[j...  138 us
    pallas_call x2, Pallas kernels, attend_back(): pl.pallas_call(attend_back_body, grid=(steps,), out_shape=jax.ShapeDtypeS...  36.3 us
    pallas_call x3, Pallas kernels, cast_call(): pl.pallas_call(functools.partial(cast_body, size, everyone), out_shape=ja...  31.6 us
    sub x7, other arithmetic, adamw(): weight - step_rate * (update + decay_rate * weight)  23.5 us

profile of v7, /device:TPU:0, one launch (start us, length us, event | category | flops | bytes accessed | tf_op | source)
XLA Modules:
  0.0 1095.4 jit_solution(15540794493832164944)
XLA Ops:
  2.8 12.6 %shard_map.425 = s32[32,8,128]{2,1,0:T(8,128)} custom-call(s32[8,128]{1,0:T(8,128)} %pad_bitcast_fusion.2.own_ref), custom_call_target="tpu_custom_call" | custom-call | tf_op jit(solution)/shard_map/pallas_call | solution.py:548
  20.7 2.3 copy-done.18
  23.6 2.0 pad.30.refs_9_
  25.6 2.7 copy.58.refs_10_
  28.3 195.9 %shard_map.426 = (bf16[32,32,3072]{2,1,0:T(8,128)(2,1)}, bf16[32,32,4096]{2,1,0:T(8,128)(2,1)}, bf16[32,128,1024]{2,1,0:T(8,128)(2,1)}, bf16[32,32,1024]{2,1,0:T...) custom-call(bf16[32,3072]{1,0:T(8,128)(2,1)S(1)} %get-tuple-element., ...), custom_call_target="tpu_custom_call" | custom-call | tf_op jit(solution)/shard_map/pallas_call | solution.py:348
  224.2 1.3 copy-done.8
  225.6 1.3 copy-done.11
  228.2 128.6 %shard_map.427 = (bf16[256,1024]{1,0:T(8,128)(2,1)}, bf16[256,1024]{1,0:T(8,128)(2,1)}, f32[8,128]{1,0:T(8,128)}) custom-call(bf16[32,256,1024]{2,1,0:T(8,128)(2,1)} %get-tuple-element.58.refs_0_.refs_1_, bf16[32,256,1024]{2,1,0:T(8,128)(2,1)} %get-tuple-element.58.refs_0_.refs_1_), custom_call_target="tpu_custom_call" | custom-call | tf_op jit(solution)/shard_map/pallas_call | solution.py:844
  356.8 1.4 maximum_convert_fusion
  358.3 1.5 fusion.25
  359.9 1.7 multiply_reduce_fusion.14
  361.7 1.6 slice_convert_fusion
  363.3 1.5 fusion.20
  364.9 2.5 add_convert_fusion.7
  367.5 3.7 add_convert_fusion.1.query_ref.key_ref.value_ref
  371.1 10.2 shard_map.428
  381.4 1.4 fusion.88
  384.4 1.5 slice-done.3
  385.9 9.5 fusion.14
  395.6 4.6 fusion.89
  400.6 4.0 add_convert_fusion.query_ref.key_ref.value_ref
  404.6 10.0 shard_map.429
  414.7 1.4 fusion.90
  417.7 1.5 slice-done.7
  419.2 7.2 fusion.65
  426.5 8.1 fusion.91
  437.3 19.7 %shard_map.430 = (bf16[16,16,1024]{2,1,0:T(8,128)(2,1)}, bf16[16,16,1024]{2,1,0:T(8,128)(2,1)}) custom-call(bf16[16,1024]{1,0:T(8,128)(2,1)} %get-tuple-element.198.refs_0_, bf16[16,1024]{1,0:T(8,128)(2,1)} %get-tuple-element.197.refs_1_), custom_call_target="tpu_custom_call" | custom-call | tf_op jit(solution)/shard_map/pallas_call | solution.py:497
  457.0 1.3 pad_maximum_fusion
  458.3 9.1 fusion.92
  467.6 3.8 exponential_reduce_fusion
  473.9 9.1 shard_map.431
  487.1 4.7 multiply_convert_fusion.1
  491.8 9.1 fusion.93
  501.0 25.9 %shard_map.432 = (f32[16,1024]{1,0:T(8,128)}, f32[16,1024]{1,0:T(8,128)}, f32[8,128]{1,0:T(8,128)}) custom-call(f32[32,16,1024]{2,1,0:T(8,128)} %bitcast.179, f32[32,16,1024]{2,1,0:T(8,128)} %bitcast.180), custom_call_target="tpu_custom_call" | custom-call | tf_op jit(solution)/shard_map/pallas_call | solution.py:844
  526.9 2.6 scatter_custom_fusion
  529.5 3.1 multiply_reduce_fusion
  534.0 15.7 %convert_reduce_fusion = (f32[4096]{0:T(1024)S(1)}, bf16[512,4096]{1,0:T(8,128)(2,1)}) fusion(f32[512,4096]{1,0:T(8,128)} %fusion.65, f32[4096]{0:T(1024)S(1)} %get-tuple-element.191, bf16[512,1024]{1,0:T(8,128)(2,1)S(1)} %get-tuple-element.140, bf16[4096,1024]{1,0:T(8,128)(2,1)} %bitcast.216), kind=kOutput, calls=%fused_computation.25 | convolution fusion | flops 4343197696 | bytes 22052864 | tf_op jit(solution)/shard_map/dot_general | solution.py:1162
  549.7 7.0 multiply_reduce_fusion.1
  559.1 18.0 %shard_map.433 = bf16[512,3072]{1,0:T(8,128)(2,1)S(1)} custom-call(s32[1]{0:T(128)S(6)} %copy.106.length_ref, bf16[512,3072]{1,0:T(8,128)(2,1)} %copy-done.1, bf16[512,3072]{1,0:T(8,128)(2,1)} %copy-done.1, bf16[512,3072]{1,0:T(8,128)(2,1)} %copy-done.1, bf16[512,1024]{1,0:T(8,128)(2,1)S(1)} %convolution_convert_fusion.1.grad_ref), custom_call_target="tpu_custom_call" | custom-call | flops 2684354560 | bytes 8388608 | tf_op jit(solution)/shard_map/pallas_call | solution.py:961
  577.1 6.1 multiply_reduce_fusion.2
  583.9 5.8 fusion.63
  589.7 7.2 fusion.64
  596.9 13.1 %fusion.67 = bf16[4096,1024]{1,0:T(8,128)(2,1)} fusion(bf16[512,1024]{1,0:T(8,128)(2,1)S(1)} %get-tuple-element.140, f32[512,4096]{1,0:T(8,128)} %fusion.65, f32[4096]{0:T(1024)S(1)} %get-tuple-element.191), kind=kOutput, calls=%fused_computation.300 | convolution fusion | flops 4315938816 | bytes 17842176 | tf_op jit(solution)/shard_map/dot_general | solution.py:1161
  610.0 2.6 fusion.59
  614.6 1.4 fusion.66
  616.0 2.7 copy.62.refs_5_
  618.7 120.5 %shard_map.434 = (f32[32,3072]{1,0:T(8,128)}, f32[32,4096]{1,0:T(8,128)}, f32[128,1024]{1,0:T(8,128)}, f32[32,1024]{1,0:T(8,128)}, f32[8,128]{1,0:T(8,128)}, /*i...) custom-call(bf16[32,32,3072]{2,1,0:T(8,128)(2,1)} %bitcast.181, ...), custom_call_target="tpu_custom_call" | custom-call | tf_op jit(solution)/shard_map/pallas_call | solution.py:844
  739.2 3.1 multiply_reduce_fusion.3
  745.3 1.5 copy-done.10
  746.9 1.3 convolution_convert_fusion.grad_ref
  748.2 18.3 %shard_map.435 = bf16[512,3072]{1,0:T(8,128)(2,1)S(1)} custom-call(s32[1]{0:T(128)S(6)} %copy.106.length_ref, bf16[512,3072]{1,0:T(8,128)(2,1)} %copy-done, bf16[512,3072]{1,0:T(8,128)(2,1)} %copy-done, bf16[512,3072]{1,0:T(8,128)(2,1)} %copy-done, bf16[512,1024]{1,0:T(8,128)(2,1)S(1)} %convolution_convert_fusion.grad_ref), custom_call_target="tpu_custom_call" | custom-call | flops 2684354560 | bytes 8388608 | tf_op jit(solution)/shard_map/pallas_call | solution.py:961
  766.6 7.2 multiply_reduce_fusion.4
  777.2 6.8 fusion.94.refs_4_
  784.0 137.8 %shard_map.436 = (f32[1600,1024]{1,0:T(8,128)}, f32[2,32,1024]{2,1,0:T(8,128)}, f32[8,1024]{1,0:T(8,128)}) custom-call(bf16[256,1024]{1,0:T(8,128)(2,1)} %get-tuple-element.162.refs_0_, bf16[256,1024]{1,0:T(8,128)(2,1)} %get-tuple-element.161.refs_1_, s32[32,1,256]{2,1,0:T(1,128)} %get-tuple-element.194.refs_2_, s32[32,1,256]{2,1,0:T(1,128)} %get-tuple-element.193.refs_3_, ...), custom_call_target="tpu_custom_call" | custom-call | tf_op jit(solution)/shard_map/pallas_call | solution.py:448
  923.6 2.3 copy.63
  925.9 8.5 fusion.16.refs_0_
  934.4 2.6 fusion.56
  939.3 112.7 %shard_map.437 = (f32[32,3072]{1,0:T(8,128)}, f32[32,4096]{1,0:T(8,128)}, f32[128,1024]{1,0:T(8,128)}, f32[32,1024]{1,0:T(8,128)}, f32[8,128]{1,0:T(8,128)}, /*index=5*/f32[8,128]{1,0:T(8,128)}) custom-call(bf16[32,32,3072]{2,1,0:T(8,128)(2,1)} %fusion.16.refs_0_, bf16[32,32,4096]{2,1,0:T(8,128)(2,1)} %bitcast.175, bf16[32,128,1024]{2,1,0:T(8,128)(2,1)} %bitcast.176, ...), custom_call_target="tpu_custom_call" | custom-call | tf_op jit(solution)/shard_map/pallas_call | solution.py:844
  1053.3 10.0 shard_map.438
  1063.3 1.6 slice_reduce_fusion.1
  1067.8 3.1 multiply_subtract_fusion.3
  1072.4 2.3 multiply_subtract_fusion.2
  1075.5 2.3 multiply_subtract_fusion.1
  1079.2 13.5 %multiply_subtract_fusion = (f32[1572,1024]{1,0:T(8,128)}, f32[1572,1024]{1,0:T(8,128)}, f32[1572,1024]{1,0:T(8,128)}) fusion(f32[1572,1024]{1,0:T(8,128)S(1)} %bitcast.164, f32[]{:T(128)S(6)} %sub.276, f32[]{:T(128)S(6)} %div.295, f32[1600,1024]{1,0:T(8,128)} %get-tuple-element.92, f32[1572,1024]{1,0:T(8,128)} %param.51, f32[1572,1024]{1,0:T(8,128)} %param.44), kind=kLoop, calls=%fused_computation.32 | loop fusion | flops 24145920 | bytes 45072392 | tf_op jit(solution)/shard_map/sub | solution.py:1223
  (386 shorter events, 42.5 us)
Async XLA Ops:
  0.7 19.5 %copy-start.36 = (f32[2,32,4096]{2,1,0:T(8,128)S(1)}, f32[2,32,4096]{2,1,0:T(8,128)}, u32[]{:S(2)}) copy-start(f32[2,32,4096]{2,1,0:T(8,128)} %param.33) | copy-start | bytes 3145732
  228.2 136.7 %copy-start.67 = (f32[1024]{0:T(1024)}, f32[1024]{0:T(1024)S(1)}, u32[]{:S(2)}) copy-start(f32[1024]{0:T(1024)S(1)} %get-tuple-element.190) | copy-start | bytes 12292
  228.2 155.0 %copy-start.69 = (f32[1024]{0:T(1024)}, f32[1024]{0:T(1024)S(1)}, u32[]{:S(2)}) copy-start(f32[1024]{0:T(1024)S(1)} %get-tuple-element.185) | copy-start | bytes 12292
  228.2 155.0 %copy-start.83 = (f32[1024]{0:T(1024)}, f32[1024]{0:T(1024)S(1)}, u32[]{:S(2)}) copy-start(f32[1024]{0:T(1024)S(1)} %get-tuple-element.184) | copy-start | bytes 12292
  359.9 3.4 copy-start.75
  361.6 3.2 copy-start.79
  361.7 3.2 copy-start.77
  361.7 5.8 slice-start.12
  363.3 4.1 slice-start.13
  364.9 16.5 %copy-start.26 = (f32[512,1024]{1,0:T(8,128)}, f32[512,1024]{1,0:T(8,128)S(1)}, u32[]{:S(2)}) copy-start(f32[512,1024]{1,0:T(8,128)S(1)} %get-tuple-element.148) | copy-start | bytes 6291460
  371.1 10.2 copy-start
  371.1 10.2 copy-start.9
  381.4 4.6 slice-start.3
  382.8 12.7 %copy-start.13 = (f32[512,1024]{1,0:T(8,128)}, f32[512,1024]{1,0:T(8,128)S(1)}, u32[]{:S(2)}) copy-start(f32[512,1024]{1,0:T(8,128)S(1)} %get-tuple-element.212) | copy-start | bytes 6291460
  382.8 12.7 %copy-start.71 = (f32[512]{0:T(512)}, f32[512]{0:T(512)S(1)}, u32[]{:S(2)}) copy-start(f32[512]{0:T(512)S(1)} %broadcast_multiply_fusion.4) | copy-start | bytes 6148
  382.8 12.7 %slice-start.4 = ((s8[8388608]{0:T(1024)(128)(4,1)}), s8[4194304]{0:T(1024)(128)(4,1)S(1)}, s32[]{:S(2)}) async-start(s8[8388608]{0:T(1024)(128)(4,1)} %bitcast.172), calls=%async_computation.4 | async-start | bytes 8388608
  383.2 12.3 %copy-start.81 = (f32[512]{0:T(512)}, f32[512]{0:T(512)S(1)}, u32[]{:S(2)}) copy-start(f32[512]{0:T(512)S(1)} %multiply_reduce_fusion.13) | copy-start | bytes 6148
  385.9 9.5 copy-start.73
  385.9 9.6 slice-start.5
  395.5 4.7 copy-start.35
  395.5 5.1 slice-start.14
  395.5 5.0 slice-start.15
  400.2 14.5 %copy-start.28 = (f32[512,1024]{1,0:T(8,128)}, f32[512,1024]{1,0:T(8,128)S(1)}, u32[]{:S(2)}) copy-start(f32[512,1024]{1,0:T(8,128)S(1)} %get-tuple-element.216) | copy-start | bytes 6291460
  404.6 10.0 copy-start.1
  404.6 10.0 copy-start.12
  414.7 4.6 slice-start.7
  414.7 11.8 %slice-start.10 = ((s8[8388608]{0:T(1024)(128)(4,1)}), s8[4194304]{0:T(1024)(128)(4,1)S(1)}, s32[]{:S(2)}) async-start(s8[8388608]{0:T(1024)(128)(4,1)} %bitcast.217), calls=%async_computation.10 | async-start | bytes 8388608
  416.1 10.4 copy-start.30
  419.2 7.2 slice-start.11
  458.3 9.1 copy-start.47
  491.8 9.2 copy-start.42
  529.5 3.5 copy-start.23
  533.0 16.7 %slice-start.8 = ((s8[8388608]{0:T(1024)(128)(4,1)}), s8[4194304]{0:T(1024)(128)(4,1)S(1)}, s32[]{:S(2)}) async-start(s8[8388608]{0:T(1024)(128)(4,1)} %bitcast.213), calls=%async_computation.8 | async-start | bytes 8388608
  534.0 15.7 %copy-start.31 = (f32[512,1024]{1,0:T(8,128)S(1)}, f32[512,1024]{1,0:T(8,128)}, u32[]{:S(2)}) copy-start(f32[512,1024]{1,0:T(8,128)} %copy-done.30) | copy-start | bytes 6291460
  534.0 15.7 %slice-start.9 = ((s8[8388608]{0:T(1024)(128)(4,1)}), s8[4194304]{0:T(1024)(128)(4,1)S(1)}, s32[]{:S(2)}) async-start(s8[8388608]{0:T(1024)(128)(4,1)} %bitcast.213), calls=%async_computation.9 | async-start | bytes 8388608
  557.8 54.8 %copy-start.19 = (f32[512,1024]{1,0:T(8,128)}, f32[512,1024]{1,0:T(8,128)S(1)}, u32[]{:S(2)}) copy-start(f32[512,1024]{1,0:T(8,128)S(1)} %get-tuple-element.142) | copy-start | bytes 6291460
  559.1 18.0 %copy-start.29 = (f32[512,1024]{1,0:T(8,128)S(1)}, f32[512,1024]{1,0:T(8,128)}, u32[]{:S(2)}) copy-start(f32[512,1024]{1,0:T(8,128)} %copy-done.28) | copy-start | bytes 6291460
  583.9 28.8 %copy-start.21 = (f32[512,1024]{1,0:T(8,128)}, f32[512,1024]{1,0:T(8,128)S(1)}, u32[]{:S(2)}) copy-start(f32[512,1024]{1,0:T(8,128)S(1)} %get-tuple-element.156) | copy-start | bytes 6291460
  583.9 5.8 copy-start.93
  596.9 13.1 %copy-start.7 = (bf16[512,1024]{1,0:T(8,128)(2,1)S(1)}, bf16[512,1024]{1,0:T(8,128)(2,1)}, u32[]{:S(2)}) copy-start(bf16[512,1024]{1,0:T(8,128)(2,1)} %copy-done.6) | copy-start | bytes 3145732
  739.2 3.5 copy-start.32
  745.3 29.1 %copy-start.24 = (f32[512,1024]{1,0:T(8,128)}, f32[512,1024]{1,0:T(8,128)S(1)}, u32[]{:S(2)}) copy-start(f32[512,1024]{1,0:T(8,128)S(1)} %get-tuple-element.146) | copy-start | bytes 6291460
  748.2 18.3 %copy-start.27 = (f32[512,1024]{1,0:T(8,128)S(1)}, f32[512,1024]{1,0:T(8,128)}, u32[]{:S(2)}) copy-start(f32[512,1024]{1,0:T(8,128)} %copy-done.26) | copy-start | bytes 6291460
  748.2 18.3 %copy-start.68 = (f32[1024]{0:T(1024)S(1)}, f32[1024]{0:T(1024)}, u32[]{:S(2)}) copy-start(f32[1024]{0:T(1024)} %copy-done.67) | copy-start | bytes 12292
  748.2 18.3 %copy-start.76 = (f32[512]{0:T(512)S(1)}, f32[512]{0:T(512)}, u32[]{:S(2)}) copy-start(f32[512]{0:T(512)} %copy-done.75) | copy-start | bytes 6148
  748.2 18.3 %copy-start.78 = (f32[512]{0:T(512)S(1)}, f32[512]{0:T(512)}, u32[]{:S(2)}) copy-start(f32[512]{0:T(512)} %copy-done.77) | copy-start | bytes 6148
  766.5 7.2 copy-start.2
  766.5 7.2 copy-start.80
  925.9 8.5 copy-start.5
  925.9 8.5 copy-start.25
  939.3 113.4 %copy-start.91 = (f32[1,128]{1,0:T(1,128)S(1)}, f32[1,128]{1,0:T(1,128)}, u32[]{:S(2)}) copy-start(f32[1,128]{1,0:T(1,128)} %pad_bitcast_fusion.3) | copy-start | bytes 1540
  939.3 128.4 %copy-start.44 = (f32[2,32,3072]{2,1,0:T(8,128)S(1)}, f32[2,32,3072]{2,1,0:T(8,128)}, u32[]{:S(2)}) copy-start(f32[2,32,3072]{2,1,0:T(8,128)} %param.31) | copy-start | bytes 2359300
  939.3 128.4 %copy-start.53 = (f32[2,32,3072]{2,1,0:T(8,128)S(1)}, f32[2,32,3072]{2,1,0:T(8,128)}, u32[]{:S(2)}) copy-start(f32[2,32,3072]{2,1,0:T(8,128)} %param.45) | copy-start | bytes 2359300
  939.3 128.4 %copy-start.54 = (f32[2,32,3072]{2,1,0:T(8,128)S(1)}, f32[2,32,3072]{2,1,0:T(8,128)}, u32[]{:S(2)}) copy-start(f32[2,32,3072]{2,1,0:T(8,128)} %param.38) | copy-start | bytes 2359300
  1067.7 3.2 copy-start.46
  1067.7 3.2 copy-start.61
  1067.8 4.2 copy-start.49
  1067.8 4.2 copy-start.50
  1067.8 4.2 copy-start.58
  1067.8 4.2 copy-start.60
  1067.8 6.9 copy-start.59
  1071.0 3.8 copy-start.57
  1072.4 6.8 slice-start
  1075.5 3.8 slice-start.1
  (46 other events, 101.0 us)
